TPU v7x, 32 devices: a whole 2x2x4 slice. The times are simulated.
32 devices in a mesh: ctx: 16 (over z, x, core), tp: 2 (over y).
Axes of the slice: x: 2, y: 2, z: 4, core: 2. Of those that a mesh axis runs over, the one named last changes fastest.
Arguments:
- layer_input: bfloat16 [2048, 2560], P('ctx'), may hold values from -6 to 6
- first_gain: bfloat16 [2560], P('ctx'), may hold values from 0.5 to 1.5
- query_down: bfloat16 [2560, 768], P('ctx'), may hold values from -0.125 to 0.125
- query_gain: bfloat16 [768], P('ctx'), may hold values from 0.5 to 1.5
- query_up: bfloat16 [768, 3840], P('ctx', 'tp'), may hold values from -0.21875 to 0.21875
- latent_down: bfloat16 [2560, 288], P('ctx'), may hold values from -0.125 to 0.125
- latent_gain: bfloat16 [256], P('ctx'), may hold values from 0.5 to 1.5
- latent_up: bfloat16 [256, 5120], P('ctx', 'tp'), may hold values from -0.375 to 0.375
- out_weight: bfloat16 [2560, 2560], P('tp', 'ctx'), may hold values from -12 to 12
- second_gain: bfloat16 [2560], P('ctx'), may hold values from 0.5 to 1.5
- gate_weight: bfloat16 [2560, 6400], P('ctx', 'tp'), may hold values from -0.125 to 0.125
- up_weight: bfloat16 [2560, 6400], P('ctx', 'tp'), may hold values from -0.125 to 0.125
- down_weight: bfloat16 [6400, 2560], P('tp', 'ctx'), may hold values from -0.4375 to 0.4375
- out_grad: bfloat16 [2048, 2560], P('ctx'), may hold values from -6 to 6
Outputs:
- layer_output: bfloat16 [2048, 2560], P('ctx')
- input_grad: float32 [2048, 2560], P('ctx')
- first_gain_grad: float32 [2560], P('ctx')
- query_down_grad: float32 [2560, 768], P('ctx')
- query_gain_grad: float32 [768], P('ctx')
- query_up_grad: float32 [768, 3840], P('ctx', 'tp')
- latent_down_grad: float32 [2560, 288], P('ctx')
- latent_gain_grad: float32 [256], P('ctx')
- latent_up_grad: float32 [256, 5120], P('ctx', 'tp')
- out_weight_grad: float32 [2560, 2560], P('tp', 'ctx')
- second_gain_grad: float32 [2560], P('ctx')
- gate_weight_grad: float32 [2560, 6400], P('ctx', 'tp')
- up_weight_grad: float32 [2560, 6400], P('ctx', 'tp')
- down_weight_grad: float32 [6400, 2560], P('tp', 'ctx')
All inputs are finite; a program needn't handle non-finite values.
Results may differ from a plain program's by a relative error of at most 0.03.
Values may be sent and summed in bfloat16 or wider, within the bound.
A program may use at most 320 MiB of HBM per device.

v0:
```python
import math

import jax
import jax.numpy as jnp
from jax import lax
from jax.sharding import PartitionSpec as P

H = 40
KVR = 256
NOPE = 64
ROPE = 32
VH = 64


eps_norm = 1e-06
residual_scale = 1.4 / math.sqrt(62.0)
rope_base = 10000.0


def matmul(left_side, right_side):
    return jnp.dot(left_side, right_side, preferred_element_type=jnp.float32)


def rms_norm(values, scale_gain):
    factor = lax.rsqrt(jnp.mean(values * values, axis=-1, keepdims=True) + eps_norm)
    return values * factor * scale_gain


def norm_back(values, scale_gain, upstream):
    factor = lax.rsqrt(jnp.mean(values * values, axis=-1, keepdims=True) + eps_norm)
    scaled = upstream * scale_gain
    inner_sum = jnp.mean(scaled * values, axis=-1, keepdims=True)
    grad_values = factor * scaled - values * factor * factor * factor * inner_sum
    grad_gain = jnp.sum(upstream * values * factor, axis=0)
    return (grad_values, grad_gain)


def rotate(values, cosine, sine_table):
    half_width = values.shape[-1] // 2
    first_half = values[..., :half_width]
    second_half = values[..., half_width:]
    return jnp.concatenate(
        [
            first_half * cosine - second_half * sine_table,
            second_half * cosine + first_half * sine_table,
        ],
        axis=-1,
    )


def rope_tables(positions):
    frequency = rope_base ** (-jnp.arange(ROPE // 2, dtype=jnp.float32) / (ROPE // 2))
    angles = positions.astype(jnp.float32)[:, None] * frequency[None, :]
    return (jnp.cos(angles), jnp.sin(angles))


def score_block(queries, keys_nope, key_rope):
    nope_part = jnp.einsum(
        "qhd,khd->hqk", queries[..., :NOPE], keys_nope, preferred_element_type=jnp.float32
    )
    rope_part = jnp.einsum(
        "qhd,kd->hqk", queries[..., NOPE:], key_rope, preferred_element_type=jnp.float32
    )
    return (nope_part + rope_part) * (NOPE + ROPE) ** (-0.5)


def shards(
    layer_input,
    first_gain,
    query_down,
    query_gain,
    query_up,
    latent_down,
    latent_gain,
    latent_up,
    out_weight,
    second_gain,
    gate_weight,
    up_weight,
    down_weight,
    out_grad,
):
    full_rows = (
        lax.all_gather(first_gain, "ctx", axis=0, tiled=True),
        lax.all_gather(query_down, "ctx", axis=0, tiled=True),
        lax.all_gather(query_gain, "ctx", axis=0, tiled=True),
        lax.all_gather(query_up, "ctx", axis=0, tiled=True),
        lax.all_gather(latent_down, "ctx", axis=0, tiled=True),
        lax.all_gather(latent_gain, "ctx", axis=0, tiled=True),
        lax.all_gather(latent_up, "ctx", axis=0, tiled=True),
        lax.all_gather(second_gain, "ctx", axis=0, tiled=True),
        lax.all_gather(gate_weight, "ctx", axis=0, tiled=True),
        lax.all_gather(up_weight, "ctx", axis=0, tiled=True),
    )
    (
        full_first_gain,
        full_query_down,
        full_query_gain,
        full_query_up,
        full_latent_down,
        full_latent_gain,
        full_latent_up,
        full_second_gain,
        full_gate,
        full_up,
    ) = full_rows
    full_out, full_down = (
        lax.all_gather(out_weight, "ctx", axis=1, tiled=True),
        lax.all_gather(down_weight, "ctx", axis=1, tiled=True),
    )
    gain_first = full_first_gain.astype(jnp.float32)
    gain_query = full_query_gain.astype(jnp.float32)
    gain_latent = full_latent_gain.astype(jnp.float32)
    gain_second = full_second_gain.astype(jnp.float32)
    local_rows = layer_input.shape[0]
    local_heads = H // lax.axis_size("tp")
    total_rows = local_rows * lax.axis_size("ctx")
    first_row = lax.axis_index("ctx") * local_rows
    positions = first_row + jnp.arange(local_rows, dtype=jnp.int32)
    last_row = first_row + local_rows - 1
    cosine, sine_table = rope_tables(positions)
    inputs_wide = layer_input.astype(jnp.float32)
    normed = rms_norm(inputs_wide, gain_first).astype(jnp.bfloat16)
    query_latent = matmul(normed, full_query_down)
    query_normed = rms_norm(query_latent, gain_query).astype(jnp.bfloat16)
    queries_raw = matmul(query_normed, full_query_up).reshape(local_rows, local_heads, NOPE + ROPE)
    queries = jnp.concatenate(
        [
            queries_raw[..., :NOPE],
            rotate(queries_raw[..., NOPE:], cosine[:, None, :], sine_table[:, None, :]),
        ],
        axis=-1,
    ).astype(jnp.bfloat16)
    compressed = matmul(normed, full_latent_down)
    latent = rms_norm(compressed[:, :KVR], gain_latent).astype(jnp.bfloat16)
    key_rope = rotate(compressed[:, KVR:], cosine, sine_table).astype(jnp.bfloat16)

    def expand(latent_rows):
        return (
            matmul(latent_rows, full_latent_up)
            .astype(jnp.bfloat16)
            .reshape(latent_rows.shape[0], local_heads, NOPE + VH)
        )

    def reshape_rows(key_rows):
        return key_rows.reshape(key_rows.shape[0], local_heads, NOPE + VH)

    def online(carried, key_rows, rope_rows, key_start):
        running_top, running_sum, running_out = carried
        scores = score_block(queries, key_rows[..., :NOPE], rope_rows)
        allowed = (key_start + jnp.arange(key_rows.shape[0], dtype=jnp.int32))[
            None, :
        ] <= positions[:, None]
        scores = jnp.where(allowed[None], scores, -1e30)
        new_top = jnp.maximum(running_top, jnp.max(scores, axis=-1))
        weights = jnp.where(allowed[None], jnp.exp(scores - new_top[..., None]), 0.0)
        decay_factor = jnp.exp(running_top - new_top)
        running_sum = running_sum * decay_factor + jnp.sum(weights, axis=-1)
        running_out = running_out * decay_factor[..., None] + jnp.einsum(
            "hqk,khd->hqd",
            weights.astype(jnp.bfloat16),
            key_rows[..., NOPE:],
            preferred_element_type=jnp.float32,
        )
        return (new_top, running_sum, running_out)

    start_state = (
        jnp.full((local_heads, local_rows), -1e30, jnp.float32),
        jnp.zeros((local_heads, local_rows), jnp.float32),
        jnp.zeros((local_heads, local_rows, VH), jnp.float32),
    )
    own_keys = matmul(latent, full_latent_up).astype(jnp.bfloat16)
    key_rows = lax.all_gather(own_keys, "ctx", axis=0, tiled=True)
    rope_rows = lax.all_gather(key_rope, "ctx", axis=0, tiled=True)
    piece_rows = key_rows.shape[0]
    fold_block_width = math.gcd(piece_rows, 512)

    def step_block(block_index, carry_state):
        key_start = block_index * fold_block_width
        rows_part = lax.dynamic_slice_in_dim(
            key_rows, block_index * fold_block_width, fold_block_width, 0
        )
        rope_part = lax.dynamic_slice_in_dim(
            rope_rows, block_index * fold_block_width, fold_block_width, 0
        )
        return lax.cond(
            key_start <= last_row,
            lambda inner_state: online(inner_state, reshape_rows(rows_part), rope_part, key_start),
            lambda inner_state: inner_state,
            carry_state,
        )

    running_top, running_sum, running_out = lax.fori_loop(
        0, piece_rows // fold_block_width, step_block, start_state
    )
    log_total = running_top + jnp.log(running_sum)
    attended_wide = running_out / running_sum[..., None]
    attended = (
        jnp.transpose(attended_wide, (1, 0, 2))
        .reshape(local_rows, local_heads * VH)
        .astype(jnp.bfloat16)
    )
    branch = lax.psum(matmul(attended, full_out).astype(jnp.bfloat16), "tp").astype(jnp.float32)
    middle = inputs_wide + residual_scale * branch
    normed_second = rms_norm(middle, gain_second).astype(jnp.bfloat16)
    gate_values = matmul(normed_second, full_gate)
    up_values = matmul(normed_second, full_up)
    sigmoid_gate = jax.nn.sigmoid(gate_values)
    hidden = (gate_values * sigmoid_gate * up_values).astype(jnp.bfloat16)
    ffn_sum = lax.psum(matmul(hidden, full_down).astype(jnp.bfloat16), "tp").astype(jnp.float32)
    layer_output = (middle + residual_scale * ffn_sum).astype(jnp.bfloat16)
    grad_out = out_grad.astype(jnp.float32)
    grad_ffn = (residual_scale * grad_out).astype(jnp.bfloat16)
    down_full = matmul(hidden.T, grad_ffn)
    grad_hidden = matmul(grad_ffn, full_down.T)
    grad_gate = (
        grad_hidden * up_values * sigmoid_gate * (1.0 + gate_values * (1.0 - sigmoid_gate))
    ).astype(jnp.bfloat16)
    grad_up = (grad_hidden * gate_values * sigmoid_gate).astype(jnp.bfloat16)
    gate_full = matmul(normed_second.T, grad_gate)
    up_full = matmul(normed_second.T, grad_up)
    grad_second = lax.psum(
        (matmul(grad_gate, full_gate.T) + matmul(grad_up, full_up.T)).astype(jnp.bfloat16), "tp"
    ).astype(jnp.float32)
    grad_middle_part, second_full = norm_back(middle, gain_second, grad_second)
    grad_middle = grad_out + grad_middle_part
    second_gain_grad, gate_weight_grad, up_weight_grad = (
        lax.psum_scatter(second_full, "ctx", scatter_dimension=0, tiled=True),
        lax.psum_scatter(gate_full, "ctx", scatter_dimension=0, tiled=True),
        lax.psum_scatter(up_full, "ctx", scatter_dimension=0, tiled=True),
    )
    down_weight_grad = lax.psum_scatter(down_full, "ctx", scatter_dimension=1, tiled=True)
    grad_branch = (residual_scale * grad_middle).astype(jnp.bfloat16)
    out_full = matmul(attended.T, grad_branch)
    grad_attended = (
        matmul(grad_branch, full_out.T).reshape(local_rows, local_heads, VH).astype(jnp.bfloat16)
    )
    row_inner = jnp.einsum("qhd,hqd->hq", grad_attended.astype(jnp.float32), attended_wide)
    all_latent, all_rope = (
        lax.all_gather(latent, "ctx", axis=0, tiled=True),
        lax.all_gather(key_rope, "ctx", axis=0, tiled=True),
    )
    block_width = min(512, total_rows)
    live_blocks = last_row // block_width + 1

    def back_block(block_index, carried):
        grad_queries, grad_latent, grad_rope, latent_up_full = carried
        key_start = block_index * block_width
        latent_block = lax.dynamic_slice_in_dim(all_latent, key_start, block_width, 0)
        rope_block = lax.dynamic_slice_in_dim(all_rope, key_start, block_width, 0)
        expanded = expand(latent_block)
        keys_nope = expanded[..., :NOPE]
        values = expanded[..., NOPE:]
        scores = score_block(queries, keys_nope, rope_block)
        allowed = (key_start + jnp.arange(block_width, dtype=jnp.int32))[None, :] <= positions[
            :, None
        ]
        probs = jnp.where(allowed[None], jnp.exp(scores - log_total[..., None]), 0.0)
        grad_probs = jnp.einsum(
            "qhd,khd->hqk", grad_attended, values, preferred_element_type=jnp.float32
        )
        grad_scores = (probs * (grad_probs - row_inner[..., None])).astype(jnp.bfloat16)
        score_scale = (NOPE + ROPE) ** (-0.5)
        query_nope_part = jnp.einsum(
            "hqk,khd->qhd", grad_scores, keys_nope, preferred_element_type=jnp.float32
        )
        query_rope_part = jnp.einsum(
            "hqk,kd->qhd", grad_scores, rope_block, preferred_element_type=jnp.float32
        )
        grad_queries = grad_queries + score_scale * jnp.concatenate(
            [query_nope_part, query_rope_part], axis=-1
        )
        grad_keys = score_scale * jnp.einsum(
            "hqk,qhd->khd", grad_scores, queries[..., :NOPE], preferred_element_type=jnp.float32
        )
        grad_rope_block = score_scale * jnp.einsum(
            "hqk,qhd->kd", grad_scores, queries[..., NOPE:], preferred_element_type=jnp.float32
        )
        grad_values = jnp.einsum(
            "hqk,qhd->khd",
            probs.astype(jnp.bfloat16),
            grad_attended,
            preferred_element_type=jnp.float32,
        )
        grad_expanded = (
            jnp.concatenate([grad_keys, grad_values], axis=-1)
            .reshape(block_width, local_heads * (NOPE + VH))
            .astype(jnp.bfloat16)
        )
        grad_latent_block = matmul(grad_expanded, full_latent_up.T)
        latent_up_full = latent_up_full + matmul(latent_block.T, grad_expanded)
        grad_latent = lax.dynamic_update_slice_in_dim(
            grad_latent,
            lax.dynamic_slice_in_dim(grad_latent, key_start, block_width, 0) + grad_latent_block,
            key_start,
            0,
        )
        grad_rope = lax.dynamic_update_slice_in_dim(
            grad_rope,
            lax.dynamic_slice_in_dim(grad_rope, key_start, block_width, 0) + grad_rope_block,
            key_start,
            0,
        )
        return (grad_queries, grad_latent, grad_rope, latent_up_full)

    back_start = (
        jnp.zeros((local_rows, local_heads, NOPE + ROPE), jnp.float32),
        jnp.zeros((total_rows, KVR), jnp.float32),
        jnp.zeros((total_rows, ROPE), jnp.float32),
        jnp.zeros((KVR, local_heads * (NOPE + VH)), jnp.float32),
    )
    grad_queries, grad_latent, grad_rope, latent_up_full = lax.fori_loop(
        0, live_blocks, back_block, back_start
    )
    grad_query_rows = (
        jnp.concatenate(
            [
                grad_queries[..., :NOPE],
                rotate(grad_queries[..., NOPE:], cosine[:, None, :], -sine_table[:, None, :]),
            ],
            axis=-1,
        )
        .reshape(local_rows, local_heads * (NOPE + ROPE))
        .astype(jnp.bfloat16)
    )
    query_up_full = matmul(query_normed.T, grad_query_rows)
    grad_query_normed = matmul(grad_query_rows, full_query_up.T)
    own_latent, own_rope = (
        lax.psum_scatter(grad_latent, "ctx", scatter_dimension=0, tiled=True),
        lax.psum_scatter(grad_rope, "ctx", scatter_dimension=0, tiled=True),
    )
    grad_query_normed, own_latent, own_rope = (
        lax.psum(grad_query_normed.astype(jnp.bfloat16), "tp").astype(jnp.float32),
        lax.psum(own_latent.astype(jnp.bfloat16), "tp").astype(jnp.float32),
        lax.psum(own_rope.astype(jnp.bfloat16), "tp").astype(jnp.float32),
    )
    grad_query_latent, query_gain_full = norm_back(query_latent, gain_query, grad_query_normed)
    grad_query_latent = grad_query_latent.astype(jnp.bfloat16)
    grad_latent_rows, latent_gain_full = norm_back(compressed[:, :KVR], gain_latent, own_latent)
    grad_compressed = jnp.concatenate(
        [grad_latent_rows, rotate(own_rope, cosine, -sine_table)], axis=-1
    ).astype(jnp.bfloat16)
    query_down_full = matmul(normed.T, grad_query_latent)
    latent_down_full = matmul(normed.T, grad_compressed)
    grad_normed = matmul(grad_query_latent, full_query_down.T) + matmul(
        grad_compressed, full_latent_down.T
    )
    grad_input_part, first_gain_full = norm_back(inputs_wide, gain_first, grad_normed)
    input_grad = grad_middle + grad_input_part
    attn_grads = (
        lax.psum_scatter(first_gain_full, "ctx", scatter_dimension=0, tiled=True),
        lax.psum_scatter(query_down_full, "ctx", scatter_dimension=0, tiled=True),
        lax.psum_scatter(query_gain_full, "ctx", scatter_dimension=0, tiled=True),
        lax.psum_scatter(query_up_full, "ctx", scatter_dimension=0, tiled=True),
        lax.psum_scatter(latent_down_full, "ctx", scatter_dimension=0, tiled=True),
        lax.psum_scatter(latent_gain_full, "ctx", scatter_dimension=0, tiled=True),
        lax.psum_scatter(latent_up_full, "ctx", scatter_dimension=0, tiled=True),
    )
    (
        first_gain_grad,
        query_down_grad,
        query_gain_grad,
        query_up_grad,
        latent_down_grad,
        latent_gain_grad,
        latent_up_grad,
    ) = attn_grads
    out_weight_grad = lax.psum_scatter(out_full, "ctx", scatter_dimension=1, tiled=True)
    return (
        layer_output,
        input_grad,
        first_gain_grad,
        query_down_grad,
        query_gain_grad,
        query_up_grad,
        latent_down_grad,
        latent_gain_grad,
        latent_up_grad,
        out_weight_grad,
        second_gain_grad,
        gate_weight_grad,
        up_weight_grad,
        down_weight_grad,
    )


def solution(mesh):
    return jax.shard_map(
        shards,
        mesh=mesh,
        in_specs=(
            P("ctx", None),
            P("ctx"),
            P("ctx", None),
            P("ctx"),
            P("ctx", "tp"),
            P("ctx", None),
            P("ctx"),
            P("ctx", "tp"),
            P("tp", "ctx"),
            P("ctx"),
            P("ctx", "tp"),
            P("ctx", "tp"),
            P("tp", "ctx"),
            P("ctx", None),
        ),
        out_specs=(
            P("ctx", None),
            P("ctx", None),
            P("ctx"),
            P("ctx", None),
            P("ctx"),
            P("ctx", "tp"),
            P("ctx", None),
            P("ctx"),
            P("ctx", "tp"),
            P("tp", "ctx"),
            P("ctx"),
            P("ctx", "tp"),
            P("ctx", "tp"),
            P("tp", "ctx"),
        ),
        check_vma=False,
    )
```

profile of v0, /device:TPU:3, one launch (start us, length us, event | category | flops | bytes accessed | tf_op | source)
XLA Modules:
  0.0 2661.4 jit_solution(13575127916568309027)
XLA Ops:
  16.7 53.1 %all-reduce.9 = (bf16[2560]{0:T(1024)(128)(2,1)S(1)}, bf16[2560]{0:T(1024)(128)(2,1)S(1)}, bf16[256]{0:T(256)(128)(2,1)S(1)}, bf16[768]{0:T(1024)(128)(2,1)S(1)}) all-reduce(bf16[2560]{0:T(1024)(128)(2,1)S(1)} %dynamic-update-slice.3, bf16[2560]{0:T(1024)(128)(2,1)S(1)} %dynamic-update-slice, ...), channel_id=1, replica_groups=mesh['ctx'=16,'tp'=2] {'ctx'}, use_global_device_ids=true, to_apply=%add.3 | all-reduce | flops 6144 | bytes 24576
  95.9 19.2 all_gather.54
  115.0 27.3 %all-gather.17.cloned.1.call-done = bf16[2560,768]{1,0:T(8,128)(2,1)} async-done(((bf16[160,768]{1,0:T(8,128)(2,1)}), bf16[2560,768]{1,0:T(8,128)(2,1)}) %all-gather.17.cloned.1.call-update) | async-done | bytes 3932176 | tf_op jit(solution)/shard_map/all_gather | solution.py:85
  145.3 43.0 %all-gather.19.cloned.1.call-done = bf16[768,1920]{1,0:T(8,128)(2,1)} async-done(((bf16[48,1920]{1,0:T(8,128)(2,1)}), bf16[768,1920]{1,0:T(8,128)(2,1)}) %all-gather.19.cloned.1.call-update) | async-done | bytes 2949136 | tf_op jit(solution)/shard_map/all_gather | solution.py:87
  191.7 85.6 %all-gather.15.cloned.1.call-done = bf16[2048,2560]{1,0:T(8,128)(2,1)} async-done(((bf16[128,2560]{1,0:T(8,128)(2,1)}), bf16[2048,2560]{1,0:T(8,128)(2,1)}) %all-gather.15.cloned.1.call-update) | async-done | bytes 10485776 | tf_op jit(solution)/shard_map/all_gather | solution.py:173
  298.6 42.4 %all-gather.21.cloned.1.call-done = bf16[1280,2560]{0,1:T(8,128)(2,1)} async-done(((bf16[1280,160]{0,1:T(8,128)(2,1)}), bf16[1280,2560]{0,1:T(8,128)(2,1)}) %all-gather.21.cloned.1.call-update) | async-done | bytes 6553616 | tf_op jit(solution)/shard_map/all_gather | solution.py:108
  349.3 28.4 %all-reduce.15.cloned.1.call-done = bf16[128,2560]{1,0:T(8,128)(2,1)} async-done(((bf16[128,2560]{1,0:T(8,128)(2,1)}), bf16[128,2560]{1,0:T(8,128)(2,1)}) %all-reduce.15.cloned.1.call-update) | async-done | bytes 655376 | tf_op jit(solution)/shard_map/psum | solution.py:203
  379.5 124.6 %all-gather.23.cloned.1.call-done = bf16[2560,3200]{1,0:T(8,128)(2,1)} async-done(((bf16[160,3200]{1,0:T(8,128)(2,1)}), bf16[2560,3200]{1,0:T(8,128)(2,1)}) %all-gather.23.cloned.1.call-update) | async-done | bytes 16384016 | tf_op jit(solution)/shard_map/all_gather | solution.py:92
  513.3 115.9 %all-gather.25.cloned.1.call-done = bf16[2560,3200]{1,0:T(8,128)(2,1)} async-done(((bf16[160,3200]{1,0:T(8,128)(2,1)}), bf16[2560,3200]{1,0:T(8,128)(2,1)}) %all-gather.25.cloned.1.call-update) | async-done | bytes 16384016 | tf_op jit(solution)/shard_map/all_gather | solution.py:93
  638.5 115.7 %all-gather.27.cloned.1.call-done = bf16[3200,2560]{0,1:T(8,128)(2,1)} async-done(((bf16[3200,160]{0,1:T(8,128)(2,1)}), bf16[3200,2560]{0,1:T(8,128)(2,1)}) %all-gather.27.cloned.1.call-update) | async-done | bytes 16384016 | tf_op jit(solution)/shard_map/all_gather | solution.py:109
  777.3 23.7 fusion.63
  801.6 29.7 %all-reduce.17.cloned.1.call-done = bf16[128,2560]{1,0:T(8,128)(2,1)} async-done(((bf16[128,2560]{1,0:T(8,128)(2,1)}), bf16[128,2560]{1,0:T(8,128)(2,1)}) %all-reduce.17.cloned.1.call-update) | async-done | bytes 655376 | tf_op jit(solution)/shard_map/psum | solution.py:222
  840.8 30.2 %all-gather.29.cloned.1.call-done = bf16[2048,256]{0,1:T(8,128)(2,1)} async-done(((bf16[128,256]{0,1:T(8,128)(2,1)}), bf16[2048,256]{0,1:T(8,128)(2,1)}) %all-gather.29.cloned.1.call-update) | async-done | bytes 1048592 | tf_op jit(solution)/shard_map/all_gather | solution.py:240
  876.1 38.3 %while.36 = (s32[]{:T(128)}, f32[128,20,96]{0,2,1:T(8,128)}, f32[2048,256]{0,1:T(8,128)}, f32[2048,32]{0,1:T(8,128)}, f32[256,2560]{1,0:T(8,128)}, /*index=5*/s3...) while((s32[]{:T(128)}, f32[128,20,96]{0,2,1:T(8,128)}, ...), condition=%wide.region_15.16_spmd.clone, body=%wide.region_14.15_spmd.clone.sunk | while | flops 3124412928 | bytes 123106680 | solution.py:312
  927.5 154.2 %reduce-scatter.13.cloned.1.call-done = f32[128,32]{0,1:T(8,128)} async-done(((f32[2048,32]{0,1:T(8,128)}), f32[128,32]{0,1:T(8,128)}) %reduce-scatter.13.cloned.1.call-update) | async-done | bytes 16400 | tf_op jit(solution)/shard_map/reduce_scatter | solution.py:330
  1090.2 55.6 %reduce-scatter.11.cloned.1.call-done = f32[128,256]{0,1:T(8,128)} async-done(((f32[2048,256]{0,1:T(8,128)}), f32[128,256]{0,1:T(8,128)}) %reduce-scatter.11.cloned.1.call-update) | async-done | bytes 131088 | tf_op jit(solution)/shard_map/reduce_scatter | solution.py:329
  1148.0 39.5 %all-reduce.19.cloned.1.call-done = (bf16[128,2560]{1,0:T(8,128)(2,1)}, bf16[128,768]{1,0:T(8,128)(2,1)}, bf16[128,256]{0,1:T(8,128)(2,1)}) async-done(((bf16[128,2560]{1,0:T(8,128)(2,1)}, bf16[128,768]{1,0:T(8,128)(2,1)}, bf16[128,256]{0,1:T(8,128)(2,1)}), (bf16[128,2560]{1,0:T(8,128)(2,1)}, bf16[128,768]{1,0:T(8,128)(2,1)}, bf16[128,256]{0,1:T(8,128)(2,1)})) %all-reduce.19.cloned.1.call-update) | async-done | bytes 917520 | tf_op jit(solution)/shard_map/psum | solution.py:210
  1265.8 53.2 %all-reduce.8 = (f32[2560]{0:T(1024)S(1)}, f32[768]{0:T(1024)S(1)}, f32[256]{0:T(256)S(1)}, f32[2560]{0:T(1024)S(1)}) all-reduce(f32[2560]{0:T(1024)S(1)} %get-tuple-element.496, f32[768]{0:T(1024)S(1)} %copy-done.46, f32[256]{0:T(256)S(1)} %copy-done.56, f32[2560]{0:T(1024)S(1)} %copy-done.38), channel_id=4, replica_groups=mesh['ctx'=16,'tp'=2] {'ctx'}, use_global_device_ids=true, to_apply=%region_25.26.clone | all-reduce | flops 6144 | bytes 49152
  1328.1 87.7 %reduce-scatter.17.cloned.1.call-done = f32[48,1920]{1,0:T(8,128)} async-done(((f32[768,1920]{1,0:T(8,128)}), f32[48,1920]{1,0:T(8,128)}) %reduce-scatter.17.cloned.1.call-update) | async-done | bytes 368656 | tf_op jit(solution)/shard_map/reduce_scatter | solution.py:354
  1415.8 99.4 %reduce-scatter.15.cloned.1.call-done = f32[160,768]{1,0:T(8,128)} async-done(((f32[2560,768]{1,0:T(8,128)}), f32[160,768]{1,0:T(8,128)}) %reduce-scatter.15.cloned.1.call-update) | async-done | bytes 491536 | tf_op jit(solution)/shard_map/reduce_scatter | solution.py:352
  1515.2 142.0 %reduce-scatter.23.cloned.1.call-done = f32[1280,160]{0,1:T(8,128)} async-done(((f32[1280,2560]{0,1:T(8,128)}), f32[1280,160]{0,1:T(8,128)}) %reduce-scatter.23.cloned.1.call-update) | async-done | bytes 819216 | tf_op jit(solution)/shard_map/reduce_scatter | solution.py:368
  1657.3 333.3 %reduce-scatter.25.cloned.1.call-done = f32[160,3200]{1,0:T(8,128)} async-done(((f32[2560,3200]{1,0:T(8,128)}), f32[160,3200]{1,0:T(8,128)}) %reduce-scatter.25.cloned.1.call-update) | async-done | bytes 2048016 | tf_op jit(solution)/shard_map/reduce_scatter | solution.py:229
  1990.6 331.5 %reduce-scatter.27.cloned.1.call-done = f32[160,3200]{1,0:T(8,128)} async-done(((f32[2560,3200]{1,0:T(8,128)}), f32[160,3200]{1,0:T(8,128)}) %reduce-scatter.27.cloned.1.call-update) | async-done | bytes 2048016 | tf_op jit(solution)/shard_map/reduce_scatter | solution.py:230
  2322.1 332.3 %reduce-scatter.29.cloned.1.call-done = f32[3200,160]{0,1:T(8,128)} async-done(((f32[3200,2560]{0,1:T(8,128)}), f32[3200,160]{0,1:T(8,128)}) %reduce-scatter.29.cloned.1.call-update) | async-done | bytes 2048016 | tf_op jit(solution)/shard_map/reduce_scatter | solution.py:232
  (304 shorter events, 287.0 us)
Async XLA Ops:
  7.2 64.0 %all-gather.11.cloned.1.call-start = ((), (), s32[]{:S(2)}) async-start(), calls=%async_computation.10 | async-start | bytes 2088960 | tf_op jit(solution)/shard_map/all_gather | solution.py:88
  7.9 84.1 %all-gather.13.cloned.1.call-start = ((), (), s32[]{:S(2)}) async-start(), calls=%async_computation.11 | async-start | bytes 1392640 | tf_op jit(solution)/shard_map/all_gather | solution.py:90
  8.7 133.7 %all-gather.17.cloned.1.call-start = ((), (), s32[]{:S(2)}) async-start(), calls=%async_computation.13 | async-start | bytes 4177920 | tf_op jit(solution)/shard_map/all_gather | solution.py:85
  9.4 178.9 %all-gather.19.cloned.1.call-start = ((), (), s32[]{:S(2)}) async-start(), calls=%async_computation.14 | async-start | bytes 3133440 | tf_op jit(solution)/shard_map/all_gather | solution.py:87
  10.0 267.3 %all-gather.15.cloned.1.call-start = ((), (), s32[]{:S(2)}) async-start(), calls=%async_computation.12 | async-start | bytes 11141120 | tf_op jit(solution)/shard_map/all_gather | solution.py:173
  94.6 246.3 %all-gather.21.cloned.1.call-start = ((), (), s32[]{:S(2)}) async-start(), calls=%async_computation.15 | async-start | bytes 6963200 | tf_op jit(solution)/shard_map/all_gather | solution.py:108
  95.2 282.5 %all-reduce.15.cloned.1.call-start = ((), (), s32[]{:S(2)}) async-start(), calls=%async_computation.16 | async-start | bytes 1310720 | tf_op jit(solution)/shard_map/psum | solution.py:203
  346.9 157.2 %all-gather.23.cloned.1.call-start = ((), (), s32[]{:S(2)}) async-start(), calls=%async_computation.17 | async-start | bytes 17408000 | tf_op jit(solution)/shard_map/all_gather | solution.py:92
  347.7 281.6 %all-gather.25.cloned.1.call-start = ((), (), s32[]{:S(2)}) async-start(), calls=%async_computation.18 | async-start | bytes 17408000 | tf_op jit(solution)/shard_map/all_gather | solution.py:93
  348.4 405.8 %all-gather.27.cloned.1.call-start = ((), (), s32[]{:S(2)}) async-start(), calls=%async_computation.19 | async-start | bytes 17408000 | tf_op jit(solution)/shard_map/all_gather | solution.py:109
  349.0 482.3 %all-reduce.17.cloned.1.call-start = ((), (), s32[]{:S(2)}) async-start(), calls=%async_computation.20 | async-start | bytes 1310720 | tf_op jit(solution)/shard_map/psum | solution.py:222
  349.3 484.3 %copy-start.32 = (f32[2560]{0:T(1024)}, f32[2560]{0:T(1024)S(1)}, u32[]{:S(2)}) copy-start(f32[2560]{0:T(1024)S(1)} %convert_element_type.160) | copy-start | bytes 30724
  801.0 70.1 %all-gather.29.cloned.1.call-start = ((), (), s32[]{:S(2)}) async-start(), calls=%async_computation.21 | async-start | bytes 1114112 | tf_op jit(solution)/shard_map/all_gather | solution.py:240
  801.5 280.2 %reduce-scatter.13.cloned.1.call-start = ((), (), s32[]{:S(2)}) async-start(), calls=%async_computation.23 | async-start | bytes 278528 | tf_op jit(solution)/shard_map/reduce_scatter | solution.py:330
  914.4 231.4 %reduce-scatter.11.cloned.1.call-start = ((), (), s32[]{:S(2)}) async-start(), calls=%async_computation.22 | async-start | bytes 2228224 | tf_op jit(solution)/shard_map/reduce_scatter | solution.py:329
  915.0 272.6 %all-reduce.19.cloned.1.call-start = ((), (), s32[]{:S(2)}) async-start(), calls=%async_computation.32 | async-start | bytes 1835008 | tf_op jit(solution)/shard_map/psum | solution.py:210
  1147.4 177.9 %reduce-scatter.21.cloned.1.call-start = ((), (), s32[]{:S(2)}) async-start(), calls=%async_computation.27 | async-start | bytes 2785280 | tf_op jit(solution)/shard_map/reduce_scatter | solution.py:357
  1148.0 180.2 %reduce-scatter.19.cloned.1.call-start = ((), (), s32[]{:S(2)}) async-start(), calls=%async_computation.26 | async-start | bytes 4177920 | tf_op jit(solution)/shard_map/reduce_scatter | solution.py:355
  1192.8 223.0 %reduce-scatter.17.cloned.1.call-start = ((), (), s32[]{:S(2)}) async-start(), calls=%async_computation.25 | async-start | bytes 6266880 | tf_op jit(solution)/shard_map/reduce_scatter | solution.py:354
  1197.4 317.8 %reduce-scatter.15.cloned.1.call-start = ((), (), s32[]{:S(2)}) async-start(), calls=%async_computation.24 | async-start | bytes 8355840 | tf_op jit(solution)/shard_map/reduce_scatter | solution.py:352
  1203.5 453.7 %reduce-scatter.23.cloned.1.call-start = ((), (), s32[]{:S(2)}) async-start(), calls=%async_computation.28 | async-start | bytes 13926400 | tf_op jit(solution)/shard_map/reduce_scatter | solution.py:368
  1213.0 777.6 %reduce-scatter.25.cloned.1.call-start = ((), (), s32[]{:S(2)}) async-start(), calls=%async_computation.29 | async-start | bytes 34816000 | tf_op jit(solution)/shard_map/reduce_scatter | solution.py:229
  1228.5 1093.6 %reduce-scatter.27.cloned.1.call-start = ((), (), s32[]{:S(2)}) async-start(), calls=%async_computation.30 | async-start | bytes 34816000 | tf_op jit(solution)/shard_map/reduce_scatter | solution.py:230
  1242.6 1411.8 %reduce-scatter.29.cloned.1.call-start = ((), (), s32[]{:S(2)}) async-start(), calls=%async_computation.31 | async-start | bytes 34816000 | tf_op jit(solution)/shard_map/reduce_scatter | solution.py:232
  (64 other events, 2610.8 us)
Sparse Core Ops, SparseCore 0:
  10.3 41.7 all-gather.10
  54.4 37.6 all-gather.12
  94.4 47.9 all-gather.16
  144.4 43.9 all-gather.18
  191.1 86.2 all-gather.14
  279.4 61.4 all-gather.20
  347.1 30.6 all-reduce.14
  380.3 123.8 all-gather.22
  506.7 122.5 all-gather.24
  631.7 122.5 all-gather.26
  801.1 30.1 all-reduce.16
  833.9 37.1 all-gather.28
  914.5 167.1 reduce-scatter.12
  1085.3 60.4 reduce-scatter.10
  1148.8 38.7 all-reduce.18
  1191.8 61.6 reduce-scatter.20
  1257.8 70.3 reduce-scatter.18
  1333.0 82.7 reduce-scatter.16
  1420.4 94.7 reduce-scatter.14
  1519.7 137.4 reduce-scatter.22
  1662.9 327.6 reduce-scatter.24
  1995.5 326.5 reduce-scatter.26
  2327.7 326.6 reduce-scatter.28
where the time goes:
time: 2670 us; the launch traced here: 2660 us
  waiting for transfers between devices  2250 us (84%)
  matrix products  197 us (7%)
  blocking collectives  129 us (5%)
  local copies, waits for them, and re-layouts  49.3 us (2%)
    reduce_scatter x1, waiting for transfers between devices, shards(): lax.psum_scatter(gate_full, 'ctx', scatter_dimension=0, tiled=True)  333 us
    reduce_scatter x1, waiting for transfers between devices, shards(): lax.psum_scatter(down_full, 'ctx', scatter_dimension=1, tiled=True)  332 us
    reduce_scatter x1, waiting for transfers between devices, shards(): lax.psum_scatter(up_full, 'ctx', scatter_dimension=0, tiled=True)  332 us
    dot_general x25, matrix products, matmul(): return jnp.dot(left_side, right_side, preferred_element_type=jnp.float32)  182 us
    reduce_scatter x1, waiting for transfers between devices, shards(): lax.psum_scatter(grad_rope, 'ctx', scatter_dimension=0, tiled=True)  154 us
    reduce_scatter x1, waiting for transfers between devices, shards(): lax.psum_scatter(out_full, 'ctx', scatter_dimension=1, tiled=True)  142 us
    all_gather x1, waiting for transfers between devices, shards(): lax.all_gather(gate_weight, 'ctx', axis=0, tiled=True)  125 us
    all_gather x1, waiting for transfers between devices, shards(): lax.all_gather(up_weight, 'ctx', axis=0, tiled=True)  116 us
  transfers between devices with their start and end apart: 23, of which 21 were waited for; matrix products, arithmetic and copies ran while one was open for 6% of the time, Pallas kernels for 0%

commit v1 on v0

v1 whole, which is shorter than its diff:
```python
import math

import jax
import jax.numpy as jnp
from jax import lax
from jax.sharding import PartitionSpec as P

H = 40
KVR = 256
NOPE = 64
ROPE = 32
VH = 64
HEAD_GROUPS = 8
FF_GROUPS = 16

eps_norm = 1e-06
residual_scale = 1.4 / math.sqrt(62.0)
score_scale = (NOPE + ROPE) ** (-0.5)
rope_base = 10000.0
BF = jnp.bfloat16
F32 = jnp.float32


def matmul(left_side, right_side):
    return jnp.dot(left_side, right_side, preferred_element_type=F32)


def matmul_nt(left_side, right_side):
    return lax.dot_general(
        left_side, right_side, (((1,), (1,)), ((), ())), preferred_element_type=F32
    )


def matmul_tn(left_side, right_side):
    return lax.dot_general(
        left_side, right_side, (((0,), (0,)), ((), ())), preferred_element_type=F32
    )


def rms_norm(values, scale_gain):
    factor = lax.rsqrt(jnp.mean(values * values, axis=-1, keepdims=True) + eps_norm)
    return values * factor * scale_gain


def norm_back(values, scale_gain, upstream):
    factor = lax.rsqrt(jnp.mean(values * values, axis=-1, keepdims=True) + eps_norm)
    scaled = upstream * scale_gain
    inner_sum = jnp.mean(scaled * values, axis=-1, keepdims=True)
    grad_values = factor * scaled - values * factor * factor * factor * inner_sum
    grad_gain = jnp.sum(upstream * values * factor, axis=0)
    return (grad_values, grad_gain)


def rotate(values, cosine, sine_table):
    half_width = values.shape[-1] // 2
    first_half = values[..., :half_width]
    second_half = values[..., half_width:]
    return jnp.concatenate(
        [
            first_half * cosine - second_half * sine_table,
            second_half * cosine + first_half * sine_table,
        ],
        axis=-1,
    )


def rope_tables(positions):
    frequency = rope_base ** (-jnp.arange(ROPE // 2, dtype=F32) / (ROPE // 2))
    angles = positions.astype(F32)[:, None] * frequency[None, :]
    return (jnp.cos(angles), jnp.sin(angles))


def member_groups(n_ctx, count):
    size = n_ctx // count
    return [[f * size + j for f in range(count)] for j in range(size)]


def gather_over(values, count):
    return lax.all_gather(
        values,
        "ctx",
        axis=0,
        tiled=True,
        axis_index_groups=member_groups(lax.axis_size("ctx"), count),
    )


def scatter_over(values, count):
    return lax.psum_scatter(
        values,
        "ctx",
        scatter_dimension=0,
        tiled=True,
        axis_index_groups=member_groups(lax.axis_size("ctx"), count),
    )


def swap_tp(values):
    return lax.ppermute(values, "tp", [(0, 1), (1, 0)])


def shards(
    layer_input,
    first_gain,
    query_down,
    query_gain,
    query_up,
    latent_down,
    latent_gain,
    latent_up,
    out_weight,
    second_gain,
    gate_weight,
    up_weight,
    down_weight,
    out_grad,
):
    n_ctx = lax.axis_size("ctx")
    n_tp = lax.axis_size("tp")
    c = lax.axis_index("ctx")
    t = lax.axis_index("tp")
    dim = layer_input.shape[1]
    ctx_rows = layer_input.shape[0]
    rows = ctx_rows // n_tp
    qr = query_down.shape[1]
    down_width = qr + KVR + ROPE
    heads = H // HEAD_GROUPS
    size_a = n_ctx // HEAD_GROUPS
    f_a, j_a = c // size_a, c % size_a
    size_f = n_ctx // FF_GROUPS
    ff_cols = gate_weight.shape[1] // FF_GROUPS

    gains = jnp.concatenate([first_gain, query_gain, latent_gain, second_gain])
    widths = [first_gain.shape[0], query_gain.shape[0], latent_gain.shape[0], second_gain.shape[0]]
    gains = lax.all_gather(gains, "ctx", axis=0).astype(F32)
    starts = [0, widths[0], widths[0] + widths[1], widths[0] + widths[1] + widths[2]]
    gain_first, gain_query, gain_latent, gain_second = [
        gains[:, s : s + w].reshape(-1) for s, w in zip(starts, widths)
    ]
    down_shard = jnp.concatenate([query_down, latent_down], axis=1)
    down_full = lax.all_gather(down_shard, "ctx", axis=0, tiled=True)

    def own_heads(mine):
        return jnp.where(f_a // (HEAD_GROUPS // n_tp) == t, mine, swap_tp(mine))

    local_f = f_a % (HEAD_GROUPS // n_tp)
    q_width = heads * (NOPE + ROPE)
    kv_width = heads * (NOPE + VH)
    o_width = heads * VH
    up_all = lax.all_gather(query_up, "ctx", axis=0, tiled=True)
    q_up = own_heads(lax.dynamic_slice_in_dim(up_all, local_f * q_width, q_width, 1))
    lat_all = lax.all_gather(latent_up, "ctx", axis=0, tiled=True)
    l_up = own_heads(lax.dynamic_slice_in_dim(lat_all, local_f * kv_width, kv_width, 1))
    out_all = lax.all_gather(out_weight, "ctx", axis=1, tiled=True)
    w_out = own_heads(lax.dynamic_slice_in_dim(out_all, local_f * o_width, o_width, 0))

    def to_units(shard):
        pieces = shard.reshape(shard.shape[0], FF_GROUPS, ff_cols)
        pieces = lax.all_to_all(
            jnp.transpose(pieces, (1, 0, 2)),
            "ctx",
            0,
            0,
            axis_index_groups=member_groups(n_ctx, FF_GROUPS),
            tiled=True,
        )
        if size_f > 1:
            pieces = lax.all_gather(
                pieces,
                "ctx",
                axis=1,
                tiled=False,
                axis_index_groups=[
                    [f * size_f + j for j in range(size_f)] for f in range(FF_GROUPS)
                ],
            )
        return pieces.reshape(dim, ff_cols)

    def from_units(grads):
        pieces = grads.reshape(FF_GROUPS, dim // FF_GROUPS, ff_cols)
        if size_f > 1:
            pieces = lax.psum_scatter(
                pieces.astype(F32),
                "ctx",
                scatter_dimension=1,
                tiled=True,
                axis_index_groups=[
                    [f * size_f + j for j in range(size_f)] for f in range(FF_GROUPS)
                ],
            ).astype(BF)
        pieces = lax.all_to_all(
            pieces,
            "ctx",
            0,
            0,
            axis_index_groups=member_groups(n_ctx, FF_GROUPS),
            tiled=True,
        )
        return jnp.transpose(pieces, (1, 0, 2)).reshape(dim // n_ctx, FF_GROUPS * ff_cols)

    gate_own, up_own, down_own = (
        to_units(gate_weight),
        to_units(up_weight),
        to_units(down_weight.T),
    )
    w_gate = jnp.concatenate([gate_own, swap_tp(gate_own)], axis=1)
    w_up = jnp.concatenate([up_own, swap_tp(up_own)], axis=1)
    w_down_t = jnp.concatenate([down_own, swap_tp(down_own)], axis=1)

    x = lax.dynamic_slice_in_dim(layer_input, t * rows, rows, 0).astype(F32)
    out_grad_rows = lax.dynamic_slice_in_dim(out_grad, t * rows, rows, 0).astype(F32)
    positions = c * ctx_rows + t * rows + jnp.arange(rows, dtype=jnp.int32)
    cosine, sine_table = rope_tables(positions)

    grad_ffn = (residual_scale * out_grad_rows).astype(BF)
    grad_ffn_all = gather_over(grad_ffn, FF_GROUPS)

    normed = rms_norm(x, gain_first).astype(BF)
    both = matmul(normed, down_full)
    query_latent, compressed = both[:, :qr], both[:, qr:]
    query_normed = rms_norm(query_latent, gain_query).astype(BF)
    latent = rms_norm(compressed[:, :KVR], gain_latent).astype(BF)
    key_rope = rotate(compressed[:, KVR:], cosine, sine_table).astype(BF)
    lat_rope = lax.all_gather(
        jnp.concatenate([latent, key_rope], axis=1), ("ctx", "tp"), axis=0, tiled=True
    )
    latent_all, rope_all = lat_rope[:, :KVR], lat_rope[:, KVR:]
    qn_all = gather_over(query_normed, HEAD_GROUPS)
    q_rows = qn_all.shape[0]
    keys = latent_all.shape[0]

    q_positions = (
        (jnp.arange(HEAD_GROUPS, dtype=jnp.int32)[:, None] * size_a + j_a) * ctx_rows
        + t * rows
        + jnp.arange(rows, dtype=jnp.int32)[None, :]
    ).reshape(-1)
    q_cos, q_sin = rope_tables(q_positions)
    queries_raw = matmul(qn_all, q_up).reshape(q_rows, heads, NOPE + ROPE)
    queries = jnp.concatenate(
        [
            queries_raw[..., :NOPE],
            rotate(queries_raw[..., NOPE:], q_cos[:, None, :], q_sin[:, None, :]),
        ],
        axis=-1,
    ).astype(BF)
    expanded = matmul(latent_all, l_up).astype(BF)
    allowed = jnp.arange(keys, dtype=jnp.int32)[None, :] <= q_positions[:, None]

    def head_keys(h):
        part = expanded[:, h * (NOPE + VH) : (h + 1) * (NOPE + VH)]
        return jnp.concatenate([part[:, :NOPE], rope_all], axis=1), part[:, NOPE:]

    outs, logs = [], []
    for h in range(heads):
        k, v = head_keys(h)
        scores = jnp.where(allowed, matmul_nt(queries[:, h], k) * score_scale, -1e30)
        top = jnp.max(scores, axis=-1, keepdims=True)
        weights = jnp.exp(scores - top)
        total = jnp.sum(weights, axis=-1, keepdims=True)
        outs.append(matmul(weights.astype(BF), v) / total)
        logs.append(top + jnp.log(total))
    attended_wide = jnp.concatenate(outs, axis=1)
    attended = attended_wide.astype(BF)

    branch = scatter_over(matmul(attended, w_out).astype(BF), HEAD_GROUPS).astype(F32)
    middle = x + residual_scale * branch
    normed_second = rms_norm(middle, gain_second).astype(BF)
    ns_all = gather_over(normed_second, FF_GROUPS)
    gate_values = matmul(ns_all, w_gate)
    up_values = matmul(ns_all, w_up)
    sigmoid_gate = jax.nn.sigmoid(gate_values)
    hidden = (gate_values * sigmoid_gate * up_values).astype(BF)
    ffn_sum = scatter_over(matmul_nt(hidden, w_down_t).astype(BF), FF_GROUPS).astype(F32)
    out_half = (middle + residual_scale * ffn_sum).astype(BF)
    layer_output = lax.all_gather(out_half, "tp", axis=0, tiled=True)

    grad_hidden = matmul(grad_ffn_all, w_down_t)
    grad_gate = (
        grad_hidden * up_values * sigmoid_gate * (1.0 + gate_values * (1.0 - sigmoid_gate))
    ).astype(BF)
    grad_up = (grad_hidden * gate_values * sigmoid_gate).astype(BF)
    grad_second = scatter_over(
        (matmul_nt(grad_gate, w_gate) + matmul_nt(grad_up, w_up)).astype(BF), FF_GROUPS
    ).astype(F32)

    def unit_grads(left, right):
        whole = matmul_tn(left, right)
        mine, other = whole[:, :ff_cols], whole[:, ff_cols:]
        mine = mine + swap_tp(other.astype(BF)).astype(F32)
        return from_units(mine.astype(BF)).astype(F32)

    gate_weight_grad = unit_grads(ns_all, grad_gate)
    up_weight_grad = unit_grads(ns_all, grad_up)
    down_weight_grad = unit_grads(grad_ffn_all, hidden).T

    grad_middle_part, second_gain_part = norm_back(middle, gain_second, grad_second)
    grad_middle = out_grad_rows + grad_middle_part

    grad_branch = (residual_scale * grad_middle).astype(BF)
    gb_all = gather_over(grad_branch, HEAD_GROUPS)
    out_part = matmul_tn(attended, gb_all)
    grad_attended = matmul_nt(gb_all, w_out).astype(BF)

    grad_q_rows, grad_kv, grad_rope = [], [], jnp.zeros((keys, ROPE), F32)
    for h in range(heads):
        k, v = head_keys(h)
        q, ga = queries[:, h], grad_attended[:, h * VH : (h + 1) * VH]
        row_inner = jnp.sum(
            ga.astype(F32) * attended_wide[:, h * VH : (h + 1) * VH], axis=-1, keepdims=True
        )
        scores = jnp.where(allowed, matmul_nt(q, k) * score_scale, -1e30)
        probs = jnp.exp(scores - logs[h])
        grad_probs = matmul_nt(ga, v)
        grad_scores = (probs * (grad_probs - row_inner)).astype(BF)
        gq = matmul(grad_scores, k) * score_scale
        grad_q_rows += [gq[:, :NOPE], rotate(gq[:, NOPE:], q_cos, -q_sin)]
        gk = matmul_tn(grad_scores, q) * score_scale
        grad_kv += [gk[:, :NOPE], matmul_tn(probs.astype(BF), ga)]
        grad_rope = grad_rope + gk[:, NOPE:]
    grad_q_rows = jnp.concatenate(grad_q_rows, axis=1).astype(BF)
    grad_expanded = jnp.concatenate(grad_kv, axis=1).astype(BF)
    grad_lat_rope = jnp.concatenate([matmul_nt(grad_expanded, l_up), grad_rope], axis=1)
    l_up_part = matmul_tn(latent_all, grad_expanded)
    q_up_part = matmul_tn(qn_all, grad_q_rows)

    grad_query_normed = scatter_over(matmul_nt(grad_q_rows, q_up).astype(BF), HEAD_GROUPS)
    own_lat_rope = lax.psum_scatter(
        grad_lat_rope.astype(BF), ("ctx", "tp"), scatter_dimension=0, tiled=True
    ).astype(F32)
    grad_query_latent, query_gain_part = norm_back(
        query_latent, gain_query, grad_query_normed.astype(F32)
    )
    grad_latent_rows, latent_gain_part = norm_back(
        compressed[:, :KVR], gain_latent, own_lat_rope[:, :KVR]
    )
    grad_both = jnp.concatenate(
        [grad_query_latent, grad_latent_rows, rotate(own_lat_rope[:, KVR:], cosine, -sine_table)],
        axis=1,
    ).astype(BF)
    down_part = matmul_tn(normed, grad_both)
    grad_normed = matmul_nt(grad_both, down_full)
    grad_input_part, first_gain_part = norm_back(x, gain_first, grad_normed)
    input_grad = lax.all_gather(grad_middle + grad_input_part, "tp", axis=0, tiled=True)

    down_grads = lax.psum(
        lax.psum_scatter(down_part.astype(BF), "ctx", scatter_dimension=0, tiled=True), "tp"
    ).astype(F32)

    def head_grads(part, axis):
        part = part.astype(BF)
        width = part.shape[axis]
        shape = list(part.shape)
        shape[axis] = width * (HEAD_GROUPS // n_tp)
        wide = lax.dynamic_update_slice_in_dim(
            jnp.zeros(shape, BF), part, local_f * width, axis
        )
        here = f_a // (HEAD_GROUPS // n_tp) == t
        mine = jnp.where(here, wide, 0)
        other = swap_tp(jnp.where(here, 0, wide))
        return lax.psum_scatter(
            mine + other, "ctx", scatter_dimension=1 - axis, tiled=True
        ).astype(F32)

    query_up_grad = head_grads(q_up_part, 1)
    latent_up_grad = head_grads(l_up_part, 1)
    out_weight_grad = head_grads(out_part, 0)

    gain_parts = jnp.concatenate(
        [
            p.reshape(n_ctx, -1)
            for p in (first_gain_part, query_gain_part, latent_gain_part, second_gain_part)
        ],
        axis=1,
    )
    gain_grads = lax.psum(
        lax.psum_scatter(gain_parts, "ctx", scatter_dimension=0, tiled=True), "tp"
    ).reshape(-1)
    first_gain_grad, query_gain_grad, latent_gain_grad, second_gain_grad = [
        gain_grads[s : s + w] for s, w in zip(starts, widths)
    ]
    return (
        layer_output,
        input_grad,
        first_gain_grad,
        down_grads[:, :qr],
        query_gain_grad,
        query_up_grad,
        down_grads[:, qr:],
        latent_gain_grad,
        latent_up_grad,
        out_weight_grad,
        second_gain_grad,
        gate_weight_grad,
        up_weight_grad,
        down_weight_grad,
    )


def solution(mesh):
    return jax.shard_map(
        shards,
        mesh=mesh,
        in_specs=(
            P("ctx", None),
            P("ctx"),
            P("ctx", None),
            P("ctx"),
            P("ctx", "tp"),
            P("ctx", None),
            P("ctx"),
            P("ctx", "tp"),
            P("tp", "ctx"),
            P("ctx"),
            P("ctx", "tp"),
            P("ctx", "tp"),
            P("tp", "ctx"),
            P("ctx", None),
        ),
        out_specs=(
            P("ctx", None),
            P("ctx", None),
            P("ctx"),
            P("ctx", None),
            P("ctx"),
            P("ctx", "tp"),
            P("ctx", None),
            P("ctx"),
            P("ctx", "tp"),
            P("tp", "ctx"),
            P("ctx"),
            P("ctx", "tp"),
            P("ctx", "tp"),
            P("tp", "ctx"),
        ),
        check_vma=False,
    )
```

time: 2670 us -> 1480 us (0.55)
  waiting for transfers between devices: 2250 us -> 932 us
  local copies, waits for them, and re-layouts: 49.3 us -> 144 us
  matrix products: 197 us -> 117 us
  starting transfers between devices: 1.42 us -> 67 us
  other arithmetic: 18.8 us -> 67.4 us
    reduce_scatter x10 -> x8, waiting for transfers between devices: 1540 us -> 267 us  [the longest x4 227 us: scatter_over(): lax.psum_scatter(values, 'ctx', scatter_dimension=0, tiled=True, axis_ind...]
    all_gather x10 -> x9, waiting for transfers between devices: 603 us -> 247 us  [the longest x1 57.1 us: shards(): down_full = lax.all_gather(down_shard, 'ctx', axis=0, tiled=True)]
    ppermute x0 -> x12, waiting for transfers between devices: none -> 200 us  [swap_tp(): return lax.ppermute(values, 'tp', [(0, 1), (1, 0)])]
    all_to_all x0 -> x6, waiting for transfers between devices: none -> 133 us  [the longest x3 106 us: to_units(): lax.all_to_all(jnp.transpose(pieces, (1, 0, 2)), 'ctx', 0, 0, axis_index_...]
    psum x3 -> x1, waiting for transfers between devices: 97.6 us -> 0.01 us  [shards(): lax.psum(lax.psum_scatter(down_part.astype(BF), 'ctx', scatter_dimension=...]
    dot_general x36 -> x51, matrix products: 197 us -> 117 us  [the longest x17 43.9 us: matmul(): return jnp.dot(left_side, right_side, preferred_element_type=F32)]
    unnamed x23 -> x20, waiting for transfers between devices: 6.78 us -> 84.7 us
    unnamed x2 -> x1, blocking collectives: 106 us -> 54.8 us
  transfers between devices with their start and end apart: 23 -> 37, of which waited for: 21 -> 23; matrix products, arithmetic and copies ran while one was open for 6% -> 17% of each run, Pallas kernels for 0% -> 0%
where the time goes in v1:
time: 1480 us; the launch traced here: 1460 us
  waiting for transfers between devices  932 us (63%)
  local copies, waits for them, and re-layouts  144 us (10%)
  matrix products  117 us (8%)
  blocking collectives  116 us (8%)
  other arithmetic  67.4 us (5%)
  starting transfers between devices  67 us (5%)
  between operations  16.2 us (1%)
    reduce_scatter x4, waiting for transfers between devices, scatter_over(): lax.psum_scatter(values, 'ctx', scatter_dimension=0, tiled=True, axis_ind...  227 us
    ppermute x12, waiting for transfers between devices, swap_tp(): return lax.ppermute(values, 'tp', [(0, 1), (1, 0)])  200 us
    all_to_all x3, waiting for transfers between devices, to_units(): lax.all_to_all(jnp.transpose(pieces, (1, 0, 2)), 'ctx', 0, 0, axis_index_...  106 us
    unnamed x20, waiting for transfers between devices  84.7 us
    all_gather x1, waiting for transfers between devices, shards(): down_full = lax.all_gather(down_shard, 'ctx', axis=0, tiled=True)  57.1 us
    unnamed x1, blocking collectives  54.8 us
    all_gather x1, waiting for transfers between devices, shards(): lax.all_gather(jnp.concatenate([latent, key_rope], axis=1), ('ctx', 'tp')...  50.7 us
    all_gather x3, waiting for transfers between devices, gather_over(): lax.all_gather(values, 'ctx', axis=0, tiled=True, axis_index_groups=membe...  46.1 us
  transfers between devices with their start and end apart: 37, of which 23 were waited for; matrix products, arithmetic and copies ran while one was open for 17% of the time, Pallas kernels for 0%

profile of v1, /device:TPU:3, one launch (start us, length us, event | category | flops | bytes accessed | tf_op | source)
XLA Modules:
  0.0 1459.4 jit_solution(5079996097341840724)
XLA Ops:
  12.0 18.7 %all-gather.1 = bf16[16,1,384]{2,1,0:T(2,128)(2,1)S(1)} all-gather(bf16[1,1,384]{2,1,0:T(2,128)(2,1)S(1)} %reshape.303), channel_id=2, replica_groups=mesh['ctx'=16,'tp'=2] {'ctx'}, dimensions={0}, use_global_device_ids=true | all-gather | bytes 13056 | tf_op jit(solution)/shard_map/all_gather | solution.py:135
  33.2 22.7 %all-gather.14.cloned.1.call-done = bf16[768,1920]{1,0:T(8,128)(2,1)} async-done(((bf16[48,1920]{1,0:T(8,128)(2,1)}), bf16[768,1920]{1,0:T(8,128)(2,1)}) %all-gather.14.cloned.1.call-update) | async-done | bytes 2949136 | tf_op jit(solution)/shard_map/all_gather | solution.py:150
  59.8 57.1 %all-gather.12.cloned.1.call-done = bf16[2560,1056]{1,0:T(8,128)(2,1)} async-done(((bf16[160,1056]{1,0:T(8,128)(2,1)}), bf16[2560,1056]{1,0:T(8,128)(2,1)}) %all-gather.12.cloned.1.call-update) | async-done | bytes 5406736 | tf_op jit(solution)/shard_map/all_gather | solution.py:141
  123.1 33.6 %all-gather.18.cloned.1.call-done = bf16[256,2560]{1,0:T(8,128)(2,1)} async-done(((bf16[16,2560]{1,0:T(8,128)(2,1)}), bf16[256,2560]{1,0:T(8,128)(2,1)}) %all-gather.18.cloned.1.call-update) | async-done | bytes 1310736 | tf_op jit(solution)/shard_map/all_gather | solution.py:152
  160.4 27.9 %all_gather.42 = bf16[512,768]{1,0:T(8,128)(2,1)S(1)} all-gather(bf16[64,768]{1,0:T(8,128)(2,1)S(1)} %multiply_convert_fusion.10), channel_id=1, replica_groups={{0,4,8,12,16,20,24,28},{2,6,10,14,18,22,26,30},{1,5,9,13,17,21,25,29},{..., dimensions={0}, use_global_device_ids=true | all-gather | bytes 884736 | tf_op jit(solution)/shard_map/all_gather | solution.py:79
  189.8 36.6 %all-gather.20.cloned.1.call-done = bf16[1280,2560]{0,1:T(8,128)(2,1)} async-done(((bf16[1280,160]{0,1:T(8,128)(2,1)}), bf16[1280,2560]{0,1:T(8,128)(2,1)}) %all-gather.20.cloned.1.call-update) | async-done | bytes 6553616 | tf_op jit(solution)/shard_map/all_gather | solution.py:154
  234.0 50.7 %all-gather.16.cloned.1.call-done = bf16[2048,288]{1,0:T(8,128)(2,1)} async-done(((bf16[64,288]{1,0:T(8,128)(2,1)}), bf16[2048,288]{1,0:T(8,128)(2,1)}) %all-gather.16.cloned.1.call-update) | async-done | bytes 1179664 | tf_op jit(solution)/shard_map/all_gather | solution.py:224
  319.8 64.8 %reduce-scatter.12.cloned.1.call-done = bf16[64,2560]{1,0:T(8,128)(2,1)} async-done(((bf16[512,2560]{1,0:T(8,128)(2,1)}), bf16[64,2560]{1,0:T(8,128)(2,1)}) %reduce-scatter.12.cloned.1.call-update) | async-done | bytes 327696 | tf_op jit(solution)/shard_map/reduce_scatter | solution.py:89
  411.4 37.7 %all-to-all-done.2 = bf16[16,160,200]{2,1,0:T(8,128)(2,1)} async-done(((bf16[16,160,200]{2,1,0:T(8,128)(2,1)}), bf16[16,160,200]{2,1,0:T(8,128)(2,1)}, u32[]{:S(2)}, u32[]{:S(2)}) %all-to-all-start.2) | async-done | bytes 1024032 | tf_op jit(solution)/shard_map/all_to_all | solution.py:159
  471.4 30.6 %all-to-all-done.1 = bf16[16,160,200]{2,1,0:T(8,128)(2,1)} async-done(((bf16[16,160,200]{2,1,0:T(8,128)(2,1)}), bf16[16,160,200]{2,1,0:T(8,128)(2,1)}, u32[]{:S(2)}, u32[]{:S(2)}) %all-to-all-start.1) | async-done | bytes 1024032 | tf_op jit(solution)/shard_map/all_to_all | solution.py:159
  515.2 37.3 %all-to-all-done = bf16[16,160,200]{2,1,0:T(8,128)(2,1)} async-done(((bf16[16,160,200]{2,1,0:T(8,128)(2,1)}), bf16[16,160,200]{2,1,0:T(8,128)(2,1)}, u32[]{:S(2)}, u32[]{:S(2)}) %all-to-all-start) | async-done | bytes 1024032 | tf_op jit(solution)/shard_map/all_to_all | solution.py:159
  560.8 19.0 %collective-permute-done.3 = bf16[2560,200]{0,1:T(8,128)(2,1)} collective-permute-done((bf16[2560,200]{0,1:T(8,128)(2,1)}, bf16[2560,200]{0,1:T(8,128)(2,1)}, u32[]{:S(2)}, u32[]{:S(2)}) %collective-permute-start.3) | collective-permute-done | bytes 1024032 | tf_op jit(solution)/shard_map/ppermute | solution.py:99
  617.0 80.0 %reduce-scatter.16.cloned.1.call-done = bf16[64,2560]{1,0:T(8,128)(2,1)} async-done(((bf16[1024,2560]{1,0:T(8,128)(2,1)}), bf16[64,2560]{1,0:T(8,128)(2,1)}) %reduce-scatter.16.cloned.1.call-update) | async-done | bytes 327696 | tf_op jit(solution)/shard_map/reduce_scatter | solution.py:89
  708.0 46.1 %all-gather.26.cloned.1.call-done = bf16[512,2560]{1,0:T(8,128)(2,1)} async-done(((bf16[64,2560]{1,0:T(8,128)(2,1)}), bf16[512,2560]{1,0:T(8,128)(2,1)}) %all-gather.26.cloned.1.call-update) | async-done | bytes 2621456 | tf_op jit(solution)/shard_map/all_gather | solution.py:79
  796.8 82.5 %reduce-scatter.28.cloned.1.call-done = bf16[64,288]{1,0:T(8,128)(2,1)} async-done(((bf16[2048,288]{1,0:T(8,128)(2,1)}), bf16[64,288]{1,0:T(8,128)(2,1)}) %reduce-scatter.28.cloned.1.call-update) | async-done | bytes 36880
  881.0 63.0 %reduce-scatter.18.cloned.1.call-done = bf16[64,768]{1,0:T(8,128)(2,1)} async-done(((bf16[512,768]{1,0:T(8,128)(2,1)}), bf16[64,768]{1,0:T(8,128)(2,1)}) %reduce-scatter.18.cloned.1.call-update) | async-done | bytes 98320 | tf_op jit(solution)/shard_map/reduce_scatter | solution.py:89
  981.7 21.2 %dynamic_update_slice.11 = bf16[1280,2560]{0,1:T(8,128)(2,1)} dynamic-update-slice(bf16[1280,2560]{0,1:T(8,128)(2,1)} %broadcast_in_dim.28, bf16[320,2560]{0,1:T(8,128)(2,1)} %copy.221, s32[]{:T(128)S(6)} %select_n.143, s32[]{:T(128)} %constant.92.clone.1) | dynamic-update-slice | bytes 3276804 | tf_op jit(solution)/shard_map/dynamic_update_slice | solution.py:354
  1008.5 18.8 %reduce-scatter.14.cloned.1.call-done = bf16[64,2560]{1,0:T(8,128)(2,1)} async-done(((bf16[1024,2560]{1,0:T(8,128)(2,1)}), bf16[64,2560]{1,0:T(8,128)(2,1)}) %reduce-scatter.14.cloned.1.call-update) | async-done | bytes 327696 | tf_op jit(solution)/shard_map/reduce_scatter | solution.py:89
  1037.5 19.8 %collective-permute-done.7 = bf16[256,2560]{1,0:T(8,128)(2,1)} collective-permute-done((bf16[256,2560]{1,0:T(8,128)(2,1)}, bf16[256,2560]{1,0:T(8,128)(2,1)}, u32[]{:S(2)}, u32[]{:S(2)}) %collective-permute-start.7) | collective-permute-done | bytes 1310752 | tf_op jit(solution)/shard_map/ppermute | solution.py:99
  1073.1 40.4 %reduce-scatter.20.cloned.1.call-done = bf16[160,1056]{1,0:T(8,128)(2,1)} async-done(((bf16[2560,1056]{1,0:T(8,128)(2,1)}), bf16[160,1056]{1,0:T(8,128)(2,1)}) %reduce-scatter.20.cloned.1.call-update) | async-done | bytes 337936 | tf_op jit(solution)/shard_map/reduce_scatter | solution.py:346
  1113.6 98.2 %collective-permute-done.8 = bf16[1280,2560]{0,1:T(8,128)(2,1)} collective-permute-done((bf16[1280,2560]{0,1:T(8,128)(2,1)}, bf16[1280,2560]{0,1:T(8,128)(2,1)}, u32[]{:S(2)}, u32[]{:S(2)}) %collective-permute-start.8) | collective-permute-done | bytes 6553632 | tf_op jit(solution)/shard_map/ppermute | solution.py:99
  1251.3 22.8 %collective-permute-done.10 = bf16[2560,200]{0,1:T(8,128)(2,1)S(1)} collective-permute-done((bf16[2560,200]{0,1:T(8,128)(2,1)S(1)}, bf16[2560,200]{0,1:T(8,128)(2,1)S(1)}, u32[]{:S(2)}, u32[]{:S(2)}) %collective-permute-start.10) | collective-permute-done | bytes 1024032 | tf_op jit(solution)/shard_map/ppermute | solution.py:99
  1298.7 26.8 %collective-permute-done.11 = bf16[2560,200]{0,1:T(8,128)(2,1)S(1)} collective-permute-done((bf16[2560,200]{0,1:T(8,128)(2,1)S(1)}, bf16[2560,200]{0,1:T(8,128)(2,1)S(1)}, u32[]{:S(2)}, u32[]{:S(2)}) %collective-permute-start.11) | collective-permute-done | bytes 1024032 | tf_op jit(solution)/shard_map/ppermute | solution.py:99
  1380.8 54.8 %all-reduce = f32[16,384]{1,0:T(8,128)S(1)} all-reduce(f32[16,384]{1,0:T(8,128)S(1)} %pad_maximum_fusion.28), channel_id=8, replica_groups=mesh['ctx'=16,'tp'=2] {'ctx'}, use_global_device_ids=true, to_apply=%region_32.33.clone | all-reduce | flops 6144 | bytes 49152
  (508 shorter events, 432.3 us)
Async XLA Ops:
  7.9 109.0 %all-gather.12.cloned.1.call-start = ((), (), s32[]{:S(2)}) async-start(), calls=%async_computation.15 | async-start | bytes 6266880 | tf_op jit(solution)/shard_map/all_gather | solution.py:141
  9.8 146.8 %all-gather.18.cloned.1.call-start = ((), (), s32[]{:S(2)}) async-start(), calls=%async_computation.18 | async-start | bytes 1392640 | tf_op jit(solution)/shard_map/all_gather | solution.py:152
  10.6 215.9 %all-gather.20.cloned.1.call-start = ((), (), s32[]{:S(2)}) async-start(), calls=%async_computation.19 | async-start | bytes 6963200 | tf_op jit(solution)/shard_map/all_gather | solution.py:154
  11.1 273.5 %all-gather.16.cloned.1.call-start = ((), (), s32[]{:S(2)}) async-start(), calls=%async_computation.17 | async-start | bytes 1622016 | tf_op jit(solution)/shard_map/all_gather | solution.py:224
  58.6 100.3 %collective-permute-start = (bf16[768,480]{0,1:T(8,128)(2,1)}, bf16[768,480]{0,1:T(8,128)(2,1)S(1)}, u32[]{:S(2)}, u32[]{:S(2)}) collective-permute-start(bf16[768,480]{0,1:T(8,128)(2,1)} %copy.199), channel_id=1, source_target_pairs={{0,1},{1,0},{2,3},{3,2},{4,5},{5,4},{6,7},{7,6},{8,9},{9,8},{10,11... | collective-permute-start | bytes 2211848 | tf_op jit(solution)/shard_map/ppermute | solution.py:99
  122.2 262.4 %reduce-scatter.12.cloned.1.call-start = ((), (), s32[]{:S(2)}) async-start(), calls=%async_computation.20 | async-start | bytes 2949120 | tf_op jit(solution)/shard_map/reduce_scatter | solution.py:89
  157.7 130.1 %collective-permute-start.1 = (bf16[256,640]{1,0:T(8,128)(2,1)S(1)}, bf16[256,640]{1,0:T(8,128)(2,1)}, u32[]{:S(2)}, u32[]{:S(2)}) collective-permute-start(bf16[256,640]{1,0:T(8,128)(2,1)S(1)} %constant_dynamic-slice_fusion.1), channel_id=1, source_target_pairs={{0,1},{1,0},{2,3},{3,2},{4,5},{5,4},{6,7},{7,6},{8,9},{9,8},{10,11... | collective-permute-start | bytes 983048 | tf_op jit(solution)/shard_map/ppermute | solution.py:99
  316.5 265.8 %all-gather.24.cloned.1.call-start = ((), (), s32[]{:S(2)}) async-start(), calls=%async_computation.23 | async-start | bytes 5570560 | tf_op jit(solution)/shard_map/all_gather | solution.py:79
  318.4 271.7 %all-gather.22.cloned.1.call-start = ((), (), s32[]{:S(2)}) async-start(), calls=%async_computation.21 | async-start | bytes 5570560 | tf_op jit(solution)/shard_map/all_gather | solution.py:79
  509.0 188.0 %reduce-scatter.16.cloned.1.call-start = ((), (), s32[]{:S(2)}) async-start(), calls=%async_computation.24 | async-start | bytes 5570560 | tf_op jit(solution)/shard_map/reduce_scatter | solution.py:89
  616.9 137.2 %all-gather.26.cloned.1.call-start = ((), (), s32[]{:S(2)}) async-start(), calls=%async_computation.25 | async-start | bytes 2949120 | tf_op jit(solution)/shard_map/all_gather | solution.py:79
  701.8 177.5 %reduce-scatter.28.cloned.1.call-start = ((), (), s32[]{:S(2)}) async-start(), calls=%async_computation.33 | async-start | bytes 1622016
  782.8 161.2 %reduce-scatter.18.cloned.1.call-start = ((), (), s32[]{:S(2)}) async-start(), calls=%async_computation.26 | async-start | bytes 884736 | tf_op jit(solution)/shard_map/reduce_scatter | solution.py:89
  788.9 238.4 %reduce-scatter.14.cloned.1.call-start = ((), (), s32[]{:S(2)}) async-start(), calls=%async_computation.22 | async-start | bytes 5570560 | tf_op jit(solution)/shard_map/reduce_scatter | solution.py:89
  796.7 316.8 %reduce-scatter.20.cloned.1.call-start = ((), (), s32[]{:S(2)}) async-start(), calls=%async_computation.28 | async-start | bytes 6266880 | tf_op jit(solution)/shard_map/reduce_scatter | solution.py:346
  950.6 491.3 %all-gather.28.cloned.1.call-start = ((), (), s32[]{:S(2)}) async-start(), calls=%async_computation.27 | async-start | bytes 1966080 | tf_op jit(solution)/shard_map/all_gather | solution.py:343
  966.2 93.7 %collective-permute-start.6 = (bf16[768,1920]{1,0:T(8,128)(2,1)}, bf16[768,1920]{1,0:T(8,128)(2,1)}, u32[]{:S(2)}, u32[]{:S(2)}) collective-permute-start(bf16[768,1920]{1,0:T(8,128)(2,1)} %broadcast_select_fusion.1), channel_id=1, source_target_pairs={{0,1},{1,0},{2,3},{3,2},{4,5},{5,4},{6,7},{7,6},{8,9},{9,8},{10,11... | collective-permute-start | bytes 8847368 | tf_op jit(solution)/shard_map/ppermute | solution.py:99
  971.1 86.2 %collective-permute-start.7 = (bf16[256,2560]{1,0:T(8,128)(2,1)}, bf16[256,2560]{1,0:T(8,128)(2,1)}, u32[]{:S(2)}, u32[]{:S(2)}) collective-permute-start(bf16[256,2560]{1,0:T(8,128)(2,1)} %broadcast_select_fusion.3), channel_id=1, source_target_pairs={{0,1},{1,0},{2,3},{3,2},{4,5},{5,4},{6,7},{7,6},{8,9},{9,8},{10,11... | collective-permute-start | bytes 3932168 | tf_op jit(solution)/shard_map/ppermute | solution.py:99
  1030.3 411.5 %reduce-scatter.24.cloned.1.call-start = ((), (), s32[]{:S(2)}) async-start(), calls=%async_computation.31 | async-start | bytes 1392640 | tf_op jit(solution)/shard_map/reduce_scatter | solution.py:360
  1033.5 178.3 %collective-permute-start.8 = (bf16[1280,2560]{0,1:T(8,128)(2,1)}, bf16[1280,2560]{0,1:T(8,128)(2,1)}, u32[]{:S(2)}, u32[]{:S(2)}) collective-permute-start(bf16[1280,2560]{0,1:T(8,128)(2,1)} %broadcast_select_fusion), channel_id=1, source_target_pairs={{0,1},{1,0},{2,3},{3,2},{4,5},{5,4},{6,7},{7,6},{8,9},{9,8},{10,11... | collective-permute-start | bytes 19660808 | tf_op jit(solution)/shard_map/ppermute | solution.py:99
  1059.8 383.7 %reduce-scatter.22.cloned.1.call-start = ((), (), s32[]{:S(2)}) async-start(), calls=%async_computation.30 | async-start | bytes 3133440 | tf_op jit(solution)/shard_map/reduce_scatter | solution.py:360
  1063.7 381.5 %all-reduce.3.cloned.1.call-start = ((), (), s32[]{:S(2)}) async-start(), calls=%async_computation.29 | async-start | bytes 737280 | tf_op jit(solution)/shard_map/psum | solution.py:345
  1071.6 162.0 %collective-permute-start.9 = (bf16[2560,200]{0,1:T(8,128)(2,1)S(1)}, bf16[2560,200]{0,1:T(8,128)(2,1)S(1)}, u32[]{:S(2)}, u32[]{:S(2)}) collective-permute-start(bf16[2560,200]{0,1:T(8,128)(2,1)S(1)} %slice.661), channel_id=1, source_target_pairs={{0,1},{1,0},{2,3},{3,2},{4,5},{5,4},{6,7},{7,6},{8,9},{9,8},{10,11... | collective-permute-start | bytes 3072008 | tf_op jit(solution)/shard_map/ppermute | solution.py:99
  1113.5 335.1 %reduce-scatter.26.cloned.1.call-start = ((), (), s32[]{:S(2)}) async-start(), calls=%async_computation.32 | async-start | bytes 6963200 | tf_op jit(solution)/shard_map/reduce_scatter | solution.py:360
  (123 other events, 2862.3 us)
Sparse Core Ops, SparseCore 0:
  10.2 45.6 all-gather.13
  58.8 58.0 all-gather.11
  119.2 37.4 all-gather.17
  158.8 67.6 all-gather.19
  229.8 54.8 all-gather.15
  316.7 67.9 reduce-scatter.11
  387.5 74.2 all-gather.23
  464.6 85.2 all-gather.21
  617.1 79.9 reduce-scatter.15
  701.9 52.1 all-gather.25
  782.9 96.3 reduce-scatter.27
  883.0 60.9 reduce-scatter.17
  948.3 78.9 reduce-scatter.13
  1031.6 81.8 reduce-scatter.19
  1115.5 38.2 all-gather.27
  1157.8 56.1 reduce-scatter.23
  1218.2 86.8 reduce-scatter.21
  1307.3 31.4 all-reduce.2
  1343.3 87.3 reduce-scatter.25

commit v2 on v1

v2 whole, which is shorter than its diff:
```python
import math

import jax
import jax.numpy as jnp
from jax import lax
from jax.experimental import pallas as pl
from jax.experimental.pallas import tpu as pltpu
from jax.sharding import PartitionSpec as P

BF = jnp.bfloat16
F32 = jnp.float32

H = 40
KVR = 256
NOPE = 64
ROPE = 32
VH = 64

eps_norm = 1e-06
residual_scale = 1.4 / math.sqrt(62.0)
score_scale = (NOPE + ROPE) ** (-0.5)
rope_base = 10000.0


def matmul(left_side, right_side):
    return jnp.dot(left_side, right_side, preferred_element_type=F32)


def matmul_nt(left_side, right_side):
    return lax.dot_general(
        left_side, right_side, (((1,), (1,)), ((), ())), preferred_element_type=F32
    )


def matmul_tn(left_side, right_side):
    return lax.dot_general(
        left_side, right_side, (((0,), (0,)), ((), ())), preferred_element_type=F32
    )


def rms_norm(values, scale_gain):
    factor = lax.rsqrt(jnp.mean(values * values, axis=-1, keepdims=True) + eps_norm)
    return values * factor * scale_gain


def norm_back(values, scale_gain, upstream):
    factor = lax.rsqrt(jnp.mean(values * values, axis=-1, keepdims=True) + eps_norm)
    scaled = upstream * scale_gain
    inner_sum = jnp.mean(scaled * values, axis=-1, keepdims=True)
    grad_values = factor * scaled - values * factor * factor * factor * inner_sum
    grad_gain = jnp.sum(upstream * values * factor, axis=0)
    return (grad_values, grad_gain)


def rotate(values, cosine, sine_table):
    half_width = values.shape[-1] // 2
    first_half = values[..., :half_width]
    second_half = values[..., half_width:]
    return jnp.concatenate(
        [
            first_half * cosine - second_half * sine_table,
            second_half * cosine + first_half * sine_table,
        ],
        axis=-1,
    )


def rope_tables(positions):
    frequency = rope_base ** (-jnp.arange(ROPE // 2, dtype=F32) / (ROPE // 2))
    angles = positions.astype(F32)[:, None] * frequency[None, :]
    return (jnp.cos(angles), jnp.sin(angles))


MESH = pl.DeviceIdType.MESH
OFFSETS = (0, -1, 1, -2, 2, -3, 3)


class Place:
    def __init__(self, n_ctx):
        c = lax.axis_index("ctx")
        self.members = n_ctx // 16
        self.c = c
        self.t = lax.axis_index("tp")
        self.m = lax.rem(c, self.members)
        g = c // self.members
        self.g = g
        self.a, self.b, self.d = g // 4, lax.rem(g // 2, 2), lax.rem(g, 2)

    def at(self, a=None, b=None, d=None):
        a = self.a if a is None else a
        b = self.b if b is None else b
        d = self.d if d is None else d
        return (((a * 2 + b) * 2 + d) * self.members + self.m, self.t)

    def up(self):
        return self.at(a=self.a + 1)

    def down(self):
        return self.at(a=self.a - 1)

    def across(self):
        return self.at(b=1 - self.b)

    def core(self):
        return self.at(d=1 - self.d)

    def other(self):
        return (self.c, 1 - self.t)

    def valid(self, o):
        return None if o == 0 else (self.a + o >= 0 if o < 0 else self.a + o <= 3)


def both_of(p, q):
    if p is None:
        return q
    return p if q is None else p & q


def when(p, body):
    if p is None:
        body()
    else:
        pl.when(p)(body)


class Net:
    def __init__(self, place, sems):
        self.place, self.sems, self.count, self.pending = place, sems, 0, []

    def sem(self):
        self.count += 1
        return self.sems.at[self.count - 1]

    def send(self, src, dst, recv, to, cond=None):
        mine = self.sem()

        def copy():
            return pltpu.make_async_remote_copy(
                src(), dst(), mine, recv, device_id=to(), device_id_type=MESH
            )

        when(cond, lambda: copy().start())
        self.pending.append((cond, lambda: copy().wait_send()))

    def recv(self, dst, sem, cond=None):
        def wait():
            ref = dst()
            pltpu.make_async_remote_copy(
                ref, ref, sem, sem, device_id=self.place.other(), device_id_type=MESH
            ).wait_recv()

        when(cond, wait)

    def finish(self):
        for cond, wait in self.pending:
            when(cond, wait)


def greet(place, line=False, across=False, core=False, other=False, everyone=0):
    barrier = pltpu.get_barrier_semaphore()

    def tell(device):
        pl.semaphore_signal(barrier, inc=1, device_id=device, device_id_type=MESH)

    count = 0
    if everyone:
        for k in range(1, everyone):
            tell((lax.rem(place.c + k * place.members, everyone * place.members), place.t))
        count = count + everyone - 1
    else:
        if line:
            pl.when(place.a < 3)(lambda: tell(place.up()))
            pl.when(place.a > 0)(lambda: tell(place.down()))
            count = count + (place.a < 3).astype(jnp.int32) + (place.a > 0).astype(jnp.int32)
        if across:
            tell(place.across())
            count = count + 1
        if core:
            tell(place.core())
            count = count + 1
    if other:
        tell(place.other())
        count = count + 1
    pl.semaphore_wait(barrier, count)


def gather_steps(net, src, out, width):
    p = net.place
    cores = width == 16

    def slot(o, b, d):
        g = (p.a + o) * 2 + b
        return out.at[g * 2 + d] if cores else out.at[g]

    z_sem = {o: net.sem() for o in OFFSETS if o}
    x_sem = {o: net.sem() for o in OFFSETS}
    c_sem = {(s, o): net.sem() for s in (0, 1) for o in OFFSETS} if cores else {}
    own_sem = net.sem()
    keep = pltpu.make_async_copy(src, slot(0, p.b, p.d), own_sem)
    keep.start()

    def forward(o):
        ok = p.valid(o)
        here = lambda: slot(o, p.b, p.d)
        origin = (lambda: src) if o == 0 else here
        if o <= 0 and o > -3:
            net.send(origin, here, z_sem[o - 1], p.up, both_of(ok, p.a < 3))
        if o >= 0 and o < 3:
            net.send(origin, here, z_sem[o + 1], p.down, both_of(ok, p.a > 0))
        net.send(origin, here, x_sem[o], p.across, ok)
        if cores:
            net.send(origin, here, c_sem[0, o], p.core, ok)

    def from_line(o):
        net.recv(lambda: slot(o, p.b, p.d), z_sem[o], p.valid(o))
        forward(o)

    def from_across(o):
        there = lambda: slot(o, 1 - p.b, p.d)
        net.recv(there, x_sem[o], p.valid(o))
        if cores:
            net.send(there, there, c_sem[1, o], p.core, p.valid(o))

    forward(0)
    yield
    for near in (1, 2, 3):
        from_line(-near)
        from_line(near)
        yield
        if near == 1:
            from_across(0)
        else:
            from_across(1 - near)
            from_across(near - 1)
        yield
    from_across(-3)
    from_across(3)
    yield
    if cores:
        for o in OFFSETS:
            net.recv(lambda: slot(o, p.b, 1 - p.d), c_sem[0, o], p.valid(o))
            net.recv(lambda: slot(o, 1 - p.b, 1 - p.d), c_sem[1, o], p.valid(o))
    keep.wait()


def add_into(out, terms, rows):
    step = 16 if rows % 16 == 0 else rows

    def body(i):
        part = pl.ds(pl.multiple_of(i * step, step), step)
        total = terms[0][part].astype(F32)
        for term in terms[1:]:
            total = total + term[part].astype(F32)
        out[part] = total.astype(out.dtype)

    pl.loop(0, rows // step)(body)


def reduce_steps(net, parts, out, near_core, near_x, line_in, line_out, rows, width):
    p = net.place
    cores = width == 16
    order = (-3, 3, -2, 2, -1, 1, 0)
    if cores:
        c_sem = {(b, o): net.sem() for b in (0, 1) for o in order}
        for o in order:
            for side in (1, 0):
                def src(o=o, side=side):
                    b = 1 - p.b if side else p.b
                    return parts.at[((p.a + o) * 2 + b) * 2 + 1 - p.d]

                def dst(o=o, side=side):
                    b = 1 - p.b if side else p.b
                    return near_core.at[(p.a + o) * 2 + b]

                net.send(src, dst, c_sem[side, o], p.core, p.valid(o))
        yield
    x_sem = {o: net.sem() for o in order}
    up_sem = {o: net.sem() for o in (0, 1, 2)}
    down_sem = {o: net.sem() for o in (0, 1, 2)}

    def mine(o, b):
        g = (p.a + o) * 2 + b
        return near_core.at[g] if cores else parts.at[g]

    for o in order:
        if cores:
            def join(o=o):
                g = (p.a + o) * 2 + 1 - p.b
                add_into(near_core.at[g], [near_core.at[g], parts.at[g * 2 + p.d]], rows)

            net.recv(lambda: near_core.at[(p.a + o) * 2 + 1 - p.b], c_sem[1, o], p.valid(o))
            when(p.valid(o), join)
        net.send(
            lambda o=o: mine(o, 1 - p.b),
            lambda o=o: near_x.at[p.a + o],
            x_sem[o],
            p.across,
            p.valid(o),
        )
    yield
    for o in order:
        ok = p.valid(o)
        if cores:
            net.recv(lambda: near_core.at[(p.a + o) * 2 + p.b], c_sem[0, o], ok)

        def terms(o=o):
            g = (p.a + o) * 2 + p.b
            own = [near_core.at[g], parts.at[g * 2 + p.d]] if cores else [parts.at[g]]
            return own + [near_x.at[p.a + o]]

        net.recv(lambda: near_x.at[p.a + o], x_sem[o], ok)
        if o == 0:
            below, above = line_in.at[0, 0], line_in.at[1, 0]
            net.recv(lambda: below, up_sem[0], p.a > 0)
            net.recv(lambda: above, down_sem[0], p.a < 3)
            inner = (p.a > 0) & (p.a < 3)
            pl.when(inner)(lambda: add_into(out, terms() + [below, above], rows))
            pl.when(p.a == 0)(lambda: add_into(out, terms() + [above], rows))
            pl.when(p.a == 3)(lambda: add_into(out, terms() + [below], rows))
            continue
        far = abs(o)
        way = 0 if o > 0 else 1
        stage = line_out.at[way, far - 1]
        sems = up_sem if o > 0 else down_sem
        first = p.a == 0 if o > 0 else p.a == 3
        if far < 3:
            came = line_in.at[way, far]
            later = ok & ~first
            net.recv(lambda: came, sems[far], later)
            pl.when(later)(lambda: add_into(stage, terms() + [came], rows))
            pl.when(ok & first)(lambda: add_into(stage, terms(), rows))
        else:
            pl.when(ok)(lambda: add_into(stage, terms(), rows))
        net.send(
            lambda stage=stage: stage,
            lambda far=far, way=way: line_in.at[way, far - 1],
            sems[far - 1],
            p.up if o > 0 else p.down,
            ok,
        )
        yield


def swap_steps(net, src, dst):
    sem = net.sem()
    net.send(lambda: src, lambda: dst, sem, net.place.other)
    yield
    net.recv(lambda: dst, sem)


def run_together(*tasks):
    tasks = list(tasks)
    while tasks:
        for task in list(tasks):
            try:
                next(task)
            except StopIteration:
                tasks.remove(task)


ANY = pl.BlockSpec(memory_space=pl.ANY)
VMEM = pl.BlockSpec(memory_space=pltpu.VMEM)


def comm_call(name, number, body, ins, in_specs, outs, out_specs, scratch, sems):
    return pl.pallas_call(
        body,
        out_shape=outs,
        in_specs=in_specs,
        out_specs=out_specs,
        scratch_shapes=list(scratch) + [pltpu.SemaphoreType.DMA((sems,))],
        compiler_params=pltpu.CompilerParams(
            collective_id=number, has_side_effects=True, vmem_limit_bytes=56 << 20
        ),
        name=name,
    )(*ins)


def shape(dims, dtype=BF):
    return jax.ShapeDtypeStruct(tuple(dims), dtype)


def reduce_scratch(rows, cols, width):
    near_core = [pltpu.VMEM((8, rows, cols), BF)] if width == 16 else []
    return near_core + [
        pltpu.VMEM((4, rows, cols), BF),
        pltpu.VMEM((2, 3, rows, cols), BF),
        pltpu.VMEM((2, 3, rows, cols), BF),
    ]


def gather_blocks(name, number, items, widths, n_ctx):
    k = len(items)

    def body(*refs):
        ins, outs, sems = refs[:k], refs[k : 2 * k], refs[-1]
        place = Place(n_ctx)
        greet(place, line=True, across=True, core=16 in widths)
        net = Net(place, sems)
        run_together(*[gather_steps(net, i, o, w) for i, o, w in zip(ins, outs, widths)])
        net.finish()

    outs = comm_call(
        name,
        number,
        body,
        items,
        [ANY] * k,
        [shape((w,) + i.shape, i.dtype) for i, w in zip(items, widths)],
        [ANY] * k,
        [],
        64 * k,
    )
    return [o.reshape((-1,) + o.shape[2:]) for o in outs]


def reduce_blocks(name, number, items, widths, n_ctx):
    k = len(items)
    blocks = [i.reshape(w, i.shape[0] // w, i.shape[1]) for i, w in zip(items, widths)]

    def body(*refs):
        ins, outs, rest = refs[:k], refs[k : 2 * k], list(refs[2 * k :])
        place = Place(n_ctx)
        greet(place, line=True, across=True, core=16 in widths)
        net = Net(place, rest.pop())
        tasks = []
        for i, o, w in zip(ins, outs, widths):
            near_core = rest.pop(0) if w == 16 else None
            near_x, line_in, line_out = rest.pop(0), rest.pop(0), rest.pop(0)
            tasks.append(
                reduce_steps(net, i, o, near_core, near_x, line_in, line_out, o.shape[0], w)
            )
        run_together(*tasks)
        net.finish()

    scratch = []
    for i, w in zip(blocks, widths):
        scratch += reduce_scratch(i.shape[1], i.shape[2], w)
    return comm_call(
        name,
        number,
        body,
        blocks,
        [VMEM] * k,
        [shape(i.shape[1:], F32) for i in blocks],
        [VMEM] * k,
        scratch,
        64 * k,
    )


def weights_in(number, ff, at, block, n_ctx):
    def body(ff_ref, at_ref, block_ref, own, oth, heads, blocks, ff_sems, at_sems, sems):
        place = Place(n_ctx)
        p = place
        greet(p, everyone=16, other=True)
        net = Net(p, sems)

        def device(g):
            return (g * p.members + p.m, p.t)

        keep_own = pltpu.make_async_copy(ff_ref.at[p.g], own.at[p.g], net.sem())
        keep_own.start()
        owner = p.b == p.t
        f = p.a * 2 + p.b

        def units():
            for k in range(1, 16):
                net.send(
                    lambda k=k: ff_ref.at[p.g ^ k],
                    lambda: own.at[p.g],
                    ff_sems.at[0, k],
                    lambda k=k: device(p.g ^ k),
                )
            net.send(lambda: ff_ref.at[p.g], lambda: oth.at[p.g], ff_sems.at[1, 0], p.other)
            yield
            for k in range(1, 16):
                there = lambda k=k: own.at[p.g ^ k]
                net.recv(there, ff_sems.at[0, k])
                net.send(there, lambda k=k: oth.at[p.g ^ k], ff_sems.at[1, k], p.other)
                yield
            for k in range(16):
                net.recv(lambda k=k: oth.at[p.g ^ k], ff_sems.at[1, k])

        def attention():
            keep = pltpu.make_async_copy(at_ref.at[p.a], heads.at[p.g], net.sem())
            pl.when(owner)(lambda: keep.start())
            for s in range(4):
                net.send(
                    lambda s=s: at_ref.at[s],
                    lambda: heads.at[p.g],
                    at_sems.at[0, f],
                    lambda s=s: p.at(a=s, b=p.t),
                    ~(owner & (p.a == s)),
                )
            pl.when(owner)(lambda: keep.wait())
            yield
            for q in range(8):
                mine = lambda q=q: heads.at[q * 2 + p.d]
                net.recv(mine, at_sems.at[0, q], owner & (f != q))
                net.send(mine, mine, at_sems.at[1, q], p.other, owner)
                net.recv(mine, at_sems.at[1, q], ~owner)
                net.send(mine, mine, at_sems.at[2, q], p.core)
                yield
            for q in range(8):
                net.recv(lambda q=q: heads.at[q * 2 + 1 - p.d], at_sems.at[2, q])

        run_together(attention(), units(), gather_steps(net, block_ref, blocks, 16))
        keep_own.wait()
        net.finish()

    outs = [
        shape(ff.shape),
        shape(ff.shape),
        shape((16,) + at.shape[1:]),
        shape((16,) + block.shape),
    ]
    return comm_call(
        "weights_in",
        number,
        body,
        [ff, at, block],
        [ANY] * 3,
        outs,
        [ANY] * 4,
        [pltpu.SemaphoreType.DMA((2, 16)), pltpu.SemaphoreType.DMA((3, 8))],
        160,
    )


def grads_out(number, ff_own, ff_oth, at, parts, n_ctx):
    def body(
        own, oth, at_ref, parts_ref,
        ff_out, at_out, sum_out,
        ff_near, ff_sum, at_core, at_tp, near_core, near_x, line_in, line_out,
        ff_sems, at_sems, sems,
    ):
        place = Place(n_ctx)
        p = place
        greet(p, everyone=16, other=True)
        net = Net(p, sems)
        owner = p.b == p.t
        f = p.a * 2 + p.b
        rows, at_rows = ff_own.shape[1], at.shape[1]

        def device(g):
            return (g * p.members + p.m, p.t)

        def units():
            order = list(range(1, 16)) + [0]
            for k in order:
                there = lambda k=k: oth.at[p.g ^ k]
                net.send(there, lambda k=k: ff_near.at[p.g ^ k], ff_sems.at[0, k], p.other)
            yield
            for k in order:
                g = p.g ^ k
                net.recv(lambda: ff_near.at[g], ff_sems.at[0, k])
                add_into(ff_sum.at[g], [own.at[g], ff_near.at[g]], rows)
                if k:
                    net.send(
                        lambda g=g: ff_sum.at[g],
                        lambda: ff_out.at[p.g],
                        ff_sems.at[1, k],
                        lambda g=g: device(g),
                    )
                else:
                    keep = pltpu.make_async_copy(ff_sum.at[g], ff_out.at[g], net.sem())
                    keep.start()
                yield
            for k in range(1, 16):
                net.recv(lambda k=k: ff_out.at[p.g ^ k], ff_sems.at[1, k])
            keep.wait()

        def attention():
            for q in range(8):
                net.send(
                    lambda q=q: at_ref.at[q * 2 + 1 - p.d],
                    lambda q=q: at_core.at[q],
                    at_sems.at[0, q],
                    p.core,
                )
            yield
            for q in range(8):
                near = at_core.at[q]
                net.recv(lambda: near, at_sems.at[0, q])
                add_into(near, [near, at_ref.at[q * 2 + p.d]], at_rows)
                net.send(
                    lambda near=near: near,
                    lambda q=q: at_tp.at[q],
                    at_sems.at[1, q],
                    p.other,
                    ~owner,
                )
                yield
            keep = pltpu.make_async_copy(at_core.at[f], at_out.at[p.a], net.sem())
            for q in range(8):
                near, tp = at_core.at[q], at_tp.at[q]
                net.recv(lambda: tp, at_sems.at[1, q], owner)
                pl.when(owner)(lambda: add_into(near, [near, tp], at_rows))
                net.send(
                    lambda near=near: near,
                    lambda: at_out.at[p.a],
                    at_sems.at[2, p.a],
                    lambda q=q: p.at(a=q // 2, b=q % 2),
                    owner & (f != q),
                )
                pl.when(owner & (f == q))(lambda: keep.start())
                yield
            for s in range(4):
                net.recv(lambda s=s: at_out.at[s], at_sems.at[2, s], ~(owner & (p.a == s)))
            pl.when(owner)(lambda: keep.wait())

        run_together(
            attention(),
            reduce_steps(
                net, parts_ref, sum_out, near_core, near_x, line_in, line_out, sum_out.shape[0], 16
            ),
            units(),
        )
        net.finish()

    outs = [
        shape(ff_own.shape),
        shape((4,) + at.shape[1:]),
        shape(parts.shape[1:], F32),
    ]
    scratch = [
        pltpu.VMEM(ff_own.shape, BF),
        pltpu.VMEM(ff_own.shape, BF),
        pltpu.VMEM((8,) + at.shape[1:], BF),
        pltpu.VMEM((8,) + at.shape[1:], BF),
    ]
    scratch += reduce_scratch(parts.shape[1], parts.shape[2], 16)
    scratch += [pltpu.SemaphoreType.DMA((2, 16)), pltpu.SemaphoreType.DMA((3, 8))]
    return comm_call(
        "grads_out",
        number,
        body,
        [ff_own, ff_oth, at, parts],
        [VMEM, ANY, VMEM, VMEM],
        outs,
        [ANY, ANY, VMEM],
        scratch,
        160,
    )


def gather_latent(number, pair_block, query_block, column_blocks, n_ctx):
    def body(pair_ref, query_ref, col_ref, pair, pairs, queries, cols, col_sems, sems):
        place = Place(n_ctx)
        p = place
        greet(p, everyone=16, other=True)
        net = Net(p, sems)

        def columns():
            keep = pltpu.make_async_copy(col_ref.at[p.g], cols.at[p.g], net.sem())
            keep.start()
            for k in range(1, 16):
                net.send(
                    lambda k=k: col_ref.at[p.g ^ k],
                    lambda: cols.at[p.g],
                    col_sems.at[k],
                    lambda k=k: ((p.g ^ k) * p.members + p.m, p.t),
                )
            yield
            yield
            yield
            for k in range(1, 16):
                net.recv(lambda k=k: cols.at[p.g ^ k], col_sems.at[k])
            keep.wait()

        def latents():
            sem = net.sem()
            keep = pltpu.make_async_copy(pair_ref, pair.at[p.t], net.sem())
            keep.start()
            net.send(lambda: pair_ref, lambda: pair.at[p.t], sem, p.other)
            yield
            net.recv(lambda: pair.at[1 - p.t], sem)
            keep.wait()
            yield from gather_steps(net, pair, pairs, 16)

        run_together(latents(), gather_steps(net, query_ref, queries, 8), columns())
        net.finish()

    pair_shape = (2,) + pair_block.shape
    return comm_call(
        "gather_latent",
        number,
        body,
        [pair_block, query_block, column_blocks],
        [ANY] * 3,
        [
            shape(pair_shape),
            shape((16,) + pair_shape),
            shape((8,) + query_block.shape),
            shape(column_blocks.shape),
        ],
        [ANY] * 4,
        [pltpu.SemaphoreType.DMA((16,))],
        180,
    )[1:]


def reduce_latent(number, pairs, queries, n_ctx):
    def body(pairs_ref, queries_ref, pair_out, query_out, tp_in, *rest):
        place = Place(n_ctx)
        p = place
        greet(p, line=True, across=True, core=True, other=True)
        rest = list(rest)
        net = Net(p, rest.pop())
        rows = pair_out.shape[0]

        def latents():
            sems = [net.sem() for _ in range(16)]
            for g in range(16):
                net.send(
                    lambda g=g: pairs_ref.at[g, 1 - p.t], lambda g=g: tp_in.at[g], sems[g], p.other
                )
            yield
            for g in range(16):
                net.recv(lambda g=g: tp_in.at[g], sems[g])
                add_into(tp_in.at[g], [tp_in.at[g], pairs_ref.at[g, p.t]], rows)
            yield from reduce_steps(net, tp_in, pair_out, *rest[:4], rows, 16)

        run_together(
            latents(),
            reduce_steps(net, queries_ref, query_out, None, *rest[4:7], query_out.shape[0], 8),
        )
        net.finish()

    rows, cols = pairs.shape[2:]
    scratch = [pltpu.VMEM((16, rows, cols), BF)]
    scratch += reduce_scratch(rows, cols, 16)
    scratch += reduce_scratch(queries.shape[1], queries.shape[2], 8)
    return comm_call(
        "reduce_latent",
        number,
        body,
        [pairs, queries],
        [VMEM] * 2,
        [shape((rows, cols), F32), shape(queries.shape[1:], F32)],
        [VMEM] * 2,
        scratch,
        180,
    )


def finish_blocks(number, swaps, gain_blocks, n_ctx):
    k = len(swaps)

    def body(*refs):
        ins, gains = refs[:k], refs[k]
        outs, gains_out = refs[k + 1 : 2 * k + 1], refs[2 * k + 1]
        rest = list(refs[2 * k + 2 :])
        net_sems = rest.pop()
        tp_in = rest.pop(0)
        place = Place(n_ctx)
        greet(place, line=True, across=True, core=True, other=True)
        net = Net(place, net_sems)

        def sums():
            sem = net.sem()
            net.send(lambda: gains, lambda: tp_in, sem, place.other)
            yield
            net.recv(lambda: tp_in, sem)
            pl.loop(0, 16)(
                lambda g: add_into(tp_in.at[g], [tp_in.at[g], gains.at[g]], gains.shape[1])
            )
            yield from reduce_steps(net, tp_in, gains_out, *rest, gains_out.shape[0], 16)

        run_together(sums(), *[swap_steps(net, i, o) for i, o in zip(ins, outs)])
        net.finish()

    scratch = [pltpu.VMEM(gain_blocks.shape, BF)]
    scratch += reduce_scratch(gain_blocks.shape[1], gain_blocks.shape[2], 16)
    return comm_call(
        "finish_blocks",
        number,
        body,
        list(swaps) + [gain_blocks],
        [ANY] * k + [VMEM],
        [shape(s.shape, s.dtype) for s in swaps] + [shape(gain_blocks.shape[1:], F32)],
        [ANY] * k + [VMEM],
        scratch,
        100,
    )


def shards(
    layer_input,
    first_gain,
    query_down,
    query_gain,
    query_up,
    latent_down,
    latent_gain,
    latent_up,
    out_weight,
    second_gain,
    gate_weight,
    up_weight,
    down_weight,
    out_grad,
):
    n_ctx = lax.axis_size("ctx")
    n_tp = lax.axis_size("tp")
    members = n_ctx // 16
    c = lax.axis_index("ctx")
    t = lax.axis_index("tp")
    g = c // members
    b = lax.rem(g // 2, 2)
    d = lax.rem(g, 2)
    member = lax.rem(c, members)
    ctx_rows, dim = layer_input.shape
    rows = ctx_rows // n_tp
    shard_rows = query_down.shape[0]
    qr = query_down.shape[1]
    heads = H // 8
    units = gate_weight.shape[1] // 16
    member_lists = [[k * members + m for m in range(members)] for k in range(16)]

    def widen(blocks):
        if members == 1:
            return blocks[:, None]
        return lax.all_gather(blocks, "ctx", axis=1, axis_index_groups=member_lists)

    def narrow(blocks):
        if members == 1:
            return blocks[:, 0]
        return lax.psum_scatter(
            blocks.astype(F32), "ctx", scatter_dimension=1, axis_index_groups=member_lists
        ).astype(BF)

    widths = [first_gain.shape[0], query_gain.shape[0], latent_gain.shape[0], second_gain.shape[0]]
    starts = [0, widths[0], widths[0] + widths[1], widths[0] + widths[1] + widths[2]]
    gains = jnp.concatenate([first_gain, query_gain, latent_gain, second_gain]).astype(F32)
    gains = jnp.broadcast_to(gains[None], (8, gains.shape[0]))
    down_shard = jnp.concatenate([query_down, latent_down], axis=1)
    down_full, gains = gather_blocks("gather_entry", 1, [down_shard, gains], [16, 16], n_ctx)
    down_full = widen(down_full.reshape(16, shard_rows, -1)).reshape(dim, -1)
    gains = widen(gains.reshape(16, 8, -1)[:, 0]).reshape(n_ctx, -1)
    gain_first, gain_query, gain_latent, gain_second = [
        gains[:, s : s + w].reshape(-1) for s, w in zip(starts, widths)
    ]

    def unit_pieces(shard):
        return jnp.transpose(shard.reshape(shard_rows, 16, units), (1, 0, 2))

    wide = 640
    ff = jnp.concatenate(
        [
            unit_pieces(gate_weight),
            unit_pieces(up_weight),
            unit_pieces(down_weight.T),
            jnp.zeros((16, shard_rows, wide - 3 * units), BF),
        ],
        axis=2,
    )
    q_rows_w, l_rows_w, o_rows_w = query_up.shape[0], latent_up.shape[0], shard_rows // 2
    q_width, o_width = heads * (NOPE + ROPE), heads * VH
    at = jnp.concatenate(
        [
            jnp.pad(
                jnp.transpose(query_up.reshape(q_rows_w, 4, q_width), (1, 0, 2)),
                ((0, 0), (0, 0), (0, wide - q_width)),
            ),
            jnp.transpose(latent_up.reshape(l_rows_w, 4, wide), (1, 0, 2)),
            jnp.transpose(out_weight.reshape(4, o_width, shard_rows), (0, 2, 1)).reshape(
                4, o_rows_w, wide
            ),
        ],
        axis=1,
    )

    x = lax.dynamic_slice_in_dim(layer_input, t * rows, rows, 0).astype(F32)
    out_grad_rows = lax.dynamic_slice_in_dim(out_grad, t * rows, rows, 0).astype(F32)
    positions = c * ctx_rows + t * rows + jnp.arange(rows, dtype=jnp.int32)
    cosine, sine_table = rope_tables(positions)
    grad_ffn = (residual_scale * out_grad_rows).astype(BF)

    ff_own, ff_oth, at_all, gf_all = weights_in(2, ff, at, grad_ffn, n_ctx)
    gf_all = gf_all.reshape(-1, dim)
    w_own = widen(ff_own).reshape(dim, wide)
    w_oth = widen(ff_oth).reshape(dim, wide)

    def third(k):
        return jnp.concatenate(
            [w[:, k * units : (k + 1) * units] for w in (w_own, w_oth)], axis=1
        )

    w_gate, w_up, w_down_t = third(0), third(1), third(2)
    at_all = widen(at_all).reshape(n_ctx, -1, wide)
    q_up = at_all[:, :q_rows_w, :q_width].reshape(qr, q_width)
    l_up = at_all[:, q_rows_w : q_rows_w + l_rows_w].reshape(KVR, wide)
    w_out_t = at_all[:, q_rows_w + l_rows_w :].reshape(dim, o_width)

    normed = rms_norm(x, gain_first).astype(BF)
    both = matmul(normed, down_full)
    query_latent, compressed = both[:, :qr], both[:, qr:]
    query_normed = rms_norm(query_latent, gain_query).astype(BF)
    latent = rms_norm(compressed[:, :KVR], gain_latent).astype(BF)
    key_rope = rotate(compressed[:, KVR:], cosine, sine_table).astype(BF)
    pair_block = jnp.concatenate(
        [latent, key_rope, jnp.zeros((rows, 384 - KVR - ROPE), BF)], axis=1
    )
    normed_columns = jnp.transpose(
        normed.reshape(rows, 16, dim // 16), (1, 0, 2)
    )
    pairs, qn_all, token_columns = gather_latent(
        3, pair_block, query_normed, normed_columns, n_ctx
    )
    lat_rope = widen(pairs).reshape(-1, 384)
    latent_all, rope_all = lat_rope[:, :KVR], lat_rope[:, KVR : KVR + ROPE]
    qn_all = qn_all.reshape(-1, qr)
    q_rows = qn_all.shape[0]
    keys = latent_all.shape[0]

    q_positions = (
        ((jnp.arange(8, dtype=jnp.int32)[:, None] * 2 + d) * members + member) * ctx_rows
        + t * rows
        + jnp.arange(rows, dtype=jnp.int32)[None, :]
    ).reshape(-1)
    q_cos, q_sin = rope_tables(q_positions)
    queries_raw = matmul(qn_all, q_up).reshape(q_rows, heads, NOPE + ROPE)
    queries = jnp.concatenate(
        [
            queries_raw[..., :NOPE],
            rotate(queries_raw[..., NOPE:], q_cos[:, None, :], q_sin[:, None, :]),
        ],
        axis=-1,
    ).astype(BF)
    expanded = matmul(latent_all, l_up).astype(BF)
    allowed = jnp.arange(keys, dtype=jnp.int32)[None, :] <= q_positions[:, None]

    def head_keys(h):
        part = expanded[:, h * (NOPE + VH) : (h + 1) * (NOPE + VH)]
        return jnp.concatenate([part[:, :NOPE], rope_all], axis=1), part[:, NOPE:]

    outs, logs = [], []
    for h in range(heads):
        k, v = head_keys(h)
        scores = jnp.where(allowed, matmul_nt(queries[:, h], k) * score_scale, -1e30)
        top = jnp.max(scores, axis=-1, keepdims=True)
        weights = jnp.exp(scores - top)
        total = jnp.sum(weights, axis=-1, keepdims=True)
        outs.append(matmul(weights.astype(BF), v) / total)
        logs.append(top + jnp.log(total))
    attended_wide = jnp.concatenate(outs, axis=1)
    attended = attended_wide.astype(BF)

    (branch,) = reduce_blocks(
        "reduce_branch", 4, [matmul_nt(attended, w_out_t).astype(BF)], [8], n_ctx
    )
    middle = x + residual_scale * branch
    normed_second = rms_norm(middle, gain_second).astype(BF)
    (ns_all,) = gather_blocks("gather_second", 5, [normed_second], [16], n_ctx)
    gate_values = matmul(ns_all, w_gate)
    up_values = matmul(ns_all, w_up)
    sigmoid_gate = jax.nn.sigmoid(gate_values)
    hidden = (gate_values * sigmoid_gate * up_values).astype(BF)
    ffn_part = matmul_nt(hidden, w_down_t).astype(BF)

    grad_hidden = matmul(gf_all, w_down_t)
    grad_gate = (
        grad_hidden * up_values * sigmoid_gate * (1.0 + gate_values * (1.0 - sigmoid_gate))
    ).astype(BF)
    grad_up = (grad_hidden * gate_values * sigmoid_gate).astype(BF)
    (grad_second,) = reduce_blocks(
        "reduce_second",
        6,
        [(matmul_nt(grad_gate, w_gate) + matmul_nt(grad_up, w_up)).astype(BF)],
        [16],
        n_ctx,
    )

    ff_grads = [
        matmul_tn(ns_all, grad_gate).astype(BF),
        matmul_tn(ns_all, grad_up).astype(BF),
        matmul_tn(gf_all, hidden).astype(BF),
        jnp.zeros((dim, 2 * (wide - 3 * units)), BF),
    ]

    def half_grads(k):
        whole = jnp.concatenate(
            [p[:, : p.shape[1] // 2] if k == 0 else p[:, p.shape[1] // 2 :] for p in ff_grads],
            axis=1,
        )
        return narrow(whole.reshape(16, members, shard_rows, wide))

    grads_own, grads_oth = half_grads(0), half_grads(1)

    grad_middle_part, second_gain_part = norm_back(middle, gain_second, grad_second)
    grad_middle = out_grad_rows + grad_middle_part

    grad_branch = (residual_scale * grad_middle).astype(BF)
    (gb_all,) = gather_blocks("gather_branch", 7, [grad_branch], [8], n_ctx)
    out_part = matmul_tn(gb_all, attended).astype(BF)
    grad_attended = matmul(gb_all, w_out_t).astype(BF)

    grad_q_rows, grad_kv, grad_rope = [], [], jnp.zeros((keys, ROPE), F32)
    for h in range(heads):
        k, v = head_keys(h)
        q, ga = queries[:, h], grad_attended[:, h * VH : (h + 1) * VH]
        row_inner = jnp.sum(
            ga.astype(F32) * attended_wide[:, h * VH : (h + 1) * VH], axis=-1, keepdims=True
        )
        scores = jnp.where(allowed, matmul_nt(q, k) * score_scale, -1e30)
        probs = jnp.exp(scores - logs[h])
        grad_probs = matmul_nt(ga, v)
        grad_scores = (probs * (grad_probs - row_inner)).astype(BF)
        gq = matmul(grad_scores, k) * score_scale
        grad_q_rows += [gq[:, :NOPE], rotate(gq[:, NOPE:], q_cos, -q_sin)]
        gk = matmul_tn(grad_scores, q) * score_scale
        grad_kv += [gk[:, :NOPE], matmul_tn(probs.astype(BF), ga)]
        grad_rope = grad_rope + gk[:, NOPE:]
    grad_q_rows = jnp.concatenate(grad_q_rows, axis=1).astype(BF)
    grad_expanded = jnp.concatenate(grad_kv, axis=1).astype(BF)
    grad_lat_rope = jnp.concatenate(
        [
            matmul_nt(grad_expanded, l_up),
            grad_rope,
            jnp.zeros((keys, 384 - KVR - ROPE), F32),
        ],
        axis=1,
    ).astype(BF)
    l_up_part = matmul_tn(latent_all, grad_expanded).astype(BF)
    q_up_part = matmul_tn(qn_all, grad_q_rows).astype(BF)
    gqn_part = matmul_nt(grad_q_rows, q_up).astype(BF)

    own_lat_rope, grad_query_normed = reduce_latent(
        8,
        narrow(grad_lat_rope.reshape(16, members, 2, rows, 384)),
        gqn_part.reshape(8, rows, qr),
        n_ctx,
    )
    grad_query_latent, query_gain_part = norm_back(query_latent, gain_query, grad_query_normed)
    grad_latent_rows, latent_gain_part = norm_back(
        compressed[:, :KVR], gain_latent, own_lat_rope[:, :KVR]
    )
    grad_both = jnp.concatenate(
        [
            grad_query_latent,
            grad_latent_rows,
            rotate(own_lat_rope[:, KVR : KVR + ROPE], cosine, -sine_table),
        ],
        axis=1,
    ).astype(BF)
    if members == 1:
        (both_all,) = gather_blocks("gather_both", 9, [grad_both], [16], n_ctx)
        down_part = matmul_tn(token_columns.reshape(16 * rows, shard_rows), both_all).astype(BF)
    else:
        down_part = lax.psum_scatter(
            matmul_tn(normed, grad_both).astype(BF), "ctx", scatter_dimension=0, tiled=True
        )
    grad_normed = matmul_nt(grad_both, down_full)
    grad_input_part, first_gain_part = norm_back(x, gain_first, grad_normed)
    input_half = (grad_middle + grad_input_part).astype(BF)

    at_part = jnp.concatenate(
        [
            jnp.pad(q_up_part, ((0, 0), (0, wide - q_width))).reshape(n_ctx, q_rows_w, wide),
            l_up_part.reshape(n_ctx, l_rows_w, wide),
            out_part.reshape(n_ctx, o_rows_w, wide),
        ],
        axis=1,
    )
    at_part = narrow(at_part.reshape(16, members, -1, wide))
    ff_sums, at_sums, ffn_sum = grads_out(
        10, grads_own, grads_oth, at_part, ffn_part.reshape(16, rows, dim), n_ctx
    )
    out_half = (middle + residual_scale * ffn_sum).astype(BF)

    gain_parts = jnp.concatenate(
        [
            p.reshape(n_ctx, -1)
            for p in (first_gain_part, query_gain_part, latent_gain_part, second_gain_part)
        ],
        axis=1,
    )
    gain_parts = narrow(gain_parts.reshape(16, members, -1)).astype(BF)
    gain_blocks = jnp.pad(gain_parts[:, None], ((0, 0), (0, 15), (0, 0)))
    out_other, input_other, down_other, gain_sums = finish_blocks(
        11, [out_half, input_half, down_part], gain_blocks, n_ctx
    )

    def in_order(mine, other):
        return jnp.where(
            t == 0, jnp.concatenate([mine, other]), jnp.concatenate([other, mine])
        )

    layer_output = in_order(out_half, out_other)
    input_grad = in_order(input_half, input_other).astype(F32)
    down_grads = down_part.astype(F32) + down_other.astype(F32)
    gain_grads = gain_sums[0]
    first_gain_grad, query_gain_grad, latent_gain_grad, second_gain_grad = [
        gain_grads[s : s + w] for s, w in zip(starts, widths)
    ]

    def unit_grads(k):
        part = ff_sums[:, :, k * units : (k + 1) * units]
        return jnp.transpose(part, (1, 0, 2)).reshape(shard_rows, 16 * units).astype(F32)

    query_up_grad = jnp.transpose(at_sums[:, :q_rows_w, :q_width], (1, 0, 2)).reshape(
        q_rows_w, 4 * q_width
    )
    latent_up_grad = jnp.transpose(at_sums[:, q_rows_w : q_rows_w + l_rows_w], (1, 0, 2)).reshape(
        l_rows_w, 4 * wide
    )
    out_weight_grad = jnp.transpose(
        at_sums[:, q_rows_w + l_rows_w :].reshape(4, shard_rows, o_width), (0, 2, 1)
    ).reshape(4 * o_width, shard_rows)
    return (
        layer_output,
        input_grad,
        first_gain_grad,
        down_grads[:, :qr],
        query_gain_grad,
        query_up_grad.astype(F32),
        down_grads[:, qr:],
        latent_gain_grad,
        latent_up_grad.astype(F32),
        out_weight_grad.astype(F32),
        second_gain_grad,
        unit_grads(0),
        unit_grads(1),
        unit_grads(2).T,
    )


def solution(mesh):
    return jax.shard_map(
        shards,
        mesh=mesh,
        in_specs=(
            P("ctx", None),
            P("ctx"),
            P("ctx", None),
            P("ctx"),
            P("ctx", "tp"),
            P("ctx", None),
            P("ctx"),
            P("ctx", "tp"),
            P("tp", "ctx"),
            P("ctx"),
            P("ctx", "tp"),
            P("ctx", "tp"),
            P("tp", "ctx"),
            P("ctx", None),
        ),
        out_specs=(
            P("ctx", None),
            P("ctx", None),
            P("ctx"),
            P("ctx", None),
            P("ctx"),
            P("ctx", "tp"),
            P("ctx", None),
            P("ctx"),
            P("ctx", "tp"),
            P("tp", "ctx"),
            P("ctx"),
            P("ctx", "tp"),
            P("ctx", "tp"),
            P("tp", "ctx"),
        ),
        check_vma=False,
    )
```

time: 1480 us -> 995 us (0.67)
  waiting for transfers between devices: 932 us -> 0 us
  Pallas kernels: 0 us -> 695 us
  blocking collectives: 116 us -> 0 us
  starting transfers between devices: 67 us -> 0 us
  local copies, waits for them, and re-layouts: 144 us -> 123 us
    pallas_call x0 -> x11, Pallas kernels: none -> 695 us  [comm_call(): pl.pallas_call(body, out_shape=outs, in_specs=in_specs, out_specs=out_spe...]
    reduce_scatter x8 -> x0, waiting for transfers between devices: 267 us -> none  [the longest x4 227 us: scatter_over(): lax.psum_scatter(values, 'ctx', scatter_dimension=0, tiled=True, axis_ind...]
    all_gather x9 -> x0, waiting for transfers between devices: 247 us -> none  [the longest x1 57.1 us: shards(): down_full = lax.all_gather(down_shard, 'ctx', axis=0, tiled=True)]
    ppermute x12 -> x0, waiting for transfers between devices: 200 us -> none  [swap_tp(): return lax.ppermute(values, 'tp', [(0, 1), (1, 0)])]
    all_to_all x6 -> x0, waiting for transfers between devices: 133 us -> none  [the longest x3 106 us: to_units(): lax.all_to_all(jnp.transpose(pieces, (1, 0, 2)), 'ctx', 0, 0, axis_index_...]
    unnamed x20 -> x0, waiting for transfers between devices: 84.7 us -> none
    all_gather x3 -> x0, blocking collectives: 56.9 us -> none  [the longest x1 27.9 us: gather_over(): lax.all_gather(values, 'ctx', axis=0, tiled=True, axis_index_groups=membe...]
    unnamed x1 -> x0, blocking collectives: 54.8 us -> none
  transfers between devices with their start and end apart: 37 -> 0, of which waited for: 23 -> 0; matrix products, arithmetic and copies ran while one was open for 17% -> 0% of each run, Pallas kernels for 0% -> 0%
where the time goes in v2:
time: 995 us; the launch traced here: 979 us
  Pallas kernels  695 us (70%)
  local copies, waits for them, and re-layouts  123 us (12%)
  matrix products  104 us (10%)
  other arithmetic  54.7 us (5%)
    pallas_call x11, Pallas kernels, comm_call(): pl.pallas_call(body, out_shape=outs, in_specs=in_specs, out_specs=out_spe...  695 us
    dot_general x17, matrix products, matmul_nt(): lax.dot_general(left_side, right_side, (((1,), (1,)), ((), ())), preferre...  41.2 us
    dot_general x17, matrix products, matmul(): return jnp.dot(left_side, right_side, preferred_element_type=F32)  35.6 us
    dot_general x17, matrix products, matmul_tn(): lax.dot_general(left_side, right_side, (((0,), (0,)), ((), ())), preferre...  26.7 us

profile of v2, /device:TPU:3, one launch (start us, length us, event | category | flops | bytes accessed | tf_op | source)
XLA Modules:
  0.0 979.4 jit_solution(17118170363633761951)
XLA Ops:
  3.8 40.9 %gather_entry.1 = (bf16[16,160,1056]{2,1,0:T(8,128)(2,1)}, f32[16,8,384]{2,1,0:T(8,128)}) custom-call(bf16[160,1056]{1,0:T(8,128)(2,1)} %pad_maximum_fusion.16.refs_0_, f32[8,384]{1,0:T(8,128)} %broadcast_in_dim.21.refs_1_), custom_call_target="tpu_custom_call" | custom-call | tf_op jit(solution)/shard_map/gather_entry/pallas_call | solution.py:367
  58.3 36.8 %gather_latent.1 = (bf16[2,64,384]{2,1,0:T(8,128)(2,1)}, bf16[16,2,64,384]{3,2,1,0:T(8,128)(2,1)}, bf16[8,64,768]{2,1,0:T(8,128)(2,1)}, bf16[16,64,160]{2,1,0:T(8,128)(2,1)}) custom-call(bf16[64,384]{1,0:T(8,128)(2,1)} %maximum_maximum_fusion.4.pair_ref, bf16[64,768]{1,0:T(8,128)(2,1)} %multiply_convert_fusion.10.query_ref, bf16[16,64,160]{2,1,0:T(8,128)(2,1)} %bitcast.188), custom_call_target="tpu_custom_call" | custom-call | tf_op jit(solution)/shard_map/gather_latent/pallas_call | solution.py:367
  100.4 5.0 reshape.448
  107.9 5.8 reshape.447
  121.9 182.4 %weights_in.1 = (bf16[16,160,640]{2,1,0:T(8,128)(2,1)}, bf16[16,160,640]{2,1,0:T(8,128)(2,1)}, bf16[16,144,640]{2,1,0:T(8,128)(2,1)}, bf16[16,64,2560]{2,1,0:T(8,128)(2,1)}) custom-call(bf16[16,160,640]{2,1,0:T(8,128)(2,1)} %maximum_maximum_fusion.ff_ref, bf16[4,144,640]{2,1,0:T(8,128)(2,1)} %fusion.66.at_ref, bf16[64,2560]{1,0:T(8,128)(2,1)} %get-tuple-element.146.block_ref), custom_call_target="tpu_custom_call" | custom-call | tf_op jit(solution)/shard_map/weights_in/pallas_call | solution.py:367
  339.4 4.7 convolution_convert_fusion.1
  344.1 40.6 %reduce_branch.1 = f32[64,2560]{1,0:T(8,128)} custom-call(bf16[8,64,2560]{2,1,0:T(8,128)(2,1)} %bitcast.186), custom_call_target="tpu_custom_call" | custom-call | tf_op jit(solution)/shard_map/reduce_branch/pallas_call | solution.py:367
  392.3 4.4 fusion.44
  399.5 37.1 %gather_second.1 = bf16[16,64,2560]{2,1,0:T(8,128)(2,1)} custom-call(bf16[64,2560]{1,0:T(8,128)(2,1)} %multiply_convert_fusion.9.refs_0_), custom_call_target="tpu_custom_call" | custom-call | tf_op jit(solution)/shard_map/gather_second/pallas_call | solution.py:367
  436.7 5.9 fusion.43
  458.3 5.6 copy.92
  463.9 5.7 copy.93
  469.6 5.8 fusion.41
  475.4 5.8 add_convert_fusion
  481.2 41.2 %reduce_second.1 = f32[64,2560]{1,0:T(8,128)} custom-call(bf16[16,64,2560]{2,1,0:T(8,128)(2,1)} %bitcast.176), custom_call_target="tpu_custom_call" | custom-call | tf_op jit(solution)/shard_map/reduce_second/pallas_call | solution.py:367
  526.7 31.5 %gather_branch.1 = bf16[8,64,2560]{2,1,0:T(8,128)(2,1)} custom-call(bf16[64,2560]{1,0:T(8,128)(2,1)} %get-tuple-element.73.refs_0_), custom_call_target="tpu_custom_call" | custom-call | tf_op jit(solution)/shard_map/gather_branch/pallas_call | solution.py:367
  566.0 4.2 reshape.464
  609.5 5.7 convolution_convert_fusion
  615.2 163.9 %grads_out.1 = (bf16[16,160,640]{2,1,0:T(8,128)(2,1)}, bf16[4,144,640]{2,1,0:T(8,128)(2,1)}, f32[64,2560]{1,0:T(8,128)}) custom-call(bf16[16,160,640]{2,1,0:T(8,128)(2,1)} %bitcast.169, bf16[16,160,640]{2,1,0:T(8,128)(2,1)} %bitcast.170, bf16[16,144,640]{2,1,0:T(8,128)(2,1)} %pad_maximum_fusion.at_ref, bf16[16,64,2560]{2,1,0:T(8,128)(2,1)} %bitcast.171), custom_call_target="tpu_custom_call" | custom-call | tf_op jit(solution)/shard_map/grads_out/pallas_call | solution.py:367
  793.0 5.6 concatenate.172
  802.8 54.8 %reduce_latent.1 = (f32[64,384]{1,0:T(8,128)}, f32[64,768]{1,0:T(8,128)}) custom-call(bf16[16,2,64,384]{3,2,1,0:T(8,128)(2,1)} %maximum_maximum_fusion.3.pairs_ref, bf16[8,64,768]{2,1,0:T(8,128)(2,1)} %bitcast.207), custom_call_target="tpu_custom_call" | custom-call | tf_op jit(solution)/shard_map/reduce_latent/pallas_call | solution.py:367
  863.0 4.8 fusion.77
  868.8 28.1 %gather_both.1 = bf16[16,64,1056]{2,1,0:T(8,128)(2,1)} custom-call(bf16[64,1056]{1,0:T(8,128)(2,1)} %copy-done.37), custom_call_target="tpu_custom_call" | custom-call | tf_op jit(solution)/shard_map/gather_both/pallas_call | solution.py:367
  901.2 38.1 %finish_blocks.1 = (bf16[64,2560]{1,0:T(8,128)(2,1)}, bf16[64,2560]{1,0:T(8,128)(2,1)}, bf16[160,1056]{1,0:T(8,128)(2,1)}, f32[16,384]{1,0:T(8,128)}) custom-call(bf16[64,2560]{1,0:T(8,128)(2,1)} %add_convert_fusion.1.refs_0_, bf16[64,2560]{1,0:T(8,128)(2,1)} %fusion.72.refs_1_, bf16[160,1056]{1,0:T(8,128)(2,1)} %fusion.15.refs_2_, ...), custom_call_target="tpu_custom_call" | custom-call | tf_op jit(solution)/shard_map/finish_blocks/pallas_call | solution.py:367
  (486 shorter events, 212.2 us)
Async XLA Ops:
  53.3 47.1 %copy-start.10 = (f32[64,1056]{1,0:T(8,128)}, f32[64,1056]{1,0:T(8,128)S(1)}, u32[]{:S(2)}) copy-start(f32[64,1056]{1,0:T(8,128)S(1)} %fusion.188) | copy-start | bytes 811012
  53.4 43.1 %copy-start.59 = (bf16[3200,160]{0,1:T(8,128)(2,1)S(1)}, bf16[3200,160]{0,1:T(8,128)(2,1)}, u32[]{:S(2)}) copy-start(bf16[3200,160]{0,1:T(8,128)(2,1)} %param.26) | copy-start | bytes 3072004
  53.4 259.2 %copy-start.82 = (f32[16]{0:T(128)}, f32[16]{0:T(128)S(1)}, u32[]{:S(2)}) copy-start(f32[16]{0:T(128)S(1)} %multiply_power_fusion) | copy-start | bytes 196
  54.2 42.2 %copy-start.110 = (f32[256]{0:T(256)}, f32[256]{0:T(256)S(1)}, u32[]{:S(2)}) copy-start(f32[256]{0:T(256)S(1)} %mul.578) | copy-start | bytes 3076
  55.0 41.4 %copy-start.115 = (bf16[384]{0:T(512)(128)(2,1)}, bf16[384]{0:T(512)(128)(2,1)S(1)}, u32[]{:S(2)}) copy-start(bf16[384]{0:T(512)(128)(2,1)S(1)} %pad.70.clone) | copy-start | bytes 2308
  55.8 40.6 %copy-start.85 = (f32[768]{0:T(1024)}, f32[768]{0:T(1024)S(1)}, u32[]{:S(2)}) copy-start(f32[768]{0:T(1024)S(1)} %mul.592) | copy-start | bytes 9220
  96.4 222.9 %copy-start.79 = (bf16[2048,32]{0,1:T(8,128)(2,1)}, bf16[2048,32]{0,1:T(8,128)(2,1)S(1)}, u32[]{:S(2)}) copy-start(bf16[2048,32]{0,1:T(8,128)(2,1)S(1)} %copy.129) | copy-start | bytes 393220
  121.9 183.4 %copy-start.34 = (bf16[16,2,64,384]{3,2,1,0:T(8,128)(2,1)S(1)}, bf16[16,2,64,384]{3,2,1,0:T(8,128)(2,1)}, u32[]{:S(2)}) copy-start(bf16[16,2,64,384]{3,2,1,0:T(8,128)(2,1)} %get-tuple-element.36) | copy-start | bytes 4718596
  339.4 45.3 %copy-start.19 = (bf16[128,2560]{1,0:T(8,128)(2,1)S(1)}, bf16[128,2560]{1,0:T(8,128)(2,1)}, u32[]{:S(2)}) copy-start(bf16[128,2560]{1,0:T(8,128)(2,1)} %param.14) | copy-start | bytes 1966084
  344.1 42.5 %copy-start.18 = (bf16[16,160,640]{2,1,0:T(8,128)(2,1)S(1)}, bf16[16,160,640]{2,1,0:T(8,128)(2,1)}, u32[]{:S(2)}) copy-start(bf16[16,160,640]{2,1,0:T(8,128)(2,1)} %get-tuple-element.39) | copy-start | bytes 9830404
  481.2 41.3 %copy-start.124 = (f32[64]{0:T(128)S(1)}, f32[64]{0:T(128)}, u32[]{:S(2)}) copy-start(f32[64]{0:T(128)} %copy-done.123) | copy-start | bytes 772
  481.2 43.1 %copy-start.60 = (bf16[128,2560]{1,0:T(8,128)(2,1)S(1)}, bf16[128,2560]{1,0:T(8,128)(2,1)}, u32[]{:S(2)}) copy-start(bf16[128,2560]{1,0:T(8,128)(2,1)} %param.27) | copy-start | bytes 1966084
  801.2 56.4 %copy-start.11 = (f32[64,1056]{1,0:T(8,128)S(1)}, f32[64,1056]{1,0:T(8,128)}, u32[]{:S(2)}) copy-start(f32[64,1056]{1,0:T(8,128)} %copy-done.10) | copy-start | bytes 811012
  801.2 56.4 %copy-start.86 = (f32[768]{0:T(1024)S(1)}, f32[768]{0:T(1024)}, u32[]{:S(2)}) copy-start(f32[768]{0:T(1024)} %copy-done.85) | copy-start | bytes 9220
  801.2 56.4 %copy-start.122 = (f32[64]{0:T(128)S(1)}, f32[64]{0:T(128)}, u32[]{:S(2)}) copy-start(f32[64]{0:T(128)} %copy-done.121) | copy-start | bytes 772
  801.2 58.6 %copy-start.111 = (f32[256]{0:T(256)S(1)}, f32[256]{0:T(256)}, u32[]{:S(2)}) copy-start(f32[256]{0:T(256)} %copy-done.110) | copy-start | bytes 3076
  801.2 58.6 %copy-start.120 = (f32[64]{0:T(128)S(1)}, f32[64]{0:T(128)}, u32[]{:S(2)}) copy-start(f32[64]{0:T(128)} %copy-done.119) | copy-start | bytes 772
  801.2 60.5 %copy-start.128 = (f32[64]{0:T(128)S(1)}, f32[64]{0:T(128)}, u32[]{:S(2)}) copy-start(f32[64]{0:T(128)} %copy-done.127) | copy-start | bytes 772
  801.3 61.7 %copy-start.20 = (bf16[128,2560]{1,0:T(8,128)(2,1)S(1)}, bf16[128,2560]{1,0:T(8,128)(2,1)}, u32[]{:S(2)}) copy-start(bf16[128,2560]{1,0:T(8,128)(2,1)} %param.14) | copy-start | bytes 1966084
  801.3 61.7 %copy-start.77 = (f32[2560]{0:T(1024)S(1)}, f32[2560]{0:T(1024)}, u32[]{:S(2)}) copy-start(f32[2560]{0:T(1024)} %copy-done.76) | copy-start | bytes 30724
  801.3 61.7 %copy-start.126 = (f32[64]{0:T(128)S(1)}, f32[64]{0:T(128)}, u32[]{:S(2)}) copy-start(f32[64]{0:T(128)} %copy-done.125) | copy-start | bytes 772
  896.9 42.4 %copy-start.23 = (bf16[64,2560]{1,0:T(8,128)(2,1)S(1)}, bf16[64,2560]{1,0:T(8,128)(2,1)}, u32[]{:S(2)}) copy-start(bf16[64,2560]{1,0:T(8,128)(2,1)} %add_convert_fusion.1.refs_0_) | copy-start | bytes 983044
  900.0 41.5 %copy-start.24 = (bf16[64,2560]{1,0:T(8,128)(2,1)S(1)}, bf16[64,2560]{1,0:T(8,128)(2,1)}, u32[]{:S(2)}) copy-start(bf16[64,2560]{1,0:T(8,128)(2,1)} %fusion.72.refs_1_) | copy-start | bytes 983044
  900.0 45.1 %copy-start.36 = (bf16[160,1056]{1,0:T(8,128)(2,1)S(1)}, bf16[160,1056]{1,0:T(8,128)(2,1)}, u32[]{:S(2)}) copy-start(bf16[160,1056]{1,0:T(8,128)(2,1)} %fusion.15.refs_2_) | copy-start | bytes 1013764
  (117 other events, 557.9 us)

commit v3 on v2

--- a/solution.py
+++ b/solution.py
@@ -190,12 +190,11 @@
     cores = width == 16
 
     def slot(o, b, d):
-        g = (p.a + o) * 2 + b
-        return out.at[g * 2 + d] if cores else out.at[g]
+        return out.at[((p.a + o) * 2 + b) * 2 + d] if cores else out.at[(p.a + o) * 2 + d]
 
     z_sem = {o: net.sem() for o in OFFSETS if o}
-    x_sem = {o: net.sem() for o in OFFSETS}
-    c_sem = {(s, o): net.sem() for s in (0, 1) for o in OFFSETS} if cores else {}
+    x_sem = {o: net.sem() for o in OFFSETS} if cores else {}
+    c_sem = {(s, o): net.sem() for s in ((0, 1) if cores else (0,)) for o in OFFSETS}
     own_sem = net.sem()
     keep = pltpu.make_async_copy(src, slot(0, p.b, p.d), own_sem)
     keep.start()
@@ -208,18 +207,18 @@
             net.send(origin, here, z_sem[o - 1], p.up, both_of(ok, p.a < 3))
         if o >= 0 and o < 3:
             net.send(origin, here, z_sem[o + 1], p.down, both_of(ok, p.a > 0))
-        net.send(origin, here, x_sem[o], p.across, ok)
         if cores:
-            net.send(origin, here, c_sem[0, o], p.core, ok)
+            net.send(origin, here, x_sem[o], p.across, ok)
+        net.send(origin, here, c_sem[0, o], p.core, ok)
 
     def from_line(o):
         net.recv(lambda: slot(o, p.b, p.d), z_sem[o], p.valid(o))
         forward(o)
 
     def from_across(o):
-        there = lambda: slot(o, 1 - p.b, p.d)
-        net.recv(there, x_sem[o], p.valid(o))
         if cores:
+            there = lambda: slot(o, 1 - p.b, p.d)
+            net.recv(there, x_sem[o], p.valid(o))
             net.send(there, there, c_sem[1, o], p.core, p.valid(o))
 
     forward(0)
@@ -237,9 +236,9 @@
     from_across(-3)
     from_across(3)
     yield
-    if cores:
-        for o in OFFSETS:
-            net.recv(lambda: slot(o, p.b, 1 - p.d), c_sem[0, o], p.valid(o))
+    for o in OFFSETS:
+        net.recv(lambda: slot(o, p.b, 1 - p.d), c_sem[0, o], p.valid(o))
+        if cores:
             net.recv(lambda: slot(o, 1 - p.b, 1 - p.d), c_sem[1, o], p.valid(o))
     keep.wait()
 
@@ -279,6 +278,8 @@
     up_sem = {o: net.sem() for o in (0, 1, 2)}
     down_sem = {o: net.sem() for o in (0, 1, 2)}
 
+    pair = p.b if cores else p.d
+
     def mine(o, b):
         g = (p.a + o) * 2 + b
         return near_core.at[g] if cores else parts.at[g]
@@ -292,10 +293,10 @@
             net.recv(lambda: near_core.at[(p.a + o) * 2 + 1 - p.b], c_sem[1, o], p.valid(o))
             when(p.valid(o), join)
         net.send(
-            lambda o=o: mine(o, 1 - p.b),
+            lambda o=o: mine(o, 1 - pair),
             lambda o=o: near_x.at[p.a + o],
             x_sem[o],
-            p.across,
+            p.across if cores else p.core,
             p.valid(o),
         )
     yield
@@ -305,7 +306,7 @@
             net.recv(lambda: near_core.at[(p.a + o) * 2 + p.b], c_sem[0, o], ok)
 
         def terms(o=o):
-            g = (p.a + o) * 2 + p.b
+            g = (p.a + o) * 2 + pair
             own = [near_core.at[g], parts.at[g * 2 + p.d]] if cores else [parts.at[g]]
             return own + [near_x.at[p.a + o]]
 
@@ -396,7 +397,7 @@
     def body(*refs):
         ins, outs, sems = refs[:k], refs[k : 2 * k], refs[-1]
         place = Place(n_ctx)
-        greet(place, line=True, across=True, core=16 in widths)
+        greet(place, line=True, across=16 in widths, core=True)
         net = Net(place, sems)
         run_together(*[gather_steps(net, i, o, w) for i, o, w in zip(ins, outs, widths)])
         net.finish()
@@ -422,7 +423,7 @@
     def body(*refs):
         ins, outs, rest = refs[:k], refs[k : 2 * k], list(refs[2 * k :])
         place = Place(n_ctx)
-        greet(place, line=True, across=True, core=16 in widths)
+        greet(place, line=True, across=16 in widths, core=True)
         net = Net(place, rest.pop())
         tasks = []
         for i, o, w in zip(ins, outs, widths):
@@ -450,38 +451,13 @@
     )
 
 
-def weights_in(number, ff, at, block, n_ctx):
-    def body(ff_ref, at_ref, block_ref, own, oth, heads, blocks, ff_sems, at_sems, sems):
-        place = Place(n_ctx)
-        p = place
+def weights_in(number, down, gains, at, n_ctx):
+    def body(down_ref, gains_ref, at_ref, downs, gain_blocks, heads, at_sems, tp_sems, sems):
+        p = Place(n_ctx)
         greet(p, everyone=16, other=True)
         net = Net(p, sems)
-
-        def device(g):
-            return (g * p.members + p.m, p.t)
-
-        keep_own = pltpu.make_async_copy(ff_ref.at[p.g], own.at[p.g], net.sem())
-        keep_own.start()
-        owner = p.b == p.t
-        f = p.a * 2 + p.b
-
-        def units():
-            for k in range(1, 16):
-                net.send(
-                    lambda k=k: ff_ref.at[p.g ^ k],
-                    lambda: own.at[p.g],
-                    ff_sems.at[0, k],
-                    lambda k=k: device(p.g ^ k),
-                )
-            net.send(lambda: ff_ref.at[p.g], lambda: oth.at[p.g], ff_sems.at[1, 0], p.other)
-            yield
-            for k in range(1, 16):
-                there = lambda k=k: own.at[p.g ^ k]
-                net.recv(there, ff_sems.at[0, k])
-                net.send(there, lambda k=k: oth.at[p.g ^ k], ff_sems.at[1, k], p.other)
-                yield
-            for k in range(16):
-                net.recv(lambda k=k: oth.at[p.g ^ k], ff_sems.at[1, k])
+        owner = p.d == p.t
+        f = p.a * 2 + p.d
 
         def attention():
             keep = pltpu.make_async_copy(at_ref.at[p.a], heads.at[p.g], net.sem())
@@ -491,158 +467,219 @@
                     lambda s=s: at_ref.at[s],
                     lambda: heads.at[p.g],
                     at_sems.at[0, f],
-                    lambda s=s: p.at(a=s, b=p.t),
+                    lambda s=s: p.at(a=s, d=p.t),
                     ~(owner & (p.a == s)),
                 )
             pl.when(owner)(lambda: keep.wait())
             yield
+            yield
             for q in range(8):
-                mine = lambda q=q: heads.at[q * 2 + p.d]
+                mine = lambda q=q: heads.at[(q // 2 * 2 + p.b) * 2 + q % 2]
                 net.recv(mine, at_sems.at[0, q], owner & (f != q))
-                net.send(mine, mine, at_sems.at[1, q], p.other, owner)
-                net.recv(mine, at_sems.at[1, q], ~owner)
-                net.send(mine, mine, at_sems.at[2, q], p.core)
-                yield
+                net.send(mine, mine, at_sems.at[1, q], p.across, owner)
+                net.send(mine, mine, tp_sems.at[0, q], p.other, owner)
+                if q % 2:
+                    yield
             for q in range(8):
-                net.recv(lambda q=q: heads.at[q * 2 + 1 - p.d], at_sems.at[2, q])
-
-        run_together(attention(), units(), gather_steps(net, block_ref, blocks, 16))
-        keep_own.wait()
+                theirs = lambda q=q: heads.at[(q // 2 * 2 + 1 - p.b) * 2 + q % 2]
+                net.recv(theirs, at_sems.at[1, q], owner)
+                net.send(theirs, theirs, tp_sems.at[1, q], p.other, owner)
+                if q % 2:
+                    yield
+            for q in range(8):
+                for side in (0, 1):
+                    b = 1 - p.b if side else p.b
+                    net.recv(
+                        lambda: heads.at[(q // 2 * 2 + b) * 2 + q % 2], tp_sems.at[side, q], ~owner
+                    )
+
+        run_together(
+            gather_steps(net, gains_ref, gain_blocks, 16),
+            gather_steps(net, down_ref, downs, 16),
+            attention(),
+        )
         net.finish()
 
     outs = [
-        shape(ff.shape),
-        shape(ff.shape),
+        shape((16,) + down.shape),
+        shape((16,) + gains.shape, gains.dtype),
         shape((16,) + at.shape[1:]),
-        shape((16,) + block.shape),
     ]
     return comm_call(
         "weights_in",
         number,
         body,
-        [ff, at, block],
+        [down, gains, at],
         [ANY] * 3,
         outs,
-        [ANY] * 4,
-        [pltpu.SemaphoreType.DMA((2, 16)), pltpu.SemaphoreType.DMA((3, 8))],
-        160,
-    )
-
-
-def grads_out(number, ff_own, ff_oth, at, parts, n_ctx):
-    def body(
-        own, oth, at_ref, parts_ref,
-        ff_out, at_out, sum_out,
-        ff_near, ff_sum, at_core, at_tp, near_core, near_x, line_in, line_out,
-        ff_sems, at_sems, sems,
-    ):
-        place = Place(n_ctx)
-        p = place
-        greet(p, everyone=16, other=True)
-        net = Net(p, sems)
-        owner = p.b == p.t
-        f = p.a * 2 + p.b
-        rows, at_rows = ff_own.shape[1], at.shape[1]
-
-        def device(g):
-            return (g * p.members + p.m, p.t)
-
-        def units():
-            order = list(range(1, 16)) + [0]
-            for k in order:
-                there = lambda k=k: oth.at[p.g ^ k]
-                net.send(there, lambda k=k: ff_near.at[p.g ^ k], ff_sems.at[0, k], p.other)
-            yield
-            for k in order:
-                g = p.g ^ k
-                net.recv(lambda: ff_near.at[g], ff_sems.at[0, k])
-                add_into(ff_sum.at[g], [own.at[g], ff_near.at[g]], rows)
-                if k:
-                    net.send(
-                        lambda g=g: ff_sum.at[g],
-                        lambda: ff_out.at[p.g],
-                        ff_sems.at[1, k],
-                        lambda g=g: device(g),
-                    )
-                else:
-                    keep = pltpu.make_async_copy(ff_sum.at[g], ff_out.at[g], net.sem())
-                    keep.start()
-                yield
-            for k in range(1, 16):
-                net.recv(lambda k=k: ff_out.at[p.g ^ k], ff_sems.at[1, k])
-            keep.wait()
-
-        def attention():
-            for q in range(8):
-                net.send(
-                    lambda q=q: at_ref.at[q * 2 + 1 - p.d],
-                    lambda q=q: at_core.at[q],
-                    at_sems.at[0, q],
-                    p.core,
-                )
-            yield
-            for q in range(8):
-                near = at_core.at[q]
-                net.recv(lambda: near, at_sems.at[0, q])
-                add_into(near, [near, at_ref.at[q * 2 + p.d]], at_rows)
-                net.send(
-                    lambda near=near: near,
-                    lambda q=q: at_tp.at[q],
-                    at_sems.at[1, q],
-                    p.other,
-                    ~owner,
-                )
-                yield
-            keep = pltpu.make_async_copy(at_core.at[f], at_out.at[p.a], net.sem())
-            for q in range(8):
-                near, tp = at_core.at[q], at_tp.at[q]
-                net.recv(lambda: tp, at_sems.at[1, q], owner)
-                pl.when(owner)(lambda: add_into(near, [near, tp], at_rows))
-                net.send(
-                    lambda near=near: near,
-                    lambda: at_out.at[p.a],
-                    at_sems.at[2, p.a],
-                    lambda q=q: p.at(a=q // 2, b=q % 2),
-                    owner & (f != q),
-                )
-                pl.when(owner & (f == q))(lambda: keep.start())
-                yield
-            for s in range(4):
-                net.recv(lambda s=s: at_out.at[s], at_sems.at[2, s], ~(owner & (p.a == s)))
-            pl.when(owner)(lambda: keep.wait())
-
-        run_together(
-            attention(),
-            reduce_steps(
-                net, parts_ref, sum_out, near_core, near_x, line_in, line_out, sum_out.shape[0], 16
-            ),
-            units(),
-        )
-        net.finish()
-
-    outs = [
-        shape(ff_own.shape),
-        shape((4,) + at.shape[1:]),
-        shape(parts.shape[1:], F32),
-    ]
-    scratch = [
-        pltpu.VMEM(ff_own.shape, BF),
-        pltpu.VMEM(ff_own.shape, BF),
-        pltpu.VMEM((8,) + at.shape[1:], BF),
-        pltpu.VMEM((8,) + at.shape[1:], BF),
-    ]
-    scratch += reduce_scratch(parts.shape[1], parts.shape[2], 16)
-    scratch += [pltpu.SemaphoreType.DMA((2, 16)), pltpu.SemaphoreType.DMA((3, 8))]
-    return comm_call(
-        "grads_out",
-        number,
+        [ANY] * 3,
+        [pltpu.SemaphoreType.DMA((2, 8)), pltpu.SemaphoreType.DMA((2, 8))],
+        180,
+    )
+
+
+def head_grads_steps(net, at_ref, at_out, at_x, at_tp, x_sems, rows):
+    p = net.place
+    owner = p.d == p.t
+    f = p.a * 2 + p.d
+    for q in range(8):
+        net.send(
+            lambda q=q: at_ref.at[(q // 2 * 2 + 1 - p.b) * 2 + q % 2],
+            lambda q=q: at_x.at[q],
+            x_sems.at[0, q],
+            p.across,
+        )
+    yield
+    for q in range(8):
+        near = at_x.at[q]
+        net.recv(lambda: near, x_sems.at[0, q])
+        add_into(near, [near, at_ref.at[(q // 2 * 2 + p.b) * 2 + q % 2]], rows)
+        net.send(
+            lambda near=near: near, lambda q=q: at_tp.at[q], x_sems.at[1, q], p.other, ~owner
+        )
+        yield
+    keep = pltpu.make_async_copy(at_x.at[f], at_out.at[p.a], net.sem())
+    for q in range(8):
+        near, tp = at_x.at[q], at_tp.at[q]
+        net.recv(lambda: tp, x_sems.at[1, q], owner)
+        pl.when(owner)(lambda: add_into(near, [near, tp], rows))
+        net.send(
+            lambda near=near: near,
+            lambda: at_out.at[p.a],
+            x_sems.at[2, p.a],
+            lambda q=q: p.at(a=q // 2, d=q % 2),
+            owner & (f != q),
+        )
+        pl.when(owner & (f == q))(lambda: keep.start())
+        yield
+    for s in range(4):
+        net.recv(lambda s=s: at_out.at[s], x_sems.at[2, s], ~(owner & (p.a == s)))
+    pl.when(owner)(lambda: keep.wait())
+
+
+def local_call(name, body, grid, ins, in_specs, outs, out_specs, members):
+    g = (lax.axis_index("ctx") // members).astype(jnp.int32).reshape(1)
+    return pl.pallas_call(
         body,
-        [ff_own, ff_oth, at, parts],
-        [VMEM, ANY, VMEM, VMEM],
-        outs,
-        [ANY, ANY, VMEM],
-        scratch,
-        160,
+        out_shape=outs,
+        grid_spec=pltpu.PrefetchScalarGridSpec(
+            num_scalar_prefetch=1, grid=grid, in_specs=in_specs, out_specs=out_specs
+        ),
+        compiler_params=pltpu.CompilerParams(vmem_limit_bytes=56 << 20),
+        name=name,
+    )(g, *ins)
+
+
+def pack(gate, up, down, wide, members):
+    rows = gate.shape[0]
+    units = gate.shape[1] // 16
+
+    def body(g_ref, gate_ref, up_ref, down_ref, *rest):
+        outs, hold, down_t = rest[:4], rest[4], rest[5]
+        down_t[...] = down_ref[...].astype(F32).T.astype(BF)
+        for n in range(16):
+            cut = slice(n * units, (n + 1) * units)
+            for k, part in enumerate((gate_ref, up_ref, down_t)):
+                hold[n, :, k * units : (k + 1) * units] = part[:, cut]
+            hold[n, :, 3 * units :] = jnp.zeros((rows, wide - 3 * units), BF)
+        for i in range(16):
+            outs[i // 4][i % 4] = hold[g_ref[0] ^ i]
+
+    def whole(*dims):
+        return pl.BlockSpec(dims, lambda i, g: (0,) * len(dims))
+
+    g = (lax.axis_index("ctx") // members).astype(jnp.int32).reshape(1)
+    return pl.pallas_call(
+        body,
+        out_shape=[shape((4, rows, wide))] * 4,
+        grid_spec=pltpu.PrefetchScalarGridSpec(
+            num_scalar_prefetch=1,
+            grid=(1,),
+            in_specs=[whole(*gate.shape), whole(*up.shape), whole(*down.shape)],
+            out_specs=[whole(4, rows, wide)] * 4,
+            scratch_shapes=[
+                pltpu.VMEM((16, rows, wide), BF),
+                pltpu.VMEM((rows, 16 * units), BF),
+            ],
+        ),
+        compiler_params=pltpu.CompilerParams(vmem_limit_bytes=56 << 20),
+        name="pack",
+    )(g, gate, up, down)
+
+
+def arrange(own, oth, units, members):
+    def body(g_ref, own_ref, oth_ref, *outs):
+        for k, out in enumerate(outs):
+            cut = slice(k * units, (k + 1) * units)
+            out[0, :, :units] = own_ref[0, :, cut]
+            out[0, :, units:] = oth_ref[0, :, cut]
+
+    rows, cols = own.shape[1:]
+    spec = pl.BlockSpec((1, rows, cols), lambda i, g: (i, 0, 0))
+    return local_call(
+        "arrange",
+        body,
+        (16,),
+        [own, oth],
+        [spec] * 2,
+        [shape((16, rows, 2 * units))] * 3,
+        [pl.BlockSpec((1, rows, 2 * units), lambda i, g: (g[0] ^ i, 0, 0))] * 3,
+        members,
+    )
+
+
+def collect(parts, wide, members):
+    rows, both = parts[0].shape[1:]
+    units = both // 2
+
+    def body(g_ref, *refs):
+        for half, out in enumerate(refs[3:]):
+            for k, part in enumerate(refs[:3]):
+                out[0, :, k * units : (k + 1) * units] = part[
+                    0, :, half * units : (half + 1) * units
+                ]
+            out[0, :, 3 * units :] = jnp.zeros((rows, wide - 3 * units), BF)
+
+    return local_call(
+        "collect",
+        body,
+        (16,),
+        parts,
+        [pl.BlockSpec((1, rows, both), lambda i, g: (g[0] ^ i, 0, 0))] * 3,
+        [shape((16, rows, wide))] * 2,
+        [pl.BlockSpec((1, rows, wide), lambda i, g: (i, 0, 0))] * 2,
+        members,
+    )
+
+
+def spread(blocks, units, members):
+    rows = blocks.shape[1]
+
+    def body(g_ref, src, gate, up, down):
+        for k in range(16):
+            part = src[g_ref[0] ^ k].astype(F32)
+            cut = slice(k * units, (k + 1) * units)
+            gate[:, cut] = part[:, :units]
+            up[:, cut] = part[:, units : 2 * units]
+            down[cut, :] = part[:, 2 * units : 3 * units].T
+
+    return local_call(
+        "spread",
+        body,
+        (1,),
+        [blocks],
+        [pl.BlockSpec(blocks.shape, lambda i, g: (0, 0, 0))],
+        [
+            shape((rows, 16 * units), F32),
+            shape((rows, 16 * units), F32),
+            shape((16 * units, rows), F32),
+        ],
+        [
+            pl.BlockSpec((rows, 16 * units), lambda i, g: (0, 0)),
+            pl.BlockSpec((rows, 16 * units), lambda i, g: (0, 0)),
+            pl.BlockSpec((16 * units, rows), lambda i, g: (0, 0)),
+        ],
+        members,
     )
 
 
@@ -702,11 +739,14 @@
     )[1:]
 
 
-def reduce_latent(number, pairs, queries, n_ctx):
-    def body(pairs_ref, queries_ref, pair_out, query_out, tp_in, *rest):
+def reduce_latent(number, pairs, queries, at, n_ctx):
+    def body(
+        pairs_ref, queries_ref, at_ref, pair_out, query_out, at_out,
+        at_x, at_tp, x_sems, tp_in, *rest,
+    ):
         place = Place(n_ctx)
         p = place
-        greet(p, line=True, across=True, core=True, other=True)
+        greet(p, everyone=16, other=True)
         rest = list(rest)
         net = Net(p, rest.pop())
         rows = pair_out.shape[0]
@@ -726,33 +766,39 @@
         run_together(
             latents(),
             reduce_steps(net, queries_ref, query_out, None, *rest[4:7], query_out.shape[0], 8),
+            head_grads_steps(net, at_ref, at_out, at_x, at_tp, x_sems, at.shape[1]),
         )
         net.finish()
 
     rows, cols = pairs.shape[2:]
-    scratch = [pltpu.VMEM((16, rows, cols), BF)]
+    scratch = [
+        pltpu.VMEM((8,) + at.shape[1:], BF),
+        pltpu.VMEM((8,) + at.shape[1:], BF),
+        pltpu.SemaphoreType.DMA((3, 8)),
+        pltpu.VMEM((16, rows, cols), BF),
+    ]
     scratch += reduce_scratch(rows, cols, 16)
     scratch += reduce_scratch(queries.shape[1], queries.shape[2], 8)
     return comm_call(
         "reduce_latent",
         number,
         body,
-        [pairs, queries],
-        [VMEM] * 2,
-        [shape((rows, cols), F32), shape(queries.shape[1:], F32)],
-        [VMEM] * 2,
+        [pairs, queries, at],
+        [VMEM] * 3,
+        [shape((rows, cols), F32), shape(queries.shape[1:], F32), shape((4,) + at.shape[1:])],
+        [VMEM] * 2 + [ANY],
         scratch,
-        180,
-    )
-
-
-def finish_blocks(number, swaps, gain_blocks, n_ctx):
+        220,
+    )
+
+
+def finish_blocks(number, block, swaps, gain_blocks, n_ctx):
     k = len(swaps)
 
     def body(*refs):
-        ins, gains = refs[:k], refs[k]
-        outs, gains_out = refs[k + 1 : 2 * k + 1], refs[2 * k + 1]
-        rest = list(refs[2 * k + 2 :])
+        block_ref, ins, gains = refs[0], refs[1 : k + 1], refs[k + 1]
+        blocks, outs, gains_out = refs[k + 2], refs[k + 3 : 2 * k + 3], refs[2 * k + 3]
+        rest = list(refs[2 * k + 4 :])
         net_sems = rest.pop()
         tp_in = rest.pop(0)
         place = Place(n_ctx)
@@ -769,7 +815,11 @@
             )
             yield from reduce_steps(net, tp_in, gains_out, *rest, gains_out.shape[0], 16)
 
-        run_together(sums(), *[swap_steps(net, i, o) for i, o in zip(ins, outs)])
+        run_together(
+            gather_steps(net, block_ref, blocks, 16),
+            sums(),
+            *[swap_steps(net, i, o) for i, o in zip(ins, outs)],
+        )
         net.finish()
 
     scratch = [pltpu.VMEM(gain_blocks.shape, BF)]
@@ -778,13 +828,200 @@
         "finish_blocks",
         number,
         body,
-        list(swaps) + [gain_blocks],
-        [ANY] * k + [VMEM],
-        [shape(s.shape, s.dtype) for s in swaps] + [shape(gain_blocks.shape[1:], F32)],
-        [ANY] * k + [VMEM],
+        [block] + list(swaps) + [gain_blocks],
+        [ANY] * (k + 1) + [VMEM],
+        [shape((16,) + block.shape)]
+        + [shape(s.shape, s.dtype) for s in swaps]
+        + [shape(gain_blocks.shape[1:], F32)],
+        [ANY] * (k + 1) + [VMEM],
         scratch,
-        100,
-    )
+        160,
+    )
+
+
+def turn(values, table, back=False):
+    near = pltpu.roll(values, 16, 1) * table[:, 256:384]
+    far = pltpu.roll(values, 112, 1) * table[:, 128:256]
+    turned = near + far
+    return values * table[:, :128] + (-turned if back else turned)
+
+
+def by_rows(rows, step, body):
+    pl.loop(0, rows // step)(lambda i: body(pl.ds(pl.multiple_of(i * step, step), step)))
+
+
+def lanes_of(h):
+    return pl.ds(pl.multiple_of(h * 128, 128), 128)
+
+
+def key_tile(expanded, ropes):
+    lane = lax.broadcasted_iota(jnp.int32, expanded.shape, 1)
+    return jnp.where(lane < NOPE, expanded, ropes)
+
+
+def attend(qn, q_up, pairs, l_up, w_out_t, table, q_pos):
+    rows, keys, heads = qn.shape[0], pairs.shape[0], q_up.shape[1] // 128
+    span, block = keys // 4, rows // 4
+    dim = w_out_t.shape[0]
+
+    def body(
+        qn_ref, q_up_ref, pairs_ref, l_up_ref, w_ref, table_ref, pos_ref,
+        branch_ref, q_ref, o_ref, lse_ref, att_ref,
+        e_ref, top_ref, sum_ref, acc_ref,
+    ):
+        by_rows(
+            keys,
+            256,
+            lambda r: e_ref.__setitem__(
+                r, matmul(pairs_ref[r, :KVR], l_up_ref[...]).astype(BF)
+            ),
+        )
+
+        def head(h):
+            lanes = lanes_of(h)
+            raw = matmul(qn_ref[...], q_up_ref[:, lanes])
+            q_ref[:, lanes] = turn(raw, table_ref[...]).astype(BF)
+            top_ref[...] = jnp.full(top_ref.shape, -1e30, F32)
+            sum_ref[...] = jnp.zeros(sum_ref.shape, F32)
+            acc_ref[...] = jnp.zeros(acc_ref.shape, F32)
+            for kb in range(4):
+                part, cols = slice(kb * block, rows), slice(kb * span, (kb + 1) * span)
+                values = e_ref[cols, lanes]
+                key = key_tile(values, pairs_ref[cols, KVR:])
+                scores = matmul_nt(q_ref[part, lanes], key) * score_scale
+                index = lax.broadcasted_iota(jnp.int32, scores.shape, 1) + kb * span
+                scores = jnp.where(index <= pos_ref[part, :1], scores, -1e30)
+                old = top_ref[part, :1]
+                top = jnp.maximum(old, jnp.max(scores, axis=1, keepdims=True))
+                weights = jnp.exp(scores - top)
+                decay = jnp.exp(old - top)
+                total = sum_ref[part, :1] * decay + jnp.sum(weights, axis=1, keepdims=True)
+                acc_ref[part] = acc_ref[part] * decay + matmul(weights.astype(BF), values)
+                top_ref[part] = jnp.broadcast_to(top, acc_ref[part].shape)
+                sum_ref[part] = jnp.broadcast_to(total, acc_ref[part].shape)
+            lane = lax.broadcasted_iota(jnp.int32, acc_ref.shape, 1)
+            o_ref[:, lanes] = jnp.where(lane < NOPE, 0.0, acc_ref[...] / sum_ref[...])
+            lse_ref[:, lanes] = top_ref[...] + jnp.log(sum_ref[...])
+
+        pl.loop(0, heads)(head)
+        for h in range(heads):
+            att_ref[:, h * VH : (h + 1) * VH] = o_ref[
+                :, h * 128 + NOPE : (h + 1) * 128
+            ].astype(BF)
+        for i in range(dim // 512):
+            cut = slice(i * 512, (i + 1) * 512)
+            branch_ref[:, cut] = matmul_nt(att_ref[...], w_ref[cut]).astype(BF)
+
+    wide = heads * 128
+    return pl.pallas_call(
+        body,
+        out_shape=[
+            shape((rows, dim)),
+            shape((rows, wide)),
+            shape((rows, wide), F32),
+            shape((rows, wide), F32),
+            shape((rows, heads * VH)),
+        ],
+        in_specs=[VMEM] * 7,
+        out_specs=[VMEM] * 5,
+        scratch_shapes=[pltpu.VMEM((keys, wide), BF)] + [pltpu.VMEM((rows, 128), F32)] * 3,
+        compiler_params=pltpu.CompilerParams(vmem_limit_bytes=60 << 20),
+        cost_estimate=pl.CostEstimate(
+            flops=20_000_000_000, bytes_accessed=20 << 20, transcendentals=0
+        ),
+        name="attend",
+    )(qn, q_up, pairs, l_up, w_out_t, table, q_pos)
+
+
+def attend_back(gb, qn, q_up, pairs, l_up, w_out_t, table, q_pos, q, o, lse, att):
+    rows, keys, heads = qn.shape[0], pairs.shape[0], q_up.shape[1] // 128
+    span, block = keys // 4, rows // 4
+    dim, wide = gb.shape[1], heads * 128
+
+    def body(
+        gb_ref, qn_ref, q_up_ref, pairs_ref, l_up_ref, w_ref, table_ref, pos_ref,
+        q_ref, o_ref, lse_ref, att_ref,
+        gp_ref, gqn_ref, gq_up_ref, gl_up_ref, gw_ref,
+        e_ref, rope_ref, go_ref, gq_ref, dq_ref, inner_ref,
+    ):
+        def expand(r):
+            e_ref[r] = matmul(pairs_ref[r, :KVR], l_up_ref[...]).astype(BF)
+            rope_ref[r] = jnp.zeros((256, 128), F32)
+
+        by_rows(keys, 256, expand)
+        ga = matmul(gb_ref[...], w_ref[...]).astype(BF)
+        for h in range(heads):
+            go_ref[:, h * 128 : h * 128 + NOPE] = jnp.zeros((rows, NOPE), BF)
+            go_ref[:, h * 128 + NOPE : (h + 1) * 128] = ga[:, h * VH : (h + 1) * VH]
+        for i in range(dim // 512):
+            cut = slice(i * 512, (i + 1) * 512)
+            gw_ref[cut] = matmul_tn(gb_ref[:, cut], att_ref[...]).astype(BF)
+
+        def head(h):
+            lanes = lanes_of(h)
+            dq_ref[...] = jnp.zeros(dq_ref.shape, F32)
+            inner = jnp.sum(
+                go_ref[:, lanes].astype(F32) * o_ref[:, lanes], axis=1, keepdims=True
+            )
+            inner_ref[...] = jnp.broadcast_to(inner, inner_ref.shape)
+            for kb in range(4):
+                part, cols = slice(kb * block, rows), slice(kb * span, (kb + 1) * span)
+                values = e_ref[cols, lanes]
+                key = key_tile(values, pairs_ref[cols, KVR:])
+                queries, grads = q_ref[part, lanes], go_ref[part, lanes]
+                scores = matmul_nt(queries, key) * score_scale
+                index = lax.broadcasted_iota(jnp.int32, scores.shape, 1) + kb * span
+                probs = jnp.where(
+                    index <= pos_ref[part, :1],
+                    jnp.exp(scores - lse_ref[part, lanes][:, :1]),
+                    0.0,
+                )
+                grad_probs = matmul_nt(grads, values)
+                grad_scores = (probs * (grad_probs - inner_ref[part, :1])).astype(BF)
+                dq_ref[part] += matmul(grad_scores, key)
+                grad_key = matmul_tn(grad_scores, queries) * score_scale
+                grad_value = matmul_tn(probs.astype(BF), grads)
+                lane = lax.broadcasted_iota(jnp.int32, grad_key.shape, 1)
+                e_ref[cols, lanes] = jnp.where(lane < NOPE, grad_key, grad_value).astype(BF)
+                rope_ref[cols] += jnp.where(lane < NOPE, 0.0, grad_key)
+            gq_ref[:, lanes] = turn(dq_ref[...] * score_scale, table_ref[...], True).astype(BF)
+
+        pl.loop(0, heads)(head)
+
+        def latents(r):
+            gp_ref[r, :KVR] = matmul_nt(e_ref[r], l_up_ref[...]).astype(BF)
+            gp_ref[r, KVR:] = rope_ref[r].astype(BF)
+
+        by_rows(keys, 256, latents)
+        gl_up_ref[...] = matmul_tn(pairs_ref[:, :KVR], e_ref[...]).astype(BF)
+        gq_up_ref[...] = matmul_tn(qn_ref[...], gq_ref[...]).astype(BF)
+        gqn_ref[...] = matmul_nt(gq_ref[...], q_up_ref[...]).astype(BF)
+
+    return pl.pallas_call(
+        body,
+        out_shape=[
+            shape(pairs.shape),
+            shape(qn.shape),
+            shape(q_up.shape),
+            shape(l_up.shape),
+            shape(w_out_t.shape),
+        ],
+        in_specs=[VMEM] * 12,
+        out_specs=[VMEM] * 5,
+        scratch_shapes=[
+            pltpu.VMEM((keys, wide), BF),
+            pltpu.VMEM((keys, 128), F32),
+            pltpu.VMEM((rows, wide), BF),
+            pltpu.VMEM((rows, wide), BF),
+            pltpu.VMEM((rows, 128), F32),
+            pltpu.VMEM((rows, 128), F32),
+        ],
+        compiler_params=pltpu.CompilerParams(vmem_limit_bytes=60 << 20),
+        cost_estimate=pl.CostEstimate(
+            flops=40_000_000_000, bytes_accessed=30 << 20, transcendentals=0
+        ),
+        name="attend_back",
+    )(gb, qn, q_up, pairs, l_up, w_out_t, table, q_pos, q, o, lse, att)
 
 
 def shards(
@@ -818,6 +1055,7 @@
     qr = query_down.shape[1]
     heads = H // 8
     units = gate_weight.shape[1] // 16
+    plane_lists = [[k * members + m for k in range(16)] for m in range(members)]
     member_lists = [[k * members + m for m in range(members)] for k in range(16)]
 
     def widen(blocks):
@@ -832,43 +1070,51 @@
             blocks.astype(F32), "ctx", scatter_dimension=1, axis_index_groups=member_lists
         ).astype(BF)
 
+    def gather_over(block):
+        return lax.all_gather(
+            block, "ctx", axis=0, tiled=True, axis_index_groups=plane_lists if members > 1 else None
+        )
+
+    def scatter_over(part):
+        return lax.psum_scatter(
+            part,
+            "ctx",
+            scatter_dimension=0,
+            tiled=True,
+            axis_index_groups=plane_lists if members > 1 else None,
+        )
+
     widths = [first_gain.shape[0], query_gain.shape[0], latent_gain.shape[0], second_gain.shape[0]]
     starts = [0, widths[0], widths[0] + widths[1], widths[0] + widths[1] + widths[2]]
     gains = jnp.concatenate([first_gain, query_gain, latent_gain, second_gain]).astype(F32)
     gains = jnp.broadcast_to(gains[None], (8, gains.shape[0]))
     down_shard = jnp.concatenate([query_down, latent_down], axis=1)
-    down_full, gains = gather_blocks("gather_entry", 1, [down_shard, gains], [16, 16], n_ctx)
-    down_full = widen(down_full.reshape(16, shard_rows, -1)).reshape(dim, -1)
-    gains = widen(gains.reshape(16, 8, -1)[:, 0]).reshape(n_ctx, -1)
-    gain_first, gain_query, gain_latent, gain_second = [
-        gains[:, s : s + w].reshape(-1) for s, w in zip(starts, widths)
-    ]
-
-    def unit_pieces(shard):
-        return jnp.transpose(shard.reshape(shard_rows, 16, units), (1, 0, 2))
+
+    def trade(block, k):
+        return lax.ppermute(
+            block, "ctx", [(i, (i // members ^ k) * members + i % members) for i in range(n_ctx)]
+        )
+
+    def swap_tp(block):
+        return lax.ppermute(block, "tp", [(0, 1), (1, 0)])
 
     wide = 640
-    ff = jnp.concatenate(
-        [
-            unit_pieces(gate_weight),
-            unit_pieces(up_weight),
-            unit_pieces(down_weight.T),
-            jnp.zeros((16, shard_rows, wide - 3 * units), BF),
-        ],
-        axis=2,
-    )
+    ff = pack(gate_weight, up_weight, down_weight, wide, members)
+    near = [ff[0]] + [trade(ff[j], 4 * j) for j in (1, 2, 3)]
     q_rows_w, l_rows_w, o_rows_w = query_up.shape[0], latent_up.shape[0], shard_rows // 2
     q_width, o_width = heads * (NOPE + ROPE), heads * VH
+    q_tiles = jnp.pad(
+        query_up.reshape(q_rows_w, 4, heads, NOPE + ROPE),
+        ((0, 0), (0, 0), (0, 0), (0, 128 - NOPE - ROPE)),
+    ).reshape(q_rows_w, 4, wide)
+    out_tiles = jnp.transpose(
+        out_weight.reshape(4, o_width, 2, o_rows_w), (0, 3, 2, 1)
+    ).reshape(4, o_rows_w, wide)
     at = jnp.concatenate(
         [
-            jnp.pad(
-                jnp.transpose(query_up.reshape(q_rows_w, 4, q_width), (1, 0, 2)),
-                ((0, 0), (0, 0), (0, wide - q_width)),
-            ),
+            jnp.transpose(q_tiles, (1, 0, 2)),
             jnp.transpose(latent_up.reshape(l_rows_w, 4, wide), (1, 0, 2)),
-            jnp.transpose(out_weight.reshape(4, o_width, shard_rows), (0, 2, 1)).reshape(
-                4, o_rows_w, wide
-            ),
+            out_tiles,
         ],
         axis=1,
     )
@@ -879,21 +1125,21 @@
     cosine, sine_table = rope_tables(positions)
     grad_ffn = (residual_scale * out_grad_rows).astype(BF)
 
-    ff_own, ff_oth, at_all, gf_all = weights_in(2, ff, at, grad_ffn, n_ctx)
-    gf_all = gf_all.reshape(-1, dim)
-    w_own = widen(ff_own).reshape(dim, wide)
-    w_oth = widen(ff_oth).reshape(dim, wide)
-
-    def third(k):
-        return jnp.concatenate(
-            [w[:, k * units : (k + 1) * units] for w in (w_own, w_oth)], axis=1
-        )
-
-    w_gate, w_up, w_down_t = third(0), third(1), third(2)
+    down_full, gains, at_all = weights_in(1, down_shard, gains, at, n_ctx)
+    down_full, near = lax.optimization_barrier((down_full, near))
+    own = [jnp.stack([r[0] for r in near])]
+    own += [trade(jnp.stack([r[k] for r in near]), k) for k in (1, 2, 3)]
+    down_full = widen(down_full).reshape(dim, -1)
+    gains = widen(gains[:, 0]).reshape(n_ctx, -1)
+    gain_first, gain_query, gain_latent, gain_second = [
+        gains[:, s : s + w].reshape(-1) for s, w in zip(starts, widths)
+    ]
     at_all = widen(at_all).reshape(n_ctx, -1, wide)
-    q_up = at_all[:, :q_rows_w, :q_width].reshape(qr, q_width)
+    q_up = at_all[:, :q_rows_w].reshape(qr, wide)
     l_up = at_all[:, q_rows_w : q_rows_w + l_rows_w].reshape(KVR, wide)
-    w_out_t = at_all[:, q_rows_w + l_rows_w :].reshape(dim, o_width)
+    w_out_t = jnp.transpose(
+        at_all[:, q_rows_w + l_rows_w :].reshape(n_ctx, o_rows_w, 2, o_width), (0, 2, 1, 3)
+    ).reshape(dim, o_width)
 
     normed = rms_norm(x, gain_first).astype(BF)
     both = matmul(normed, down_full)
@@ -902,7 +1148,7 @@
     latent = rms_norm(compressed[:, :KVR], gain_latent).astype(BF)
     key_rope = rotate(compressed[:, KVR:], cosine, sine_table).astype(BF)
     pair_block = jnp.concatenate(
-        [latent, key_rope, jnp.zeros((rows, 384 - KVR - ROPE), BF)], axis=1
+        [latent, jnp.zeros((rows, NOPE), BF), key_rope, jnp.zeros((rows, ROPE), BF)], axis=1
     )
     normed_columns = jnp.transpose(
         normed.reshape(rows, 16, dim // 16), (1, 0, 2)
@@ -910,51 +1156,44 @@
     pairs, qn_all, token_columns = gather_latent(
         3, pair_block, query_normed, normed_columns, n_ctx
     )
+    own, pairs, grad_ffn = lax.optimization_barrier((own, pairs, grad_ffn))
+    gf_all = gather_over(grad_ffn)
+    oth = [swap_tp(r) for r in own]
     lat_rope = widen(pairs).reshape(-1, 384)
-    latent_all, rope_all = lat_rope[:, :KVR], lat_rope[:, KVR : KVR + ROPE]
     qn_all = qn_all.reshape(-1, qr)
-    q_rows = qn_all.shape[0]
-    keys = latent_all.shape[0]
-
+
+    block = jnp.arange(8, dtype=jnp.int32)
+    block_ctx = ((block // 2 * 2 + b) * 2 + block % 2) * members + member
     q_positions = (
-        ((jnp.arange(8, dtype=jnp.int32)[:, None] * 2 + d) * members + member) * ctx_rows
-        + t * rows
-        + jnp.arange(rows, dtype=jnp.int32)[None, :]
+        block_ctx[:, None] * ctx_rows + t * rows + jnp.arange(rows, dtype=jnp.int32)[None, :]
     ).reshape(-1)
     q_cos, q_sin = rope_tables(q_positions)
-    queries_raw = matmul(qn_all, q_up).reshape(q_rows, heads, NOPE + ROPE)
-    queries = jnp.concatenate(
-        [
-            queries_raw[..., :NOPE],
-            rotate(queries_raw[..., NOPE:], q_cos[:, None, :], q_sin[:, None, :]),
-        ],
-        axis=-1,
-    ).astype(BF)
-    expanded = matmul(latent_all, l_up).astype(BF)
-    allowed = jnp.arange(keys, dtype=jnp.int32)[None, :] <= q_positions[:, None]
-
-    def head_keys(h):
-        part = expanded[:, h * (NOPE + VH) : (h + 1) * (NOPE + VH)]
-        return jnp.concatenate([part[:, :NOPE], rope_all], axis=1), part[:, NOPE:]
-
-    outs, logs = [], []
-    for h in range(heads):
-        k, v = head_keys(h)
-        scores = jnp.where(allowed, matmul_nt(queries[:, h], k) * score_scale, -1e30)
-        top = jnp.max(scores, axis=-1, keepdims=True)
-        weights = jnp.exp(scores - top)
-        total = jnp.sum(weights, axis=-1, keepdims=True)
-        outs.append(matmul(weights.astype(BF), v) / total)
-        logs.append(top + jnp.log(total))
-    attended_wide = jnp.concatenate(outs, axis=1)
-    attended = attended_wide.astype(BF)
-
-    (branch,) = reduce_blocks(
-        "reduce_branch", 4, [matmul_nt(attended, w_out_t).astype(BF)], [8], n_ctx
-    )
+    none, half = jnp.zeros((q_positions.shape[0], NOPE), F32), jnp.zeros_like(q_cos)
+    table = jnp.concatenate(
+        [none + 1, q_cos, q_cos, half, half]
+        + [none, -q_sin, half, half, half]
+        + [none, half, q_sin, half, half],
+        axis=1,
+    )
+    q_pos = jnp.broadcast_to(q_positions[:, None], (q_positions.shape[0], 128))
+    branch_part, queries, attended_wide, log_total, attended = attend(
+        qn_all, q_up, lat_rope, l_up, w_out_t, table, q_pos
+    )
+
+    (branch,) = reduce_blocks("reduce_branch", 4, [branch_part], [8], n_ctx)
     middle = x + residual_scale * branch
     normed_second = rms_norm(middle, gain_second).astype(BF)
     (ns_all,) = gather_blocks("gather_second", 5, [normed_second], [16], n_ctx)
+    ns_all, oth = lax.optimization_barrier((ns_all, oth))
+    w_gate, w_up, w_down_t = [
+        widen(w).reshape(dim, 2 * units)
+        for w in arrange(
+            jnp.stack(own, axis=1).reshape(16, shard_rows, wide),
+            jnp.stack(oth, axis=1).reshape(16, shard_rows, wide),
+            units,
+            members,
+        )
+    ]
     gate_values = matmul(ns_all, w_gate)
     up_values = matmul(ns_all, w_up)
     sigmoid_gate = jax.nn.sigmoid(gate_values)
@@ -975,65 +1214,50 @@
     )
 
     ff_grads = [
-        matmul_tn(ns_all, grad_gate).astype(BF),
-        matmul_tn(ns_all, grad_up).astype(BF),
-        matmul_tn(gf_all, hidden).astype(BF),
-        jnp.zeros((dim, 2 * (wide - 3 * units)), BF),
+        narrow(matmul_tn(left, right).astype(BF).reshape(16, members, shard_rows, 2 * units))
+        for left, right in ((ns_all, grad_gate), (ns_all, grad_up), (gf_all, hidden))
     ]
-
-    def half_grads(k):
-        whole = jnp.concatenate(
-            [p[:, : p.shape[1] // 2] if k == 0 else p[:, p.shape[1] // 2 :] for p in ff_grads],
-            axis=1,
-        )
-        return narrow(whole.reshape(16, members, shard_rows, wide))
-
-    grads_own, grads_oth = half_grads(0), half_grads(1)
+    grads_own, grads_oth = collect(ff_grads, wide, members)
+    grads_oth = swap_tp(grads_oth)
 
     grad_middle_part, second_gain_part = norm_back(middle, gain_second, grad_second)
     grad_middle = out_grad_rows + grad_middle_part
 
     grad_branch = (residual_scale * grad_middle).astype(BF)
     (gb_all,) = gather_blocks("gather_branch", 7, [grad_branch], [8], n_ctx)
-    out_part = matmul_tn(gb_all, attended).astype(BF)
-    grad_attended = matmul(gb_all, w_out_t).astype(BF)
-
-    grad_q_rows, grad_kv, grad_rope = [], [], jnp.zeros((keys, ROPE), F32)
-    for h in range(heads):
-        k, v = head_keys(h)
-        q, ga = queries[:, h], grad_attended[:, h * VH : (h + 1) * VH]
-        row_inner = jnp.sum(
-            ga.astype(F32) * attended_wide[:, h * VH : (h + 1) * VH], axis=-1, keepdims=True
-        )
-        scores = jnp.where(allowed, matmul_nt(q, k) * score_scale, -1e30)
-        probs = jnp.exp(scores - logs[h])
-        grad_probs = matmul_nt(ga, v)
-        grad_scores = (probs * (grad_probs - row_inner)).astype(BF)
-        gq = matmul(grad_scores, k) * score_scale
-        grad_q_rows += [gq[:, :NOPE], rotate(gq[:, NOPE:], q_cos, -q_sin)]
-        gk = matmul_tn(grad_scores, q) * score_scale
-        grad_kv += [gk[:, :NOPE], matmul_tn(probs.astype(BF), ga)]
-        grad_rope = grad_rope + gk[:, NOPE:]
-    grad_q_rows = jnp.concatenate(grad_q_rows, axis=1).astype(BF)
-    grad_expanded = jnp.concatenate(grad_kv, axis=1).astype(BF)
-    grad_lat_rope = jnp.concatenate(
+    gb_all, grads_oth, ffn_part = lax.optimization_barrier((gb_all, grads_oth, ffn_part))
+    ffn_sum = scatter_over(ffn_part).astype(F32)
+    out_half = (middle + residual_scale * ffn_sum).astype(BF)
+    ff_back = (grads_own.astype(F32) + grads_oth.astype(F32)).astype(BF)
+    ff_back = ff_back.reshape(4, 4, shard_rows, wide)
+    back = [ff_back[0]] + [trade(ff_back[j], 4 * j) for j in (1, 2, 3)]
+    grad_lat_rope, gqn_part, q_up_part, l_up_part, out_part = attend_back(
+        gb_all, qn_all, q_up, lat_rope, l_up, w_out_t, table, q_pos,
+        queries, attended_wide, log_total, attended,
+    )
+
+    at_part = jnp.concatenate(
         [
-            matmul_nt(grad_expanded, l_up),
-            grad_rope,
-            jnp.zeros((keys, 384 - KVR - ROPE), F32),
+            q_up_part.reshape(n_ctx, q_rows_w, wide),
+            l_up_part.reshape(n_ctx, l_rows_w, wide),
+            jnp.transpose(
+                out_part.reshape(n_ctx, 2, o_rows_w, o_width), (0, 2, 1, 3)
+            ).reshape(n_ctx, o_rows_w, wide),
         ],
         axis=1,
-    ).astype(BF)
-    l_up_part = matmul_tn(latent_all, grad_expanded).astype(BF)
-    q_up_part = matmul_tn(qn_all, grad_q_rows).astype(BF)
-    gqn_part = matmul_nt(grad_q_rows, q_up).astype(BF)
-
-    own_lat_rope, grad_query_normed = reduce_latent(
+    )
+    at_part = narrow(at_part.reshape(16, members, -1, wide))
+
+    own_lat_rope, grad_query_normed, at_sums = reduce_latent(
         8,
         narrow(grad_lat_rope.reshape(16, members, 2, rows, 384)),
         gqn_part.reshape(8, rows, qr),
+        at_part,
         n_ctx,
     )
+    own_lat_rope, back = lax.optimization_barrier((own_lat_rope, back))
+    sums = [jnp.stack([r[0] for r in back])]
+    sums += [trade(jnp.stack([r[k] for r in back]), k) for k in (1, 2, 3)]
     grad_query_latent, query_gain_part = norm_back(query_latent, gain_query, grad_query_normed)
     grad_latent_rows, latent_gain_part = norm_back(
         compressed[:, :KVR], gain_latent, own_lat_rope[:, :KVR]
@@ -1042,35 +1266,13 @@
         [
             grad_query_latent,
             grad_latent_rows,
-            rotate(own_lat_rope[:, KVR : KVR + ROPE], cosine, -sine_table),
+            rotate(own_lat_rope[:, KVR + NOPE : KVR + NOPE + ROPE], cosine, -sine_table),
         ],
         axis=1,
     ).astype(BF)
-    if members == 1:
-        (both_all,) = gather_blocks("gather_both", 9, [grad_both], [16], n_ctx)
-        down_part = matmul_tn(token_columns.reshape(16 * rows, shard_rows), both_all).astype(BF)
-    else:
-        down_part = lax.psum_scatter(
-            matmul_tn(normed, grad_both).astype(BF), "ctx", scatter_dimension=0, tiled=True
-        )
     grad_normed = matmul_nt(grad_both, down_full)
     grad_input_part, first_gain_part = norm_back(x, gain_first, grad_normed)
     input_half = (grad_middle + grad_input_part).astype(BF)
-
-    at_part = jnp.concatenate(
-        [
-            jnp.pad(q_up_part, ((0, 0), (0, wide - q_width))).reshape(n_ctx, q_rows_w, wide),
-            l_up_part.reshape(n_ctx, l_rows_w, wide),
-            out_part.reshape(n_ctx, o_rows_w, wide),
-        ],
-        axis=1,
-    )
-    at_part = narrow(at_part.reshape(16, members, -1, wide))
-    ff_sums, at_sums, ffn_sum = grads_out(
-        10, grads_own, grads_oth, at_part, ffn_part.reshape(16, rows, dim), n_ctx
-    )
-    out_half = (middle + residual_scale * ffn_sum).astype(BF)
-
     gain_parts = jnp.concatenate(
         [
             p.reshape(n_ctx, -1)
@@ -1080,9 +1282,21 @@
     )
     gain_parts = narrow(gain_parts.reshape(16, members, -1)).astype(BF)
     gain_blocks = jnp.pad(gain_parts[:, None], ((0, 0), (0, 15), (0, 0)))
-    out_other, input_other, down_other, gain_sums = finish_blocks(
-        11, [out_half, input_half, down_part], gain_blocks, n_ctx
-    )
+    both_all, out_other, input_other, gain_sums = finish_blocks(
+        9, grad_both, [out_half, input_half], gain_blocks, n_ctx
+    )
+    both_all, sums = lax.optimization_barrier((both_all, sums))
+    ff_sums = jnp.stack(sums, axis=1).reshape(16, shard_rows, wide)
+    if members == 1:
+        down_part = matmul_tn(
+            token_columns.reshape(16 * rows, shard_rows), both_all.reshape(16 * rows, -1)
+        ).astype(BF)
+    else:
+        down_part = lax.psum_scatter(
+            matmul_tn(normed, grad_both).astype(BF), "ctx", scatter_dimension=0, tiled=True
+        )
+
+    down_other = swap_tp(down_part)
 
     def in_order(mine, other):
         return jnp.where(
@@ -1097,18 +1311,15 @@
         gain_grads[s : s + w] for s, w in zip(starts, widths)
     ]
 
-    def unit_grads(k):
-        part = ff_sums[:, :, k * units : (k + 1) * units]
-        return jnp.transpose(part, (1, 0, 2)).reshape(shard_rows, 16 * units).astype(F32)
-
-    query_up_grad = jnp.transpose(at_sums[:, :q_rows_w, :q_width], (1, 0, 2)).reshape(
-        q_rows_w, 4 * q_width
-    )
+    gate_weight_grad, up_weight_grad, down_weight_grad = spread(ff_sums, units, members)
+    query_up_grad = jnp.transpose(
+        at_sums[:, :q_rows_w].reshape(4, q_rows_w, heads, 128)[..., : NOPE + ROPE], (1, 0, 2, 3)
+    ).reshape(q_rows_w, 4 * q_width)
     latent_up_grad = jnp.transpose(at_sums[:, q_rows_w : q_rows_w + l_rows_w], (1, 0, 2)).reshape(
         l_rows_w, 4 * wide
     )
     out_weight_grad = jnp.transpose(
-        at_sums[:, q_rows_w + l_rows_w :].reshape(4, shard_rows, o_width), (0, 2, 1)
+        at_sums[:, q_rows_w + l_rows_w :].reshape(4, o_rows_w, 2, o_width), (0, 3, 2, 1)
     ).reshape(4 * o_width, shard_rows)
     return (
         layer_output,
@@ -1122,9 +1333,9 @@
         latent_up_grad.astype(F32),
         out_weight_grad.astype(F32),
         second_gain_grad,
-        unit_grads(0),
-        unit_grads(1),
-        unit_grads(2).T,
+        gate_weight_grad,
+        up_weight_grad,
+        down_weight_grad,
     )
 
 

time: 995 us -> 781 us (0.78)
  Pallas kernels: 695 us -> 553 us
  matrix products: 104 us -> 53.1 us
  local copies, waits for them, and re-layouts: 123 us -> 80.3 us
  starting transfers between devices: 0 us -> 19.1 us
  between operations: 2.89 us -> 15.4 us
    pallas_call x11 -> x8, Pallas kernels: 695 us -> 460 us  [comm_call(): pl.pallas_call(body, out_shape=outs, in_specs=in_specs, out_specs=out_spe...]
    pallas_call x0 -> x6, Pallas kernels: none -> 93.7 us  [the longest x3 30.8 us: local_call(): pl.pallas_call(body, out_shape=outs, grid_spec=pltpu.PrefetchScalarGridSp...]
    concatenate x15 -> x3, local copies, waits for them, and re-layouts: 27.2 us -> 3.2 us  [the longest x2 2.48 us: shards(): jnp.concatenate([none + 1, q_cos, q_cos, half, half] + [none, -q_sin, hal...]
    dot_general x17 -> x4, matrix products: 41.2 us -> 19.6 us  [matmul_nt(): lax.dot_general(left_side, right_side, (((1,), (1,)), ((), ())), preferre...]
    ppermute x0 -> x18, starting transfers between devices: none -> 18.8 us  [the longest x12 13.2 us: trade(): lax.ppermute(block, 'ctx', [(i, (i // members ^ k) * members + i % member...]
    dot_general x17 -> x4, matrix products: 35.6 us -> 19.3 us  [matmul(): return jnp.dot(left_side, right_side, preferred_element_type=F32)]
    dot_general x17 -> x4, matrix products: 26.7 us -> 14.2 us  [matmul_tn(): lax.dot_general(left_side, right_side, (((0,), (0,)), ((), ())), preferre...]
    reshape x11, local copies, waits for them, and re-layouts: 26.1 us -> 14 us  [the longest x2 5.94 us: shards(): at_all[:, q_rows_w + l_rows_w:].reshape(n_ctx, o_rows_w, 2, o_width)]
  transfers between devices with their start and end apart: 0 -> 20, of which waited for: 0 -> 0; matrix products, arithmetic and copies ran while one was open for 0% -> 15% of each run, Pallas kernels for 0% -> 70%
where the time goes in v3:
time: 781 us; the launch traced here: 767 us
  Pallas kernels  553 us (71%)
  local copies, waits for them, and re-layouts  80.3 us (10%)
  matrix products  53.1 us (7%)
  other arithmetic  45.8 us (6%)
  starting transfers between devices  19.1 us (2%)
  between operations  15.4 us (2%)
    pallas_call x8, Pallas kernels, comm_call(): pl.pallas_call(body, out_shape=outs, in_specs=in_specs, out_specs=out_spe...  460 us
    pallas_call x3, Pallas kernels, local_call(): pl.pallas_call(body, out_shape=outs, grid_spec=pltpu.PrefetchScalarGridSp...  30.8 us
    pallas_call x1, Pallas kernels, attend_back(): pl.pallas_call(body, out_shape=[shape(pairs.shape), shape(qn.shape), shap...  28.7 us
    pallas_call x1, Pallas kernels, attend(): pl.pallas_call(body, out_shape=[shape((rows, dim)), shape((rows, wide)),...  28.4 us
    dot_general x4, matrix products, matmul_nt(): lax.dot_general(left_side, right_side, (((1,), (1,)), ((), ())), preferre...  19.6 us
    dot_general x4, matrix products, matmul(): return jnp.dot(left_side, right_side, preferred_element_type=F32)  19.3 us
  transfers between devices with their start and end apart: 20, of which 0 were waited for; matrix products, arithmetic and copies ran while one was open for 15% of the time, Pallas kernels for 70%

profile of v3, /device:TPU:3, one launch (start us, length us, event | category | flops | bytes accessed | tf_op | source)
XLA Modules:
  0.0 767.2 jit_solution(14437227305002805323)
XLA Ops:
  9.9 5.9 pack.1
  25.2 134.1 %weights_in.1 = (bf16[16,160,1056]{2,1,0:T(8,128)(2,1)}, f32[16,8,384]{2,1,0:T(8,128)}, bf16[16,144,640]{2,1,0:T(8,128)(2,1)}) custom-call(bf16[160,1056]{1,0:T(8,128)(2,1)} %pad_maximum_fusion.13.down_ref, f32[8,384]{1,0:T(8,128)} %broadcast_in_dim.12.gains_ref, bf16[4,144,640]{2,1,0:T(8,128)(2,1)} %pad_maximum_fusion.12.at_ref), custom_call_target="tpu_custom_call" | custom-call | tf_op jit(solution)/shard_map/weights_in/pallas_call | solution.py:368
  179.2 51.6 %gather_latent.1 = (bf16[2,64,384]{2,1,0:T(8,128)(2,1)}, bf16[16,2,64,384]{3,2,1,0:T(8,128)(2,1)}, bf16[8,64,768]{2,1,0:T(8,128)(2,1)}, bf16[16,64,160]{2,1,0:T(8,128)(2,1)}) custom-call(bf16[64,384]{1,0:T(8,128)(2,1)} %concatenate.66.pair_ref, bf16[64,768]{1,0:T(8,128)(2,1)} %multiply_convert_fusion.5.query_ref, bf16[16,64,160]{2,1,0:T(8,128)(2,1)} %bitcast.131), custom_call_target="tpu_custom_call" | custom-call | tf_op jit(solution)/shard_map/gather_latent/pallas_call | solution.py:368
  240.3 4.4 reshape.354
  258.3 28.4 %attend.1 = (bf16[512,2560]{1,0:T(8,128)(2,1)}, bf16[512,640]{1,0:T(8,128)(2,1)}, f32[512,640]{1,0:T(8,128)}, f32[512,640]{1,0:T(8,128)}, bf16[512,320]{1,0:T(8,128)(2,1)}) custom-call(bf16[512,768]{1,0:T(8,128)(2,1)} %bitcast.166, bf16[768,640]{1,0:T(8,128)(2,1)} %bitcast.137, bf16[2048,384]{1,0:T(8,128)(2,1)} %bitcast.164, bf16[256,640]{1,0:T(8,128)(2,1)} %bitcast.147, ...), custom_call_target="tpu_custom_call" | custom-call | flops 20000000000 | bytes 20971520 | tf_op jit(solution)/shard_map/attend/pallas_call | solution.py:916
  286.7 28.1 %reduce_branch.1 = f32[64,2560]{1,0:T(8,128)} custom-call(bf16[8,64,2560]{2,1,0:T(8,128)(2,1)} %bitcast.130), custom_call_target="tpu_custom_call" | custom-call | tf_op jit(solution)/shard_map/reduce_branch/pallas_call | solution.py:368
  317.0 36.1 %gather_second.1 = bf16[16,64,2560]{2,1,0:T(8,128)(2,1)} custom-call(bf16[64,2560]{1,0:T(8,128)(2,1)} %multiply_convert_fusion.4.refs_0_), custom_call_target="tpu_custom_call" | custom-call | tf_op jit(solution)/shard_map/gather_second/pallas_call | solution.py:368
  357.2 12.1 %arrange.1 = (bf16[16,160,400]{2,1,0:T(8,128)(2,1)}, bf16[16,160,400]{2,1,0:T(8,128)(2,1)}, bf16[16,160,400]{2,1,0:T(8,128)(2,1)}) custom-call(s32[1]{0:T(128)} %bitcast.3.g_ref, bf16[16,160,640]{2,1,0:T(8,128)(2,1)} %bitcast.109, bf16[16,160,640]{2,1,0:T(8,128)(2,1)} %bitcast.110), custom_call_target="tpu_custom_call" | custom-call | tf_op jit(solution)/shard_map/arrange/pallas_call | solution.py:562
  369.3 5.3 fusion.59
  374.7 5.8 fusion.58
  389.1 4.5 copy.76
  393.6 6.5 convolution_convert_fusion.3
  403.7 4.3 copy.75
  412.2 12.4 %collect.1 = (bf16[16,160,640]{2,1,0:T(8,128)(2,1)}, bf16[16,160,640]{2,1,0:T(8,128)(2,1)}) custom-call(s32[1]{0:T(128)} %bitcast.3.g_ref, bf16[16,160,400]{2,1,0:T(8,128)(2,1)} %bitcast.113, bf16[16,160,400]{2,1,0:T(8,128)(2,1)} %bitcast.112, bf16[16,160,400]{2,1,0:T(8,128)(2,1)} %bitcast.111), custom_call_target="tpu_custom_call" | custom-call | tf_op jit(solution)/shard_map/collect/pallas_call | solution.py:562
  427.2 4.9 fusion.60
  432.1 4.9 add_convert_fusion
  437.0 37.4 %reduce_second.1 = f32[64,2560]{1,0:T(8,128)} custom-call(bf16[16,64,2560]{2,1,0:T(8,128)(2,1)} %bitcast.125), custom_call_target="tpu_custom_call" | custom-call | tf_op jit(solution)/shard_map/reduce_second/pallas_call | solution.py:368
  478.3 33.2 %gather_branch.1 = bf16[8,64,2560]{2,1,0:T(8,128)(2,1)} custom-call(bf16[64,2560]{1,0:T(8,128)(2,1)} %get-tuple-element.192.refs_0_), custom_call_target="tpu_custom_call" | custom-call | tf_op jit(solution)/shard_map/gather_branch/pallas_call | solution.py:368
  511.5 5.0 convolution_convert_fusion
  525.7 28.7 %attend_back.1 = (bf16[2048,384]{1,0:T(8,128)(2,1)}, bf16[512,768]{1,0:T(8,128)(2,1)}, bf16[768,640]{1,0:T(8,128)(2,1)}, bf16[256,640]{1,0:T(8,128)(2,1)}, bf16[2560,320]{1,0:T(8,128)(2,1)}) custom-call(bf16[512,2560]{1,0:T(8,128)(2,1)} %bitcast.129, bf16[512,768]{1,0:T(8,128)(2,1)} %bitcast.167, bf16[768,640]{1,0:T(8,128)(2,1)} %bitcast.138, ...), custom_call_target="tpu_custom_call" | custom-call | flops 40000000000 | bytes 31457280 | tf_op jit(solution)/shard_map/attend_back/pallas_call | solution.py:1000
  563.8 85.0 %reduce_latent.1 = (f32[64,384]{1,0:T(8,128)}, f32[64,768]{1,0:T(8,128)}, bf16[4,144,640]{2,1,0:T(8,128)(2,1)}) custom-call(bf16[16,2,64,384]{3,2,1,0:T(8,128)(2,1)} %bitcast.136, bf16[8,64,768]{2,1,0:T(8,128)(2,1)} %bitcast.144, bf16[16,144,640]{2,1,0:T(8,128)(2,1)} %pad_maximum_fusion.3.at_ref), custom_call_target="tpu_custom_call" | custom-call | tf_op jit(solution)/shard_map/reduce_latent/pallas_call | solution.py:368
  663.1 4.8 fusion.13
  682.7 54.3 %finish_blocks.1 = (bf16[16,64,1056]{2,1,0:T(8,128)(2,1)}, bf16[64,2560]{1,0:T(8,128)(2,1)}, bf16[64,2560]{1,0:T(8,128)(2,1)}, f32[16,384]{1,0:T(8,128)}) custom-call(bf16[64,1056]{1,0:T(8,128)(2,1)} %copy-done.8, bf16[64,2560]{1,0:T(8,128)(2,1)} %add_convert_fusion.2.refs_1_, bf16[64,2560]{1,0:T(8,128)(2,1)} %fusion.8.refs_2_, ...), custom_call_target="tpu_custom_call" | custom-call | tf_op jit(solution)/shard_map/finish_blocks/pallas_call | solution.py:368
  746.7 6.3 spread.1
  (297 shorter events, 148.0 us)
Async XLA Ops:
  7.2 367.5 %all-gather.2.cloned.1.call-start = ((), (), s32[]{:S(2)}) async-start(), calls=%async_computation.1 | async-start | bytes 5570560 | tf_op jit(solution)/shard_map/all_gather | solution.py:1074
  15.8 148.5 %collective-permute-start = (bf16[4,160,640]{2,1,0:T(8,128)(2,1)}, bf16[4,160,640]{2,1,0:T(8,128)(2,1)}, u32[]{:S(2)}, u32[]{:S(2)}) collective-permute-start(bf16[4,160,640]{2,1,0:T(8,128)(2,1)} %get-tuple-element.81), channel_id=1, source_target_pairs={{0,8},{2,10},{4,12},{6,14},{8,0},{10,2},{12,4},{14,6},{16,24},{18,... | collective-permute-start | bytes 2457608 | tf_op jit(solution)/shard_map/ppermute | solution.py:1094
  17.1 147.2 %collective-permute-start.1 = (bf16[4,160,640]{2,1,0:T(8,128)(2,1)}, bf16[4,160,640]{2,1,0:T(8,128)(2,1)S(1)}, u32[]{:S(2)}, u32[]{:S(2)}) collective-permute-start(bf16[4,160,640]{2,1,0:T(8,128)(2,1)} %get-tuple-element.82), channel_id=1, source_target_pairs={{0,16},{2,18},{4,20},{6,22},{8,24},{10,26},{12,28},{14,30},{16,0},... | collective-permute-start | bytes 2457608 | tf_op jit(solution)/shard_map/ppermute | solution.py:1094
  19.4 144.9 %collective-permute-start.2 = (bf16[4,160,640]{2,1,0:T(8,128)(2,1)}, bf16[4,160,640]{2,1,0:T(8,128)(2,1)}, u32[]{:S(2)}, u32[]{:S(2)}) collective-permute-start(bf16[4,160,640]{2,1,0:T(8,128)(2,1)} %get-tuple-element.83), channel_id=1, source_target_pairs={{0,24},{2,26},{4,28},{6,30},{8,16},{10,18},{12,20},{14,22},{16,8},... | collective-permute-start | bytes 2457608 | tf_op jit(solution)/shard_map/ppermute | solution.py:1094
  19.6 140.8 %copy-start.35 = (f32[64]{0:T(128)}, f32[64]{0:T(128)S(1)}, u32[]{:S(2)}) copy-start(f32[64]{0:T(128)S(1)} %add_rsqrt_fusion.3) | copy-start | bytes 772
  173.1 59.6 %collective-permute-start.3 = (bf16[4,160,640]{2,1,0:T(8,128)(2,1)}, bf16[4,160,640]{2,1,0:T(8,128)(2,1)S(1)}, u32[]{:S(2)}, u32[]{:S(2)}) collective-permute-start(bf16[4,160,640]{2,1,0:T(8,128)(2,1)} %pad_maximum_fusion.5), channel_id=1, source_target_pairs={{0,2},{2,0},{4,6},{6,4},{8,10},{10,8},{12,14},{14,12},{16,18},{18,... | collective-permute-start | bytes 2457608 | tf_op jit(solution)/shard_map/ppermute | solution.py:1094
  174.1 58.6 %collective-permute-start.4 = (bf16[4,160,640]{2,1,0:T(8,128)(2,1)}, bf16[4,160,640]{2,1,0:T(8,128)(2,1)S(1)}, u32[]{:S(2)}, u32[]{:S(2)}) collective-permute-start(bf16[4,160,640]{2,1,0:T(8,128)(2,1)} %pad_maximum_fusion.6), channel_id=1, source_target_pairs={{0,4},{2,6},{4,0},{6,2},{8,12},{10,14},{12,8},{14,10},{16,20},{18,... | collective-permute-start | bytes 2457608 | tf_op jit(solution)/shard_map/ppermute | solution.py:1094
  176.4 56.4 %collective-permute-start.5 = (bf16[4,160,640]{2,1,0:T(8,128)(2,1)}, bf16[4,160,640]{2,1,0:T(8,128)(2,1)}, u32[]{:S(2)}, u32[]{:S(2)}) collective-permute-start(bf16[4,160,640]{2,1,0:T(8,128)(2,1)} %pad_maximum_fusion.7), channel_id=1, source_target_pairs={{0,6},{2,4},{4,2},{6,0},{8,14},{10,12},{12,10},{14,8},{16,22},{18,... | collective-permute-start | bytes 2457608 | tf_op jit(solution)/shard_map/ppermute | solution.py:1094
  232.8 448.1 %reduce-scatter.2.cloned.1.call-start = ((), (), s32[]{:S(2)}) async-start(), calls=%async_computation.2 | async-start | bytes 5570560 | tf_op jit(solution)/shard_map/reduce_scatter | solution.py:1079
  250.6 102.5 %collective-permute-start.6 = (bf16[4,160,640]{2,1,0:T(8,128)(2,1)S(1)}, bf16[4,160,640]{2,1,0:T(8,128)(2,1)S(1)}, u32[]{:S(2)}, u32[]{:S(2)}) collective-permute-start(bf16[4,160,640]{2,1,0:T(8,128)(2,1)S(1)} %copy-done.3), channel_id=1, source_target_pairs={{0,1},{1,0},{2,3},{3,2},{4,5},{5,4},{6,7},{7,6},{8,9},{9,8},{10,11... | collective-permute-start | bytes 2457608 | tf_op jit(solution)/shard_map/ppermute | solution.py:1099
  251.9 101.2 %collective-permute-start.7 = (bf16[4,160,640]{2,1,0:T(8,128)(2,1)}, bf16[4,160,640]{2,1,0:T(8,128)(2,1)}, u32[]{:S(2)}, u32[]{:S(2)}) collective-permute-start(bf16[4,160,640]{2,1,0:T(8,128)(2,1)} %copy-done.9), channel_id=1, source_target_pairs={{0,1},{1,0},{2,3},{3,2},{4,5},{5,4},{6,7},{7,6},{8,9},{9,8},{10,11... | collective-permute-start | bytes 2457608 | tf_op jit(solution)/shard_map/ppermute | solution.py:1099
  252.1 101.0 %collective-permute-start.8 = (bf16[4,160,640]{2,1,0:T(8,128)(2,1)}, bf16[4,160,640]{2,1,0:T(8,128)(2,1)}, u32[]{:S(2)}, u32[]{:S(2)}) collective-permute-start(bf16[4,160,640]{2,1,0:T(8,128)(2,1)} %copy-done.10), channel_id=1, source_target_pairs={{0,1},{1,0},{2,3},{3,2},{4,5},{5,4},{6,7},{7,6},{8,9},{9,8},{10,11... | collective-permute-start | bytes 2457608 | tf_op jit(solution)/shard_map/ppermute | solution.py:1099
  253.3 99.7 %collective-permute-start.9 = (bf16[4,160,640]{2,1,0:T(8,128)(2,1)}, bf16[4,160,640]{2,1,0:T(8,128)(2,1)}, u32[]{:S(2)}, u32[]{:S(2)}) collective-permute-start(bf16[4,160,640]{2,1,0:T(8,128)(2,1)} %collective-permute-done.5), channel_id=1, source_target_pairs={{0,1},{1,0},{2,3},{3,2},{4,5},{5,4},{6,7},{7,6},{8,9},{9,8},{10,11... | collective-permute-start | bytes 2457608 | tf_op jit(solution)/shard_map/ppermute | solution.py:1099
  424.6 91.9 %collective-permute-start.10 = (bf16[16,160,640]{2,1,0:T(8,128)(2,1)}, bf16[16,160,640]{2,1,0:T(8,128)(2,1)}, u32[]{:S(2)}, u32[]{:S(2)}) collective-permute-start(bf16[16,160,640]{2,1,0:T(8,128)(2,1)} %get-tuple-element.107), channel_id=1, source_target_pairs={{0,1},{1,0},{2,3},{3,2},{4,5},{5,4},{6,7},{7,6},{8,9},{9,8},{10,11... | collective-permute-start | bytes 9830408 | tf_op jit(solution)/shard_map/ppermute | solution.py:1099
  522.1 140.3 %collective-permute-start.13 = (bf16[4,160,640]{2,1,0:T(8,128)(2,1)}, bf16[4,160,640]{2,1,0:T(8,128)(2,1)}, u32[]{:S(2)}, u32[]{:S(2)}) collective-permute-start(bf16[4,160,640]{2,1,0:T(8,128)(2,1)} %get-tuple-element.196), channel_id=1, source_target_pairs={{0,24},{2,26},{4,28},{6,30},{8,16},{10,18},{12,20},{14,22},{16,8},... | collective-permute-start | bytes 2457608 | tf_op jit(solution)/shard_map/ppermute | solution.py:1094
  522.2 140.2 %collective-permute-start.12 = (bf16[4,160,640]{2,1,0:T(8,128)(2,1)}, bf16[4,160,640]{2,1,0:T(8,128)(2,1)}, u32[]{:S(2)}, u32[]{:S(2)}) collective-permute-start(bf16[4,160,640]{2,1,0:T(8,128)(2,1)} %get-tuple-element.197), channel_id=1, source_target_pairs={{0,16},{2,18},{4,20},{6,22},{8,24},{10,26},{12,28},{14,30},{16,0},... | collective-permute-start | bytes 2457608 | tf_op jit(solution)/shard_map/ppermute | solution.py:1094
  522.3 140.2 %collective-permute-start.11 = (bf16[4,160,640]{2,1,0:T(8,128)(2,1)}, bf16[4,160,640]{2,1,0:T(8,128)(2,1)}, u32[]{:S(2)}, u32[]{:S(2)}) collective-permute-start(bf16[4,160,640]{2,1,0:T(8,128)(2,1)} %get-tuple-element.198), channel_id=1, source_target_pairs={{0,8},{2,10},{4,12},{6,14},{8,0},{10,2},{12,4},{14,6},{16,24},{18,... | collective-permute-start | bytes 2457608 | tf_op jit(solution)/shard_map/ppermute | solution.py:1094
  563.8 88.9 %copy-start.1 = (f32[64,1056]{1,0:T(8,128)S(1)}, f32[64,1056]{1,0:T(8,128)}, u32[]{:S(2)}) copy-start(f32[64,1056]{1,0:T(8,128)} %copy-done) | copy-start | bytes 811012
  563.8 88.9 %copy-start.26 = (f32[768]{0:T(1024)S(1)}, f32[768]{0:T(1024)}, u32[]{:S(2)}) copy-start(f32[768]{0:T(1024)} %copy-done.25) | copy-start | bytes 9220
  563.8 88.9 %copy-start.34 = (f32[64]{0:T(128)S(1)}, f32[64]{0:T(128)}, u32[]{:S(2)}) copy-start(f32[64]{0:T(128)} %copy-done.33) | copy-start | bytes 772
  673.1 67.9 %collective-permute-start.14 = (bf16[4,160,640]{2,1,0:T(8,128)(2,1)}, bf16[4,160,640]{2,1,0:T(8,128)(2,1)}, u32[]{:S(2)}, u32[]{:S(2)}) collective-permute-start(bf16[4,160,640]{2,1,0:T(8,128)(2,1)} %pad_maximum_fusion.9), channel_id=1, source_target_pairs={{0,2},{2,0},{4,6},{6,4},{8,10},{10,8},{12,14},{14,12},{16,18},{18,... | collective-permute-start | bytes 2457608 | tf_op jit(solution)/shard_map/ppermute | solution.py:1094
  674.1 66.9 %collective-permute-start.15 = (bf16[4,160,640]{2,1,0:T(8,128)(2,1)}, bf16[4,160,640]{2,1,0:T(8,128)(2,1)}, u32[]{:S(2)}, u32[]{:S(2)}) collective-permute-start(bf16[4,160,640]{2,1,0:T(8,128)(2,1)} %pad_maximum_fusion.10), channel_id=1, source_target_pairs={{0,4},{2,6},{4,0},{6,2},{8,12},{10,14},{12,8},{14,10},{16,20},{18,... | collective-permute-start | bytes 2457608 | tf_op jit(solution)/shard_map/ppermute | solution.py:1094
  678.9 62.0 %collective-permute-start.16 = (bf16[4,160,640]{2,1,0:T(8,128)(2,1)}, bf16[4,160,640]{2,1,0:T(8,128)(2,1)}, u32[]{:S(2)}, u32[]{:S(2)}) collective-permute-start(bf16[4,160,640]{2,1,0:T(8,128)(2,1)} %pad_maximum_fusion.11), channel_id=1, source_target_pairs={{0,6},{2,4},{4,2},{6,0},{8,14},{10,12},{12,10},{14,8},{16,22},{18,... | collective-permute-start | bytes 2457608 | tf_op jit(solution)/shard_map/ppermute | solution.py:1094
  746.6 12.0 %collective-permute-start.17 = (bf16[160,1056]{1,0:T(8,128)(2,1)S(1)}, bf16[160,1056]{1,0:T(8,128)(2,1)S(1)}, u32[]{:S(2)}, u32[]{:S(2)}) collective-permute-start(bf16[160,1056]{1,0:T(8,128)(2,1)S(1)} %fusion), channel_id=1, source_target_pairs={{0,1},{1,0},{2,3},{3,2},{4,5},{5,4},{6,7},{7,6},{8,9},{9,8},{10,11... | collective-permute-start | bytes 1013768 | tf_op jit(solution)/shard_map/ppermute | solution.py:1099
  (57 other events, 585.4 us)
Sparse Core Ops, SparseCore 0:
  232.9 54.6 all-gather.1
  522.2 103.2 reduce-scatter.1

commit v4 on v3

--- a/solution.py
+++ b/solution.py
@@ -183,6 +183,31 @@
         tell(place.other())
         count = count + 1
     pl.semaphore_wait(barrier, count)
+
+
+def trade_away(place, src, out, sems, first):
+    barrier = pltpu.get_barrier_semaphore()
+    count = src.shape[0]
+    devices = [
+        ((place.g ^ (first + k)) * place.members + place.m, place.t) for k in range(count)
+    ]
+    for device in devices:
+        pl.semaphore_signal(barrier, inc=1, device_id=device, device_id_type=MESH)
+    pl.semaphore_wait(barrier, count)
+    copies = [
+        pltpu.make_async_remote_copy(
+            src.at[k],
+            out.at[k],
+            sems.at[0, k],
+            sems.at[1, k],
+            device_id=devices[k],
+            device_id_type=MESH,
+        )
+        for k in range(count)
+    ]
+    for copy in copies:
+        copy.start()
+    return copies
 
 
 def gather_steps(net, src, out, width):
@@ -451,8 +476,38 @@
     )
 
 
-def weights_in(number, down, gains, at, n_ctx):
-    def body(down_ref, gains_ref, at_ref, downs, gain_blocks, heads, at_sems, tp_sems, sems):
+def trade_steps(net, src, out, sems, onward=None):
+    p = net.place
+
+    def device(i):
+        return ((p.g ^ i) * p.members + p.m, p.t)
+
+    keep = pltpu.make_async_copy(src.at[0], out.at[0], net.sem())
+    keep.start()
+    if onward is not None:
+        net.send(lambda: src.at[0], lambda: onward.at[0], sems.at[1, 0], p.other)
+    yield
+    for i in (4, 5, 6, 7, 2, 3, 1):
+        net.send(lambda i=i: src.at[i], lambda i=i: out.at[i], sems.at[0, i], lambda i=i: device(i))
+        yield
+    for i in (1, 2, 3, 4, 5, 6, 7):
+        here = lambda i=i: out.at[i]
+        net.recv(here, sems.at[0, i])
+        if onward is not None and i < 4:
+            net.send(here, lambda i=i: onward.at[i], sems.at[1, i], p.other)
+        yield
+    if onward is not None:
+        for i in range(4):
+            net.recv(lambda i=i: onward.at[i], sems.at[1, i])
+    keep.wait()
+
+
+def weights_in(number, down, gains, at, ff, n_ctx):
+    def body(
+        down_ref, gains_ref, at_ref, ff_ref,
+        downs, gain_blocks, heads, near, other_near,
+        at_sems, tp_sems, ff_sems, sems,
+    ):
         p = Place(n_ctx)
         greet(p, everyone=16, other=True)
         net = Net(p, sems)
@@ -497,6 +552,7 @@
             gather_steps(net, gains_ref, gain_blocks, 16),
             gather_steps(net, down_ref, downs, 16),
             attention(),
+            trade_steps(net, ff_ref, near, ff_sems, other_near),
         )
         net.finish()
 
@@ -504,17 +560,19 @@
         shape((16,) + down.shape),
         shape((16,) + gains.shape, gains.dtype),
         shape((16,) + at.shape[1:]),
+        shape((8,) + ff.shape[1:]),
+        shape((4,) + ff.shape[1:]),
     ]
     return comm_call(
         "weights_in",
         number,
         body,
-        [down, gains, at],
-        [ANY] * 3,
+        [down, gains, at, ff],
+        [ANY] * 4,
         outs,
-        [ANY] * 3,
-        [pltpu.SemaphoreType.DMA((2, 8)), pltpu.SemaphoreType.DMA((2, 8))],
-        180,
+        [ANY] * 5,
+        [pltpu.SemaphoreType.DMA((2, 8))] * 3,
+        200,
     )
 
 
@@ -557,128 +615,138 @@
     pl.when(owner)(lambda: keep.wait())
 
 
-def local_call(name, body, grid, ins, in_specs, outs, out_specs, members):
+def plain_call(name, body, ins, outs, scratch, members):
+    def whole(array):
+        return pl.BlockSpec(array.shape, lambda i, g: (0,) * len(array.shape))
+
     g = (lax.axis_index("ctx") // members).astype(jnp.int32).reshape(1)
     return pl.pallas_call(
         body,
         out_shape=outs,
         grid_spec=pltpu.PrefetchScalarGridSpec(
-            num_scalar_prefetch=1, grid=grid, in_specs=in_specs, out_specs=out_specs
+            num_scalar_prefetch=1,
+            grid=(1,),
+            in_specs=[whole(i) for i in ins],
+            out_specs=[whole(o) for o in outs],
+            scratch_shapes=scratch,
         ),
-        compiler_params=pltpu.CompilerParams(vmem_limit_bytes=56 << 20),
+        compiler_params=pltpu.CompilerParams(vmem_limit_bytes=62 << 20),
+        cost_estimate=pl.CostEstimate(
+            flops=1_000_000_000, bytes_accessed=20 << 20, transcendentals=0
+        ),
         name=name,
     )(g, *ins)
 
 
-def pack(gate, up, down, wide, members):
+def pack(gate, up, down_t, wide, members):
     rows = gate.shape[0]
     units = gate.shape[1] // 16
 
-    def body(g_ref, gate_ref, up_ref, down_ref, *rest):
-        outs, hold, down_t = rest[:4], rest[4], rest[5]
-        down_t[...] = down_ref[...].astype(F32).T.astype(BF)
+    def body(g_ref, gate_ref, up_ref, down_ref, out):
         for n in range(16):
             cut = slice(n * units, (n + 1) * units)
-            for k, part in enumerate((gate_ref, up_ref, down_t)):
-                hold[n, :, k * units : (k + 1) * units] = part[:, cut]
-            hold[n, :, 3 * units :] = jnp.zeros((rows, wide - 3 * units), BF)
+            i = g_ref[0] ^ n
+            for k, part in enumerate((gate_ref, up_ref, down_ref)):
+                out[i, :, k * units : (k + 1) * units] = part[:, cut]
+            out[i, :, 3 * units :] = jnp.zeros((rows, wide - 3 * units), BF)
+
+    return plain_call(
+        "pack", body, [gate, up, down_t], [shape((16, rows, wide))], [], members
+    )[0]
+
+
+def feed_forward(ns, gf, own, oth, units, members):
+    tokens, dim = ns.shape
+    rows, wide = own[0].shape[1:]
+    lanes = 256
+    both = 2 * lanes
+    places = [[(a, k) for a, w in enumerate(side) for k in range(w.shape[0])] for side in (own, oth)]
+
+    def body(g_ref, ns_ref, gf_ref, *refs):
+        own_refs, oth_refs = refs[: len(own)], refs[len(own) : len(own) + len(oth)]
+        out_ref, gs_ref, gown_ref, goth_ref = refs[len(own) + len(oth) :][:4]
+        wgu_ref, wd_ref, hidden_ref, ggu_ref = refs[-4:]
+        g = g_ref[0]
         for i in range(16):
-            outs[i // 4][i % 4] = hold[g_ref[0] ^ i]
-
-    def whole(*dims):
-        return pl.BlockSpec(dims, lambda i, g: (0,) * len(dims))
-
-    g = (lax.axis_index("ctx") // members).astype(jnp.int32).reshape(1)
-    return pl.pallas_call(
+            cut = pl.ds(pl.multiple_of((g ^ i) * rows, rows), rows)
+            for half, side in enumerate((own_refs, oth_refs)):
+                a, k = places[half][i]
+                block = side[a][k]
+                pad = jnp.zeros((rows, lanes - units), BF)
+                for k in range(3):
+                    part = jnp.concatenate([block[:, k * units : (k + 1) * units], pad], axis=1)
+                    into = wgu_ref if k < 2 else wd_ref
+                    at = (both * k if k < 2 else 0) + half * lanes
+                    into[cut, at : at + lanes] = part
+
+        def forth(i):
+            r = pl.ds(pl.multiple_of(i * 256, 256), 256)
+            gate_up = matmul(ns_ref[r], wgu_ref[...])
+            gate, up = gate_up[:, :both], gate_up[:, both:]
+            grad_hidden = matmul(gf_ref[r], wd_ref[...])
+            sigmoid_gate = 1.0 / (1.0 + jnp.exp(-gate))
+            silu = gate * sigmoid_gate
+            hidden_ref[r] = (silu * up).astype(BF)
+            ggu_ref[r, :both] = (
+                grad_hidden * up * sigmoid_gate * (1.0 + gate * (1.0 - sigmoid_gate))
+            ).astype(BF)
+            ggu_ref[r, both:] = (grad_hidden * silu).astype(BF)
+            gs_ref[r] = matmul_nt(ggu_ref[r], wgu_ref[...]).astype(BF)
+            out_ref[r] = matmul_nt(hidden_ref[r], wd_ref[...]).astype(BF)
+
+        pl.loop(0, tokens // 256)(forth)
+
+        span = dim // 4
+
+        def give(q, k, grads):
+            for jj in range(4):
+                for half, out in enumerate((gown_ref, goth_ref)):
+                    out[g ^ (4 * q + jj), :, k * units : (k + 1) * units] = grads[
+                        jj * rows : (jj + 1) * rows, half * lanes : half * lanes + units
+                    ].astype(BF)
+
+        for q in range(4):
+            cut = slice(q * span, (q + 1) * span)
+            grads = matmul_tn(ns_ref[:, cut], ggu_ref[...])
+            give(q, 0, grads[:, :both])
+            give(q, 1, grads[:, both:])
+            give(q, 2, matmul_tn(gf_ref[:, cut], hidden_ref[...]))
+        for out in (gown_ref, goth_ref):
+            out[:, :, 3 * units :] = jnp.zeros((16, rows, wide - 3 * units), BF)
+
+    return plain_call(
+        "feed_forward",
         body,
-        out_shape=[shape((4, rows, wide))] * 4,
-        grid_spec=pltpu.PrefetchScalarGridSpec(
-            num_scalar_prefetch=1,
-            grid=(1,),
-            in_specs=[whole(*gate.shape), whole(*up.shape), whole(*down.shape)],
-            out_specs=[whole(4, rows, wide)] * 4,
-            scratch_shapes=[
-                pltpu.VMEM((16, rows, wide), BF),
-                pltpu.VMEM((rows, 16 * units), BF),
-            ],
-        ),
-        compiler_params=pltpu.CompilerParams(vmem_limit_bytes=56 << 20),
-        name="pack",
-    )(g, gate, up, down)
-
-
-def arrange(own, oth, units, members):
-    def body(g_ref, own_ref, oth_ref, *outs):
-        for k, out in enumerate(outs):
-            cut = slice(k * units, (k + 1) * units)
-            out[0, :, :units] = own_ref[0, :, cut]
-            out[0, :, units:] = oth_ref[0, :, cut]
-
-    rows, cols = own.shape[1:]
-    spec = pl.BlockSpec((1, rows, cols), lambda i, g: (i, 0, 0))
-    return local_call(
-        "arrange",
-        body,
-        (16,),
-        [own, oth],
-        [spec] * 2,
-        [shape((16, rows, 2 * units))] * 3,
-        [pl.BlockSpec((1, rows, 2 * units), lambda i, g: (g[0] ^ i, 0, 0))] * 3,
+        [ns, gf, *own, *oth],
+        [shape((tokens, dim))] * 2 + [shape((16, rows, wide))] * 2,
+        [
+            pltpu.VMEM((dim, 2 * both), BF),
+            pltpu.VMEM((dim, both), BF),
+            pltpu.VMEM((tokens, both), BF),
+            pltpu.VMEM((tokens, 2 * both), BF),
+        ],
         members,
     )
 
 
-def collect(parts, wide, members):
-    rows, both = parts[0].shape[1:]
-    units = both // 2
+def spread(parts, units, members):
+    rows, cols = parts[0].shape[1:]
+    places = [(a, k) for a, w in enumerate(parts) for k in range(w.shape[0])]
 
     def body(g_ref, *refs):
-        for half, out in enumerate(refs[3:]):
-            for k, part in enumerate(refs[:3]):
-                out[0, :, k * units : (k + 1) * units] = part[
-                    0, :, half * units : (half + 1) * units
-                ]
-            out[0, :, 3 * units :] = jnp.zeros((rows, wide - 3 * units), BF)
-
-    return local_call(
-        "collect",
-        body,
-        (16,),
-        parts,
-        [pl.BlockSpec((1, rows, both), lambda i, g: (g[0] ^ i, 0, 0))] * 3,
-        [shape((16, rows, wide))] * 2,
-        [pl.BlockSpec((1, rows, wide), lambda i, g: (i, 0, 0))] * 2,
-        members,
-    )
-
-
-def spread(blocks, units, members):
-    rows = blocks.shape[1]
-
-    def body(g_ref, src, gate, up, down):
-        for k in range(16):
-            part = src[g_ref[0] ^ k].astype(F32)
-            cut = slice(k * units, (k + 1) * units)
-            gate[:, cut] = part[:, :units]
-            up[:, cut] = part[:, units : 2 * units]
-            down[cut, :] = part[:, 2 * units : 3 * units].T
-
-    return local_call(
+        hold = refs[-1]
+        for i, (a, k) in enumerate(places):
+            hold[g_ref[0] ^ i] = refs[a][k].astype(F32)
+        for n in range(16):
+            for k, out in enumerate(refs[len(parts) : len(parts) + 3]):
+                out[:, n * units : (n + 1) * units] = hold[n, :, k * units : (k + 1) * units]
+
+    return plain_call(
         "spread",
         body,
-        (1,),
-        [blocks],
-        [pl.BlockSpec(blocks.shape, lambda i, g: (0, 0, 0))],
-        [
-            shape((rows, 16 * units), F32),
-            shape((rows, 16 * units), F32),
-            shape((16 * units, rows), F32),
-        ],
-        [
-            pl.BlockSpec((rows, 16 * units), lambda i, g: (0, 0)),
-            pl.BlockSpec((rows, 16 * units), lambda i, g: (0, 0)),
-            pl.BlockSpec((16 * units, rows), lambda i, g: (0, 0)),
-        ],
+        list(parts),
+        [shape((rows, 16 * units), F32)] * 3,
+        [pltpu.VMEM((16, rows, cols), F32)],
         members,
     )
 
@@ -792,17 +860,19 @@
     )
 
 
-def finish_blocks(number, block, swaps, gain_blocks, n_ctx):
+def finish_blocks(number, block, swaps, gain_blocks, ff, n_ctx):
     k = len(swaps)
 
     def body(*refs):
-        block_ref, ins, gains = refs[0], refs[1 : k + 1], refs[k + 1]
-        blocks, outs, gains_out = refs[k + 2], refs[k + 3 : 2 * k + 3], refs[2 * k + 3]
-        rest = list(refs[2 * k + 4 :])
+        ff_ref, block_ref, ins, gains = refs[0], refs[1], refs[2 : k + 2], refs[k + 2]
+        ff_out, blocks, outs = refs[k + 3], refs[k + 4], refs[k + 5 : 2 * k + 5]
+        gains_out = refs[2 * k + 5]
+        rest = list(refs[2 * k + 6 :])
+        ff_sems = rest.pop(0)
         net_sems = rest.pop()
         tp_in = rest.pop(0)
         place = Place(n_ctx)
-        greet(place, line=True, across=True, core=True, other=True)
+        greet(place, everyone=16, other=True)
         net = Net(place, net_sems)
 
         def sums():
@@ -819,23 +889,121 @@
             gather_steps(net, block_ref, blocks, 16),
             sums(),
             *[swap_steps(net, i, o) for i, o in zip(ins, outs)],
+            trade_steps(net, ff_ref, ff_out, ff_sems),
         )
         net.finish()
 
-    scratch = [pltpu.VMEM(gain_blocks.shape, BF)]
+    scratch = [pltpu.SemaphoreType.DMA((2, 8)), pltpu.VMEM(gain_blocks.shape, BF)]
     scratch += reduce_scratch(gain_blocks.shape[1], gain_blocks.shape[2], 16)
     return comm_call(
         "finish_blocks",
         number,
         body,
-        [block] + list(swaps) + [gain_blocks],
-        [ANY] * (k + 1) + [VMEM],
-        [shape((16,) + block.shape)]
+        [ff, block] + list(swaps) + [gain_blocks],
+        [ANY] * (k + 2) + [VMEM],
+        [shape(ff.shape), shape((16,) + block.shape)]
         + [shape(s.shape, s.dtype) for s in swaps]
         + [shape(gain_blocks.shape[1:], F32)],
-        [ANY] * (k + 1) + [VMEM],
+        [ANY] * (k + 2) + [VMEM],
         scratch,
-        160,
+        180,
+    )
+
+
+def norm_factor(values):
+    return lax.rsqrt(jnp.mean(values * values, axis=-1, keepdims=True) + eps_norm)
+
+
+def branch_and_norm(number, parts, x, gain, gf, n_ctx):
+    rows, dim = x.shape
+    parts = parts.reshape(8, rows, dim)
+
+    def body(
+        parts_ref, x_ref, gain_ref, gf_ref,
+        middle, norms, gfs,
+        branch, normed, near, line_in, line_out, sems,
+    ):
+        place = Place(n_ctx)
+        greet(place, line=True, across=True, core=True)
+        net = Net(place, sems)
+
+        def second():
+            yield from reduce_steps(
+                net, parts_ref, branch, None, near, line_in, line_out, rows, 8
+            )
+
+            def norm(r):
+                values = x_ref[r] + residual_scale * branch[r]
+                middle[r] = values
+                normed[r] = (values * norm_factor(values) * gain_ref[...]).astype(BF)
+
+            by_rows(rows, 16, norm)
+            yield from gather_steps(net, normed, norms, 16)
+
+        run_together(second(), gather_steps(net, gf_ref, gfs, 16))
+        net.finish()
+
+    return comm_call(
+        "branch_and_norm",
+        number,
+        body,
+        [parts, x, gain, gf],
+        [VMEM] * 3 + [ANY],
+        [shape((rows, dim), F32), shape((16, rows, dim)), shape((16, rows, dim))],
+        [VMEM, ANY, ANY],
+        [pltpu.VMEM((rows, dim), F32), pltpu.VMEM((rows, dim), BF)]
+        + reduce_scratch(rows, dim, 8),
+        220,
+    )
+
+
+def norm_and_branch_back(number, parts, middle, out_grad, gain, n_ctx):
+    rows, dim = middle.shape
+    parts = parts.reshape(16, rows, dim)
+
+    def body(
+        parts_ref, middle_ref, out_grad_ref, gain_ref,
+        grad_middle, gain_part, branches,
+        upstream, branch, near_core, near, line_in, line_out, sems,
+    ):
+        place = Place(n_ctx)
+        greet(place, line=True, across=True, core=True)
+        net = Net(place, sems)
+        run_together(
+            reduce_steps(
+                net, parts_ref, upstream, near_core, near, line_in, line_out, rows, 16
+            )
+        )
+        gain_part[...] = jnp.zeros((8, dim), F32)
+
+        def back(r):
+            values, grads = middle_ref[r], upstream[r]
+            factor = norm_factor(values)
+            scaled = grads * gain_ref[...]
+            inner = jnp.mean(scaled * values, axis=-1, keepdims=True)
+            total = out_grad_ref[r] + (
+                factor * scaled - values * factor * factor * factor * inner
+            )
+            grad_middle[r] = total
+            branch[r] = (residual_scale * total).astype(BF)
+            share = grads * values * factor
+            gain_part[...] += share[:8] + share[8:]
+
+        by_rows(rows, 16, back)
+        run_together(gather_steps(net, branch, branches, 8))
+        net.finish()
+
+    return comm_call(
+        "norm_and_branch_back",
+        number,
+        body,
+        [parts, middle, out_grad, gain],
+        [VMEM] * 4,
+        [shape((rows, dim), F32), shape((8, dim), F32), shape((8, rows, dim))],
+        [VMEM, VMEM, ANY],
+        [pltpu.VMEM((rows, dim), F32), pltpu.VMEM((rows, dim), BF)]
+        + reduce_scratch(rows, dim, 16),
+        180,
     )
 
 
@@ -859,16 +1027,17 @@
     return jnp.where(lane < NOPE, expanded, ropes)
 
 
-def attend(qn, q_up, pairs, l_up, w_out_t, table, q_pos):
+def attend(number, qn, q_up, pairs, l_up, w_out_t, table, q_pos, ff, n_ctx):
     rows, keys, heads = qn.shape[0], pairs.shape[0], q_up.shape[1] // 128
     span, block = keys // 4, rows // 4
     dim = w_out_t.shape[0]
 
     def body(
-        qn_ref, q_up_ref, pairs_ref, l_up_ref, w_ref, table_ref, pos_ref,
-        branch_ref, q_ref, o_ref, lse_ref, att_ref,
-        e_ref, top_ref, sum_ref, acc_ref,
+        qn_ref, q_up_ref, pairs_ref, l_up_ref, w_ref, table_ref, pos_ref, ff_ref,
+        branch_ref, q_ref, o_ref, lse_ref, att_ref, far_ref,
+        e_ref, top_ref, sum_ref, acc_ref, sems,
     ):
+        copies = trade_away(Place(n_ctx), ff_ref, far_ref, sems, 12)
         by_rows(
             keys,
             256,
@@ -911,6 +1080,8 @@
         for i in range(dim // 512):
             cut = slice(i * 512, (i + 1) * 512)
             branch_ref[:, cut] = matmul_nt(att_ref[...], w_ref[cut]).astype(BF)
+        for copy in copies:
+            copy.wait()
 
     wide = heads * 128
     return pl.pallas_call(
@@ -921,29 +1092,38 @@
             shape((rows, wide), F32),
             shape((rows, wide), F32),
             shape((rows, heads * VH)),
+            shape(ff.shape),
         ],
-        in_specs=[VMEM] * 7,
-        out_specs=[VMEM] * 5,
-        scratch_shapes=[pltpu.VMEM((keys, wide), BF)] + [pltpu.VMEM((rows, 128), F32)] * 3,
-        compiler_params=pltpu.CompilerParams(vmem_limit_bytes=60 << 20),
+        in_specs=[VMEM] * 7 + [ANY],
+        out_specs=[VMEM] * 5 + [ANY],
+        scratch_shapes=[pltpu.VMEM((keys, wide), BF)]
+        + [pltpu.VMEM((rows, 128), F32)] * 3
+        + [pltpu.SemaphoreType.DMA((2, ff.shape[0]))],
+        compiler_params=pltpu.CompilerParams(
+            collective_id=number, has_side_effects=True, vmem_limit_bytes=60 << 20
+        ),
         cost_estimate=pl.CostEstimate(
             flops=20_000_000_000, bytes_accessed=20 << 20, transcendentals=0
         ),
         name="attend",
-    )(qn, q_up, pairs, l_up, w_out_t, table, q_pos)
-
-
-def attend_back(gb, qn, q_up, pairs, l_up, w_out_t, table, q_pos, q, o, lse, att):
+    )(qn, q_up, pairs, l_up, w_out_t, table, q_pos, ff)
+
+
+def attend_back(
+    number, gb, qn, q_up, pairs, l_up, w_out_t, table, q_pos, q, o, lse, att, ff, n_ctx
+):
     rows, keys, heads = qn.shape[0], pairs.shape[0], q_up.shape[1] // 128
     span, block = keys // 4, rows // 4
     dim, wide = gb.shape[1], heads * 128
 
     def body(
         gb_ref, qn_ref, q_up_ref, pairs_ref, l_up_ref, w_ref, table_ref, pos_ref,
-        q_ref, o_ref, lse_ref, att_ref,
-        gp_ref, gqn_ref, gq_up_ref, gl_up_ref, gw_ref,
-        e_ref, rope_ref, go_ref, gq_ref, dq_ref, inner_ref,
+        q_ref, o_ref, lse_ref, att_ref, ff_ref,
+        gp_ref, gqn_ref, gq_up_ref, gl_up_ref, gw_ref, far_ref,
+        e_ref, rope_ref, go_ref, gq_ref, dq_ref, inner_ref, sems,
     ):
+        copies = trade_away(Place(n_ctx), ff_ref, far_ref, sems, 12)
+
         def expand(r):
             e_ref[r] = matmul(pairs_ref[r, :KVR], l_up_ref[...]).astype(BF)
             rope_ref[r] = jnp.zeros((256, 128), F32)
@@ -996,6 +1176,8 @@
         gl_up_ref[...] = matmul_tn(pairs_ref[:, :KVR], e_ref[...]).astype(BF)
         gq_up_ref[...] = matmul_tn(qn_ref[...], gq_ref[...]).astype(BF)
         gqn_ref[...] = matmul_nt(gq_ref[...], q_up_ref[...]).astype(BF)
+        for copy in copies:
+            copy.wait()
 
     return pl.pallas_call(
         body,
@@ -1005,9 +1187,10 @@
             shape(q_up.shape),
             shape(l_up.shape),
             shape(w_out_t.shape),
+            shape(ff.shape),
         ],
-        in_specs=[VMEM] * 12,
-        out_specs=[VMEM] * 5,
+        in_specs=[VMEM] * 12 + [ANY],
+        out_specs=[VMEM] * 5 + [ANY],
         scratch_shapes=[
             pltpu.VMEM((keys, wide), BF),
             pltpu.VMEM((keys, 128), F32),
@@ -1015,13 +1198,16 @@
             pltpu.VMEM((rows, wide), BF),
             pltpu.VMEM((rows, 128), F32),
             pltpu.VMEM((rows, 128), F32),
+            pltpu.SemaphoreType.DMA((2, ff.shape[0])),
         ],
-        compiler_params=pltpu.CompilerParams(vmem_limit_bytes=60 << 20),
+        compiler_params=pltpu.CompilerParams(
+            collective_id=number, has_side_effects=True, vmem_limit_bytes=60 << 20
+        ),
         cost_estimate=pl.CostEstimate(
             flops=40_000_000_000, bytes_accessed=30 << 20, transcendentals=0
         ),
         name="attend_back",
-    )(gb, qn, q_up, pairs, l_up, w_out_t, table, q_pos, q, o, lse, att)
+    )(gb, qn, q_up, pairs, l_up, w_out_t, table, q_pos, q, o, lse, att, ff)
 
 
 def shards(
@@ -1099,8 +1285,7 @@
         return lax.ppermute(block, "tp", [(0, 1), (1, 0)])
 
     wide = 640
-    ff = pack(gate_weight, up_weight, down_weight, wide, members)
-    near = [ff[0]] + [trade(ff[j], 4 * j) for j in (1, 2, 3)]
+    ff = pack(gate_weight, up_weight, down_weight.T, wide, members)
     q_rows_w, l_rows_w, o_rows_w = query_up.shape[0], latent_up.shape[0], shard_rows // 2
     q_width, o_width = heads * (NOPE + ROPE), heads * VH
     q_tiles = jnp.pad(
@@ -1125,10 +1310,12 @@
     cosine, sine_table = rope_tables(positions)
     grad_ffn = (residual_scale * out_grad_rows).astype(BF)
 
-    down_full, gains, at_all = weights_in(1, down_shard, gains, at, n_ctx)
-    down_full, near = lax.optimization_barrier((down_full, near))
-    own = [jnp.stack([r[0] for r in near])]
-    own += [trade(jnp.stack([r[k] for r in near]), k) for k in (1, 2, 3)]
+    down_full, gains, at_all, own_near, oth_near = weights_in(
+        1, down_shard, gains, at, ff, n_ctx
+    )
+    own_near, ff = lax.optimization_barrier((own_near, ff))
+    own_mid = [trade(ff[i : i + 1], i) for i in (8, 9, 10, 11)]
+    oth_next = swap_tp(own_near[4:])
     down_full = widen(down_full).reshape(dim, -1)
     gains = widen(gains[:, 0]).reshape(n_ctx, -1)
     gain_first, gain_query, gain_latent, gain_second = [
@@ -1156,9 +1343,9 @@
     pairs, qn_all, token_columns = gather_latent(
         3, pair_block, query_normed, normed_columns, n_ctx
     )
-    own, pairs, grad_ffn = lax.optimization_barrier((own, pairs, grad_ffn))
-    gf_all = gather_over(grad_ffn)
-    oth = [swap_tp(r) for r in own]
+    pairs, own_mid, ff = lax.optimization_barrier((pairs, own_mid, ff))
+    own_mid = jnp.concatenate(own_mid)
+    oth_mid = swap_tp(own_mid)
     lat_rope = widen(pairs).reshape(-1, 384)
     qn_all = qn_all.reshape(-1, qr)
 
@@ -1176,64 +1363,43 @@
         axis=1,
     )
     q_pos = jnp.broadcast_to(q_positions[:, None], (q_positions.shape[0], 128))
-    branch_part, queries, attended_wide, log_total, attended = attend(
-        qn_all, q_up, lat_rope, l_up, w_out_t, table, q_pos
-    )
-
-    (branch,) = reduce_blocks("reduce_branch", 4, [branch_part], [8], n_ctx)
-    middle = x + residual_scale * branch
-    normed_second = rms_norm(middle, gain_second).astype(BF)
-    (ns_all,) = gather_blocks("gather_second", 5, [normed_second], [16], n_ctx)
+    branch_part, queries, attended_wide, log_total, attended, own_far = attend(
+        5, qn_all, q_up, lat_rope, l_up, w_out_t, table, q_pos, ff[12:], n_ctx
+    )
+
+    middle, ns_all, gf_all = branch_and_norm(
+        4, branch_part, x, gain_second[None], grad_ffn, n_ctx
+    )
+    ns_all, gf_all = ns_all.reshape(-1, dim), gf_all.reshape(-1, dim)
+    oth_far = swap_tp(own_far)
+    own = [own_near, own_mid, own_far]
+    oth = [oth_near, oth_next, oth_mid, oth_far]
     ns_all, oth = lax.optimization_barrier((ns_all, oth))
-    w_gate, w_up, w_down_t = [
-        widen(w).reshape(dim, 2 * units)
-        for w in arrange(
-            jnp.stack(own, axis=1).reshape(16, shard_rows, wide),
-            jnp.stack(oth, axis=1).reshape(16, shard_rows, wide),
-            units,
-            members,
-        )
+    if members > 1:
+        own, oth = [
+            [widen(jnp.concatenate(w)).reshape(16, dim // 16, wide)] for w in (own, oth)
+        ]
+    ffn_part, second_part, grads_own, grads_oth = feed_forward(
+        ns_all, gf_all, own, oth, units, members
+    )
+    grads_own = narrow(grads_own.reshape(16, members, shard_rows, wide))
+    grads_oth = narrow(grads_oth.reshape(16, members, shard_rows, wide))
+    gots = [swap_tp(grads_oth[12:]), swap_tp(grads_oth[8:12]), swap_tp(grads_oth[:8])]
+    grad_middle, second_gain_part, gb_all = norm_and_branch_back(
+        6, second_part, middle, out_grad_rows, gain_second[None], n_ctx
+    )
+    second_gain_part = jnp.sum(second_gain_part, axis=0)
+    gb_all = gb_all.reshape(-1, dim)
+    gb_all, gots, ffn_part = lax.optimization_barrier((gb_all, gots, ffn_part))
+    back_far, back_mid, back_near = [
+        (mine.astype(F32) + got.astype(F32)).astype(BF)
+        for mine, got in zip((grads_own[12:], grads_own[8:12], grads_own[:8]), gots)
     ]
-    gate_values = matmul(ns_all, w_gate)
-    up_values = matmul(ns_all, w_up)
-    sigmoid_gate = jax.nn.sigmoid(gate_values)
-    hidden = (gate_values * sigmoid_gate * up_values).astype(BF)
-    ffn_part = matmul_nt(hidden, w_down_t).astype(BF)
-
-    grad_hidden = matmul(gf_all, w_down_t)
-    grad_gate = (
-        grad_hidden * up_values * sigmoid_gate * (1.0 + gate_values * (1.0 - sigmoid_gate))
-    ).astype(BF)
-    grad_up = (grad_hidden * gate_values * sigmoid_gate).astype(BF)
-    (grad_second,) = reduce_blocks(
-        "reduce_second",
-        6,
-        [(matmul_nt(grad_gate, w_gate) + matmul_nt(grad_up, w_up)).astype(BF)],
-        [16],
-        n_ctx,
-    )
-
-    ff_grads = [
-        narrow(matmul_tn(left, right).astype(BF).reshape(16, members, shard_rows, 2 * units))
-        for left, right in ((ns_all, grad_gate), (ns_all, grad_up), (gf_all, hidden))
-    ]
-    grads_own, grads_oth = collect(ff_grads, wide, members)
-    grads_oth = swap_tp(grads_oth)
-
-    grad_middle_part, second_gain_part = norm_back(middle, gain_second, grad_second)
-    grad_middle = out_grad_rows + grad_middle_part
-
-    grad_branch = (residual_scale * grad_middle).astype(BF)
-    (gb_all,) = gather_blocks("gather_branch", 7, [grad_branch], [8], n_ctx)
-    gb_all, grads_oth, ffn_part = lax.optimization_barrier((gb_all, grads_oth, ffn_part))
     ffn_sum = scatter_over(ffn_part).astype(F32)
     out_half = (middle + residual_scale * ffn_sum).astype(BF)
-    ff_back = (grads_own.astype(F32) + grads_oth.astype(F32)).astype(BF)
-    ff_back = ff_back.reshape(4, 4, shard_rows, wide)
-    back = [ff_back[0]] + [trade(ff_back[j], 4 * j) for j in (1, 2, 3)]
-    grad_lat_rope, gqn_part, q_up_part, l_up_part, out_part = attend_back(
-        gb_all, qn_all, q_up, lat_rope, l_up, w_out_t, table, q_pos,
-        queries, attended_wide, log_total, attended,
+    grad_lat_rope, gqn_part, q_up_part, l_up_part, out_part, sums_far = attend_back(
+        7, gb_all, qn_all, q_up, lat_rope, l_up, w_out_t, table, q_pos,
+        queries, attended_wide, log_total, attended, back_far, n_ctx,
     )
 
     at_part = jnp.concatenate(
@@ -1255,9 +1421,8 @@
         at_part,
         n_ctx,
     )
-    own_lat_rope, back = lax.optimization_barrier((own_lat_rope, back))
-    sums = [jnp.stack([r[0] for r in back])]
-    sums += [trade(jnp.stack([r[k] for r in back]), k) for k in (1, 2, 3)]
+    own_lat_rope, back_mid = lax.optimization_barrier((own_lat_rope, back_mid))
+    sums_mid = [trade(back_mid[i : i + 1], 8 + i) for i in range(4)]
     grad_query_latent, query_gain_part = norm_back(query_latent, gain_query, grad_query_normed)
     grad_latent_rows, latent_gain_part = norm_back(
         compressed[:, :KVR], gain_latent, own_lat_rope[:, :KVR]
@@ -1282,11 +1447,11 @@
     )
     gain_parts = narrow(gain_parts.reshape(16, members, -1)).astype(BF)
     gain_blocks = jnp.pad(gain_parts[:, None], ((0, 0), (0, 15), (0, 0)))
-    both_all, out_other, input_other, gain_sums = finish_blocks(
-        9, grad_both, [out_half, input_half], gain_blocks, n_ctx
-    )
-    both_all, sums = lax.optimization_barrier((both_all, sums))
-    ff_sums = jnp.stack(sums, axis=1).reshape(16, shard_rows, wide)
+    sums_near, both_all, out_other, input_other, gain_sums = finish_blocks(
+        9, grad_both, [out_half, input_half], gain_blocks, back_near, n_ctx
+    )
+    both_all, sums_mid = lax.optimization_barrier((both_all, sums_mid))
+    sums = [sums_near, *sums_mid, sums_far]
     if members == 1:
         down_part = matmul_tn(
             token_columns.reshape(16 * rows, shard_rows), both_all.reshape(16 * rows, -1)
@@ -1311,7 +1476,7 @@
         gain_grads[s : s + w] for s, w in zip(starts, widths)
     ]
 
-    gate_weight_grad, up_weight_grad, down_weight_grad = spread(ff_sums, units, members)
+    gate_weight_grad, up_weight_grad, down_grad_t = spread(sums, units, members)
     query_up_grad = jnp.transpose(
         at_sums[:, :q_rows_w].reshape(4, q_rows_w, heads, 128)[..., : NOPE + ROPE], (1, 0, 2, 3)
     ).reshape(q_rows_w, 4 * q_width)
@@ -1335,7 +1500,7 @@
         second_gain_grad,
         gate_weight_grad,
         up_weight_grad,
-        down_weight_grad,
+        down_grad_t.T,
     )
 
 

time: 781 us -> 725 us (0.928)
  matrix products: 53.1 us -> 12 us
  Pallas kernels: 553 us -> 572 us
  other arithmetic: 45.8 us -> 32.7 us
  local copies, waits for them, and re-layouts: 80.3 us -> 67.5 us
    dot_general x4 -> x1, matrix products: 19.3 us -> 3.93 us  [matmul(): return jnp.dot(left_side, right_side, preferred_element_type=F32)]
    pallas_call x4 -> x3, Pallas kernels: 36.7 us -> 50.6 us  [plain_call(): pl.pallas_call(body, out_shape=outs, grid_spec=pltpu.PrefetchScalarGridSp...]
    dot_general x4 -> x1, matrix products: 19.6 us -> 5.61 us  [matmul_nt(): lax.dot_general(left_side, right_side, (((1,), (1,)), ((), ())), preferre...]
    convert_element_type x3 -> x0, local copies, waits for them, and re-layouts: 13 us -> none  [shards(): matmul_tn(left, right).astype(BF)]
    dot_general x4 -> x1, matrix products: 14.2 us -> 2.41 us  [matmul_tn(): lax.dot_general(left_side, right_side, (((0,), (0,)), ((), ())), preferre...]
    another operation x15 -> x4, other arithmetic: 14.7 us -> 3.19 us  [the longest x3 3.05 us: shards(): sums += [trade(jnp.stack([r[k] for r in back]), k) for k in (1, 2, 3)]]
    pallas_call x8 -> x6, Pallas kernels: 460 us -> 458 us  [comm_call(): pl.pallas_call(body, out_shape=outs, in_specs=in_specs, out_specs=out_spe...]
  transfers between devices with their start and end apart: 20 -> 16, of which waited for: 0 -> 1; matrix products, arithmetic and copies ran while one was open for 15% -> 13% of each run, Pallas kernels for 70% -> 60%
where the time goes in v4:
time: 725 us; the launch traced here: 716 us
  Pallas kernels  572 us (79%)
  local copies, waits for them, and re-layouts  67.5 us (9%)
  other arithmetic  32.7 us (5%)
  starting transfers between devices  16.3 us (2%)
  between operations  15.1 us (2%)
  matrix products  12 us (2%)
    pallas_call x6, Pallas kernels, comm_call(): pl.pallas_call(body, out_shape=outs, in_specs=in_specs, out_specs=out_spe...  458 us
    pallas_call x3, Pallas kernels, plain_call(): pl.pallas_call(body, out_shape=outs, grid_spec=pltpu.PrefetchScalarGridSp...  50.6 us
    pallas_call x1, Pallas kernels, attend_back(): pl.pallas_call(body, out_shape=[shape(pairs.shape), shape(qn.shape), shap...  31.7 us
    pallas_call x1, Pallas kernels, attend(): pl.pallas_call(body, out_shape=[shape((rows, dim)), shape((rows, wide)),...  31.6 us
  transfers between devices with their start and end apart: 16, of which 1 were waited for; matrix products, arithmetic and copies ran while one was open for 13% of the time, Pallas kernels for 60%

profile of v4, /device:TPU:3, one launch (start us, length us, event | category | flops | bytes accessed | tf_op | source)
XLA Modules:
  0.0 715.6 jit_solution(17314339186874099226)
XLA Ops:
  13.1 5.1 pack.1.ff_ref
  18.8 100.5 %weights_in.1 = (bf16[16,160,1056]{2,1,0:T(8,128)(2,1)}, f32[16,8,384]{2,1,0:T(8,128)}, bf16[16,144,640]{2,1,0:T(8,128)(2,1)}, bf16[8,160,640]{2,1,0:T(8,128)(2,1)}, bf16[4,160,640]{2,1,0:T(8,128)(2,1)}) custom-call(bf16[160,1056]{1,0:T(8,128)(2,1)} %pad_maximum_fusion.2.down_ref, f32[8,384]{1,0:T(8,128)} %broadcast_in_dim.12.gains_ref, ...), custom_call_target="tpu_custom_call" | custom-call | tf_op jit(solution)/shard_map/weights_in/pallas_call | solution.py:393
  120.2 3.4 collective-permute-start.2
  123.5 2.8 collective-permute-start
  132.3 3.9 fusion.38
  148.6 5.4 reshape.325
  154.0 3.1 copy.53
  158.9 39.8 %gather_latent.1 = (bf16[2,64,384]{2,1,0:T(8,128)(2,1)}, bf16[16,2,64,384]{3,2,1,0:T(8,128)(2,1)}, bf16[8,64,768]{2,1,0:T(8,128)(2,1)}, bf16[16,64,160]{2,1,0:T(8,128)(2,1)}) custom-call(bf16[64,384]{1,0:T(8,128)(2,1)} %concatenate.69.pair_ref, bf16[64,768]{1,0:T(8,128)(2,1)} %multiply_convert_fusion.2.query_ref, bf16[16,64,160]{2,1,0:T(8,128)(2,1)} %bitcast.78), custom_call_target="tpu_custom_call" | custom-call | tf_op jit(solution)/shard_map/gather_latent/pallas_call | solution.py:393
  203.5 2.9 concatenate.71.table_ref
  212.2 31.6 %attend.1 = (bf16[512,2560]{1,0:T(8,128)(2,1)}, bf16[512,640]{1,0:T(8,128)(2,1)}, f32[512,640]{1,0:T(8,128)}, f32[512,640]{1,0:T(8,128)}, bf16[512,320]{1,0:T(8,128)(2,1)}, /*index=5*/bf16[4,160,640]{2,1,0:T(8,128)(2,1)}) custom-call(bf16[512,768]{1,0:T(8,128)(2,1)} %bitcast.104, bf16[768,640]{1,0:T(8,128)(2,1)} %bitcast.85, bf16[2048,384]{1,0:T(8,128)(2,1)} %bitcast.102, ...), custom_call_target="tpu_custom_call" | custom-call | flops 20000000000 | bytes 20971520 | tf_op jit(solution)/shard_map/attend/pallas_call | solution.py:1087
  248.2 78.6 %branch_and_norm.1 = (f32[64,2560]{1,0:T(8,128)}, bf16[16,64,2560]{2,1,0:T(8,128)(2,1)}, bf16[16,64,2560]{2,1,0:T(8,128)(2,1)}) custom-call(bf16[8,64,2560]{2,1,0:T(8,128)(2,1)} %bitcast.77, f32[64,2560]{1,0:T(8,128)} %get-tuple-element.179.x_ref, f32[1,2560]{1,0:T(1,128)} %broadcast_in_dim_reshape.2.gain_ref, bf16[64,2560]{1,0:T(8,128)(2,1)} %get-tuple-element.176.gf_ref), custom_call_target="tpu_custom_call" | custom-call | tf_op jit(solution)/shard_map/branch_and_norm/pallas_call | solution.py:393
  328.6 38.3 %feed_forward.1 = (bf16[1024,2560]{1,0:T(8,128)(2,1)}, bf16[1024,2560]{1,0:T(8,128)(2,1)}, bf16[16,160,640]{2,1,0:T(8,128)(2,1)}, bf16[16,160,640]{2,1,0:T(8,128)(2,1)}) custom-call(s32[1]{0:T(128)} %bitcast.3.g_ref, bf16[1024,2560]{1,0:T(8,128)(2,1)} %bitcast.73, bf16[1024,2560]{1,0:T(8,128)(2,1)} %bitcast.74, ...), custom_call_target="tpu_custom_call" | custom-call | flops 1000000000 | bytes 20971520 | tf_op jit(solution)/shard_map/feed_forward/pallas_call | solution.py:623
  366.9 2.9 slice.170
  372.6 73.1 %norm_and_branch_back.1 = (f32[64,2560]{1,0:T(8,128)}, f32[8,2560]{1,0:T(8,128)}, bf16[8,64,2560]{2,1,0:T(8,128)(2,1)}) custom-call(bf16[16,64,2560]{2,1,0:T(8,128)(2,1)} %bitcast.75, f32[64,2560]{1,0:T(8,128)} %get-tuple-element.90.middle_ref, f32[64,2560]{1,0:T(8,128)} %get-tuple-element.178.out_grad_ref, f32[1,2560]{1,0:T(1,128)} %broadcast_in_dim_reshape.2.gain_ref), custom_call_target="tpu_custom_call" | custom-call | tf_op jit(solution)/shard_map/norm_and_branch_back/pallas_call | solution.py:393
  448.1 3.2 add_convert_fusion.1
  451.3 31.7 %attend_back.1 = (bf16[2048,384]{1,0:T(8,128)(2,1)}, bf16[512,768]{1,0:T(8,128)(2,1)}, bf16[768,640]{1,0:T(8,128)(2,1)}, bf16[256,640]{1,0:T(8,128)(2,1)}, bf16[...) custom-call(bf16[512,2560]{1,0:T(8,128)(2,1)} %bitcast.101, bf16[512,768]{1,0:T(8,128)(2,1)} %bitcast.105, ...), custom_call_target="tpu_custom_call" | custom-call | flops 40000000000 | bytes 31457280 | tf_op jit(solution)/shard_map/attend_back/pallas_call | solution.py:1182
  483.0 3.1 copy.73
  488.4 3.7 pad_maximum_fusion.at_ref
  492.2 103.0 %reduce_latent.1 = (f32[64,384]{1,0:T(8,128)}, f32[64,768]{1,0:T(8,128)}, bf16[4,144,640]{2,1,0:T(8,128)(2,1)}) custom-call(bf16[16,2,64,384]{3,2,1,0:T(8,128)(2,1)} %bitcast.83, bf16[8,64,768]{2,1,0:T(8,128)(2,1)} %bitcast.89, bf16[16,144,640]{2,1,0:T(8,128)(2,1)} %pad_maximum_fusion.at_ref), custom_call_target="tpu_custom_call" | custom-call | tf_op jit(solution)/shard_map/reduce_latent/pallas_call | solution.py:393
  601.9 5.6 multiply_reduce_fusion
  609.2 3.6 collective-permute-start.13
  621.3 3.6 add_convert_fusion.refs_0_
  627.8 62.8 %finish_blocks.1 = (bf16[8,160,640]{2,1,0:T(8,128)(2,1)}, bf16[16,64,1056]{2,1,0:T(8,128)(2,1)}, bf16[64,2560]{1,0:T(8,128)(2,1)}, bf16[64,2560]{1,0:T(8,128)(2,1)}, f32[16,384]{1,0:T(8,128)}) custom-call(bf16[8,160,640]{2,1,0:T(8,128)(2,1)} %add_convert_fusion.refs_0_, bf16[64,1056]{1,0:T(8,128)(2,1)} %copy-done.13, ...), custom_call_target="tpu_custom_call" | custom-call | tf_op jit(solution)/shard_map/finish_blocks/pallas_call | solution.py:393
  698.4 7.3 %spread.1 = (f32[160,3200]{1,0:T(8,128)}, f32[160,3200]{1,0:T(8,128)}, f32[160,3200]{1,0:T(8,128)}) custom-call(s32[1]{0:T(128)} %bitcast.3.g_ref, bf16[8,160,640]{2,1,0:T(8,128)(2,1)} %get-tuple-element.137.refs_0_, bf16[1,160,640]{2,1,0:T(8,128)(2,1)} %collective-permute-done.10.refs_1_, bf16[1,160,640]{2,1,0:T(8,128)(2,1)} %collective-permute-done.11.refs_2_, ...), custom_call_target="tpu_custom_call" | custom-call | flops 1000000000 | bytes 20971520 | tf_op jit(solution)/shard_map/spread/pallas_call | solution.py:623
  (230 shorter events, 81.7 us)
Async XLA Ops:
  7.2 618.8 %reduce-scatter.2.cloned.1.call-start = ((), (), s32[]{:S(2)}) async-start(), calls=%async_computation.1 | async-start | bytes 5570560 | tf_op jit(solution)/shard_map/reduce_scatter | solution.py:1265
  18.8 100.5 %copy-start = (bf16[16,160,640]{2,1,0:T(8,128)(2,1)S(1)}, bf16[16,160,640]{2,1,0:T(8,128)(2,1)}, u32[]{:S(2)}) copy-start(bf16[16,160,640]{2,1,0:T(8,128)(2,1)} %pack.1.ff_ref) | copy-start | bytes 9830404
  120.2 86.2 %collective-permute-start.3 = (bf16[1,160,640]{2,1,0:T(8,128)(2,1)}, bf16[1,160,640]{2,1,0:T(8,128)(2,1)}, u32[]{:S(2)}, u32[]{:S(2)}) collective-permute-start(bf16[1,160,640]{2,1,0:T(8,128)(2,1)} %get-tuple-element.156), channel_id=1, source_target_pairs={{0,22},{2,20},{4,18},{6,16},{8,30},{10,28},{12,26},{14,24},{16,6},... | collective-permute-start | bytes 614408 | tf_op jit(solution)/shard_map/ppermute | solution.py:1280
  120.2 86.2 %collective-permute-start.2 = (bf16[1,160,640]{2,1,0:T(8,128)(2,1)}, bf16[1,160,640]{2,1,0:T(8,128)(2,1)}, u32[]{:S(2)}, u32[]{:S(2)}) collective-permute-start(bf16[1,160,640]{2,1,0:T(8,128)(2,1)} %get-tuple-element.157), channel_id=1, source_target_pairs={{0,20},{2,22},{4,16},{6,18},{8,28},{10,30},{12,24},{14,26},{16,4},... | collective-permute-start | bytes 614408 | tf_op jit(solution)/shard_map/ppermute | solution.py:1280
  123.5 82.9 %collective-permute-start.1 = (bf16[1,160,640]{2,1,0:T(8,128)(2,1)}, bf16[1,160,640]{2,1,0:T(8,128)(2,1)}, u32[]{:S(2)}, u32[]{:S(2)}) collective-permute-start(bf16[1,160,640]{2,1,0:T(8,128)(2,1)} %get-tuple-element.158), channel_id=1, source_target_pairs={{0,18},{2,16},{4,22},{6,20},{8,26},{10,24},{12,30},{14,28},{16,2},... | collective-permute-start | bytes 614408 | tf_op jit(solution)/shard_map/ppermute | solution.py:1280
  123.5 82.9 %collective-permute-start = (bf16[1,160,640]{2,1,0:T(8,128)(2,1)}, bf16[1,160,640]{2,1,0:T(8,128)(2,1)}, u32[]{:S(2)}, u32[]{:S(2)}) collective-permute-start(bf16[1,160,640]{2,1,0:T(8,128)(2,1)} %get-tuple-element.159), channel_id=1, source_target_pairs={{0,16},{2,18},{4,20},{6,22},{8,24},{10,26},{12,28},{14,30},{16,0},... | collective-permute-start | bytes 614408 | tf_op jit(solution)/shard_map/ppermute | solution.py:1280
  127.3 199.5 %collective-permute-start.4 = (bf16[4,160,640]{2,1,0:T(8,128)(2,1)}, bf16[4,160,640]{2,1,0:T(8,128)(2,1)}, u32[]{:S(2)}, u32[]{:S(2)}) collective-permute-start(bf16[4,160,640]{2,1,0:T(8,128)(2,1)} %slice.167), channel_id=1, source_target_pairs={{0,1},{1,0},{2,3},{3,2},{4,5},{5,4},{6,7},{7,6},{8,9},{9,8},{10,11... | collective-permute-start | bytes 2457608 | tf_op jit(solution)/shard_map/ppermute | solution.py:1285
  211.2 115.6 %collective-permute-start.5 = (bf16[4,160,640]{2,1,0:T(8,128)(2,1)S(1)}, bf16[4,160,640]{2,1,0:T(8,128)(2,1)S(1)}, u32[]{:S(2)}, u32[]{:S(2)}) collective-permute-start(bf16[4,160,640]{2,1,0:T(8,128)(2,1)S(1)} %constant_dynamic-update-slice_fusion.refs_1_), channel_id=1, source_target_pairs={{0,1},{1,0},{2,3},{3,2},{4,5},{5,4},{6,7},{7,6},{8,9},{9,8},{10,11... | collective-permute-start | bytes 2457608 | tf_op jit(solution)/shard_map/ppermute | solution.py:1285
  243.8 83.9 %collective-permute-start.6 = (bf16[4,160,640]{2,1,0:T(8,128)(2,1)}, bf16[4,160,640]{2,1,0:T(8,128)(2,1)S(1)}, u32[]{:S(2)}, u32[]{:S(2)}) collective-permute-start(bf16[4,160,640]{2,1,0:T(8,128)(2,1)} %get-tuple-element.98.refs_2_), channel_id=1, source_target_pairs={{0,1},{1,0},{2,3},{3,2},{4,5},{5,4},{6,7},{7,6},{8,9},{9,8},{10,11... | collective-permute-start | bytes 2457608 | tf_op jit(solution)/shard_map/ppermute | solution.py:1285
  369.8 77.0 %collective-permute-start.9 = (bf16[8,160,640]{2,1,0:T(8,128)(2,1)}, bf16[8,160,640]{2,1,0:T(8,128)(2,1)S(1)}, u32[]{:S(2)}, u32[]{:S(2)}) collective-permute-start(bf16[8,160,640]{2,1,0:T(8,128)(2,1)} %slice.170), channel_id=1, source_target_pairs={{0,1},{1,0},{2,3},{3,2},{4,5},{5,4},{6,7},{7,6},{8,9},{9,8},{10,11... | collective-permute-start | bytes 4915208 | tf_op jit(solution)/shard_map/ppermute | solution.py:1285
  371.1 75.6 %collective-permute-start.8 = (bf16[4,160,640]{2,1,0:T(8,128)(2,1)}, bf16[4,160,640]{2,1,0:T(8,128)(2,1)S(1)}, u32[]{:S(2)}, u32[]{:S(2)}) collective-permute-start(bf16[4,160,640]{2,1,0:T(8,128)(2,1)} %get-tuple-element.154), channel_id=1, source_target_pairs={{0,1},{1,0},{2,3},{3,2},{4,5},{5,4},{6,7},{7,6},{8,9},{9,8},{10,11... | collective-permute-start | bytes 2457608 | tf_op jit(solution)/shard_map/ppermute | solution.py:1285
  372.5 74.2 %collective-permute-start.7 = (bf16[4,160,640]{2,1,0:T(8,128)(2,1)}, bf16[4,160,640]{2,1,0:T(8,128)(2,1)}, u32[]{:S(2)}, u32[]{:S(2)}) collective-permute-start(bf16[4,160,640]{2,1,0:T(8,128)(2,1)} %get-tuple-element.155), channel_id=1, source_target_pairs={{0,1},{1,0},{2,3},{3,2},{4,5},{5,4},{6,7},{7,6},{8,9},{9,8},{10,11... | collective-permute-start | bytes 2457608 | tf_op jit(solution)/shard_map/ppermute | solution.py:1285
  492.1 103.0 %copy-start.3 = (f32[64,1056]{1,0:T(8,128)S(1)}, f32[64,1056]{1,0:T(8,128)}, u32[]{:S(2)}) copy-start(f32[64,1056]{1,0:T(8,128)} %copy-done.1) | copy-start | bytes 811012
  492.1 103.1 %copy-start.37 = (f32[64]{0:T(128)S(1)}, f32[64]{0:T(128)}, u32[]{:S(2)}) copy-start(f32[64]{0:T(128)} %copy-done.36) | copy-start | bytes 772
  492.1 104.9 %copy-start.31 = (f32[256]{0:T(256)S(1)}, f32[256]{0:T(256)}, u32[]{:S(2)}) copy-start(f32[256]{0:T(256)} %copy-done.30) | copy-start | bytes 3076
  492.1 104.9 %copy-start.33 = (f32[64]{0:T(128)S(1)}, f32[64]{0:T(128)}, u32[]{:S(2)}) copy-start(f32[64]{0:T(128)} %copy-done.32) | copy-start | bytes 772
  492.1 106.6 %copy-start.35 = (f32[16]{0:T(128)S(1)}, f32[16]{0:T(128)}, u32[]{:S(2)}) copy-start(f32[16]{0:T(128)} %copy-done.34) | copy-start | bytes 196
  492.2 106.6 %copy-start.42 = (f32[64]{0:T(128)S(1)}, f32[64]{0:T(128)}, u32[]{:S(2)}) copy-start(f32[64]{0:T(128)} %copy-done.41) | copy-start | bytes 772
  492.2 109.7 %copy-start.39 = (f32[64]{0:T(128)S(1)}, f32[64]{0:T(128)}, u32[]{:S(2)}) copy-start(f32[64]{0:T(128)} %copy-done.38) | copy-start | bytes 772
  609.2 85.4 %collective-permute-start.13 = (bf16[1,160,640]{2,1,0:T(8,128)(2,1)}, bf16[1,160,640]{2,1,0:T(8,128)(2,1)S(1)}, u32[]{:S(2)}, u32[]{:S(2)}) collective-permute-start(bf16[1,160,640]{2,1,0:T(8,128)(2,1)} %get-tuple-element.160), channel_id=1, source_target_pairs={{0,22},{2,20},{4,18},{6,16},{8,30},{10,28},{12,26},{14,24},{16,6},... | collective-permute-start | bytes 614408 | tf_op jit(solution)/shard_map/ppermute | solution.py:1280
  612.8 81.8 %collective-permute-start.12 = (bf16[1,160,640]{2,1,0:T(8,128)(2,1)}, bf16[1,160,640]{2,1,0:T(8,128)(2,1)S(1)}, u32[]{:S(2)}, u32[]{:S(2)}) collective-permute-start(bf16[1,160,640]{2,1,0:T(8,128)(2,1)} %get-tuple-element.161), channel_id=1, source_target_pairs={{0,20},{2,22},{4,16},{6,18},{8,28},{10,30},{12,24},{14,26},{16,4},... | collective-permute-start | bytes 614408 | tf_op jit(solution)/shard_map/ppermute | solution.py:1280
  612.8 81.8 %collective-permute-start.11 = (bf16[1,160,640]{2,1,0:T(8,128)(2,1)}, bf16[1,160,640]{2,1,0:T(8,128)(2,1)}, u32[]{:S(2)}, u32[]{:S(2)}) collective-permute-start(bf16[1,160,640]{2,1,0:T(8,128)(2,1)} %get-tuple-element.162), channel_id=1, source_target_pairs={{0,18},{2,16},{4,22},{6,20},{8,26},{10,24},{12,30},{14,28},{16,2},... | collective-permute-start | bytes 614408 | tf_op jit(solution)/shard_map/ppermute | solution.py:1280
  613.7 81.0 %collective-permute-start.10 = (bf16[1,160,640]{2,1,0:T(8,128)(2,1)}, bf16[1,160,640]{2,1,0:T(8,128)(2,1)}, u32[]{:S(2)}, u32[]{:S(2)}) collective-permute-start(bf16[1,160,640]{2,1,0:T(8,128)(2,1)} %get-tuple-element.163), channel_id=1, source_target_pairs={{0,16},{2,18},{4,20},{6,22},{8,24},{10,26},{12,28},{14,30},{16,0},... | collective-permute-start | bytes 614408 | tf_op jit(solution)/shard_map/ppermute | solution.py:1280
  697.1 9.8 %collective-permute-start.14 = (bf16[160,1056]{1,0:T(8,128)(2,1)S(1)}, bf16[160,1056]{1,0:T(8,128)(2,1)S(1)}, u32[]{:S(2)}, u32[]{:S(2)}) collective-permute-start(bf16[160,1056]{1,0:T(8,128)(2,1)S(1)} %fusion), channel_id=1, source_target_pairs={{0,1},{1,0},{2,3},{3,2},{4,5},{5,4},{6,7},{7,6},{8,9},{9,8},{10,11... | collective-permute-start | bytes 1013768 | tf_op jit(solution)/shard_map/ppermute | solution.py:1285
  (42 other events, 390.1 us)
Sparse Core Ops, SparseCore 0:
  446.9 83.8 reduce-scatter.1

commit v5 on v4

--- a/solution.py
+++ b/solution.py
@@ -73,6 +73,9 @@
 
 MESH = pl.DeviceIdType.MESH
 OFFSETS = (0, -1, 1, -2, 2, -3, 3)
+
+
+TRADED_FIRST, TRADED_NEXT, TRADED_LAST = (8, 9, 12, 4, 5, 2, 3, 1), (10, 11, 6, 7), (13, 14, 15)
 
 
 class Place:
@@ -185,12 +188,10 @@
     pl.semaphore_wait(barrier, count)
 
 
-def trade_away(place, src, out, sems, first):
+def trade_away(place, src, out, sems):
     barrier = pltpu.get_barrier_semaphore()
-    count = src.shape[0]
-    devices = [
-        ((place.g ^ (first + k)) * place.members + place.m, place.t) for k in range(count)
-    ]
+    count = len(TRADED_LAST)
+    devices = [((place.g ^ i) * place.members + place.m, place.t) for i in TRADED_LAST]
     for device in devices:
         pl.semaphore_signal(barrier, inc=1, device_id=device, device_id_type=MESH)
     pl.semaphore_wait(barrier, count)
@@ -210,7 +211,7 @@
     return copies
 
 
-def gather_steps(net, src, out, width):
+def gather_steps(net, src, out, width, start, pace):
     p = net.place
     cores = width == 16
 
@@ -247,20 +248,20 @@
             net.send(there, there, c_sem[1, o], p.core, p.valid(o))
 
     forward(0)
-    yield
     for near in (1, 2, 3):
+        yield start + near * (pace + 2)
         from_line(-near)
         from_line(near)
-        yield
+        yield start + near * (pace + 2) + 0.5
         if near == 1:
             from_across(0)
         else:
             from_across(1 - near)
             from_across(near - 1)
-        yield
+    yield start + 4 * (pace + 2)
     from_across(-3)
     from_across(3)
-    yield
+    yield start + 4 * (pace + 2) + 2
     for o in OFFSETS:
         net.recv(lambda: slot(o, p.b, 1 - p.d), c_sem[0, o], p.valid(o))
         if cores:
@@ -281,7 +282,9 @@
     pl.loop(0, rows // step)(body)
 
 
-def reduce_steps(net, parts, out, near_core, near_x, line_in, line_out, rows, width):
+def reduce_steps(
+    net, parts, out, near_core, near_x, line_in, line_out, rows, width, start, pace
+):
     p = net.place
     cores = width == 16
     order = (-3, 3, -2, 2, -1, 1, 0)
@@ -298,7 +301,7 @@
                     return near_core.at[(p.a + o) * 2 + b]
 
                 net.send(src, dst, c_sem[side, o], p.core, p.valid(o))
-        yield
+        yield min(start, 1.0)
     x_sem = {o: net.sem() for o in order}
     up_sem = {o: net.sem() for o in (0, 1, 2)}
     down_sem = {o: net.sem() for o in (0, 1, 2)}
@@ -324,8 +327,8 @@
             p.across if cores else p.core,
             p.valid(o),
         )
-    yield
-    for o in order:
+    for number, o in enumerate(order):
+        yield start + 3 + (number // 2 + 1) * (pace + 0.5)
         ok = p.valid(o)
         if cores:
             net.recv(lambda: near_core.at[(p.a + o) * 2 + p.b], c_sem[0, o], ok)
@@ -365,24 +368,35 @@
             p.up if o > 0 else p.down,
             ok,
         )
-        yield
 
 
 def swap_steps(net, src, dst):
     sem = net.sem()
     net.send(lambda: src, lambda: dst, sem, net.place.other)
-    yield
+    yield 90.0
     net.recv(lambda: dst, sem)
 
 
+def together(*tasks):
+    tasks = [[0.0, number, task] for number, task in enumerate(tasks)]
+    while tasks:
+        first = min(tasks)
+        try:
+            first[0] = next(first[2])
+        except StopIteration:
+            tasks.remove(first)
+        if tasks:
+            yield min(tasks)[0]
+
+
 def run_together(*tasks):
-    tasks = list(tasks)
-    while tasks:
-        for task in list(tasks):
-            try:
-                next(task)
-            except StopIteration:
-                tasks.remove(task)
+    for _ in together(*tasks):
+        pass
+
+
+def after(start, task):
+    yield start
+    yield from task
 
 
 ANY = pl.BlockSpec(memory_space=pl.ANY)
@@ -416,152 +430,74 @@
     ]
 
 
-def gather_blocks(name, number, items, widths, n_ctx):
-    k = len(items)
-
-    def body(*refs):
-        ins, outs, sems = refs[:k], refs[k : 2 * k], refs[-1]
-        place = Place(n_ctx)
-        greet(place, line=True, across=16 in widths, core=True)
-        net = Net(place, sems)
-        run_together(*[gather_steps(net, i, o, w) for i, o, w in zip(ins, outs, widths)])
-        net.finish()
-
-    outs = comm_call(
-        name,
-        number,
-        body,
-        items,
-        [ANY] * k,
-        [shape((w,) + i.shape, i.dtype) for i, w in zip(items, widths)],
-        [ANY] * k,
-        [],
-        64 * k,
-    )
-    return [o.reshape((-1,) + o.shape[2:]) for o in outs]
-
-
-def reduce_blocks(name, number, items, widths, n_ctx):
-    k = len(items)
-    blocks = [i.reshape(w, i.shape[0] // w, i.shape[1]) for i, w in zip(items, widths)]
-
-    def body(*refs):
-        ins, outs, rest = refs[:k], refs[k : 2 * k], list(refs[2 * k :])
-        place = Place(n_ctx)
-        greet(place, line=True, across=16 in widths, core=True)
-        net = Net(place, rest.pop())
-        tasks = []
-        for i, o, w in zip(ins, outs, widths):
-            near_core = rest.pop(0) if w == 16 else None
-            near_x, line_in, line_out = rest.pop(0), rest.pop(0), rest.pop(0)
-            tasks.append(
-                reduce_steps(net, i, o, near_core, near_x, line_in, line_out, o.shape[0], w)
-            )
-        run_together(*tasks)
-        net.finish()
-
-    scratch = []
-    for i, w in zip(blocks, widths):
-        scratch += reduce_scratch(i.shape[1], i.shape[2], w)
-    return comm_call(
-        name,
-        number,
-        body,
-        blocks,
-        [VMEM] * k,
-        [shape(i.shape[1:], F32) for i in blocks],
-        [VMEM] * k,
-        scratch,
-        64 * k,
-    )
-
-
-def trade_steps(net, src, out, sems, onward=None):
+def trade_sends(net, block, out, sems, timed):
     p = net.place
-
-    def device(i):
-        return ((p.g ^ i) * p.members + p.m, p.t)
-
-    keep = pltpu.make_async_copy(src.at[0], out.at[0], net.sem())
-    keep.start()
-    if onward is not None:
-        net.send(lambda: src.at[0], lambda: onward.at[0], sems.at[1, 0], p.other)
-    yield
-    for i in (4, 5, 6, 7, 2, 3, 1):
-        net.send(lambda i=i: src.at[i], lambda i=i: out.at[i], sems.at[0, i], lambda i=i: device(i))
-        yield
-    for i in (1, 2, 3, 4, 5, 6, 7):
-        here = lambda i=i: out.at[i]
-        net.recv(here, sems.at[0, i])
-        if onward is not None and i < 4:
-            net.send(here, lambda i=i: onward.at[i], sems.at[1, i], p.other)
-        yield
-    if onward is not None:
-        for i in range(4):
-            net.recv(lambda i=i: onward.at[i], sems.at[1, i])
-    keep.wait()
+    for i, when_to in timed:
+        yield when_to
+        net.send(
+            lambda i=i: block(i),
+            lambda i=i: out(i),
+            sems.at[i],
+            lambda i=i: ((p.g ^ i) * p.members + p.m, p.t),
+        )
+
+
+def trade_receives(net, out, sems, which):
+    for i in which:
+        net.recv(lambda i=i: out(i), sems.at[i])
 
 
 def weights_in(number, down, gains, at, ff, n_ctx):
     def body(
         down_ref, gains_ref, at_ref, ff_ref,
-        downs, gain_blocks, heads, near, other_near,
-        at_sems, tp_sems, ff_sems, sems,
+        downs, gain_blocks, heads, near,
+        at_sems, ff_sems, sems,
     ):
         p = Place(n_ctx)
-        greet(p, everyone=16, other=True)
+        greet(p, everyone=16)
         net = Net(p, sems)
         owner = p.d == p.t
         f = p.a * 2 + p.d
 
         def attention():
-            keep = pltpu.make_async_copy(at_ref.at[p.a], heads.at[p.g], net.sem())
+            keep = pltpu.make_async_copy(at_ref.at[p.a], heads.at[f], net.sem())
             pl.when(owner)(lambda: keep.start())
             for s in range(4):
                 net.send(
                     lambda s=s: at_ref.at[s],
-                    lambda: heads.at[p.g],
-                    at_sems.at[0, f],
+                    lambda: heads.at[f],
+                    at_sems.at[f],
                     lambda s=s: p.at(a=s, d=p.t),
                     ~(owner & (p.a == s)),
                 )
+            yield 50.0
             pl.when(owner)(lambda: keep.wait())
-            yield
-            yield
             for q in range(8):
-                mine = lambda q=q: heads.at[(q // 2 * 2 + p.b) * 2 + q % 2]
-                net.recv(mine, at_sems.at[0, q], owner & (f != q))
-                net.send(mine, mine, at_sems.at[1, q], p.across, owner)
-                net.send(mine, mine, tp_sems.at[0, q], p.other, owner)
-                if q % 2:
-                    yield
-            for q in range(8):
-                theirs = lambda q=q: heads.at[(q // 2 * 2 + 1 - p.b) * 2 + q % 2]
-                net.recv(theirs, at_sems.at[1, q], owner)
-                net.send(theirs, theirs, tp_sems.at[1, q], p.other, owner)
-                if q % 2:
-                    yield
-            for q in range(8):
-                for side in (0, 1):
-                    b = 1 - p.b if side else p.b
-                    net.recv(
-                        lambda: heads.at[(q // 2 * 2 + b) * 2 + q % 2], tp_sems.at[side, q], ~owner
-                    )
+                net.recv(lambda q=q: heads.at[q], at_sems.at[q], owner & (f != q))
+
+        def trades():
+            keep = pltpu.make_async_copy(ff_ref.at[0], near.at[0], net.sem())
+            keep.start()
+            out = lambda i: near.at[1 + TRADED_FIRST.index(i)]
+            timed = ((1, 1), (4, 2), (8, 4), (5, 9), (9, 12), (2, 18), (12, 20), (3, 24))
+            yield from trade_sends(net, lambda i: ff_ref.at[i], out, ff_sems, timed)
+            yield 60.0
+            trade_receives(net, out, ff_sems, TRADED_FIRST)
+            keep.wait()
 
         run_together(
-            gather_steps(net, gains_ref, gain_blocks, 16),
-            gather_steps(net, down_ref, downs, 16),
-            attention(),
-            trade_steps(net, ff_ref, near, ff_sems, other_near),
+            gather_steps(net, gains_ref, gain_blocks, 16, 0, 3),
+            gather_steps(net, down_ref, downs, 16, 0, 8),
+            after(1.5, attention()),
+            trades(),
         )
         net.finish()
 
     outs = [
         shape((16,) + down.shape),
         shape((16,) + gains.shape, gains.dtype),
-        shape((16,) + at.shape[1:]),
-        shape((8,) + ff.shape[1:]),
-        shape((4,) + ff.shape[1:]),
+        shape((8,) + at.shape[1:]),
+        shape((1 + len(TRADED_FIRST),) + ff.shape[1:]),
     ]
     return comm_call(
         "weights_in",
@@ -570,48 +506,52 @@
         [down, gains, at, ff],
         [ANY] * 4,
         outs,
-        [ANY] * 5,
-        [pltpu.SemaphoreType.DMA((2, 8))] * 3,
+        [ANY] * 4,
+        [pltpu.SemaphoreType.DMA((8,)), pltpu.SemaphoreType.DMA((16,))],
         200,
     )
 
 
-def head_grads_steps(net, at_ref, at_out, at_x, at_tp, x_sems, rows):
+def head_grads_steps(net, at_ref, at_out, at_x, at_tp, x_sems, tp_sems, rows, start):
     p = net.place
     owner = p.d == p.t
     f = p.a * 2 + p.d
+    place = lambda q, side: (q // 2 * 2 + (1 - p.b if side else p.b)) * 2 + q % 2
+    for side in (1, 0):
+        for q in range(8):
+            net.send(
+                lambda q=q, side=side: at_ref.at[place(q, side)],
+                lambda q=q, side=side: at_tp.at[side, q],
+                tp_sems.at[side, q],
+                p.other,
+                ~owner,
+            )
     for q in range(8):
+        yield start + 4 + 2 * (q + 1)
+        here = at_tp.at[1, q]
+        net.recv(lambda: here, tp_sems.at[1, q], owner)
+        pl.when(owner)(lambda: add_into(here, [here, at_ref.at[place(q, 1)]], rows))
         net.send(
-            lambda q=q: at_ref.at[(q // 2 * 2 + 1 - p.b) * 2 + q % 2],
-            lambda q=q: at_x.at[q],
-            x_sems.at[0, q],
-            p.across,
+            lambda here=here: here, lambda q=q: at_x.at[q], x_sems.at[0, q], p.across, owner
         )
-    yield
+    keep = pltpu.make_async_copy(at_tp.at[0, f], at_out.at[p.a], net.sem())
     for q in range(8):
-        near = at_x.at[q]
-        net.recv(lambda: near, x_sems.at[0, q])
-        add_into(near, [near, at_ref.at[(q // 2 * 2 + p.b) * 2 + q % 2]], rows)
+        yield start + 20 + 2 * (q + 1)
+        here, near = at_tp.at[0, q], at_x.at[q]
+        net.recv(lambda: here, tp_sems.at[0, q], owner)
+        net.recv(lambda: near, x_sems.at[0, q], owner)
+        pl.when(owner)(lambda: add_into(here, [here, near, at_ref.at[place(q, 0)]], rows))
         net.send(
-            lambda near=near: near, lambda q=q: at_tp.at[q], x_sems.at[1, q], p.other, ~owner
-        )
-        yield
-    keep = pltpu.make_async_copy(at_x.at[f], at_out.at[p.a], net.sem())
-    for q in range(8):
-        near, tp = at_x.at[q], at_tp.at[q]
-        net.recv(lambda: tp, x_sems.at[1, q], owner)
-        pl.when(owner)(lambda: add_into(near, [near, tp], rows))
-        net.send(
-            lambda near=near: near,
+            lambda here=here: here,
             lambda: at_out.at[p.a],
-            x_sems.at[2, p.a],
+            x_sems.at[1, p.a],
             lambda q=q: p.at(a=q // 2, d=q % 2),
             owner & (f != q),
         )
         pl.when(owner & (f == q))(lambda: keep.start())
-        yield
+    yield start + 60
     for s in range(4):
-        net.recv(lambda s=s: at_out.at[s], x_sems.at[2, s], ~(owner & (p.a == s)))
+        net.recv(lambda s=s: at_out.at[s], x_sems.at[1, s], ~(owner & (p.a == s)))
     pl.when(owner)(lambda: keep.wait())
 
 
@@ -655,7 +595,7 @@
     )[0]
 
 
-def feed_forward(ns, gf, own, oth, units, members):
+def feed_forward(ns, gf, own, oth, order, units, members):
     tokens, dim = ns.shape
     rows, wide = own[0].shape[1:]
     lanes = 256
@@ -667,10 +607,10 @@
         out_ref, gs_ref, gown_ref, goth_ref = refs[len(own) + len(oth) :][:4]
         wgu_ref, wd_ref, hidden_ref, ggu_ref = refs[-4:]
         g = g_ref[0]
-        for i in range(16):
+        for place, i in enumerate(order):
             cut = pl.ds(pl.multiple_of((g ^ i) * rows, rows), rows)
             for half, side in enumerate((own_refs, oth_refs)):
-                a, k = places[half][i]
+                a, k = places[half][place]
                 block = side[a][k]
                 pad = jnp.zeros((rows, lanes - units), BF)
                 for k in range(3):
@@ -751,162 +691,296 @@
     )
 
 
-def gather_latent(number, pair_block, query_block, column_blocks, n_ctx):
-    def body(pair_ref, query_ref, col_ref, pair, pairs, queries, cols, col_sems, sems):
-        place = Place(n_ctx)
-        p = place
+def project(number, x, down, gains, cosine, sine_table, ff, heads_in, n_ctx):
+    rows, dim = x.shape
+    wide = down.shape[1]
+    qr = wide - KVR - 128
+    cols = dim // 16
+
+    def body(
+        x_ref, down_ref, g1_ref, gq_ref, gl_ref, cos_ref, sin_ref, ff_ref, heads_ref,
+        both, pair, pairs, queries, columns, mid, heads,
+        normed, column_blocks, pair_block, query_block,
+        col_sems, ff_sems, x_sems, tp_sems, sems,
+    ):
+        p = Place(n_ctx)
         greet(p, everyone=16, other=True)
         net = Net(p, sems)
-
-        def columns():
-            keep = pltpu.make_async_copy(col_ref.at[p.g], cols.at[p.g], net.sem())
+        owner = p.d == p.t
+        place = lambda q, side: (q // 2 * 2 + (1 - p.b if side else p.b)) * 2 + q % 2
+        keep_heads = [net.sem() for _ in range(8)]
+
+        def keep_head(q):
+            return pltpu.make_async_copy(heads_ref.at[q], heads.at[place(q, 0)], keep_heads[q])
+
+        def send_head(q, sems_of, to):
+            net.send(
+                lambda: heads_ref.at[q], lambda: heads.at[place(q, 0)], sems_of.at[q], to, owner
+            )
+
+        for q in range(8):
+            send_head(q, x_sems, p.across)
+
+        def spread_heads():
+            yield 9.5
+            for q in range(8):
+                pl.when(owner)(lambda: keep_head(q).start())
+                send_head(q, tp_sems.at[0], p.other)
+            for q in range(8):
+                yield 16.0 + 2 * q
+                theirs = lambda q=q: heads.at[place(q, 1)]
+                net.recv(theirs, x_sems.at[q], owner)
+                net.send(theirs, theirs, tp_sems.at[1, q], p.other, owner)
+            yield 60.0
+            for q in range(8):
+                for side in (0, 1):
+                    net.recv(lambda: heads.at[place(q, side)], tp_sems.at[side, q], ~owner)
+                pl.when(owner)(lambda: keep_head(q).wait())
+
+        out = lambda i: mid.at[TRADED_NEXT.index(i)]
+        run_together(trade_sends(net, lambda i: ff_ref.at[i], out, ff_sems, ((10, 0), (6, 0))))
+        values = x_ref[...]
+        normed[...] = (values * norm_factor(values) * g1_ref[...]).astype(BF)
+        both[...] = matmul(normed[...], down_ref[...])
+        query, latent = both[:, :qr], both[:, qr : qr + KVR]
+        query_block[...] = (query * norm_factor(query) * gq_ref[...]).astype(BF)
+        pair_block[:, :KVR] = (latent * norm_factor(latent) * gl_ref[...]).astype(BF)
+        pair_block[:, KVR:] = turn(both[:, qr + KVR :], cos_ref[...], sin_ref[...]).astype(BF)
+
+        def send_columns():
+            for n in range(16):
+                column_blocks[n] = normed[:, n * cols : (n + 1) * cols]
+            keep = pltpu.make_async_copy(column_blocks.at[p.g], columns.at[p.g], net.sem())
             keep.start()
             for k in range(1, 16):
+                if k % 4 == 1:
+                    yield 13.0 + k
                 net.send(
-                    lambda k=k: col_ref.at[p.g ^ k],
-                    lambda: cols.at[p.g],
+                    lambda k=k: column_blocks.at[p.g ^ k],
+                    lambda: columns.at[p.g],
                     col_sems.at[k],
                     lambda k=k: ((p.g ^ k) * p.members + p.m, p.t),
                 )
-            yield
-            yield
-            yield
+            yield 50.0
             for k in range(1, 16):
-                net.recv(lambda k=k: cols.at[p.g ^ k], col_sems.at[k])
+                net.recv(lambda k=k: columns.at[p.g ^ k], col_sems.at[k])
             keep.wait()
 
         def latents():
             sem = net.sem()
-            keep = pltpu.make_async_copy(pair_ref, pair.at[p.t], net.sem())
+            keep = pltpu.make_async_copy(pair_block, pair.at[p.t], net.sem())
             keep.start()
-            net.send(lambda: pair_ref, lambda: pair.at[p.t], sem, p.other)
-            yield
+            net.send(lambda: pair_block, lambda: pair.at[p.t], sem, p.other)
+            yield 11.0
             net.recv(lambda: pair.at[1 - p.t], sem)
             keep.wait()
-            yield from gather_steps(net, pair, pairs, 16)
-
-        run_together(latents(), gather_steps(net, query_ref, queries, 8), columns())
+            yield from gather_steps(net, pair, pairs, 16, 12, 2.2)
+
+        run_together(
+            latents(),
+            gather_steps(net, query_block, queries, 8, 9, 2.2),
+            after(9.0, send_columns()),
+            spread_heads(),
+            trade_sends(net, lambda i: ff_ref.at[i], out, ff_sems, ((7, 20), (11, 22))),
+        )
+        trade_receives(net, out, ff_sems, TRADED_NEXT)
         net.finish()
 
-    pair_shape = (2,) + pair_block.shape
     return comm_call(
-        "gather_latent",
+        "project",
         number,
         body,
-        [pair_block, query_block, column_blocks],
-        [ANY] * 3,
+        [x, down, *gains, cosine, sine_table, ff, heads_in],
+        [VMEM] * 7 + [ANY] * 2,
         [
-            shape(pair_shape),
-            shape((16,) + pair_shape),
-            shape((8,) + query_block.shape),
-            shape(column_blocks.shape),
+            shape((rows, wide), F32),
+            shape((2, rows, KVR + 128)),
+            shape((16, 2, rows, KVR + 128)),
+            shape((8, rows, qr)),
+            shape((16, rows, cols)),
+            shape((len(TRADED_NEXT),) + ff.shape[1:]),
+            shape((16,) + heads_in.shape[1:]),
         ],
-        [ANY] * 4,
-        [pltpu.SemaphoreType.DMA((16,))],
-        180,
-    )[1:]
-
-
-def reduce_latent(number, pairs, queries, at, n_ctx):
+        [VMEM] + [ANY] * 6,
+        [
+            pltpu.VMEM((rows, dim), BF),
+            pltpu.VMEM((16, rows, cols), BF),
+            pltpu.VMEM((rows, KVR + 128), BF),
+            pltpu.VMEM((rows, qr), BF),
+            pltpu.SemaphoreType.DMA((16,)),
+            pltpu.SemaphoreType.DMA((16,)),
+            pltpu.SemaphoreType.DMA((8,)),
+            pltpu.SemaphoreType.DMA((2, 8)),
+        ],
+        240,
+    )
+
+
+def norm_back_rows(values, gain, upstream):
+    factor = norm_factor(values)
+    scaled = upstream * gain
+    inner = jnp.mean(scaled * values, axis=-1, keepdims=True)
+    share = upstream * values * factor
+    total = share[:8]
+    for i in range(1, share.shape[0] // 8):
+        total = total + share[8 * i : 8 * i + 8]
+    return factor * scaled - values * factor * factor * factor * inner, total
+
+
+def wind_up(
+    number, pairs, queries, at, both, x, grad_middle, down, gains, second, cosine, sine_table,
+    ff_own, ff_got, widths, n_ctx,
+):
+    rows, dim = x.shape
+    wide = down.shape[1]
+    qr = wide - KVR - 128
+    members = n_ctx // 16
+    unit_rows = ff_own.shape[1]
+    traded = TRADED_FIRST + TRADED_NEXT
+
     def body(
-        pairs_ref, queries_ref, at_ref, pair_out, query_out, at_out,
-        at_x, at_tp, x_sems, tp_in, *rest,
+        pairs_ref, queries_ref, at_ref, both_ref, x_ref, middle_ref, down_ref,
+        g1_ref, gq_ref, gl_ref, second_ref, cos_ref, sin_ref, own_ref, got_ref,
+        at_out, ff_out, both_all, input_half, input_other, gains_out,
+        ff_sum, at_x, at_tp, tp_in, pair_sum, query_sum, grad_both, gain_blocks, gain_tp,
+        *rest,
     ):
-        place = Place(n_ctx)
-        p = place
+        p = Place(n_ctx)
         greet(p, everyone=16, other=True)
         rest = list(rest)
         net = Net(p, rest.pop())
-        rows = pair_out.shape[0]
+        tp_sems, x_sems, ff_sems, pair_sems = [rest.pop() for _ in range(4)]
 
         def latents():
-            sems = [net.sem() for _ in range(16)]
             for g in range(16):
                 net.send(
-                    lambda g=g: pairs_ref.at[g, 1 - p.t], lambda g=g: tp_in.at[g], sems[g], p.other
+                    lambda g=g: pairs_ref.at[g, 1 - p.t],
+                    lambda g=g: tp_in.at[g],
+                    pair_sems.at[g],
+                    p.other,
                 )
-            yield
             for g in range(16):
-                net.recv(lambda g=g: tp_in.at[g], sems[g])
+                yield 3.0 + 1.1 * (g + 1)
+                net.recv(lambda g=g: tp_in.at[g], pair_sems.at[g])
                 add_into(tp_in.at[g], [tp_in.at[g], pairs_ref.at[g, p.t]], rows)
-            yield from reduce_steps(net, tp_in, pair_out, *rest[:4], rows, 16)
+            yield from reduce_steps(net, tp_in, pair_sum, *rest[:4], rows, 16, 21, 1.1)
+
+        def trades():
+            timed = (
+                ((8, 1), (2, 2), (4, 3), (3, 6), (9, 10), (5, 12), (12, 19), (6, 22), (1, 23))
+                + ((7, 26), (10, 28), (11, 37))
+            )
+            for i, when_to in timed:
+                yield when_to
+                add_into(ff_sum.at[i], [got_ref.at[i], own_ref.at[i]], unit_rows)
+                yield from trade_sends(
+                    net, lambda i: ff_sum.at[i], lambda i: ff_out.at[i], ff_sems, ((i, when_to),)
+                )
+            add_into(ff_sum.at[0], [got_ref.at[0], own_ref.at[0]], unit_rows)
+            keep = pltpu.make_async_copy(ff_sum.at[0], ff_out.at[0], net.sem())
+            keep.start()
+            yield 95.0
+            trade_receives(net, lambda i: ff_out.at[i], ff_sems, traded)
+            keep.wait()
+
+        def gain_sums():
+            sem = net.sem()
+            net.send(lambda: gain_blocks, lambda: gain_tp, sem, p.other)
+            yield 52.0
+            net.recv(lambda: gain_tp, sem)
+            pl.loop(0, 16)(lambda g: add_into(gain_tp.at[g], [gain_tp.at[g], gain_blocks.at[g]], 16))
+            yield from reduce_steps(net, gain_tp, gains_out, *rest[7:11], 16, 16, 53, 2)
+
+        def chain():
+            yield from together(
+                latents(),
+                reduce_steps(net, queries_ref, query_sum, None, *rest[4:7], rows, 8, 0, 2.2),
+            )
+            query_back, query_share = norm_back_rows(
+                both_ref[:, :qr], gq_ref[...], query_sum[...]
+            )
+            grad_both[:, :qr] = query_back.astype(BF)
+            latent_back, latent_share = norm_back_rows(
+                both_ref[:, qr : qr + KVR], gl_ref[...], pair_sum[:, :KVR]
+            )
+            grad_both[:, qr : qr + KVR] = latent_back.astype(BF)
+            grad_both[:, qr + KVR :] = turn(
+                pair_sum[:, KVR:], cos_ref[...], sin_ref[...], True
+            ).astype(BF)
+
+            gather = gather_steps(net, grad_both, both_all, 16, 38, 3.3)
+            next(gather)
+            input_back, input_share = norm_back_rows(
+                x_ref[...], g1_ref[...], matmul_nt(grad_both[...], down_ref[...])
+            )
+            input_half[...] = (middle_ref[...] + input_back).astype(BF)
+            swap = swap_steps(net, input_half, input_other)
+            next(swap)
+            shares = [
+                jnp.sum(share, axis=0, keepdims=True)
+                for share in (input_share, query_share, latent_share, second_ref[...])
+            ]
+            for n in range(16):
+                parts = []
+                for m in range(members):
+                    for share, w in zip(shares, widths):
+                        at_lane = (n * members + m) * w
+                        parts.append(share[:, at_lane : at_lane + w])
+                row = jnp.concatenate(parts, axis=1)
+                gain_blocks[n] = jnp.broadcast_to(row, gain_blocks.shape[1:]).astype(BF)
+            yield from together(gather, gain_sums(), swap)
 
         run_together(
-            latents(),
-            reduce_steps(net, queries_ref, query_out, None, *rest[4:7], query_out.shape[0], 8),
-            head_grads_steps(net, at_ref, at_out, at_x, at_tp, x_sems, at.shape[1]),
+            chain(),
+            after(
+                0.5,
+                head_grads_steps(
+                    net, at_ref, at_out, at_x, at_tp, x_sems, tp_sems, at.shape[1], 17
+                ),
+            ),
+            trades(),
         )
         net.finish()
 
-    rows, cols = pairs.shape[2:]
+    lanes = pairs.shape[3]
+    gain_lanes = members * sum(widths)
     scratch = [
+        pltpu.VMEM((13,) + ff_own.shape[1:], BF),
         pltpu.VMEM((8,) + at.shape[1:], BF),
-        pltpu.VMEM((8,) + at.shape[1:], BF),
-        pltpu.SemaphoreType.DMA((3, 8)),
-        pltpu.VMEM((16, rows, cols), BF),
+        pltpu.VMEM((2, 8) + at.shape[1:], BF),
+        pltpu.VMEM((16, rows, lanes), BF),
+        pltpu.VMEM((rows, lanes), F32),
+        pltpu.VMEM((rows, qr), F32),
+        pltpu.VMEM((rows, wide), BF),
+        pltpu.VMEM((16, 16, gain_lanes), BF),
+        pltpu.VMEM((16, 16, gain_lanes), BF),
     ]
-    scratch += reduce_scratch(rows, cols, 16)
-    scratch += reduce_scratch(queries.shape[1], queries.shape[2], 8)
+    scratch += reduce_scratch(rows, lanes, 16) + reduce_scratch(rows, qr, 8)
+    scratch += reduce_scratch(16, gain_lanes, 16)
+    scratch += [
+        pltpu.SemaphoreType.DMA((16,)),
+        pltpu.SemaphoreType.DMA((16,)),
+        pltpu.SemaphoreType.DMA((2, 8)),
+        pltpu.SemaphoreType.DMA((2, 8)),
+    ]
     return comm_call(
-        "reduce_latent",
+        "wind_up",
         number,
         body,
-        [pairs, queries, at],
-        [VMEM] * 3,
-        [shape((rows, cols), F32), shape(queries.shape[1:], F32), shape((4,) + at.shape[1:])],
-        [VMEM] * 2 + [ANY],
+        [pairs, queries, at, both, x, grad_middle, down, *gains, second, cosine, sine_table]
+        + [ff_own, ff_got],
+        [VMEM] * 15,
+        [
+            shape((4,) + at.shape[1:]),
+            shape((13,) + ff_own.shape[1:]),
+            shape((16, rows, wide)),
+            shape((rows, dim)),
+            shape((rows, dim)),
+            shape((16, gain_lanes), F32),
+        ],
+        [ANY, ANY, ANY, VMEM, ANY, VMEM],
         scratch,
-        220,
-    )
-
-
-def finish_blocks(number, block, swaps, gain_blocks, ff, n_ctx):
-    k = len(swaps)
-
-    def body(*refs):
-        ff_ref, block_ref, ins, gains = refs[0], refs[1], refs[2 : k + 2], refs[k + 2]
-        ff_out, blocks, outs = refs[k + 3], refs[k + 4], refs[k + 5 : 2 * k + 5]
-        gains_out = refs[2 * k + 5]
-        rest = list(refs[2 * k + 6 :])
-        ff_sems = rest.pop(0)
-        net_sems = rest.pop()
-        tp_in = rest.pop(0)
-        place = Place(n_ctx)
-        greet(place, everyone=16, other=True)
-        net = Net(place, net_sems)
-
-        def sums():
-            sem = net.sem()
-            net.send(lambda: gains, lambda: tp_in, sem, place.other)
-            yield
-            net.recv(lambda: tp_in, sem)
-            pl.loop(0, 16)(
-                lambda g: add_into(tp_in.at[g], [tp_in.at[g], gains.at[g]], gains.shape[1])
-            )
-            yield from reduce_steps(net, tp_in, gains_out, *rest, gains_out.shape[0], 16)
-
-        run_together(
-            gather_steps(net, block_ref, blocks, 16),
-            sums(),
-            *[swap_steps(net, i, o) for i, o in zip(ins, outs)],
-            trade_steps(net, ff_ref, ff_out, ff_sems),
-        )
-        net.finish()
-
-    scratch = [pltpu.SemaphoreType.DMA((2, 8)), pltpu.VMEM(gain_blocks.shape, BF)]
-    scratch += reduce_scratch(gain_blocks.shape[1], gain_blocks.shape[2], 16)
-    return comm_call(
-        "finish_blocks",
-        number,
-        body,
-        [ff, block] + list(swaps) + [gain_blocks],
-        [ANY] * (k + 2) + [VMEM],
-        [shape(ff.shape), shape((16,) + block.shape)]
-        + [shape(s.shape, s.dtype) for s in swaps]
-        + [shape(gain_blocks.shape[1:], F32)],
-        [ANY] * (k + 2) + [VMEM],
-        scratch,
-        180,
+        260,
     )
 
 
@@ -929,7 +1003,7 @@
 
         def second():
             yield from reduce_steps(
-                net, parts_ref, branch, None, near, line_in, line_out, rows, 8
+                net, parts_ref, branch, None, near, line_in, line_out, rows, 8, 0, 7
             )
 
             def norm(r):
@@ -938,9 +1012,9 @@
                 normed[r] = (values * norm_factor(values) * gain_ref[...]).astype(BF)
 
             by_rows(rows, 16, norm)
-            yield from gather_steps(net, normed, norms, 16)
-
-        run_together(second(), gather_steps(net, gf_ref, gfs, 16))
+            yield from gather_steps(net, normed, norms, 16, 32, 7)
+
+        run_together(second(), after(0.5, gather_steps(net, gf_ref, gfs, 16, 0, 11)))
         net.finish()
 
     return comm_call(
@@ -957,61 +1031,80 @@
     )
 
 
-def norm_and_branch_back(number, parts, middle, out_grad, gain, n_ctx):
+def norm_and_branch_back(number, parts, ffn_parts, middle, out_grad, gain, n_ctx):
     rows, dim = middle.shape
-    parts = parts.reshape(16, rows, dim)
+    parts, ffn_parts = parts.reshape(16, rows, dim), ffn_parts.reshape(16, rows, dim)
 
     def body(
-        parts_ref, middle_ref, out_grad_ref, gain_ref,
-        grad_middle, gain_part, branches,
-        upstream, branch, near_core, near, line_in, line_out, sems,
+        parts_ref, ffn_ref, middle_ref, out_grad_ref, gain_ref,
+        grad_middle, gain_part, branches, output,
+        upstream, branch, ffn_sum, *rest,
     ):
         place = Place(n_ctx)
         greet(place, line=True, across=True, core=True)
-        net = Net(place, sems)
+        net = Net(place, rest[-1])
+
+        def chain():
+            yield from reduce_steps(net, parts_ref, upstream, *rest[:4], rows, 16, 0, 7)
+            gain_part[...] = jnp.zeros((8, dim), F32)
+
+            def back(r):
+                grads, share = norm_back_rows(middle_ref[r], gain_ref[...], upstream[r])
+                total = out_grad_ref[r] + grads
+                grad_middle[r] = total
+                branch[r] = (residual_scale * total).astype(BF)
+                gain_part[...] += share
+
+            by_rows(rows, 16, back)
+            yield from gather_steps(net, branch, branches, 8, 38, 7)
+
         run_together(
-            reduce_steps(
-                net, parts_ref, upstream, near_core, near, line_in, line_out, rows, 16
-            )
+            chain(), after(0.5, reduce_steps(net, ffn_ref, ffn_sum, *rest[4:8], rows, 16, 28, 7))
         )
-        gain_part[...] = jnp.zeros((8, dim), F32)
-
-        def back(r):
-            values, grads = middle_ref[r], upstream[r]
-            factor = norm_factor(values)
-            scaled = grads * gain_ref[...]
-            inner = jnp.mean(scaled * values, axis=-1, keepdims=True)
-            total = out_grad_ref[r] + (
-                factor * scaled - values * factor * factor * factor * inner
-            )
-            grad_middle[r] = total
-            branch[r] = (residual_scale * total).astype(BF)
-            share = grads * values * factor
-            gain_part[...] += share[:8] + share[8:]
-
-        by_rows(rows, 16, back)
-        run_together(gather_steps(net, branch, branches, 8))
+        output[...] = (middle_ref[...] + residual_scale * ffn_sum[...]).astype(BF)
         net.finish()
 
     return comm_call(
         "norm_and_branch_back",
         number,
         body,
-        [parts, middle, out_grad, gain],
-        [VMEM] * 4,
-        [shape((rows, dim), F32), shape((8, dim), F32), shape((8, rows, dim))],
-        [VMEM, VMEM, ANY],
-        [pltpu.VMEM((rows, dim), F32), pltpu.VMEM((rows, dim), BF)]
-        + reduce_scratch(rows, dim, 16),
-        180,
-    )
-
-
-def turn(values, table, back=False):
-    near = pltpu.roll(values, 16, 1) * table[:, 256:384]
-    far = pltpu.roll(values, 112, 1) * table[:, 128:256]
-    turned = near + far
-    return values * table[:, :128] + (-turned if back else turned)
+        [parts, ffn_parts, middle, out_grad, gain],
+        [VMEM] * 5,
+        [
+            shape((rows, dim), F32),
+            shape((8, dim), F32),
+            shape((8, rows, dim)),
+            shape((rows, dim)),
+        ],
+        [VMEM, VMEM, ANY, VMEM],
+        [
+            pltpu.VMEM((rows, dim), F32),
+            pltpu.VMEM((rows, dim), BF),
+            pltpu.VMEM((rows, dim), F32),
+        ]
+        + reduce_scratch(rows, dim, 16) * 2,
+        240,
+    )
+
+
+def turn(values, cosine, sine_table, back=False):
+    lane = lax.broadcasted_iota(jnp.int32, values.shape, 1)
+    near = jnp.where((lane >= 80) & (lane < 96), pltpu.roll(values, 16, 1), 0.0)
+    far = jnp.where((lane >= 64) & (lane < 80), pltpu.roll(values, 112, 1), 0.0)
+    turned = (near - far) * sine_table
+    kept = values * jnp.where(lane < 64, 1.0, jnp.where(lane < 96, cosine, 0.0))
+    return kept - turned if back else kept + turned
+
+
+def unpack_heads(at_ref, q_up_ref, l_up_ref, w_ref, q_rows, l_rows):
+    o_rows, width = w_ref.shape[0] // 32, w_ref.shape[1]
+    first = q_rows + l_rows
+    for n in range(16):
+        q_up_ref[n * q_rows : (n + 1) * q_rows] = at_ref[n, :q_rows]
+        l_up_ref[n * l_rows : (n + 1) * l_rows] = at_ref[n, q_rows:first]
+        for half in (0, 1):
+            row = (2 * n + half) * o_rows
+            w_ref[row : row + o_rows] = at_ref[n, first:, half * width : (half + 1) * width]
 
 
 def by_rows(rows, step, body):
@@ -1027,17 +1120,19 @@
     return jnp.where(lane < NOPE, expanded, ropes)
 
 
-def attend(number, qn, q_up, pairs, l_up, w_out_t, table, q_pos, ff, n_ctx):
-    rows, keys, heads = qn.shape[0], pairs.shape[0], q_up.shape[1] // 128
+def attend(number, qn, at, pairs, cosine, sine_table, q_pos, ff, width, n_ctx):
+    rows, keys, heads = qn.shape[0], pairs.shape[0], at.shape[2] // 128
     span, block = keys // 4, rows // 4
-    dim = w_out_t.shape[0]
+    q_rows, l_rows = qn.shape[1] // 16, KVR // 16
+    dim = (at.shape[1] - q_rows - l_rows) * 32
 
     def body(
-        qn_ref, q_up_ref, pairs_ref, l_up_ref, w_ref, table_ref, pos_ref, ff_ref,
-        branch_ref, q_ref, o_ref, lse_ref, att_ref, far_ref,
+        qn_ref, at_ref, pairs_ref, cos_ref, sin_ref, pos_ref, ff_ref,
+        branch_ref, q_ref, o_ref, lse_ref, att_ref, q_up_ref, l_up_ref, w_ref, far_ref,
         e_ref, top_ref, sum_ref, acc_ref, sems,
     ):
-        copies = trade_away(Place(n_ctx), ff_ref, far_ref, sems, 12)
+        copies = trade_away(Place(n_ctx), ff_ref.at[pl.ds(13, 3)], far_ref, sems)
+        unpack_heads(at_ref, q_up_ref, l_up_ref, w_ref, q_rows, l_rows)
         by_rows(
             keys,
             256,
@@ -1049,7 +1144,7 @@
         def head(h):
             lanes = lanes_of(h)
             raw = matmul(qn_ref[...], q_up_ref[:, lanes])
-            q_ref[:, lanes] = turn(raw, table_ref[...]).astype(BF)
+            q_ref[:, lanes] = turn(raw, cos_ref[...], sin_ref[...]).astype(BF)
             top_ref[...] = jnp.full(top_ref.shape, -1e30, F32)
             sum_ref[...] = jnp.zeros(sum_ref.shape, F32)
             acc_ref[...] = jnp.zeros(acc_ref.shape, F32)
@@ -1092,13 +1187,16 @@
             shape((rows, wide), F32),
             shape((rows, wide), F32),
             shape((rows, heads * VH)),
-            shape(ff.shape),
+            shape((qn.shape[1], wide)),
+            shape((KVR, wide)),
+            shape((dim, width)),
+            shape((3,) + ff.shape[1:]),
         ],
-        in_specs=[VMEM] * 7 + [ANY],
-        out_specs=[VMEM] * 5 + [ANY],
+        in_specs=[VMEM] * 6 + [ANY],
+        out_specs=[VMEM] * 8 + [ANY],
         scratch_shapes=[pltpu.VMEM((keys, wide), BF)]
         + [pltpu.VMEM((rows, 128), F32)] * 3
-        + [pltpu.SemaphoreType.DMA((2, ff.shape[0]))],
+        + [pltpu.SemaphoreType.DMA((2, 3))],
         compiler_params=pltpu.CompilerParams(
             collective_id=number, has_side_effects=True, vmem_limit_bytes=60 << 20
         ),
@@ -1106,23 +1204,37 @@
             flops=20_000_000_000, bytes_accessed=20 << 20, transcendentals=0
         ),
         name="attend",
-    )(qn, q_up, pairs, l_up, w_out_t, table, q_pos, ff)
+    )(qn, at, pairs, cosine, sine_table, q_pos, ff)
 
 
 def attend_back(
-    number, gb, qn, q_up, pairs, l_up, w_out_t, table, q_pos, q, o, lse, att, ff, n_ctx
+    number, gb, qn, q_up, pairs, l_up, w_out_t, cosine, sine_table, q_pos, q, o, lse, att,
+    ff_own, ff_got, n_ctx,
 ):
     rows, keys, heads = qn.shape[0], pairs.shape[0], q_up.shape[1] // 128
     span, block = keys // 4, rows // 4
     dim, wide = gb.shape[1], heads * 128
+    q_rows, l_rows, o_rows, width = qn.shape[1] // 16, KVR // 16, dim // 32, att.shape[1]
+    first = q_rows + l_rows
+    unit_rows = ff_own.shape[1]
 
     def body(
-        gb_ref, qn_ref, q_up_ref, pairs_ref, l_up_ref, w_ref, table_ref, pos_ref,
-        q_ref, o_ref, lse_ref, att_ref, ff_ref,
-        gp_ref, gqn_ref, gq_up_ref, gl_up_ref, gw_ref, far_ref,
-        e_ref, rope_ref, go_ref, gq_ref, dq_ref, inner_ref, sems,
+        gb_ref, qn_ref, q_up_ref, pairs_ref, l_up_ref, w_ref, cos_ref, sin_ref, pos_ref,
+        q_ref, o_ref, lse_ref, att_ref, own_ref, got_ref,
+        gp_ref, gqn_ref, at_ref, far_ref,
+        e_ref, rope_ref, go_ref, gq_ref, dq_ref, inner_ref, mine_ref, theirs_ref, sems, load_sems,
     ):
-        copies = trade_away(Place(n_ctx), ff_ref, far_ref, sems, 12)
+        loads = [
+            pltpu.make_async_copy(part.at[pl.ds(13, 3)], hold, load_sems.at[i])
+            for i, (part, hold) in enumerate(((own_ref, mine_ref), (got_ref, theirs_ref)))
+        ]
+        for load in loads:
+            load.start()
+        for load in loads:
+            load.wait()
+        for k in range(3):
+            add_into(mine_ref.at[k], [mine_ref.at[k], theirs_ref.at[k]], unit_rows)
+        copies = trade_away(Place(n_ctx), mine_ref, far_ref, sems)
 
         def expand(r):
             e_ref[r] = matmul(pairs_ref[r, :KVR], l_up_ref[...]).astype(BF)
@@ -1133,9 +1245,13 @@
         for h in range(heads):
             go_ref[:, h * 128 : h * 128 + NOPE] = jnp.zeros((rows, NOPE), BF)
             go_ref[:, h * 128 + NOPE : (h + 1) * 128] = ga[:, h * VH : (h + 1) * VH]
-        for i in range(dim // 512):
-            cut = slice(i * 512, (i + 1) * 512)
-            gw_ref[cut] = matmul_tn(gb_ref[:, cut], att_ref[...]).astype(BF)
+        for i in range(4):
+            part = matmul_tn(gb_ref[:, i * dim // 4 : (i + 1) * dim // 4], att_ref[...]).astype(BF)
+            for k in range(8):
+                half = k % 2
+                at_ref[4 * i + k // 2, first:, half * width : (half + 1) * width] = part[
+                    k * o_rows : (k + 1) * o_rows
+                ]
 
         def head(h):
             lanes = lanes_of(h)
@@ -1164,7 +1280,9 @@
                 lane = lax.broadcasted_iota(jnp.int32, grad_key.shape, 1)
                 e_ref[cols, lanes] = jnp.where(lane < NOPE, grad_key, grad_value).astype(BF)
                 rope_ref[cols] += jnp.where(lane < NOPE, 0.0, grad_key)
-            gq_ref[:, lanes] = turn(dq_ref[...] * score_scale, table_ref[...], True).astype(BF)
+            gq_ref[:, lanes] = turn(
+                dq_ref[...] * score_scale, cos_ref[...], sin_ref[...], True
+            ).astype(BF)
 
         pl.loop(0, heads)(head)
 
@@ -1173,8 +1291,11 @@
             gp_ref[r, KVR:] = rope_ref[r].astype(BF)
 
         by_rows(keys, 256, latents)
-        gl_up_ref[...] = matmul_tn(pairs_ref[:, :KVR], e_ref[...]).astype(BF)
-        gq_up_ref[...] = matmul_tn(qn_ref[...], gq_ref[...]).astype(BF)
+        gl_up = matmul_tn(pairs_ref[:, :KVR], e_ref[...]).astype(BF)
+        gq_up = matmul_tn(qn_ref[...], gq_ref[...]).astype(BF)
+        for n in range(16):
+            at_ref[n, :q_rows] = gq_up[n * q_rows : (n + 1) * q_rows]
+            at_ref[n, q_rows:first] = gl_up[n * l_rows : (n + 1) * l_rows]
         gqn_ref[...] = matmul_nt(gq_ref[...], q_up_ref[...]).astype(BF)
         for copy in copies:
             copy.wait()
@@ -1184,13 +1305,11 @@
         out_shape=[
             shape(pairs.shape),
             shape(qn.shape),
-            shape(q_up.shape),
-            shape(l_up.shape),
-            shape(w_out_t.shape),
-            shape(ff.shape),
+            shape((16, first + o_rows, wide)),
+            shape((3,) + ff_own.shape[1:]),
         ],
-        in_specs=[VMEM] * 12 + [ANY],
-        out_specs=[VMEM] * 5 + [ANY],
+        in_specs=[VMEM] * 13 + [ANY] * 2,
+        out_specs=[VMEM] * 3 + [ANY],
         scratch_shapes=[
             pltpu.VMEM((keys, wide), BF),
             pltpu.VMEM((keys, 128), F32),
@@ -1198,7 +1317,10 @@
             pltpu.VMEM((rows, wide), BF),
             pltpu.VMEM((rows, 128), F32),
             pltpu.VMEM((rows, 128), F32),
-            pltpu.SemaphoreType.DMA((2, ff.shape[0])),
+            pltpu.VMEM((3,) + ff_own.shape[1:], BF),
+            pltpu.VMEM((3,) + ff_own.shape[1:], BF),
+            pltpu.SemaphoreType.DMA((2, 3)),
+            pltpu.SemaphoreType.DMA((2,)),
         ],
         compiler_params=pltpu.CompilerParams(
             collective_id=number, has_side_effects=True, vmem_limit_bytes=60 << 20
@@ -1207,7 +1329,7 @@
             flops=40_000_000_000, bytes_accessed=30 << 20, transcendentals=0
         ),
         name="attend_back",
-    )(gb, qn, q_up, pairs, l_up, w_out_t, table, q_pos, q, o, lse, att, ff)
+    )(gb, qn, q_up, pairs, l_up, w_out_t, cosine, sine_table, q_pos, q, o, lse, att, ff_own, ff_got)
 
 
 def shards(
@@ -1241,7 +1363,6 @@
     qr = query_down.shape[1]
     heads = H // 8
     units = gate_weight.shape[1] // 16
-    plane_lists = [[k * members + m for k in range(16)] for m in range(members)]
     member_lists = [[k * members + m for m in range(members)] for k in range(16)]
 
     def widen(blocks):
@@ -1256,25 +1377,20 @@
             blocks.astype(F32), "ctx", scatter_dimension=1, axis_index_groups=member_lists
         ).astype(BF)
 
-    def gather_over(block):
-        return lax.all_gather(
-            block, "ctx", axis=0, tiled=True, axis_index_groups=plane_lists if members > 1 else None
-        )
-
-    def scatter_over(part):
-        return lax.psum_scatter(
-            part,
-            "ctx",
-            scatter_dimension=0,
-            tiled=True,
-            axis_index_groups=plane_lists if members > 1 else None,
-        )
-
     widths = [first_gain.shape[0], query_gain.shape[0], latent_gain.shape[0], second_gain.shape[0]]
     starts = [0, widths[0], widths[0] + widths[1], widths[0] + widths[1] + widths[2]]
     gains = jnp.concatenate([first_gain, query_gain, latent_gain, second_gain]).astype(F32)
     gains = jnp.broadcast_to(gains[None], (8, gains.shape[0]))
-    down_shard = jnp.concatenate([query_down, latent_down], axis=1)
+    down_shard = jnp.concatenate(
+        [
+            query_down,
+            latent_down[:, :KVR],
+            jnp.zeros((shard_rows, NOPE), BF),
+            latent_down[:, KVR:],
+            jnp.zeros((shard_rows, 128 - NOPE - ROPE), BF),
+        ],
+        axis=1,
+    )
 
     def trade(block, k):
         return lax.ppermute(
@@ -1306,161 +1422,116 @@
 
     x = lax.dynamic_slice_in_dim(layer_input, t * rows, rows, 0).astype(F32)
     out_grad_rows = lax.dynamic_slice_in_dim(out_grad, t * rows, rows, 0).astype(F32)
-    positions = c * ctx_rows + t * rows + jnp.arange(rows, dtype=jnp.int32)
-    cosine, sine_table = rope_tables(positions)
     grad_ffn = (residual_scale * out_grad_rows).astype(BF)
 
-    down_full, gains, at_all, own_near, oth_near = weights_in(
-        1, down_shard, gains, at, ff, n_ctx
-    )
+    def rope_tiles(positions):
+        lane = jnp.arange(128, dtype=jnp.int32) % (ROPE // 2)
+        frequency = rope_base ** (-lane.astype(F32) / (ROPE // 2))
+        angles = positions.astype(F32)[:, None] * frequency[None, :]
+        return jnp.cos(angles), jnp.sin(angles)
+
+    row = jnp.arange(rows, dtype=jnp.int32)
+    cosine, sine_table = rope_tiles(c * ctx_rows + t * rows + row)
+    block = jnp.arange(8, dtype=jnp.int32)
+    block_ctx = ((block // 2 * 2 + b) * 2 + block % 2) * members + member
+    q_positions = (block_ctx[:, None] * ctx_rows + t * rows + row[None, :]).reshape(-1)
+    q_cos, q_sin = rope_tiles(q_positions)
+    q_pos = jnp.broadcast_to(q_positions[:, None], (q_positions.shape[0], 128))
+
+    down_full, gains, at_mine, own_near = weights_in(1, down_shard, gains, at, ff, n_ctx)
     own_near, ff = lax.optimization_barrier((own_near, ff))
-    own_mid = [trade(ff[i : i + 1], i) for i in (8, 9, 10, 11)]
-    oth_next = swap_tp(own_near[4:])
     down_full = widen(down_full).reshape(dim, -1)
     gains = widen(gains[:, 0]).reshape(n_ctx, -1)
     gain_first, gain_query, gain_latent, gain_second = [
-        gains[:, s : s + w].reshape(-1) for s, w in zip(starts, widths)
+        gains[:, s : s + w].reshape(1, -1) for s, w in zip(starts, widths)
     ]
-    at_all = widen(at_all).reshape(n_ctx, -1, wide)
-    q_up = at_all[:, :q_rows_w].reshape(qr, wide)
-    l_up = at_all[:, q_rows_w : q_rows_w + l_rows_w].reshape(KVR, wide)
-    w_out_t = jnp.transpose(
-        at_all[:, q_rows_w + l_rows_w :].reshape(n_ctx, o_rows_w, 2, o_width), (0, 2, 1, 3)
-    ).reshape(dim, o_width)
-
-    normed = rms_norm(x, gain_first).astype(BF)
-    both = matmul(normed, down_full)
-    query_latent, compressed = both[:, :qr], both[:, qr:]
-    query_normed = rms_norm(query_latent, gain_query).astype(BF)
-    latent = rms_norm(compressed[:, :KVR], gain_latent).astype(BF)
-    key_rope = rotate(compressed[:, KVR:], cosine, sine_table).astype(BF)
-    pair_block = jnp.concatenate(
-        [latent, jnp.zeros((rows, NOPE), BF), key_rope, jnp.zeros((rows, ROPE), BF)], axis=1
-    )
-    normed_columns = jnp.transpose(
-        normed.reshape(rows, 16, dim // 16), (1, 0, 2)
-    )
-    pairs, qn_all, token_columns = gather_latent(
-        3, pair_block, query_normed, normed_columns, n_ctx
-    )
-    pairs, own_mid, ff = lax.optimization_barrier((pairs, own_mid, ff))
-    own_mid = jnp.concatenate(own_mid)
-    oth_mid = swap_tp(own_mid)
-    lat_rope = widen(pairs).reshape(-1, 384)
+    first_gains = (gain_first, gain_query, gain_latent)
+    both, _, pairs, qn_all, token_columns, own_mid, at_all = project(
+        3, x, down_full, first_gains, cosine, sine_table, ff, at_mine, n_ctx
+    )
+    own_near, own_mid = lax.optimization_barrier((own_near, own_mid))
+    oth_near, oth_mid = swap_tp(own_near), swap_tp(own_mid)
+    lat_rope = widen(pairs).reshape(-1, KVR + 128)
+    if members > 1:
+        at_all = widen(at_all).reshape(n_ctx, -1, wide)
+        out_tiles = at_all[:, q_rows_w + l_rows_w :].reshape(n_ctx, o_rows_w, 2, o_width)
+        out_tiles = jnp.transpose(out_tiles, (0, 2, 1, 3)).reshape(16, 2, dim // 32, o_width)
+        at_all = jnp.concatenate(
+            [
+                at_all[:, :q_rows_w].reshape(16, -1, wide),
+                at_all[:, q_rows_w : q_rows_w + l_rows_w].reshape(16, -1, wide),
+                jnp.transpose(out_tiles, (0, 2, 1, 3)).reshape(16, -1, wide),
+            ],
+            axis=1,
+        )
+    branch_part, queries, attended_wide, log_total, attended, q_up, l_up, w_out_t, own_far = attend(
+        5, qn_all.reshape(-1, qr), at_all, lat_rope, q_cos, q_sin, q_pos, ff, o_width, n_ctx
+    )
     qn_all = qn_all.reshape(-1, qr)
 
-    block = jnp.arange(8, dtype=jnp.int32)
-    block_ctx = ((block // 2 * 2 + b) * 2 + block % 2) * members + member
-    q_positions = (
-        block_ctx[:, None] * ctx_rows + t * rows + jnp.arange(rows, dtype=jnp.int32)[None, :]
-    ).reshape(-1)
-    q_cos, q_sin = rope_tables(q_positions)
-    none, half = jnp.zeros((q_positions.shape[0], NOPE), F32), jnp.zeros_like(q_cos)
-    table = jnp.concatenate(
-        [none + 1, q_cos, q_cos, half, half]
-        + [none, -q_sin, half, half, half]
-        + [none, half, q_sin, half, half],
-        axis=1,
-    )
-    q_pos = jnp.broadcast_to(q_positions[:, None], (q_positions.shape[0], 128))
-    branch_part, queries, attended_wide, log_total, attended, own_far = attend(
-        5, qn_all, q_up, lat_rope, l_up, w_out_t, table, q_pos, ff[12:], n_ctx
-    )
-
     middle, ns_all, gf_all = branch_and_norm(
-        4, branch_part, x, gain_second[None], grad_ffn, n_ctx
+        4, branch_part, x, gain_second, grad_ffn, n_ctx
     )
     ns_all, gf_all = ns_all.reshape(-1, dim), gf_all.reshape(-1, dim)
     oth_far = swap_tp(own_far)
     own = [own_near, own_mid, own_far]
-    oth = [oth_near, oth_next, oth_mid, oth_far]
+    oth = [oth_near, oth_mid, oth_far]
     ns_all, oth = lax.optimization_barrier((ns_all, oth))
     if members > 1:
         own, oth = [
             [widen(jnp.concatenate(w)).reshape(16, dim // 16, wide)] for w in (own, oth)
         ]
+    order = (0,) + TRADED_FIRST + TRADED_NEXT + TRADED_LAST
     ffn_part, second_part, grads_own, grads_oth = feed_forward(
-        ns_all, gf_all, own, oth, units, members
+        ns_all, gf_all, own, oth, order, units, members
     )
     grads_own = narrow(grads_own.reshape(16, members, shard_rows, wide))
     grads_oth = narrow(grads_oth.reshape(16, members, shard_rows, wide))
-    gots = [swap_tp(grads_oth[12:]), swap_tp(grads_oth[8:12]), swap_tp(grads_oth[:8])]
-    grad_middle, second_gain_part, gb_all = norm_and_branch_back(
-        6, second_part, middle, out_grad_rows, gain_second[None], n_ctx
-    )
-    second_gain_part = jnp.sum(second_gain_part, axis=0)
-    gb_all = gb_all.reshape(-1, dim)
-    gb_all, gots, ffn_part = lax.optimization_barrier((gb_all, gots, ffn_part))
-    back_far, back_mid, back_near = [
-        (mine.astype(F32) + got.astype(F32)).astype(BF)
-        for mine, got in zip((grads_own[12:], grads_own[8:12], grads_own[:8]), gots)
-    ]
-    ffn_sum = scatter_over(ffn_part).astype(F32)
-    out_half = (middle + residual_scale * ffn_sum).astype(BF)
-    grad_lat_rope, gqn_part, q_up_part, l_up_part, out_part, sums_far = attend_back(
-        7, gb_all, qn_all, q_up, lat_rope, l_up, w_out_t, table, q_pos,
-        queries, attended_wide, log_total, attended, back_far, n_ctx,
-    )
-
-    at_part = jnp.concatenate(
-        [
-            q_up_part.reshape(n_ctx, q_rows_w, wide),
-            l_up_part.reshape(n_ctx, l_rows_w, wide),
-            jnp.transpose(
-                out_part.reshape(n_ctx, 2, o_rows_w, o_width), (0, 2, 1, 3)
-            ).reshape(n_ctx, o_rows_w, wide),
-        ],
-        axis=1,
-    )
-    at_part = narrow(at_part.reshape(16, members, -1, wide))
-
-    own_lat_rope, grad_query_normed, at_sums = reduce_latent(
+    grads_got = swap_tp(grads_oth)
+    grad_middle, second_gain_part, gb_all, out_half = norm_and_branch_back(
+        6, second_part, ffn_part, middle, out_grad_rows, gain_second, n_ctx
+    )
+    gb_all, grads_got = lax.optimization_barrier((gb_all, grads_got))
+    out_other = swap_tp(out_half)
+    grad_pairs, gqn_part, at_part, sums_far = attend_back(
+        7, gb_all.reshape(-1, dim), qn_all, q_up, lat_rope, l_up, w_out_t, q_cos, q_sin, q_pos,
+        queries, attended_wide, log_total, attended, grads_own, grads_got, n_ctx,
+    )
+    if members > 1:
+        q_part = at_part[:, : qr // 16].reshape(n_ctx, q_rows_w, wide)
+        l_part = at_part[:, qr // 16 : (qr + KVR) // 16].reshape(n_ctx, l_rows_w, wide)
+        o_part = at_part[:, (qr + KVR) // 16 :].reshape(16, dim // 32, 2, o_width)
+        o_part = jnp.transpose(o_part, (0, 2, 1, 3)).reshape(n_ctx, 2, o_rows_w, o_width)
+        o_part = jnp.transpose(o_part, (0, 2, 1, 3)).reshape(n_ctx, o_rows_w, wide)
+        at_part = narrow(
+            jnp.concatenate([q_part, l_part, o_part], axis=1).reshape(16, members, -1, wide)
+        )
+    at_sums, sums, both_all, input_half, input_other, gain_sums = wind_up(
         8,
-        narrow(grad_lat_rope.reshape(16, members, 2, rows, 384)),
+        narrow(grad_pairs.reshape(16, members, 2, rows, KVR + 128)),
         gqn_part.reshape(8, rows, qr),
         at_part,
+        both,
+        x,
+        grad_middle,
+        down_full,
+        first_gains,
+        second_gain_part,
+        cosine,
+        sine_table,
+        grads_own,
+        grads_got,
+        widths,
         n_ctx,
     )
-    own_lat_rope, back_mid = lax.optimization_barrier((own_lat_rope, back_mid))
-    sums_mid = [trade(back_mid[i : i + 1], 8 + i) for i in range(4)]
-    grad_query_latent, query_gain_part = norm_back(query_latent, gain_query, grad_query_normed)
-    grad_latent_rows, latent_gain_part = norm_back(
-        compressed[:, :KVR], gain_latent, own_lat_rope[:, :KVR]
-    )
-    grad_both = jnp.concatenate(
-        [
-            grad_query_latent,
-            grad_latent_rows,
-            rotate(own_lat_rope[:, KVR + NOPE : KVR + NOPE + ROPE], cosine, -sine_table),
-        ],
-        axis=1,
+    both_all, out_other = lax.optimization_barrier((both_all, out_other))
+    down_part = matmul_tn(
+        token_columns.reshape(16 * rows, dim // 16), both_all.reshape(16 * rows, -1)
     ).astype(BF)
-    grad_normed = matmul_nt(grad_both, down_full)
-    grad_input_part, first_gain_part = norm_back(x, gain_first, grad_normed)
-    input_half = (grad_middle + grad_input_part).astype(BF)
-    gain_parts = jnp.concatenate(
-        [
-            p.reshape(n_ctx, -1)
-            for p in (first_gain_part, query_gain_part, latent_gain_part, second_gain_part)
-        ],
-        axis=1,
-    )
-    gain_parts = narrow(gain_parts.reshape(16, members, -1)).astype(BF)
-    gain_blocks = jnp.pad(gain_parts[:, None], ((0, 0), (0, 15), (0, 0)))
-    sums_near, both_all, out_other, input_other, gain_sums = finish_blocks(
-        9, grad_both, [out_half, input_half], gain_blocks, back_near, n_ctx
-    )
-    both_all, sums_mid = lax.optimization_barrier((both_all, sums_mid))
-    sums = [sums_near, *sums_mid, sums_far]
-    if members == 1:
-        down_part = matmul_tn(
-            token_columns.reshape(16 * rows, shard_rows), both_all.reshape(16 * rows, -1)
+    if members > 1:
+        down_part = lax.psum_scatter(
+            down_part.astype(F32), "ctx", axis_index_groups=member_lists, tiled=True
         ).astype(BF)
-    else:
-        down_part = lax.psum_scatter(
-            matmul_tn(normed, grad_both).astype(BF), "ctx", scatter_dimension=0, tiled=True
-        )
-
     down_other = swap_tp(down_part)
 
     def in_order(mine, other):
@@ -1472,11 +1543,15 @@
     input_grad = in_order(input_half, input_other).astype(F32)
     down_grads = down_part.astype(F32) + down_other.astype(F32)
     gain_grads = gain_sums[0]
+    if members > 1:
+        gain_grads = lax.psum_scatter(
+            gain_grads.reshape(members, -1), "ctx", axis_index_groups=member_lists
+        )
     first_gain_grad, query_gain_grad, latent_gain_grad, second_gain_grad = [
         gain_grads[s : s + w] for s, w in zip(starts, widths)
     ]
 
-    gate_weight_grad, up_weight_grad, down_grad_t = spread(sums, units, members)
+    gate_weight_grad, up_weight_grad, down_grad_t = spread([sums, sums_far], units, members)
     query_up_grad = jnp.transpose(
         at_sums[:, :q_rows_w].reshape(4, q_rows_w, heads, 128)[..., : NOPE + ROPE], (1, 0, 2, 3)
     ).reshape(q_rows_w, 4 * q_width)
@@ -1493,7 +1568,9 @@
         down_grads[:, :qr],
         query_gain_grad,
         query_up_grad.astype(F32),
-        down_grads[:, qr:],
+        jnp.concatenate(
+            [down_grads[:, qr : qr + KVR], down_grads[:, qr + KVR + NOPE : qr + KVR + NOPE + ROPE]], axis=1
+        ),
         latent_gain_grad,
         latent_up_grad.astype(F32),
         out_weight_grad.astype(F32),

time: 725 us -> 591 us (0.82)
  local copies, waits for them, and re-layouts: 67.5 us -> 24.3 us
  Pallas kernels: 572 us -> 537 us
  other arithmetic: 32.7 us -> 10.6 us
  between operations: 15.1 us -> 1.29 us
  starting transfers between devices: 16.3 us -> 5.66 us
  matrix products: 12 us -> 2.28 us
    pallas_call x6 -> x5, Pallas kernels: 458 us -> 418 us  [comm_call(): pl.pallas_call(body, out_shape=outs, in_specs=in_specs, out_specs=out_spe...]
    slice x13 -> x9, local copies, waits for them, and re-layouts: 16.1 us -> 0.32 us  [the longest x3 0.22 us: shards(): gains[:, s:s + w].reshape(1, -1)]
    reshape x6 -> x4, local copies, waits for them, and re-layouts: 18.3 us -> 2.68 us  [shards(): gains[:, s:s + w].reshape(1, -1)]
    ppermute x8 -> x0, starting transfers between devices: 13.1 us -> none  [trade(): lax.ppermute(block, 'ctx', [(i, (i // members ^ k) * members + i % member...]
    convert_element_type x8 -> x2, other arithmetic: 10.4 us -> 0.01 us  [rope_tiles(): angles = positions.astype(F32)[:, None] * frequency[None, :]]
    dot_general x2 -> x0, matrix products: 9.55 us -> none  [the longest x1 5.61 us: matmul_nt(): lax.dot_general(left_side, right_side, (((1,), (1,)), ((), ())), preferre...]
  transfers between devices with their start and end apart: 16 -> 6, of which waited for: 1 -> 0; matrix products, arithmetic and copies ran while one was open for 13% -> 2% of each run, Pallas kernels for 60% -> 59%
where the time goes in v5:
time: 591 us; the launch traced here: 581 us
  Pallas kernels  537 us (91%)
  local copies, waits for them, and re-layouts  24.3 us (4%)
  other arithmetic  10.6 us (2%)
    pallas_call x5, Pallas kernels, comm_call(): pl.pallas_call(body, out_shape=outs, in_specs=in_specs, out_specs=out_spe...  418 us
    pallas_call x3, Pallas kernels, plain_call(): pl.pallas_call(body, out_shape=outs, grid_spec=pltpu.PrefetchScalarGridSp...  50.8 us
    pallas_call x1, Pallas kernels, attend_back(): pl.pallas_call(body, out_shape=[shape(pairs.shape), shape(qn.shape), shap...  34.9 us
    pallas_call x1, Pallas kernels, attend(): pl.pallas_call(body, out_shape=[shape((rows, dim)), shape((rows, wide)),...  33.7 us
  transfers between devices with their start and end apart: 6, of which 0 were waited for; matrix products, arithmetic and copies ran while one was open for 2% of the time, Pallas kernels for 59%

profile of v5, /device:TPU:3, one launch (start us, length us, event | category | flops | bytes accessed | tf_op | source)
XLA Modules:
  0.0 581.5 jit_solution(11476742656645463487)
XLA Ops:
  1.6 1.3 reshape.206
  5.8 5.1 pack.1.ff_ref
  12.4 82.7 %weights_in.1 = (bf16[16,160,1152]{2,1,0:T(8,128)(2,1)}, f32[16,8,384]{2,1,0:T(8,128)}, bf16[8,144,640]{2,1,0:T(8,128)(2,1)}, bf16[9,160,640]{2,1,0:T(8,128)(2,1)}) custom-call(bf16[160,1152]{1,0:T(8,128)(2,1)} %concatenate.28.down_ref, f32[8,384]{1,0:T(8,128)} %broadcast_in_dim.10.gains_ref, bf16[4,144,640]{2,1,0:T(8,128)(2,1)} %pad_maximum_fusion.at_ref, ...), custom_call_target="tpu_custom_call" | custom-call | tf_op jit(solution)/shard_map/weights_in/pallas_call | solution.py:407
  99.1 1.2 dynamic-slice_convert_fusion
  100.3 67.4 %project.1 = (f32[64,1152]{1,0:T(8,128)}, bf16[2,64,384]{2,1,0:T(8,128)(2,1)}, bf16[16,2,64,384]{3,2,1,0:T(8,128)(2,1)}, bf16[8,64,768]{2,1,0:T(8,128)(2,1)}, bf...) custom-call(f32[64,2560]{1,0:T(8,128)} %get-tuple-element.133.x_ref, ...), custom_call_target="tpu_custom_call" | custom-call | tf_op jit(solution)/shard_map/project/pallas_call | solution.py:407
  167.7 1.4 collective-permute-start
  169.4 1.8 multiply_sine_fusion
  172.0 33.7 %attend.1 = (bf16[512,2560]{1,0:T(8,128)(2,1)}, bf16[512,640]{1,0:T(8,128)(2,1)}, f32[512,640]{1,0:T(8,128)}, f32[512,640]{1,0:T(8,128)}, bf16[512,320]{1,0:T(8,...) custom-call(bf16[512,768]{1,0:T(8,128)(2,1)} %bitcast.77, ...), custom_call_target="tpu_custom_call" | custom-call | flops 20000000000 | bytes 20971520 | tf_op jit(solution)/shard_map/attend/pallas_call | solution.py:1182
  205.7 1.7 collective-permute-start.2
  208.9 78.1 %branch_and_norm.1 = (f32[64,2560]{1,0:T(8,128)}, bf16[16,64,2560]{2,1,0:T(8,128)(2,1)}, bf16[16,64,2560]{2,1,0:T(8,128)(2,1)}) custom-call(bf16[8,64,2560]{2,1,0:T(8,128)(2,1)} %bitcast.60, f32[64,2560]{1,0:T(8,128)} %get-tuple-element.133.x_ref, f32[1,2560]{1,0:T(1,128)} %reshape.216.gain_ref, bf16[64,2560]{1,0:T(8,128)(2,1)} %multiply_convert_fusion.gf_ref), custom_call_target="tpu_custom_call" | custom-call | tf_op jit(solution)/shard_map/branch_and_norm/pallas_call | solution.py:407
  287.9 38.5 %feed_forward.1 = (bf16[1024,2560]{1,0:T(8,128)(2,1)}, bf16[1024,2560]{1,0:T(8,128)(2,1)}, bf16[16,160,640]{2,1,0:T(8,128)(2,1)}, bf16[16,160,640]{2,1,0:T(8,128)(2,1)}) custom-call(s32[1]{0:T(128)} %bitcast.g_ref, bf16[1024,2560]{1,0:T(8,128)(2,1)} %bitcast.55, bf16[1024,2560]{1,0:T(8,128)(2,1)} %bitcast.56, ...), custom_call_target="tpu_custom_call" | custom-call | flops 1000000000 | bytes 20971520 | tf_op jit(solution)/shard_map/feed_forward/pallas_call | solution.py:563
  326.4 1.7 collective-permute-start.3
  328.2 85.2 %norm_and_branch_back.1 = (f32[64,2560]{1,0:T(8,128)}, f32[8,2560]{1,0:T(8,128)}, bf16[8,64,2560]{2,1,0:T(8,128)(2,1)}, bf16[64,2560]{1,0:T(8,128)(2,1)}) custom-call(bf16[16,64,2560]{2,1,0:T(8,128)(2,1)} %bitcast.58, bf16[16,64,2560]{2,1,0:T(8,128)(2,1)} %bitcast.57, f32[64,2560]{1,0:T(8,128)} %get-tuple-element.91.middle_ref, ...), custom_call_target="tpu_custom_call" | custom-call | tf_op jit(solution)/shard_map/norm_and_branch_back/pallas_call | solution.py:407
  413.5 1.7 copy-done
  415.2 34.9 %attend_back.1 = (bf16[2048,384]{1,0:T(8,128)(2,1)}, bf16[512,768]{1,0:T(8,128)(2,1)}, bf16[16,144,640]{2,1,0:T(8,128)(2,1)}, bf16[3,160,640]{2,1,0:T(8,128)(2,1)}) custom-call(bf16[512,2560]{1,0:T(8,128)(2,1)} %bitcast.74, bf16[512,768]{1,0:T(8,128)(2,1)} %bitcast.78, bf16[768,640]{1,0:T(8,128)(2,1)} %get-tuple-element.96.q_up_ref, ...), custom_call_target="tpu_custom_call" | custom-call | flops 40000000000 | bytes 31457280 | tf_op jit(solution)/shard_map/attend_back/pallas_call | solution.py:1303
  450.1 104.5 %wind_up.1 = (bf16[4,144,640]{2,1,0:T(8,128)(2,1)}, bf16[13,160,640]{2,1,0:T(8,128)(2,1)}, bf16[16,64,1152]{2,1,0:T(8,128)(2,1)}, bf16[64,2560]{1,0:T(8,128)(2,1...) custom-call(bf16[16,2,64,384]{3,2,1,0:T(8,128)(2,1)} %bitcast.62, bf16[8,64,768]{2,1,0:T(8,128)(2,1)} %bitcast.65, ...), custom_call_target="tpu_custom_call" | custom-call | tf_op jit(solution)/shard_map/wind_up/pallas_call | solution.py:407
  554.6 1.3 slice_bitcast_fusion
  555.9 1.4 fusion.12
  558.2 1.3 slice_bitcast_fusion.1
  560.4 1.1 slice_convert_fusion
  564.6 1.5 reshape.226
  566.1 2.3 fusion
  571.1 7.2 %spread.1 = (f32[160,3200]{1,0:T(8,128)}, f32[160,3200]{1,0:T(8,128)}, f32[160,3200]{1,0:T(8,128)}) custom-call(s32[1]{0:T(128)} %bitcast.g_ref, bf16[13,160,640]{2,1,0:T(8,128)(2,1)} %get-tuple-element.119.refs_0_, bf16[3,160,640]{2,1,0:T(8,128)(2,1)} %get-tuple-element.120.refs_1_), custom_call_target="tpu_custom_call" | custom-call | flops 1000000000 | bytes 20971520 | tf_op jit(solution)/shard_map/spread/pallas_call | solution.py:563
  578.4 1.2 fusion.1
  (92 shorter events, 22.0 us)
Async XLA Ops:
  0.6 2.6 copy-start.4
  3.8 1.8 copy-start.12
  3.8 1.8 copy-start.13
  3.8 1.8 copy-start.14
  3.9 1.8 copy-start.15
  5.7 5.2 slice-start
  5.7 5.2 slice-start.1
  5.8 5.2 copy-start.10
  12.4 86.7 %copy-start.3 = (bf16[128,2560]{1,0:T(8,128)(2,1)S(1)}, bf16[128,2560]{1,0:T(8,128)(2,1)}, u32[]{:S(2)}) copy-start(bf16[128,2560]{1,0:T(8,128)(2,1)} %param.27) | copy-start | bytes 1966084
  12.4 86.7 %copy-start.11 = (bf16[128,2560]{1,0:T(8,128)(2,1)S(1)}, bf16[128,2560]{1,0:T(8,128)(2,1)}, u32[]{:S(2)}) copy-start(bf16[128,2560]{1,0:T(8,128)(2,1)} %param.14) | copy-start | bytes 1966084
  100.3 67.4 %copy-start.1 = (bf16[9,160,640]{2,1,0:T(8,128)(2,1)S(1)}, bf16[9,160,640]{2,1,0:T(8,128)(2,1)}, u32[]{:S(2)}) copy-start(bf16[9,160,640]{2,1,0:T(8,128)(2,1)} %get-tuple-element.81.refs_0_) | copy-start | bytes 5529604
  167.6 119.4 %collective-permute-start.1 = (bf16[4,160,640]{2,1,0:T(8,128)(2,1)}, bf16[4,160,640]{2,1,0:T(8,128)(2,1)S(1)}, u32[]{:S(2)}, u32[]{:S(2)}) collective-permute-start(bf16[4,160,640]{2,1,0:T(8,128)(2,1)} %get-tuple-element.82.refs_1_), channel_id=1, source_target_pairs={{0,1},{1,0},{2,3},{3,2},{4,5},{5,4},{6,7},{7,6},{8,9},{9,8},{10,11... | collective-permute-start | bytes 2457608 | tf_op jit(solution)/shard_map/ppermute | solution.py:1401
  167.7 119.3 %collective-permute-start = (bf16[9,160,640]{2,1,0:T(8,128)(2,1)S(1)}, bf16[9,160,640]{2,1,0:T(8,128)(2,1)}, u32[]{:S(2)}, u32[]{:S(2)}) collective-permute-start(bf16[9,160,640]{2,1,0:T(8,128)(2,1)S(1)} %copy-done.1), channel_id=1, source_target_pairs={{0,1},{1,0},{2,3},{3,2},{4,5},{5,4},{6,7},{7,6},{8,9},{9,8},{10,11... | collective-permute-start | bytes 5529608 | tf_op jit(solution)/shard_map/ppermute | solution.py:1401
  205.7 81.3 %collective-permute-start.2 = (bf16[3,160,640]{2,1,0:T(8,128)(2,1)}, bf16[3,160,640]{2,1,0:T(8,128)(2,1)}, u32[]{:S(2)}, u32[]{:S(2)}) collective-permute-start(bf16[3,160,640]{2,1,0:T(8,128)(2,1)} %get-tuple-element.83.refs_2_), channel_id=1, source_target_pairs={{0,1},{1,0},{2,3},{3,2},{4,5},{5,4},{6,7},{7,6},{8,9},{9,8},{10,11... | collective-permute-start | bytes 1843208 | tf_op jit(solution)/shard_map/ppermute | solution.py:1401
  287.0 0.9 copy-start.2
  326.4 87.0 %collective-permute-start.3 = (bf16[16,160,640]{2,1,0:T(8,128)(2,1)}, bf16[16,160,640]{2,1,0:T(8,128)(2,1)S(1)}, u32[]{:S(2)}, u32[]{:S(2)}) collective-permute-start(bf16[16,160,640]{2,1,0:T(8,128)(2,1)} %get-tuple-element.94), channel_id=1, source_target_pairs={{0,1},{1,0},{2,3},{3,2},{4,5},{5,4},{6,7},{7,6},{8,9},{9,8},{10,11... | collective-permute-start | bytes 9830408 | tf_op jit(solution)/shard_map/ppermute | solution.py:1401
  413.4 148.1 %collective-permute-start.4 = (bf16[64,2560]{1,0:T(8,128)(2,1)}, bf16[64,2560]{1,0:T(8,128)(2,1)S(1)}, u32[]{:S(2)}, u32[]{:S(2)}) collective-permute-start(bf16[64,2560]{1,0:T(8,128)(2,1)} %get-tuple-element.92), channel_id=1, source_target_pairs={{0,1},{1,0},{2,3},{3,2},{4,5},{5,4},{6,7},{7,6},{8,9},{9,8},{10,11... | collective-permute-start | bytes 983048 | tf_op jit(solution)/shard_map/ppermute | solution.py:1401
  413.4 1.7 copy-start
  563.9 2.1 copy-start.16
  568.4 1.8 copy-start.5
  568.4 1.8 copy-start.7
  568.4 11.2 %collective-permute-start.5 = (bf16[160,1152]{1,0:T(8,128)(2,1)S(1)}, bf16[160,1152]{1,0:T(8,128)(2,1)S(1)}, u32[]{:S(2)}, u32[]{:S(2)}) collective-permute-start(bf16[160,1152]{1,0:T(8,128)(2,1)S(1)} %fusion), channel_id=1, source_target_pairs={{0,1},{1,0},{2,3},{3,2},{4,5},{5,4},{6,7},{7,6},{8,9},{9,8},{10,11... | collective-permute-start | bytes 1105928 | tf_op jit(solution)/shard_map/ppermute | solution.py:1401
  571.1 7.2 %copy-start.8 = (bf16[64,2560]{1,0:T(8,128)(2,1)S(1)}, bf16[64,2560]{1,0:T(8,128)(2,1)}, u32[]{:S(2)}) copy-start(bf16[64,2560]{1,0:T(8,128)(2,1)} %get-tuple-element.113) | copy-start | bytes 983044
  571.1 7.2 %copy-start.9 = (bf16[64,2560]{1,0:T(8,128)(2,1)S(1)}, bf16[64,2560]{1,0:T(8,128)(2,1)}, u32[]{:S(2)}) copy-start(bf16[64,2560]{1,0:T(8,128)(2,1)} %get-tuple-element.114) | copy-start | bytes 983044
  (1 other events, 0.7 us)

commit v6 on v5

--- a/solution.py
+++ b/solution.py
@@ -75,7 +75,8 @@
 OFFSETS = (0, -1, 1, -2, 2, -3, 3)
 
 
-TRADED_FIRST, TRADED_NEXT, TRADED_LAST = (8, 9, 12, 4, 5, 2, 3, 1), (10, 11, 6, 7), (13, 14, 15)
+TRADED_FIRST, TRADED_NEXT, TRADED_LAST = (1, 8, 2, 9, 3, 12), (10, 11, 6, 7), (13, 14, 15, 4, 5)
+TRADED_BACK = (0,) + TRADED_FIRST + TRADED_NEXT
 
 
 class Place:
@@ -145,6 +146,11 @@
 
         when(cond, lambda: copy().start())
         self.pending.append((cond, lambda: copy().wait_send()))
+        return self.pending[-1]
+
+    def sent(self, one):
+        self.pending.remove(one)
+        when(one[0], one[1])
 
     def recv(self, dst, sem, cond=None):
         def wait():
@@ -188,17 +194,21 @@
     pl.semaphore_wait(barrier, count)
 
 
-def trade_away(place, src, out, sems):
+def trade_away(place, src, out, sems, swap=None):
     barrier = pltpu.get_barrier_semaphore()
     count = len(TRADED_LAST)
     devices = [((place.g ^ i) * place.members + place.m, place.t) for i in TRADED_LAST]
+    pairs = [(src.at[k], out.at[k]) for k in range(count)]
+    if swap is not None:
+        devices.append(place.other())
+        pairs.append(swap)
+        count += 1
     for device in devices:
         pl.semaphore_signal(barrier, inc=1, device_id=device, device_id_type=MESH)
     pl.semaphore_wait(barrier, count)
     copies = [
         pltpu.make_async_remote_copy(
-            src.at[k],
-            out.at[k],
+            *pairs[k],
             sems.at[0, k],
             sems.at[1, k],
             device_id=devices[k],
@@ -211,7 +221,7 @@
     return copies
 
 
-def gather_steps(net, src, out, width, start, pace):
+def gather_steps(net, src, out, width, start, pace, ready=None):
     p = net.place
     cores = width == 16
 
@@ -247,26 +257,29 @@
             net.recv(there, x_sem[o], p.valid(o))
             net.send(there, there, c_sem[1, o], p.core, p.valid(o))
 
-    forward(0)
-    for near in (1, 2, 3):
-        yield start + near * (pace + 2)
-        from_line(-near)
-        from_line(near)
-        yield start + near * (pace + 2) + 0.5
-        if near == 1:
-            from_across(0)
-        else:
-            from_across(1 - near)
-            from_across(near - 1)
-    yield start + 4 * (pace + 2)
-    from_across(-3)
-    from_across(3)
-    yield start + 4 * (pace + 2) + 2
-    for o in OFFSETS:
+    def from_core(o):
         net.recv(lambda: slot(o, p.b, 1 - p.d), c_sem[0, o], p.valid(o))
         if cores:
             net.recv(lambda: slot(o, 1 - p.b, 1 - p.d), c_sem[1, o], p.valid(o))
-    keep.wait()
+
+    forward(0)
+    step = pace + 2
+    for near in (1, 2, 3, 4):
+        yield start + near * step
+        if near < 4:
+            from_line(-near)
+            from_line(near)
+            yield start + near * step + 0.5
+        around = (0,) if near == 1 else (1 - near, near - 1)
+        for o in around:
+            from_across(o)
+        yield start + near * step + 2
+        for o in around:
+            from_core(o)
+        if near == 1:
+            keep.wait()
+        if ready is not None:
+            ready(near - 1)
 
 
 def add_into(out, terms, rows):
@@ -283,7 +296,7 @@
 
 
 def reduce_steps(
-    net, parts, out, near_core, near_x, line_in, line_out, rows, width, start, pace
+    net, parts, out, near_core, near_x, line_in, line_out, rows, width, start, pace, across=False
 ):
     p = net.place
     cores = width == 16
@@ -306,7 +319,8 @@
     up_sem = {o: net.sem() for o in (0, 1, 2)}
     down_sem = {o: net.sem() for o in (0, 1, 2)}
 
-    pair = p.b if cores else p.d
+    across = across or cores
+    pair = p.b if across else p.d
 
     def mine(o, b):
         g = (p.a + o) * 2 + b
@@ -324,7 +338,7 @@
             lambda o=o: mine(o, 1 - pair),
             lambda o=o: near_x.at[p.a + o],
             x_sem[o],
-            p.across if cores else p.core,
+            p.across if across else p.core,
             p.valid(o),
         )
     for number, o in enumerate(order):
@@ -411,7 +425,7 @@
         out_specs=out_specs,
         scratch_shapes=list(scratch) + [pltpu.SemaphoreType.DMA((sems,))],
         compiler_params=pltpu.CompilerParams(
-            collective_id=number, has_side_effects=True, vmem_limit_bytes=56 << 20
+            collective_id=number, has_side_effects=True, vmem_limit_bytes=62 << 20
         ),
         name=name,
     )(*ins)
@@ -430,15 +444,20 @@
     ]
 
 
-def trade_sends(net, block, out, sems, timed):
+def trade_sends(net, block, out, sems, timed, ahead=2):
     p = net.place
+    going = []
     for i, when_to in timed:
         yield when_to
-        net.send(
-            lambda i=i: block(i),
-            lambda i=i: out(i),
-            sems.at[i],
-            lambda i=i: ((p.g ^ i) * p.members + p.m, p.t),
+        if len(going) == ahead:
+            net.sent(going.pop(0))
+        going.append(
+            net.send(
+                lambda i=i: block(i),
+                lambda i=i: out(i),
+                sems.at[i],
+                lambda i=i: ((p.g ^ i) * p.members + p.m, p.t),
+            )
         )
 
 
@@ -479,7 +498,7 @@
             keep = pltpu.make_async_copy(ff_ref.at[0], near.at[0], net.sem())
             keep.start()
             out = lambda i: near.at[1 + TRADED_FIRST.index(i)]
-            timed = ((1, 1), (4, 2), (8, 4), (5, 9), (9, 12), (2, 18), (12, 20), (3, 24))
+            timed = ((1, 1), (8, 4), (9, 12), (2, 18), (12, 20), (3, 24))
             yield from trade_sends(net, lambda i: ff_ref.at[i], out, ff_sems, timed)
             yield 60.0
             trade_receives(net, out, ff_sems, TRADED_FIRST)
@@ -509,6 +528,251 @@
         [ANY] * 4,
         [pltpu.SemaphoreType.DMA((8,)), pltpu.SemaphoreType.DMA((16,))],
         200,
+    )
+
+
+class RowBlocks:
+    def __init__(self, ref, rows):
+        self.ref, self.rows, self.at = ref, rows, self
+
+    def __getitem__(self, i):
+        return self.ref.at[pl.ds(pl.multiple_of(i * self.rows, self.rows), self.rows)]
+
+
+def front(
+    number, x, query_down, latent_down, gains, gate, up, down_t, query_up, latent_up, out_t,
+    cosine, sine_table, widths, n_ctx,
+):
+    rows, dim = x.shape
+    shard, qr = query_down.shape
+    wide = qr + KVR + 128
+    units = gate.shape[1] // 16
+    q_rows, l_rows, o_rows = query_up.shape[0], latent_up.shape[0], shard // 2
+    heads, width = H // 8, H // 8 * VH
+    lanes = heads * 128
+    at_rows = q_rows + l_rows + o_rows
+
+    def body(
+        x_ref, qd_ref, ld_ref, gains_ref, gate_ref, up_ref, down_ref, qu_ref, lu_ref, ow_ref,
+        cos_ref, sin_ref,
+        both, down_out, g1, gq, gl, g2, pairs, queries, columns, first, mid, last,
+        other_first, heads_out,
+        down_block, downs, gain_blocks, ff, at, normed, column_blocks, pair, query_block,
+        heads_mine,
+        at_sems, x_sems, tp_sems, keep_sems, col_sems, ff_sems, other_sems, sems,
+    ):
+        p = Place(n_ctx)
+        down_block[:, :qr] = qd_ref[...]
+        down_block[:, qr : qr + KVR] = ld_ref[:, :KVR]
+        none = jnp.zeros((shard, NOPE), BF)
+        down_block[:, qr + KVR :] = jnp.concatenate(
+            [none, ld_ref[:, KVR:], none[:, :ROPE]], axis=1
+        )
+        greet(p, everyone=16, other=True)
+        net = Net(p, sems)
+        owner = p.d == p.t
+        f = p.a * 2 + p.d
+        place = lambda q, side: (q // 2 * 2 + (1 - p.b if side else p.b)) * 2 + q % 2
+        first_out = lambda i: first.at[1 + TRADED_FIRST.index(i)]
+        mid_out = lambda i: mid.at[TRADED_NEXT.index(i)]
+
+        def pack_heads():
+            for s in range(4):
+                for h in range(heads):
+                    cut = (s * heads + h) * (NOPE + ROPE)
+                    at[s, :q_rows, h * 128 : h * 128 + NOPE + ROPE] = qu_ref[
+                        :, cut : cut + NOPE + ROPE
+                    ]
+                    at[s, :q_rows, h * 128 + NOPE + ROPE : (h + 1) * 128] = jnp.zeros(
+                        (q_rows, 128 - NOPE - ROPE), BF
+                    )
+                at[s, q_rows : q_rows + l_rows] = lu_ref[:, s * lanes : (s + 1) * lanes]
+                for half in (0, 1):
+                    at[s, q_rows + l_rows :, half * width : (half + 1) * width] = ow_ref[
+                        half * o_rows : (half + 1) * o_rows, s * width : (s + 1) * width
+                    ]
+
+        def pack_units():
+            for n in range(16):
+                cut = slice(n * units, (n + 1) * units)
+                i = p.g ^ n
+                for k, part in enumerate((gate_ref, up_ref, down_ref)):
+                    ff[i, :, k * units : (k + 1) * units] = part[:, cut]
+                ff[i, :, 3 * units :] = jnp.zeros((shard, lanes - 3 * units), BF)
+
+        def trades():
+            yield 1.0
+            pack_units()
+            keeps = [pltpu.make_async_copy(ff.at[0], first.at[0], net.sem())]
+            keeps += [
+                pltpu.make_async_copy(ff.at[i], last.at[k], net.sem())
+                for k, i in enumerate(TRADED_LAST)
+            ]
+            for keep in keeps:
+                keep.start()
+            block = lambda i: ff.at[i]
+
+            def onward(k, src):
+                net.send(src, lambda: other_first.at[k], other_sems.at[k], p.other)
+
+            onward(0, lambda: ff.at[0])
+            timed = ((1, 3), (8, 5), (2, 12), (9, 30), (3, 34), (12, 38))
+            yield from trade_sends(net, block, first_out, ff_sems, timed)
+            timed = [each for each in ((10, 49), (6, 57), (11, 62), (7, 70)) if each[0] in TRADED_NEXT]
+            for k, i in enumerate(TRADED_FIRST[:3]):
+                yield 42.0 + 3 * k
+                trade_receives(net, first_out, ff_sems, (i,))
+                onward(1 + k, lambda i=i: first_out(i))
+            yield from trade_sends(net, block, mid_out, ff_sems, timed)
+            yield 90.0
+            trade_receives(net, first_out, ff_sems, TRADED_FIRST[3:])
+            trade_receives(net, mid_out, ff_sems, TRADED_NEXT)
+            for k in range(4):
+                net.recv(lambda k=k: other_first.at[k], other_sems.at[k])
+            for keep in keeps:
+                keep.wait()
+
+        def attention():
+            pack_heads()
+            yield 1.0
+            keep = pltpu.make_async_copy(at.at[p.a], heads_mine.at[f], net.sem())
+            pl.when(owner)(lambda: keep.start())
+            for s in range(4):
+                net.send(
+                    lambda s=s: at.at[s],
+                    lambda: heads_mine.at[f],
+                    at_sems.at[f],
+                    lambda s=s: p.at(a=s, d=p.t),
+                    ~(owner & (p.a == s)),
+                )
+
+            def keep_head(q):
+                return pltpu.make_async_copy(
+                    heads_mine.at[q], heads_out.at[place(q, 0)], keep_sems.at[q]
+                )
+
+            yield 24.0
+            pl.when(owner)(lambda: keep.wait())
+            for q in range(8):
+                yield 24.0 + q
+                net.recv(lambda q=q: heads_mine.at[q], at_sems.at[q], owner & (f != q))
+                pl.when(owner)(lambda: keep_head(q).start())
+                for sems_of, to in ((x_sems, p.across), (tp_sems.at[0], p.other)):
+                    net.send(
+                        lambda q=q: heads_mine.at[q],
+                        lambda q=q: heads_out.at[place(q, 0)],
+                        sems_of.at[q],
+                        to,
+                        owner,
+                    )
+            for q in range(8):
+                yield 38.0 + 2 * q
+                theirs = lambda q=q: heads_out.at[place(q, 1)]
+                net.recv(theirs, x_sems.at[q], owner)
+                net.send(theirs, theirs, tp_sems.at[1, q], p.other, owner)
+            yield 85.0
+            for q in range(8):
+                for side in (0, 1):
+                    net.recv(lambda: heads_out.at[place(q, side)], tp_sems.at[side, q], ~owner)
+                pl.when(owner)(lambda: keep_head(q).wait())
+
+        def send_columns():
+            for n in range(16):
+                column_blocks[n] = normed[:, n * shard : (n + 1) * shard]
+            keep = pltpu.make_async_copy(column_blocks.at[p.g], columns.at[p.g], net.sem())
+            keep.start()
+            for k in range(1, 16):
+                if k % 4 == 1:
+                    yield 56.0 + k
+                net.send(
+                    lambda k=k: column_blocks.at[p.g ^ k],
+                    lambda: columns.at[p.g],
+                    col_sems.at[k],
+                    lambda k=k: ((p.g ^ k) * p.members + p.m, p.t),
+                )
+            yield 88.0
+            for k in range(1, 16):
+                net.recv(lambda k=k: columns.at[p.g ^ k], col_sems.at[k])
+            keep.wait()
+
+        def latents():
+            sem = net.sem()
+            net.send(lambda: pair.at[p.t], lambda: pair.at[p.t], sem, p.other)
+            yield 54.0
+            net.recv(lambda: pair.at[1 - p.t], sem)
+            yield from gather_steps(net, pair, pairs, 16, 55, 2.2)
+
+        def chain():
+            yield from gather_steps(net, down_block, RowBlocks(downs, shard), 16, 0, 8)
+            keep = pltpu.make_async_copy(downs, down_out, net.sem())
+            keep.start()
+            at_lane = 0
+            for out, w in zip((g1, gq, gl, g2), widths):
+                for n in range(16):
+                    out[:, n * w : (n + 1) * w] = gain_blocks[n, :1, at_lane : at_lane + w]
+                at_lane += w
+            values = x_ref[...]
+            normed[...] = (values * norm_factor(values) * g1[...]).astype(BF)
+            both[...] = matmul(normed[...], downs[...])
+            query, latent = both[:, :qr], both[:, qr : qr + KVR]
+            query_block[...] = (query * norm_factor(query) * gq[...]).astype(BF)
+            pair[p.t, :, :KVR] = (latent * norm_factor(latent) * gl[...]).astype(BF)
+            pair[p.t, :, KVR:] = turn(both[:, qr + KVR :], cos_ref[...], sin_ref[...]).astype(BF)
+            yield from together(
+                latents(), gather_steps(net, query_block, queries, 8, 51, 2.2), send_columns()
+            )
+            keep.wait()
+
+        run_together(
+            chain(),
+            after(0.5, gather_steps(net, gains_ref, gain_blocks, 16, 0.5, 1)),
+            trades(),
+            attention(),
+        )
+        net.finish()
+
+    ff_shape = (shard, lanes)
+    return comm_call(
+        "front",
+        number,
+        body,
+        [x, query_down, latent_down, gains, gate, up, down_t, query_up, latent_up, out_t]
+        + [cosine, sine_table],
+        [VMEM] * 12,
+        [
+            shape((rows, wide), F32),
+            shape((dim, wide)),
+            *[shape((1, 16 * w), F32) for w in widths],
+            shape((16, 2, rows, KVR + 128)),
+            shape((8, rows, qr)),
+            shape((16, rows, shard)),
+            shape((1 + len(TRADED_FIRST),) + ff_shape),
+            shape((len(TRADED_NEXT),) + ff_shape),
+            shape((len(TRADED_LAST),) + ff_shape),
+            shape((4,) + ff_shape),
+            shape((16, at_rows, lanes)),
+        ],
+        [VMEM, ANY] + [VMEM] * 4 + [ANY] * 8,
+        [
+            pltpu.VMEM((shard, wide), BF),
+            pltpu.VMEM((dim, wide), BF),
+            pltpu.VMEM((16,) + gains.shape, F32),
+            pltpu.VMEM((16,) + ff_shape, BF),
+            pltpu.VMEM((4, at_rows, lanes), BF),
+            pltpu.VMEM((rows, dim), BF),
+            pltpu.VMEM((16, rows, shard), BF),
+            pltpu.VMEM((2, rows, KVR + 128), BF),
+            pltpu.VMEM((rows, qr), BF),
+            pltpu.VMEM((8, at_rows, lanes), BF),
+            pltpu.SemaphoreType.DMA((8,)),
+            pltpu.SemaphoreType.DMA((8,)),
+            pltpu.SemaphoreType.DMA((2, 8)),
+            pltpu.SemaphoreType.DMA((8,)),
+            pltpu.SemaphoreType.DMA((16,)),
+            pltpu.SemaphoreType.DMA((16,)),
+            pltpu.SemaphoreType.DMA((16,)),
+        ],
+        300,
     )
 
 
@@ -669,23 +933,65 @@
     )
 
 
-def spread(parts, units, members):
+def spread(parts, order, at, down, halves, units, members):
     rows, cols = parts[0].shape[1:]
     places = [(a, k) for a, w in enumerate(parts) for k in range(w.shape[0])]
+    n_parts = len(parts)
+    heads, width = H // 8, H // 8 * VH
+    o_rows = rows // 2
+    q_rows, l_rows = 3 * KVR // 16, KVR // 16
+    outs = [shape((rows, 16 * units), F32)] * 3
+    if members == 1:
+        outs += [
+            shape((q_rows, 4 * heads * (NOPE + ROPE)), F32),
+            shape((l_rows, 4 * cols), F32),
+            shape((rows, 4 * width), F32),
+            shape((rows, down.shape[1] - KVR - 128), F32),
+            shape((rows, KVR + ROPE), F32),
+        ]
+    own_rows, dim = halves[0].shape
+    outs = [shape((2 * own_rows, dim)), shape((2 * own_rows, dim), F32)] + outs
+    ins = list(halves) + ([at, down] if members == 1 else []) + list(parts)
+    first = len(ins) - n_parts
 
     def body(g_ref, *refs):
+        out_refs = refs[len(ins) : -1]
+        t = lax.axis_index("tp")
+        for k in range(4):
+            start = pl.multiple_of((t if k % 2 == 0 else 1 - t) * own_rows, own_rows)
+            out = out_refs[k // 2]
+            out[pl.ds(start, own_rows)] = refs[k][...].astype(out.dtype)
         hold = refs[-1]
-        for i, (a, k) in enumerate(places):
-            hold[g_ref[0] ^ i] = refs[a][k].astype(F32)
+        for i, (a, k) in zip(order, places):
+            hold[g_ref[0] ^ i] = refs[first + a][k].astype(F32)
+        rest = out_refs[2:]
         for n in range(16):
-            for k, out in enumerate(refs[len(parts) : len(parts) + 3]):
+            for k, out in enumerate(rest[:3]):
                 out[:, n * units : (n + 1) * units] = hold[n, :, k * units : (k + 1) * units]
+        if members == 1:
+            at_ref, down_ref = refs[4], refs[5]
+            qr = down_ref.shape[1] - KVR - 128
+            rest[6][...] = down_ref[:, :qr]
+            rest[7][:, :KVR] = down_ref[:, qr : qr + KVR]
+            rest[7][:, KVR:] = down_ref[:, qr + KVR + NOPE : qr + KVR + NOPE + ROPE]
+            for s in range(4):
+                part = at_ref[s].astype(F32)
+                for h in range(heads):
+                    cut = (s * heads + h) * (NOPE + ROPE)
+                    rest[3][:, cut : cut + NOPE + ROPE] = part[
+                        :q_rows, h * 128 : h * 128 + NOPE + ROPE
+                    ]
+                rest[4][:, s * cols : (s + 1) * cols] = part[q_rows : q_rows + l_rows]
+                for half in (0, 1):
+                    rest[5][half * o_rows : (half + 1) * o_rows, s * width : (s + 1) * width] = (
+                        part[q_rows + l_rows :, half * width : (half + 1) * width]
+                    )
 
     return plain_call(
         "spread",
         body,
-        list(parts),
-        [shape((rows, 16 * units), F32)] * 3,
+        ins,
+        outs,
         [pltpu.VMEM((16, rows, cols), F32)],
         members,
     )
@@ -738,7 +1044,7 @@
                 pl.when(owner)(lambda: keep_head(q).wait())
 
         out = lambda i: mid.at[TRADED_NEXT.index(i)]
-        run_together(trade_sends(net, lambda i: ff_ref.at[i], out, ff_sems, ((10, 0), (6, 0))))
+        run_together(trade_sends(net, lambda i: ff_ref.at[i], out, ff_sems, [(i, 0) for i in TRADED_NEXT]))
         values = x_ref[...]
         normed[...] = (values * norm_factor(values) * g1_ref[...]).astype(BF)
         both[...] = matmul(normed[...], down_ref[...])
@@ -781,7 +1087,6 @@
             gather_steps(net, query_block, queries, 8, 9, 2.2),
             after(9.0, send_columns()),
             spread_heads(),
-            trade_sends(net, lambda i: ff_ref.at[i], out, ff_sems, ((7, 20), (11, 22))),
         )
         trade_receives(net, out, ff_sems, TRADED_NEXT)
         net.finish()
@@ -829,72 +1134,114 @@
 
 def wind_up(
     number, pairs, queries, at, both, x, grad_middle, down, gains, second, cosine, sine_table,
-    ff_own, ff_got, widths, n_ctx,
+    ff_own, ff_got, columns, widths, n_ctx,
 ):
     rows, dim = x.shape
     wide = down.shape[1]
     qr = wide - KVR - 128
     members = n_ctx // 16
+    down_shape = down.shape
     unit_rows = ff_own.shape[1]
     traded = TRADED_FIRST + TRADED_NEXT
 
     def body(
-        pairs_ref, queries_ref, at_ref, both_ref, x_ref, middle_ref, down_ref,
-        g1_ref, gq_ref, gl_ref, second_ref, cos_ref, sin_ref, own_ref, got_ref,
-        at_out, ff_out, both_all, input_half, input_other, gains_out,
-        ff_sum, at_x, at_tp, tp_in, pair_sum, query_sum, grad_both, gain_blocks, gain_tp,
-        *rest,
+        pairs_ref, queries_ref, at_ref, both_ref, x_ref, middle_ref, down_hbm,
+        g1_ref, gq_ref, gl_ref, second_ref, cos_ref, sin_ref, columns_ref, own_ref, got_ref,
+        at_out, ff_out, down_sum, input_half, input_other, gains_out,
+        own_hold, ff_sum, at_x, at_tp, core_in, tp_in, pair_sum, query_sum, grad_both, gain_blocks, gain_tp,
+        down, both_all, down_part, down_other, *rest,
     ):
         p = Place(n_ctx)
         greet(p, everyone=16, other=True)
         rest = list(rest)
         net = Net(p, rest.pop())
-        tp_sems, x_sems, ff_sems, pair_sems = [rest.pop() for _ in range(4)]
+        load_sems, tp_sems, x_sems, ff_sems, pair_sems = [rest.pop() for _ in range(5)]
+        load_down = pltpu.make_async_copy(down_hbm, down, net.sem())
+        load_down.start()
 
         def latents():
-            for g in range(16):
+            for q in range(8):
                 net.send(
-                    lambda g=g: pairs_ref.at[g, 1 - p.t],
-                    lambda g=g: tp_in.at[g],
-                    pair_sems.at[g],
+                    lambda q=q: pairs_ref.at[2 * q + 1 - p.d],
+                    lambda q=q: core_in.at[q],
+                    pair_sems.at[0, q],
+                    p.core,
+                )
+            for q in range(8):
+                yield 1.5 + 0.2 * q
+                net.recv(lambda q=q: core_in.at[q], pair_sems.at[0, q])
+                for half in (0, 1):
+                    near = core_in.at[q, half]
+                    add_into(near, [near, pairs_ref.at[2 * q + p.d, half]], rows)
+                net.send(
+                    lambda q=q: core_in.at[q, 1 - p.t],
+                    lambda q=q: tp_in.at[q],
+                    pair_sems.at[1, q],
                     p.other,
                 )
-            for g in range(16):
-                yield 3.0 + 1.1 * (g + 1)
-                net.recv(lambda g=g: tp_in.at[g], pair_sems.at[g])
-                add_into(tp_in.at[g], [tp_in.at[g], pairs_ref.at[g, p.t]], rows)
-            yield from reduce_steps(net, tp_in, pair_sum, *rest[:4], rows, 16, 21, 1.1)
+            for q in range(8):
+                yield 4.0 + 1.1 * (q + 1)
+                net.recv(lambda q=q: tp_in.at[q], pair_sems.at[1, q])
+                add_into(tp_in.at[q], [tp_in.at[q], core_in.at[q, p.t]], rows)
+            yield from reduce_steps(net, tp_in, pair_sum, None, *rest[:3], rows, 8, 14, 1.1, True)
 
         def trades():
-            timed = (
-                ((8, 1), (2, 2), (4, 3), (3, 6), (9, 10), (5, 12), (12, 19), (6, 22), (1, 23))
-                + ((7, 26), (10, 28), (11, 37))
-            )
-            for i, when_to in timed:
+            loads = {
+                i: [
+                    pltpu.make_async_copy(ref.at[i], hold.at[k], load_sems.at[n, k])
+                    for n, (ref, hold) in enumerate(((own_ref, own_hold), (got_ref, ff_sum)))
+                ]
+                for k, i in enumerate(TRADED_BACK)
+            }
+            for load in loads.values():
+                for part in load:
+                    part.start()
+
+            def block(i):
+                return ff_sum.at[TRADED_BACK.index(i)]
+
+            def joined(i):
+                for part in loads[i]:
+                    part.wait()
+                k = TRADED_BACK.index(i)
+                add_into(block(i), [block(i), own_hold.at[k]], unit_rows)
+                return block(i)
+
+            out = lambda i: ff_out.at[TRADED_BACK.index(i)]
+            timed = ((8, 1), (2, 2), (3, 6), (9, 10), (12, 19), (6, 22), (1, 23), (7, 26))
+            for i, when_to in timed + ((10, 28), (11, 37)):
+                if i not in traded:
+                    continue
                 yield when_to
-                add_into(ff_sum.at[i], [got_ref.at[i], own_ref.at[i]], unit_rows)
-                yield from trade_sends(
-                    net, lambda i: ff_sum.at[i], lambda i: ff_out.at[i], ff_sems, ((i, when_to),)
-                )
-            add_into(ff_sum.at[0], [got_ref.at[0], own_ref.at[0]], unit_rows)
-            keep = pltpu.make_async_copy(ff_sum.at[0], ff_out.at[0], net.sem())
+                joined(i)
+                yield from trade_sends(net, block, out, ff_sems, ((i, when_to),))
+            keep = pltpu.make_async_copy(joined(0), out(0), net.sem())
             keep.start()
             yield 95.0
-            trade_receives(net, lambda i: ff_out.at[i], ff_sems, traded)
+            trade_receives(net, out, ff_sems, traded)
             keep.wait()
 
         def gain_sums():
             sem = net.sem()
             net.send(lambda: gain_blocks, lambda: gain_tp, sem, p.other)
-            yield 52.0
+            yield 45.0
             net.recv(lambda: gain_tp, sem)
             pl.loop(0, 16)(lambda g: add_into(gain_tp.at[g], [gain_tp.at[g], gain_blocks.at[g]], 16))
-            yield from reduce_steps(net, gain_tp, gains_out, *rest[7:11], 16, 16, 53, 2)
+            yield from reduce_steps(net, gain_tp, gains_out, *rest[6:10], 16, 16, 46, 2)
+
+        def gather_and_multiply(gather):
+            yield from gather
+            columns = columns_ref[...].reshape(16 * rows, columns_ref.shape[2])
+            down_part[...] = matmul_tn(columns, both_all[...]).astype(BF)
+            swap = swap_steps(net, down_part, down_other)
+            yield next(swap)
+            yield from swap
+            down_sum[...] = down_part[...].astype(F32) + down_other[...].astype(F32)
 
         def chain():
             yield from together(
                 latents(),
-                reduce_steps(net, queries_ref, query_sum, None, *rest[4:7], rows, 8, 0, 2.2),
+                reduce_steps(net, queries_ref, query_sum, None, *rest[3:6], rows, 8, 0, 2.2),
             )
             query_back, query_share = norm_back_rows(
                 both_ref[:, :qr], gq_ref[...], query_sum[...]
@@ -908,10 +1255,11 @@
                 pair_sum[:, KVR:], cos_ref[...], sin_ref[...], True
             ).astype(BF)
 
-            gather = gather_steps(net, grad_both, both_all, 16, 38, 3.3)
+            gather = gather_steps(net, grad_both, RowBlocks(both_all, rows), 16, 31, 3.3)
             next(gather)
+            load_down.wait()
             input_back, input_share = norm_back_rows(
-                x_ref[...], g1_ref[...], matmul_nt(grad_both[...], down_ref[...])
+                x_ref[...], g1_ref[...], matmul_nt(grad_both[...], down[...])
             )
             input_half[...] = (middle_ref[...] + input_back).astype(BF)
             swap = swap_steps(net, input_half, input_other)
@@ -928,14 +1276,14 @@
                         parts.append(share[:, at_lane : at_lane + w])
                 row = jnp.concatenate(parts, axis=1)
                 gain_blocks[n] = jnp.broadcast_to(row, gain_blocks.shape[1:]).astype(BF)
-            yield from together(gather, gain_sums(), swap)
+            yield from together(gather_and_multiply(gather), gain_sums(), swap)
 
         run_together(
             chain(),
             after(
-                0.5,
+                3.5,
                 head_grads_steps(
-                    net, at_ref, at_out, at_x, at_tp, x_sems, tp_sems, at.shape[1], 17
+                    net, at_ref, at_out, at_x, at_tp, x_sems, tp_sems, at.shape[1], 12
                 ),
             ),
             trades(),
@@ -945,40 +1293,47 @@
     lanes = pairs.shape[3]
     gain_lanes = members * sum(widths)
     scratch = [
-        pltpu.VMEM((13,) + ff_own.shape[1:], BF),
+        pltpu.VMEM((len(TRADED_BACK),) + ff_own.shape[1:], BF),
+        pltpu.VMEM((len(TRADED_BACK),) + ff_own.shape[1:], BF),
         pltpu.VMEM((8,) + at.shape[1:], BF),
         pltpu.VMEM((2, 8) + at.shape[1:], BF),
-        pltpu.VMEM((16, rows, lanes), BF),
+        pltpu.VMEM((8, 2, rows, lanes), BF),
+        pltpu.VMEM((8, rows, lanes), BF),
         pltpu.VMEM((rows, lanes), F32),
         pltpu.VMEM((rows, qr), F32),
         pltpu.VMEM((rows, wide), BF),
         pltpu.VMEM((16, 16, gain_lanes), BF),
         pltpu.VMEM((16, 16, gain_lanes), BF),
+        pltpu.VMEM(down_shape, BF),
+        pltpu.VMEM((16 * rows, wide), BF),
+        pltpu.VMEM((dim // 16, wide), BF),
+        pltpu.VMEM((dim // 16, wide), BF),
     ]
-    scratch += reduce_scratch(rows, lanes, 16) + reduce_scratch(rows, qr, 8)
+    scratch += reduce_scratch(rows, lanes, 8) + reduce_scratch(rows, qr, 8)
     scratch += reduce_scratch(16, gain_lanes, 16)
     scratch += [
-        pltpu.SemaphoreType.DMA((16,)),
+        pltpu.SemaphoreType.DMA((2, 8)),
         pltpu.SemaphoreType.DMA((16,)),
         pltpu.SemaphoreType.DMA((2, 8)),
         pltpu.SemaphoreType.DMA((2, 8)),
+        pltpu.SemaphoreType.DMA((2, len(TRADED_BACK))),
     ]
     return comm_call(
         "wind_up",
         number,
         body,
         [pairs, queries, at, both, x, grad_middle, down, *gains, second, cosine, sine_table]
-        + [ff_own, ff_got],
-        [VMEM] * 15,
+        + [columns, ff_own, ff_got],
+        [VMEM] * 6 + [ANY] + [VMEM] * 7 + [ANY] * 2,
         [
             shape((4,) + at.shape[1:]),
-            shape((13,) + ff_own.shape[1:]),
-            shape((16, rows, wide)),
+            shape((len(TRADED_BACK),) + ff_own.shape[1:]),
+            shape((dim // 16, wide), F32),
             shape((rows, dim)),
             shape((rows, dim)),
             shape((16, gain_lanes), F32),
         ],
-        [ANY, ANY, ANY, VMEM, ANY, VMEM],
+        [ANY, ANY, VMEM, VMEM, ANY, VMEM],
         scratch,
         260,
     )
@@ -1087,6 +1442,287 @@
     )
 
 
+def unit_weights(g, sides, order, units, rows, lanes, wgu_ref, wd_ref):
+    pad = jnp.zeros((rows, lanes - units), BF)
+    for place, i in enumerate(order):
+        cut = pl.ds(pl.multiple_of((g ^ i) * rows, rows), rows)
+        for half, side in enumerate(sides):
+            block = side(place)
+            for k in range(3):
+                part = jnp.concatenate([block[:, k * units : (k + 1) * units], pad], axis=1)
+                into = wgu_ref if k < 2 else wd_ref
+                at = (2 * lanes * k if k < 2 else 0) + half * lanes
+                into[cut, at : at + lanes] = part
+
+
+def forward(number, parts, x, gain, gf, own, oth, own_last, order, units, n_ctx):
+    rows, dim = x.shape
+    tokens, shard, wide = 16 * rows, own_last.shape[1], own_last.shape[2]
+    lanes = 256
+    both = 2 * lanes
+    parts = parts.reshape(8, rows, dim)
+    n_own, n_oth, n_last = len(own), len(oth), own_last.shape[0]
+    own_places, oth_places = [
+        [(a, k) for a, w in enumerate(side) for k in range(w.shape[0])] for side in (own, oth)
+    ]
+    n_early = len(own_places)
+
+    def body(parts_ref, x_ref, gain_ref, gf_ref, *refs):
+        own_refs, oth_refs, last_ref = refs[:n_own], refs[n_own : n_own + n_oth], refs[n_own + n_oth]
+        middle, ns_out, gf_out, acts_out, gs_out, ffn_out = refs[n_own + n_oth + 1 :][:6]
+        (
+            branch, normed, ns_ref, gf_all, acts_ref, gs_ref, ffn_ref, wgu_ref, wd_ref, other_last,
+            near, line_in, line_out, last_sems, out_sems, sems,
+        ) = refs[n_own + n_oth + 7 :]
+        p = Place(n_ctx)
+        greet(p, line=True, across=True, core=True, other=True)
+        net = Net(p, sems)
+
+        def weights():
+            for k in range(n_last):
+                net.send(
+                    lambda k=k: last_ref.at[k],
+                    lambda k=k: other_last.at[k],
+                    last_sems.at[k],
+                    p.other,
+                )
+            yield 3.0
+            own_block = lambda n: own_refs[own_places[n][0]][own_places[n][1]]
+            oth_block = lambda n: oth_refs[oth_places[n][0]][oth_places[n][1]]
+            unit_weights(
+                p.g, (own_block, oth_block), order[:n_early], units, shard, lanes, wgu_ref, wd_ref
+            )
+            yield 30.5
+            for k in range(n_last):
+                net.recv(lambda k=k: other_last.at[k], last_sems.at[k])
+            unit_weights(
+                p.g,
+                (lambda k: last_ref[k], lambda k: other_last[k]),
+                order[n_early:],
+                units,
+                shard,
+                lanes,
+                wgu_ref,
+                wd_ref,
+            )
+
+        a = p.a
+        nth = (
+            a,
+            jnp.where(a == 0, 1, a - 1),
+            jnp.where(a < 2, 2, jnp.where(a == 2, 3, 1)),
+            jnp.where(a < 2, 3, 0),
+        )
+        stores = []
+
+        def compute(n):
+            r = pl.ds(pl.multiple_of(nth[n] * 4 * rows, 4 * rows), 4 * rows)
+            gate_up = matmul(ns_ref[r], wgu_ref[...])
+            gate, up = gate_up[:, :both], gate_up[:, both:]
+            grad_hidden = matmul(gf_all[r], wd_ref[...])
+            sigmoid_gate = 1.0 / (1.0 + jnp.exp(-gate))
+            silu = gate * sigmoid_gate
+            acts_ref[r, 2 * both :] = (silu * up).astype(BF)
+            acts_ref[r, :both] = (
+                grad_hidden * up * sigmoid_gate * (1.0 + gate * (1.0 - sigmoid_gate))
+            ).astype(BF)
+            acts_ref[r, both : 2 * both] = (grad_hidden * silu).astype(BF)
+            gs_ref[r] = matmul_nt(acts_ref[r, : 2 * both], wgu_ref[...]).astype(BF)
+            ffn_ref[r] = matmul_nt(acts_ref[r, 2 * both :], wd_ref[...]).astype(BF)
+            pairs = (
+                (ns_ref, ns_out), (gf_all, gf_out), (acts_ref, acts_out), (gs_ref, gs_out),
+                (ffn_ref, ffn_out),
+            )
+            for k, (src, dst) in enumerate(pairs):
+                stores.append(pltpu.make_async_copy(src.at[r], dst.at[r], out_sems.at[n, k]))
+                stores[-1].start()
+
+        def second():
+            yield from reduce_steps(
+                net, parts_ref, branch, None, near, line_in, line_out, rows, 8, 0, 7
+            )
+
+            def norm(r):
+                values = x_ref[r] + residual_scale * branch[r]
+                middle[r] = values
+                normed[r] = (values * norm_factor(values) * gain_ref[...]).astype(BF)
+
+            by_rows(rows, 16, norm)
+            yield from gather_steps(net, normed, RowBlocks(ns_ref, rows), 16, 32, 7, compute)
+
+        run_together(
+            second(),
+            after(0.5, gather_steps(net, gf_ref, RowBlocks(gf_all, rows), 16, 0, 8, lambda n: None)),
+            after(0.7, weights()),
+        )
+        for store in stores:
+            store.wait()
+        net.finish()
+
+    ins = [parts, x, gain, gf, *own, *oth, own_last]
+    return comm_call(
+        "forward",
+        number,
+        body,
+        ins,
+        [VMEM] * len(ins),
+        [
+            shape((rows, dim), F32),
+            shape((tokens, dim)),
+            shape((tokens, dim)),
+            shape((tokens, 3 * both)),
+            shape((tokens, dim)),
+            shape((tokens, dim)),
+        ],
+        [VMEM] + [ANY] * 5,
+        [
+            pltpu.VMEM((rows, dim), F32),
+            pltpu.VMEM((rows, dim), BF),
+            pltpu.VMEM((tokens, dim), BF),
+            pltpu.VMEM((tokens, dim), BF),
+            pltpu.VMEM((tokens, 3 * both), BF),
+            pltpu.VMEM((tokens, dim), BF),
+            pltpu.VMEM((tokens, dim), BF),
+            pltpu.VMEM((dim, 2 * both), BF),
+            pltpu.VMEM((dim, both), BF),
+            pltpu.VMEM(own_last.shape, BF),
+        ]
+        + reduce_scratch(rows, dim, 8)
+        + [pltpu.SemaphoreType.DMA((n_last,)), pltpu.SemaphoreType.DMA((4, 5))],
+        240,
+    )
+
+
+def backward(number, gs, ffn, ns, gf, acts, middle, out_grad, gain, units, wide, n_ctx):
+    rows, dim = middle.shape
+    tokens, shard = 16 * rows, dim // 16
+    lanes = 256
+    both = 2 * lanes
+
+    def body(
+        gs_hbm, ffn_hbm, ns_hbm, gf_hbm, acts_hbm, middle_ref, out_grad_ref, gain_ref,
+        grad_middle, gain_part, branches, output, own_out, got_out,
+        upstream, branch, ffn_sum, gs_ref, ffn_ref, ns_ref, gf_ref, acts_ref, own, oth,
+        *rest,
+    ):
+        rest = list(rest)
+        sems, other_sems, own_sems, load_sems = [rest.pop() for _ in range(4)]
+        pairs = (
+            (gs_hbm, gs_ref), (ffn_hbm, ffn_ref), (ns_hbm, ns_ref), (acts_hbm, acts_ref),
+            (gf_hbm, gf_ref),
+        )
+        loads = [
+            pltpu.make_async_copy(src, dst, load_sems.at[k]) for k, (src, dst) in enumerate(pairs)
+        ]
+        for load in loads:
+            load.start()
+        p = Place(n_ctx)
+        greet(p, line=True, across=True, core=True, other=True)
+        net = Net(p, sems)
+        stores = []
+
+        def chain():
+            loads[0].wait()
+            yield from reduce_steps(
+                net, RowBlocks(gs_ref, rows), upstream, *rest[:4], rows, 16, 0, 7
+            )
+            gain_part[...] = jnp.zeros((8, dim), F32)
+
+            def back(r):
+                grads, share = norm_back_rows(middle_ref[r], gain_ref[...], upstream[r])
+                total = out_grad_ref[r] + grads
+                grad_middle[r] = total
+                branch[r] = (residual_scale * total).astype(BF)
+                gain_part[...] += share
+
+            by_rows(rows, 16, back)
+            yield from gather_steps(net, branch, branches, 8, 38, 7)
+
+        def output_sum():
+            loads[1].wait()
+            yield from reduce_steps(
+                net, RowBlocks(ffn_ref, rows), ffn_sum, *rest[4:8], rows, 16, 28, 7
+            )
+
+        def give(q, k, grads):
+            for jj in range(4):
+                for half, out in enumerate((own, oth)):
+                    out[p.g ^ (4 * q + jj), :, k * units : (k + 1) * units] = grads[
+                        jj * shard : (jj + 1) * shard, half * lanes : half * lanes + units
+                    ].astype(BF)
+
+        def weight_grads():
+            for out in (own, oth):
+                out[:, :, 3 * units :] = jnp.zeros((16, shard, wide - 3 * units), BF)
+            for load in loads[2:]:
+                load.wait()
+            span = dim // 4
+            for q in range(4):
+                yield 5.0 + 7.5 * q
+                cut = slice(q * span, (q + 1) * span)
+                grads = matmul_tn(ns_ref[:, cut], acts_ref[:, : 2 * both])
+                give(q, 0, grads[:, :both])
+                give(q, 1, grads[:, both:])
+                give(q, 2, matmul_tn(gf_ref[:, cut], acts_ref[:, 2 * both :]))
+                for n in range(4 * q, 4 * q + 4):
+                    net.send(
+                        lambda n=n: oth.at[p.g ^ n],
+                        lambda n=n: got_out.at[p.g ^ n],
+                        other_sems.at[n],
+                        p.other,
+                    )
+                    stores.append(
+                        pltpu.make_async_copy(own.at[p.g ^ n], own_out.at[p.g ^ n], own_sems.at[n])
+                    )
+                    stores[-1].start()
+            yield 80.0
+            for n in range(16):
+                net.recv(lambda n=n: got_out.at[p.g ^ n], other_sems.at[n])
+
+        run_together(chain(), after(0.5, output_sum()), after(3.5, weight_grads()))
+        output[...] = (middle_ref[...] + residual_scale * ffn_sum[...]).astype(BF)
+        for store in stores:
+            store.wait()
+        net.finish()
+
+    block_shape = (16, shard, wide)
+    return comm_call(
+        "backward",
+        number,
+        body,
+        [gs, ffn, ns, gf, acts, middle, out_grad, gain],
+        [ANY] * 5 + [VMEM] * 3,
+        [
+            shape((rows, dim), F32),
+            shape((8, dim), F32),
+            shape((8, rows, dim)),
+            shape((rows, dim)),
+            shape(block_shape),
+            shape(block_shape),
+        ],
+        [VMEM, VMEM, ANY, VMEM, ANY, ANY],
+        [
+            pltpu.VMEM((rows, dim), F32),
+            pltpu.VMEM((rows, dim), BF),
+            pltpu.VMEM((rows, dim), F32),
+            pltpu.VMEM((tokens, dim), BF),
+            pltpu.VMEM((tokens, dim), BF),
+            pltpu.VMEM((tokens, dim), BF),
+            pltpu.VMEM((tokens, dim), BF),
+            pltpu.VMEM((tokens, 3 * both), BF),
+            pltpu.VMEM(block_shape, BF),
+            pltpu.VMEM(block_shape, BF),
+        ]
+        + reduce_scratch(rows, dim, 16) * 2
+        + [
+            pltpu.SemaphoreType.DMA((5,)),
+            pltpu.SemaphoreType.DMA((16,)),
+            pltpu.SemaphoreType.DMA((16,)),
+        ],
+        240,
+    )
+
+
 def turn(values, cosine, sine_table, back=False):
     lane = lax.broadcasted_iota(jnp.int32, values.shape, 1)
     near = jnp.where((lane >= 80) & (lane < 96), pltpu.roll(values, 16, 1), 0.0)
@@ -1131,7 +1767,7 @@
         branch_ref, q_ref, o_ref, lse_ref, att_ref, q_up_ref, l_up_ref, w_ref, far_ref,
         e_ref, top_ref, sum_ref, acc_ref, sems,
     ):
-        copies = trade_away(Place(n_ctx), ff_ref.at[pl.ds(13, 3)], far_ref, sems)
+        copies = trade_away(Place(n_ctx), ff_ref, far_ref, sems)
         unpack_heads(at_ref, q_up_ref, l_up_ref, w_ref, q_rows, l_rows)
         by_rows(
             keys,
@@ -1190,13 +1826,13 @@
             shape((qn.shape[1], wide)),
             shape((KVR, wide)),
             shape((dim, width)),
-            shape((3,) + ff.shape[1:]),
+            shape(ff.shape),
         ],
         in_specs=[VMEM] * 6 + [ANY],
         out_specs=[VMEM] * 8 + [ANY],
         scratch_shapes=[pltpu.VMEM((keys, wide), BF)]
         + [pltpu.VMEM((rows, 128), F32)] * 3
-        + [pltpu.SemaphoreType.DMA((2, 3))],
+        + [pltpu.SemaphoreType.DMA((2, len(TRADED_LAST)))],
         compiler_params=pltpu.CompilerParams(
             collective_id=number, has_side_effects=True, vmem_limit_bytes=60 << 20
         ),
@@ -1209,7 +1845,7 @@
 
 def attend_back(
     number, gb, qn, q_up, pairs, l_up, w_out_t, cosine, sine_table, q_pos, q, o, lse, att,
-    ff_own, ff_got, n_ctx,
+    ff_own, ff_got, half, n_ctx,
 ):
     rows, keys, heads = qn.shape[0], pairs.shape[0], q_up.shape[1] // 128
     span, block = keys // 4, rows // 4
@@ -1220,21 +1856,22 @@
 
     def body(
         gb_ref, qn_ref, q_up_ref, pairs_ref, l_up_ref, w_ref, cos_ref, sin_ref, pos_ref,
-        q_ref, o_ref, lse_ref, att_ref, own_ref, got_ref,
-        gp_ref, gqn_ref, at_ref, far_ref,
+        q_ref, o_ref, lse_ref, att_ref, own_ref, got_ref, half_ref,
+        gp_ref, gqn_ref, at_ref, far_ref, other_ref,
         e_ref, rope_ref, go_ref, gq_ref, dq_ref, inner_ref, mine_ref, theirs_ref, sems, load_sems,
     ):
         loads = [
-            pltpu.make_async_copy(part.at[pl.ds(13, 3)], hold, load_sems.at[i])
-            for i, (part, hold) in enumerate(((own_ref, mine_ref), (got_ref, theirs_ref)))
+            pltpu.make_async_copy(part.at[i], hold.at[k], load_sems.at[n, k])
+            for n, (part, hold) in enumerate(((own_ref, mine_ref), (got_ref, theirs_ref)))
+            for k, i in enumerate(TRADED_LAST)
         ]
         for load in loads:
             load.start()
         for load in loads:
             load.wait()
-        for k in range(3):
+        for k in range(len(TRADED_LAST)):
             add_into(mine_ref.at[k], [mine_ref.at[k], theirs_ref.at[k]], unit_rows)
-        copies = trade_away(Place(n_ctx), mine_ref, far_ref, sems)
+        copies = trade_away(Place(n_ctx), mine_ref, far_ref, sems, (half_ref, other_ref))
 
         def expand(r):
             e_ref[r] = matmul(pairs_ref[r, :KVR], l_up_ref[...]).astype(BF)
@@ -1306,10 +1943,11 @@
             shape(pairs.shape),
             shape(qn.shape),
             shape((16, first + o_rows, wide)),
-            shape((3,) + ff_own.shape[1:]),
+            shape((len(TRADED_LAST),) + ff_own.shape[1:]),
+            shape(half.shape),
         ],
-        in_specs=[VMEM] * 13 + [ANY] * 2,
-        out_specs=[VMEM] * 3 + [ANY],
+        in_specs=[VMEM] * 13 + [ANY] * 3,
+        out_specs=[VMEM] * 3 + [ANY] * 2,
         scratch_shapes=[
             pltpu.VMEM((keys, wide), BF),
             pltpu.VMEM((keys, 128), F32),
@@ -1317,10 +1955,10 @@
             pltpu.VMEM((rows, wide), BF),
             pltpu.VMEM((rows, 128), F32),
             pltpu.VMEM((rows, 128), F32),
-            pltpu.VMEM((3,) + ff_own.shape[1:], BF),
-            pltpu.VMEM((3,) + ff_own.shape[1:], BF),
-            pltpu.SemaphoreType.DMA((2, 3)),
-            pltpu.SemaphoreType.DMA((2,)),
+            pltpu.VMEM((len(TRADED_LAST),) + ff_own.shape[1:], BF),
+            pltpu.VMEM((len(TRADED_LAST),) + ff_own.shape[1:], BF),
+            pltpu.SemaphoreType.DMA((2, len(TRADED_LAST) + 1)),
+            pltpu.SemaphoreType.DMA((2, len(TRADED_LAST))),
         ],
         compiler_params=pltpu.CompilerParams(
             collective_id=number, has_side_effects=True, vmem_limit_bytes=60 << 20
@@ -1329,7 +1967,7 @@
             flops=40_000_000_000, bytes_accessed=30 << 20, transcendentals=0
         ),
         name="attend_back",
-    )(gb, qn, q_up, pairs, l_up, w_out_t, cosine, sine_table, q_pos, q, o, lse, att, ff_own, ff_got)
+    )(gb, qn, q_up, pairs, l_up, w_out_t, cosine, sine_table, q_pos, q, o, lse, att, ff_own, ff_got, half)
 
 
 def shards(
@@ -1381,45 +2019,13 @@
     starts = [0, widths[0], widths[0] + widths[1], widths[0] + widths[1] + widths[2]]
     gains = jnp.concatenate([first_gain, query_gain, latent_gain, second_gain]).astype(F32)
     gains = jnp.broadcast_to(gains[None], (8, gains.shape[0]))
-    down_shard = jnp.concatenate(
-        [
-            query_down,
-            latent_down[:, :KVR],
-            jnp.zeros((shard_rows, NOPE), BF),
-            latent_down[:, KVR:],
-            jnp.zeros((shard_rows, 128 - NOPE - ROPE), BF),
-        ],
-        axis=1,
-    )
-
-    def trade(block, k):
-        return lax.ppermute(
-            block, "ctx", [(i, (i // members ^ k) * members + i % members) for i in range(n_ctx)]
-        )
 
     def swap_tp(block):
         return lax.ppermute(block, "tp", [(0, 1), (1, 0)])
 
     wide = 640
-    ff = pack(gate_weight, up_weight, down_weight.T, wide, members)
     q_rows_w, l_rows_w, o_rows_w = query_up.shape[0], latent_up.shape[0], shard_rows // 2
     q_width, o_width = heads * (NOPE + ROPE), heads * VH
-    q_tiles = jnp.pad(
-        query_up.reshape(q_rows_w, 4, heads, NOPE + ROPE),
-        ((0, 0), (0, 0), (0, 0), (0, 128 - NOPE - ROPE)),
-    ).reshape(q_rows_w, 4, wide)
-    out_tiles = jnp.transpose(
-        out_weight.reshape(4, o_width, 2, o_rows_w), (0, 3, 2, 1)
-    ).reshape(4, o_rows_w, wide)
-    at = jnp.concatenate(
-        [
-            jnp.transpose(q_tiles, (1, 0, 2)),
-            jnp.transpose(latent_up.reshape(l_rows_w, 4, wide), (1, 0, 2)),
-            out_tiles,
-        ],
-        axis=1,
-    )
-
     x = lax.dynamic_slice_in_dim(layer_input, t * rows, rows, 0).astype(F32)
     out_grad_rows = lax.dynamic_slice_in_dim(out_grad, t * rows, rows, 0).astype(F32)
     grad_ffn = (residual_scale * out_grad_rows).astype(BF)
@@ -1438,19 +2044,60 @@
     q_cos, q_sin = rope_tiles(q_positions)
     q_pos = jnp.broadcast_to(q_positions[:, None], (q_positions.shape[0], 128))
 
-    down_full, gains, at_mine, own_near = weights_in(1, down_shard, gains, at, ff, n_ctx)
-    own_near, ff = lax.optimization_barrier((own_near, ff))
-    down_full = widen(down_full).reshape(dim, -1)
-    gains = widen(gains[:, 0]).reshape(n_ctx, -1)
-    gain_first, gain_query, gain_latent, gain_second = [
-        gains[:, s : s + w].reshape(1, -1) for s, w in zip(starts, widths)
-    ]
-    first_gains = (gain_first, gain_query, gain_latent)
-    both, _, pairs, qn_all, token_columns, own_mid, at_all = project(
-        3, x, down_full, first_gains, cosine, sine_table, ff, at_mine, n_ctx
-    )
-    own_near, own_mid = lax.optimization_barrier((own_near, own_mid))
-    oth_near, oth_mid = swap_tp(own_near), swap_tp(own_mid)
+    if members == 1:
+        (
+            both, down_full, *all_gains, pairs, qn_all, token_columns,
+            own_near, own_mid, own_last, oth_near, at_all,
+        ) = front(
+            1, x, query_down, latent_down, gains, gate_weight, up_weight, down_weight.T,
+            query_up, latent_up, out_weight.T, cosine, sine_table, widths, n_ctx,
+        )
+        gain_first, gain_query, gain_latent, gain_second = all_gains
+        first_gains = (gain_first, gain_query, gain_latent)
+    else:
+        down_shard = jnp.concatenate(
+            [
+                query_down,
+                latent_down[:, :KVR],
+                jnp.zeros((shard_rows, NOPE), BF),
+                latent_down[:, KVR:],
+                jnp.zeros((shard_rows, 128 - NOPE - ROPE), BF),
+            ],
+            axis=1,
+        )
+
+        ff = pack(gate_weight, up_weight, down_weight.T, wide, members)
+        q_tiles = jnp.pad(
+            query_up.reshape(q_rows_w, 4, heads, NOPE + ROPE),
+            ((0, 0), (0, 0), (0, 0), (0, 128 - NOPE - ROPE)),
+        ).reshape(q_rows_w, 4, wide)
+        out_tiles = jnp.transpose(
+            out_weight.reshape(4, o_width, 2, o_rows_w), (0, 3, 2, 1)
+        ).reshape(4, o_rows_w, wide)
+        at = jnp.concatenate(
+            [
+                jnp.transpose(q_tiles, (1, 0, 2)),
+                jnp.transpose(latent_up.reshape(l_rows_w, 4, wide), (1, 0, 2)),
+                out_tiles,
+            ],
+            axis=1,
+        )
+
+        down_full, gains, at_mine, own_near = weights_in(1, down_shard, gains, at, ff, n_ctx)
+        own_near, ff = lax.optimization_barrier((own_near, ff))
+        down_full = widen(down_full).reshape(dim, -1)
+        gains = widen(gains[:, 0]).reshape(n_ctx, -1)
+        gain_first, gain_query, gain_latent, gain_second = [
+            gains[:, s : s + w].reshape(1, -1) for s, w in zip(starts, widths)
+        ]
+        first_gains = (gain_first, gain_query, gain_latent)
+        both, _, pairs, qn_all, token_columns, own_mid, at_all = project(
+            3, x, down_full, first_gains, cosine, sine_table, ff, at_mine, n_ctx
+        )
+        own_last = jnp.stack([ff[i] for i in TRADED_LAST])
+        own_near, own_mid = lax.optimization_barrier((own_near, own_mid))
+        oth_near = swap_tp(own_near[:4])
+    oth_next, oth_mid = swap_tp(own_near[4:]), swap_tp(own_mid)
     lat_rope = widen(pairs).reshape(-1, KVR + 128)
     if members > 1:
         at_all = widen(at_all).reshape(n_ctx, -1, wide)
@@ -1465,37 +2112,43 @@
             axis=1,
         )
     branch_part, queries, attended_wide, log_total, attended, q_up, l_up, w_out_t, own_far = attend(
-        5, qn_all.reshape(-1, qr), at_all, lat_rope, q_cos, q_sin, q_pos, ff, o_width, n_ctx
+        5, qn_all.reshape(-1, qr), at_all, lat_rope, q_cos, q_sin, q_pos, own_last, o_width, n_ctx
     )
     qn_all = qn_all.reshape(-1, qr)
 
-    middle, ns_all, gf_all = branch_and_norm(
-        4, branch_part, x, gain_second, grad_ffn, n_ctx
-    )
-    ns_all, gf_all = ns_all.reshape(-1, dim), gf_all.reshape(-1, dim)
-    oth_far = swap_tp(own_far)
-    own = [own_near, own_mid, own_far]
-    oth = [oth_near, oth_mid, oth_far]
-    ns_all, oth = lax.optimization_barrier((ns_all, oth))
-    if members > 1:
-        own, oth = [
-            [widen(jnp.concatenate(w)).reshape(16, dim // 16, wide)] for w in (own, oth)
-        ]
     order = (0,) + TRADED_FIRST + TRADED_NEXT + TRADED_LAST
-    ffn_part, second_part, grads_own, grads_oth = feed_forward(
-        ns_all, gf_all, own, oth, order, units, members
-    )
-    grads_own = narrow(grads_own.reshape(16, members, shard_rows, wide))
-    grads_oth = narrow(grads_oth.reshape(16, members, shard_rows, wide))
-    grads_got = swap_tp(grads_oth)
-    grad_middle, second_gain_part, gb_all, out_half = norm_and_branch_back(
-        6, second_part, ffn_part, middle, out_grad_rows, gain_second, n_ctx
-    )
+    if members == 1:
+        middle, ns_all, gf_all, acts, second_part, ffn_part = forward(
+            4, branch_part, x, gain_second, grad_ffn, [own_near, own_mid], [oth_near, oth_next, oth_mid],
+            own_far, order, units, n_ctx,
+        )
+        grad_middle, second_gain_part, gb_all, out_half, grads_own, grads_got = backward(
+            6, second_part, ffn_part, ns_all, gf_all, acts, middle, out_grad_rows, gain_second,
+            units, wide, n_ctx,
+        )
+    else:
+        middle, ns_all, gf_all = branch_and_norm(
+            4, branch_part, x, gain_second, grad_ffn, n_ctx
+        )
+        ns_all, gf_all = ns_all.reshape(-1, dim), gf_all.reshape(-1, dim)
+        oth_far = swap_tp(own_far)
+        own = [own_near, own_mid, own_far]
+        oth = [oth_near, oth_next, oth_mid, oth_far]
+        ns_all, oth = lax.optimization_barrier((ns_all, oth))
+        own, oth = [[widen(jnp.concatenate(w)).reshape(16, dim // 16, wide)] for w in (own, oth)]
+        ffn_part, second_part, grads_own, grads_oth = feed_forward(
+            ns_all, gf_all, own, oth, order, units, members
+        )
+        grads_own = narrow(grads_own.reshape(16, members, shard_rows, wide))
+        grads_oth = narrow(grads_oth.reshape(16, members, shard_rows, wide))
+        grads_got = swap_tp(grads_oth)
+        grad_middle, second_gain_part, gb_all, out_half = norm_and_branch_back(
+            6, second_part, ffn_part, middle, out_grad_rows, gain_second, n_ctx
+        )
     gb_all, grads_got = lax.optimization_barrier((gb_all, grads_got))
-    out_other = swap_tp(out_half)
-    grad_pairs, gqn_part, at_part, sums_far = attend_back(
+    grad_pairs, gqn_part, at_part, sums_far, out_other = attend_back(
         7, gb_all.reshape(-1, dim), qn_all, q_up, lat_rope, l_up, w_out_t, q_cos, q_sin, q_pos,
-        queries, attended_wide, log_total, attended, grads_own, grads_got, n_ctx,
+        queries, attended_wide, log_total, attended, grads_own, grads_got, out_half, n_ctx,
     )
     if members > 1:
         q_part = at_part[:, : qr // 16].reshape(n_ctx, q_rows_w, wide)
@@ -1506,7 +2159,7 @@
         at_part = narrow(
             jnp.concatenate([q_part, l_part, o_part], axis=1).reshape(16, members, -1, wide)
         )
-    at_sums, sums, both_all, input_half, input_other, gain_sums = wind_up(
+    at_sums, sums, down_sum, input_half, input_other, gain_sums = wind_up(
         8,
         narrow(grad_pairs.reshape(16, members, 2, rows, KVR + 128)),
         gqn_part.reshape(8, rows, qr),
@@ -1521,27 +2174,12 @@
         sine_table,
         grads_own,
         grads_got,
+        token_columns,
         widths,
         n_ctx,
     )
-    both_all, out_other = lax.optimization_barrier((both_all, out_other))
-    down_part = matmul_tn(
-        token_columns.reshape(16 * rows, dim // 16), both_all.reshape(16 * rows, -1)
-    ).astype(BF)
     if members > 1:
-        down_part = lax.psum_scatter(
-            down_part.astype(F32), "ctx", axis_index_groups=member_lists, tiled=True
-        ).astype(BF)
-    down_other = swap_tp(down_part)
-
-    def in_order(mine, other):
-        return jnp.where(
-            t == 0, jnp.concatenate([mine, other]), jnp.concatenate([other, mine])
-        )
-
-    layer_output = in_order(out_half, out_other)
-    input_grad = in_order(input_half, input_other).astype(F32)
-    down_grads = down_part.astype(F32) + down_other.astype(F32)
+        down_sum = lax.psum_scatter(down_sum, "ctx", axis_index_groups=member_lists, tiled=True)
     gain_grads = gain_sums[0]
     if members > 1:
         gain_grads = lax.psum_scatter(
@@ -1551,26 +2189,45 @@
         gain_grads[s : s + w] for s, w in zip(starts, widths)
     ]
 
-    gate_weight_grad, up_weight_grad, down_grad_t = spread([sums, sums_far], units, members)
-    query_up_grad = jnp.transpose(
-        at_sums[:, :q_rows_w].reshape(4, q_rows_w, heads, 128)[..., : NOPE + ROPE], (1, 0, 2, 3)
-    ).reshape(q_rows_w, 4 * q_width)
-    latent_up_grad = jnp.transpose(at_sums[:, q_rows_w : q_rows_w + l_rows_w], (1, 0, 2)).reshape(
-        l_rows_w, 4 * wide
+    layer_output, input_grad, *spread_out = spread(
+        [sums, sums_far],
+        TRADED_BACK + TRADED_LAST,
+        at_sums,
+        down_sum,
+        [out_half, out_other, input_half, input_other],
+        units,
+        members,
     )
-    out_weight_grad = jnp.transpose(
-        at_sums[:, q_rows_w + l_rows_w :].reshape(4, o_rows_w, 2, o_width), (0, 3, 2, 1)
-    ).reshape(4 * o_width, shard_rows)
+    gate_weight_grad, up_weight_grad, down_grad_t = spread_out[:3]
+    if members == 1:
+        query_up_grad, latent_up_grad, out_grad_t, query_down_grad, latent_down_grad = spread_out[3:]
+        out_weight_grad = out_grad_t.T
+    else:
+        query_up_grad = jnp.transpose(
+            at_sums[:, :q_rows_w].reshape(4, q_rows_w, heads, 128)[..., : NOPE + ROPE], (1, 0, 2, 3)
+        ).reshape(q_rows_w, 4 * q_width)
+        latent_up_grad = jnp.transpose(at_sums[:, q_rows_w : q_rows_w + l_rows_w], (1, 0, 2)).reshape(
+            l_rows_w, 4 * wide
+        )
+        out_weight_grad = jnp.transpose(
+            at_sums[:, q_rows_w + l_rows_w :].reshape(4, o_rows_w, 2, o_width), (0, 3, 2, 1)
+        ).reshape(4 * o_width, shard_rows)
+        query_down_grad = down_sum[:, :qr]
+        latent_down_grad = jnp.concatenate(
+            [
+                down_sum[:, qr : qr + KVR],
+                down_sum[:, qr + KVR + NOPE : qr + KVR + NOPE + ROPE],
+            ],
+            axis=1,
+        )
     return (
         layer_output,
         input_grad,
         first_gain_grad,
-        down_grads[:, :qr],
+        query_down_grad,
         query_gain_grad,
         query_up_grad.astype(F32),
-        jnp.concatenate(
-            [down_grads[:, qr : qr + KVR], down_grads[:, qr + KVR + NOPE : qr + KVR + NOPE + ROPE]], axis=1
-        ),
+        latent_down_grad,
         latent_gain_grad,
         latent_up_grad.astype(F32),
         out_weight_grad.astype(F32),

time: 591 us -> 535 us (0.905)
  the two profiles are of different devices: /device:TPU:3 before, /device:TPU:11 now
where the time goes in v6:
time: 535 us; the launch traced here: 525 us
  Pallas kernels  505 us (94%)
  local copies, waits for them, and re-layouts  7.65 us (1%)
  other arithmetic  7.02 us (1%)
    pallas_call x4, Pallas kernels, comm_call(): pl.pallas_call(body, out_shape=outs, in_specs=in_specs, out_specs=out_spe...  419 us
    pallas_call x1, Pallas kernels, attend_back(): pl.pallas_call(body, out_shape=[shape(pairs.shape), shape(qn.shape), shap...  40 us
    pallas_call x1, Pallas kernels, attend(): pl.pallas_call(body, out_shape=[shape((rows, dim)), shape((rows, wide)),...  37.2 us
  transfers between devices with their start and end apart: 2, of which 0 were waited for; matrix products, arithmetic and copies ran while one was open for 1% of the time, Pallas kernels for 7%

profile of v6, /device:TPU:11, one launch (start us, length us, event | category | flops | bytes accessed | tf_op | source)
XLA Modules:
  0.0 524.7 jit_solution(6873300251144326558)
XLA Ops:
  0.7 0.8 multiply_sine_fusion.1
  1.5 1.9 dynamic-slice_convert_fusion.1.x_ref
  3.4 0.8 maximum_convert_fusion
  4.1 0.6 broadcast_in_dim.4.gains_ref
  4.7 131.6 %front.1 = (f32[64,1152]{1,0:T(8,128)}, bf16[2560,1152]{1,0:T(8,128)(2,1)}, f32[1,2560]{1,0:T(1,128)}, f32[1,768]{1,0:T(1,128)}, f32[1,256]{1,0:T(1,128)}, /*ind...) custom-call(f32[64,2560]{1,0:T(8,128)} %dynamic-slice_convert_fusion, ...), custom_call_target="tpu_custom_call" | custom-call | tf_op jit(solution)/shard_map/front/pallas_call | solution.py:421
  136.4 1.1 slice.32
  137.5 3.4 collective-permute-start
  141.0 0.1 collective-permute-start.1
  141.1 0.1 add.117
  141.2 1.8 multiply_sine_fusion
  143.0 0.8 broadcast_in_dim.5.pos_ref
  143.8 37.2 %attend.1 = (bf16[512,2560]{1,0:T(8,128)(2,1)}, bf16[512,640]{1,0:T(8,128)(2,1)}, f32[512,640]{1,0:T(8,128)}, f32[512,640]{1,0:T(8,128)}, bf16[512,320]{1,0:T(8,...) custom-call(bf16[512,768]{1,0:T(8,128)(2,1)} %bitcast.29, ...), custom_call_target="tpu_custom_call" | custom-call | flops 20000000000 | bytes 20971520 | tf_op jit(solution)/shard_map/attend/pallas_call | solution.py:1818
  181.1 0.8 multiply_convert_fusion.gf_ref
  181.9 0.9 dynamic-slice_convert_fusion.out_grad_ref
  182.8 0.8 copy-done.2
  183.6 0.3 copy-done
  183.8 88.9 %forward.1 = (f32[64,2560]{1,0:T(8,128)}, bf16[1024,2560]{1,0:T(8,128)(2,1)}, bf16[1024,2560]{1,0:T(8,128)(2,1)}, bf16[1024,1536]{1,0:T(8,128)(2,1)}, bf16[1024,...) custom-call(bf16[8,64,2560]{2,1,0:T(8,128)(2,1)} %bitcast.17, f32[64,2560]{1,0:T(8,128)} %dynamic-slice_convert_fusion.1.x_ref, ...), custom_call_target="tpu_custom_call" | custom-call | tf_op jit(solution)/shard_map/forward/pallas_call | solution.py:421
  272.8 91.0 %backward.1 = (f32[64,2560]{1,0:T(8,128)}, f32[8,2560]{1,0:T(8,128)}, bf16[8,64,2560]{2,1,0:T(8,128)(2,1)}, bf16[64,2560]{1,0:T(8,128)(2,1)}, bf16[16,160,640]{2...) custom-call(bf16[1024,2560]{1,0:T(8,128)(2,1)} %get-tuple-element.82.gs_hbm, bf16[1024,2560]{1,0:T(8,128)(2,1)} %get-tuple-element.83.ffn_hbm, ...), custom_call_target="tpu_custom_call" | custom-call | tf_op jit(solution)/shard_map/backward/pallas_call | solution.py:421
  363.8 40.0 %attend_back.1 = (bf16[2048,384]{1,0:T(8,128)(2,1)}, bf16[512,768]{1,0:T(8,128)(2,1)}, bf16[16,144,640]{2,1,0:T(8,128)(2,1)}, bf16[5,160,640]{2,1,0:T(8,128)(2,1)}, bf16[64,2560]{1,0:T(8,128)(2,1)}) custom-call(bf16[512,2560]{1,0:T(8,128)(2,1)} %bitcast.24, bf16[512,768]{1,0:T(8,128)(2,1)} %bitcast.30, bf16[768,640]{1,0:T(8,128)(2,1)} %get-tuple-element.92.q_up_ref, ...), custom_call_target="tpu_custom_call" | custom-call | flops 40000000000 | bytes 31457280 | tf_op jit(solution)/shard_map/attend_back/pallas_call | solution.py:1940
  403.8 107.1 %wind_up.1 = (bf16[4,144,640]{2,1,0:T(8,128)(2,1)}, bf16[11,160,640]{2,1,0:T(8,128)(2,1)}, f32[160,1152]{1,0:T(8,128)}, bf16[64,2560]{1,0:T(8,128)(2,1)}, bf16[64,2560]{1,0:T(8,128)(2,1)}, /*index=5*/f32[16,384]{1,0:T(8,128)}) custom-call(bf16[16,2,64,384]{3,2,1,0:T(8,128)(2,1)} %bitcast.18, bf16[8,64,768]{2,1,0:T(8,128)(2,1)} %bitcast.20, ...), custom_call_target="tpu_custom_call" | custom-call | tf_op jit(solution)/shard_map/wind_up/pallas_call | solution.py:421
  510.9 1.3 slice_bitcast_fusion
  512.2 1.3 slice_bitcast_fusion.1
  513.4 1.4 fusion.10
  514.8 9.4 %spread.1 = (bf16[128,2560]{1,0:T(8,128)(2,1)}, f32[128,2560]{1,0:T(8,128)}, f32[160,3200]{1,0:T(8,128)}, f32[160,3200]{1,0:T(8,128)}, f32[160,3200]{1,0:T(8,128...) custom-call(s32[1]{0:T(128)} %bitcast.g_ref, ...), custom_call_target="tpu_custom_call" | custom-call | flops 1000000000 | bytes 20971520 | tf_op jit(solution)/shard_map/spread/pallas_call | solution.py:827
  (11 shorter events, 0.1 us)
Async XLA Ops:
  137.5 45.2 %collective-permute-start = (bf16[3,160,640]{2,1,0:T(8,128)(2,1)S(1)}, bf16[3,160,640]{2,1,0:T(8,128)(2,1)S(1)}, u32[]{:S(2)}, u32[]{:S(2)}) collective-permute-start(bf16[3,160,640]{2,1,0:T(8,128)(2,1)S(1)} %slice.32), channel_id=1, source_target_pairs={{0,1},{1,0},{2,3},{3,2},{4,5},{5,4},{6,7},{7,6},{8,9},{9,8},{10,11... | collective-permute-start | bytes 1843208 | tf_op jit(solution)/shard_map/ppermute | solution.py:2024
  141.0 41.8 %collective-permute-start.1 = (bf16[4,160,640]{2,1,0:T(8,128)(2,1)}, bf16[4,160,640]{2,1,0:T(8,128)(2,1)S(1)}, u32[]{:S(2)}, u32[]{:S(2)}) collective-permute-start(bf16[4,160,640]{2,1,0:T(8,128)(2,1)} %get-tuple-element.79.refs_1_), channel_id=1, source_target_pairs={{0,1},{1,0},{2,3},{3,2},{4,5},{5,4},{6,7},{7,6},{8,9},{9,8},{10,11... | collective-permute-start | bytes 2457608 | tf_op jit(solution)/shard_map/ppermute | solution.py:2024
  143.8 37.2 %copy-start.1 = (bf16[128,2560]{1,0:T(8,128)(2,1)S(1)}, bf16[128,2560]{1,0:T(8,128)(2,1)}, u32[]{:S(2)}) copy-start(bf16[128,2560]{1,0:T(8,128)(2,1)} %param.27) | copy-start | bytes 1966084
  182.7 0.8 copy-start.2
  182.7 1.1 copy-start

commit v7 on v6

--- a/solution.py
+++ b/solution.py
@@ -75,7 +75,7 @@
 OFFSETS = (0, -1, 1, -2, 2, -3, 3)
 
 
-TRADED_FIRST, TRADED_NEXT, TRADED_LAST = (1, 8, 2, 9, 3, 12), (10, 11, 6, 7), (13, 14, 15, 4, 5)
+TRADED_FIRST, TRADED_NEXT, TRADED_LAST = (1, 8, 9, 12, 13), (11, 5, 6, 7), (14, 15, 10, 2, 3, 4)
 TRADED_BACK = (0,) + TRADED_FIRST + TRADED_NEXT
 
 
@@ -194,18 +194,17 @@
     pl.semaphore_wait(barrier, count)
 
 
-def trade_away(place, src, out, sems, swap=None):
+def trade_away(place, src, out, sems, swaps):
     barrier = pltpu.get_barrier_semaphore()
     count = len(TRADED_LAST)
     devices = [((place.g ^ i) * place.members + place.m, place.t) for i in TRADED_LAST]
     pairs = [(src.at[k], out.at[k]) for k in range(count)]
-    if swap is not None:
-        devices.append(place.other())
-        pairs.append(swap)
-        count += 1
+    devices.append(place.other())
+    pairs += swaps
     for device in devices:
         pl.semaphore_signal(barrier, inc=1, device_id=device, device_id_type=MESH)
-    pl.semaphore_wait(barrier, count)
+    pl.semaphore_wait(barrier, count + 1)
+    devices += [place.other()] * (len(swaps) - 1)
     copies = [
         pltpu.make_async_remote_copy(
             *pairs[k],
@@ -214,7 +213,7 @@
             device_id=devices[k],
             device_id_type=MESH,
         )
-        for k in range(count)
+        for k in range(len(pairs))
     ]
     for copy in copies:
         copy.start()
@@ -498,7 +497,7 @@
             keep = pltpu.make_async_copy(ff_ref.at[0], near.at[0], net.sem())
             keep.start()
             out = lambda i: near.at[1 + TRADED_FIRST.index(i)]
-            timed = ((1, 1), (8, 4), (9, 12), (2, 18), (12, 20), (3, 24))
+            timed = [(i, 3 * n) for n, i in enumerate(TRADED_FIRST)]
             yield from trade_sends(net, lambda i: ff_ref.at[i], out, ff_sems, timed)
             yield 60.0
             trade_receives(net, out, ff_sems, TRADED_FIRST)
@@ -540,10 +539,10 @@
 
 
 def front(
-    number, x, query_down, latent_down, gains, gate, up, down_t, query_up, latent_up, out_t,
+    number, layer_input, query_down, latent_down, gains, gate, up, down_t, query_up, latent_up, out_t,
     cosine, sine_table, widths, n_ctx,
 ):
-    rows, dim = x.shape
+    rows, dim = layer_input.shape[0] // 2, layer_input.shape[1]
     shard, qr = query_down.shape
     wide = qr + KVR + 128
     units = gate.shape[1] // 16
@@ -555,13 +554,14 @@
     def body(
         x_ref, qd_ref, ld_ref, gains_ref, gate_ref, up_ref, down_ref, qu_ref, lu_ref, ow_ref,
         cos_ref, sin_ref,
-        both, down_out, g1, gq, gl, g2, pairs, queries, columns, first, mid, last,
+        both, x_out, down_out, g1, gq, gl, g2, pairs, queries, columns, first, mid, last,
         other_first, heads_out,
-        down_block, downs, gain_blocks, ff, at, normed, column_blocks, pair, query_block,
+        down_block, downs, gain_blocks, ff, at, normed, pair, query_block,
         heads_mine,
-        at_sems, x_sems, tp_sems, keep_sems, col_sems, ff_sems, other_sems, sems,
+        at_sems, x_sems, tp_sems, keep_sems, ff_sems, other_sems, sems,
     ):
         p = Place(n_ctx)
+        x_out[...] = x_ref[pl.ds(pl.multiple_of(p.t * rows, rows), rows)].astype(F32)
         down_block[:, :qr] = qd_ref[...]
         down_block[:, qr : qr + KVR] = ld_ref[:, :KVR]
         none = jnp.zeros((shard, NOPE), BF)
@@ -616,9 +616,9 @@
                 net.send(src, lambda: other_first.at[k], other_sems.at[k], p.other)
 
             onward(0, lambda: ff.at[0])
-            timed = ((1, 3), (8, 5), (2, 12), (9, 30), (3, 34), (12, 38))
+            timed = ((1, 3), (8, 5), (9, 12), (12, 30), (13, 38))
             yield from trade_sends(net, block, first_out, ff_sems, timed)
-            timed = [each for each in ((10, 49), (6, 57), (11, 62), (7, 70)) if each[0] in TRADED_NEXT]
+            timed = ((5, 44), (11, 49), (6, 57), (7, 62))
             for k, i in enumerate(TRADED_FIRST[:3]):
                 yield 42.0 + 3 * k
                 trade_receives(net, first_out, ff_sems, (i,))
@@ -676,25 +676,6 @@
                     net.recv(lambda: heads_out.at[place(q, side)], tp_sems.at[side, q], ~owner)
                 pl.when(owner)(lambda: keep_head(q).wait())
 
-        def send_columns():
-            for n in range(16):
-                column_blocks[n] = normed[:, n * shard : (n + 1) * shard]
-            keep = pltpu.make_async_copy(column_blocks.at[p.g], columns.at[p.g], net.sem())
-            keep.start()
-            for k in range(1, 16):
-                if k % 4 == 1:
-                    yield 56.0 + k
-                net.send(
-                    lambda k=k: column_blocks.at[p.g ^ k],
-                    lambda: columns.at[p.g],
-                    col_sems.at[k],
-                    lambda k=k: ((p.g ^ k) * p.members + p.m, p.t),
-                )
-            yield 88.0
-            for k in range(1, 16):
-                net.recv(lambda k=k: columns.at[p.g ^ k], col_sems.at[k])
-            keep.wait()
-
         def latents():
             sem = net.sem()
             net.send(lambda: pair.at[p.t], lambda: pair.at[p.t], sem, p.other)
@@ -711,16 +692,18 @@
                 for n in range(16):
                     out[:, n * w : (n + 1) * w] = gain_blocks[n, :1, at_lane : at_lane + w]
                 at_lane += w
-            values = x_ref[...]
+            values = x_out[...]
             normed[...] = (values * norm_factor(values) * g1[...]).astype(BF)
             both[...] = matmul(normed[...], downs[...])
             query, latent = both[:, :qr], both[:, qr : qr + KVR]
             query_block[...] = (query * norm_factor(query) * gq[...]).astype(BF)
             pair[p.t, :, :KVR] = (latent * norm_factor(latent) * gl[...]).astype(BF)
             pair[p.t, :, KVR:] = turn(both[:, qr + KVR :], cos_ref[...], sin_ref[...]).astype(BF)
-            yield from together(
-                latents(), gather_steps(net, query_block, queries, 8, 51, 2.2), send_columns()
-            )
+            tasks = together(latents(), gather_steps(net, query_block, queries, 8, 51, 2.2))
+            yield next(tasks)
+            for n in range(16):
+                columns[n] = normed[:, n * shard : (n + 1) * shard]
+            yield from tasks
             keep.wait()
 
         run_together(
@@ -736,11 +719,12 @@
         "front",
         number,
         body,
-        [x, query_down, latent_down, gains, gate, up, down_t, query_up, latent_up, out_t]
+        [layer_input, query_down, latent_down, gains, gate, up, down_t, query_up, latent_up, out_t]
         + [cosine, sine_table],
         [VMEM] * 12,
         [
             shape((rows, wide), F32),
+            shape((rows, dim), F32),
             shape((dim, wide)),
             *[shape((1, 16 * w), F32) for w in widths],
             shape((16, 2, rows, KVR + 128)),
@@ -752,7 +736,7 @@
             shape((4,) + ff_shape),
             shape((16, at_rows, lanes)),
         ],
-        [VMEM, ANY] + [VMEM] * 4 + [ANY] * 8,
+        [VMEM, VMEM, ANY] + [VMEM] * 4 + [ANY] * 2 + [VMEM] + [ANY] * 5,
         [
             pltpu.VMEM((shard, wide), BF),
             pltpu.VMEM((dim, wide), BF),
@@ -760,7 +744,6 @@
             pltpu.VMEM((16,) + ff_shape, BF),
             pltpu.VMEM((4, at_rows, lanes), BF),
             pltpu.VMEM((rows, dim), BF),
-            pltpu.VMEM((16, rows, shard), BF),
             pltpu.VMEM((2, rows, KVR + 128), BF),
             pltpu.VMEM((rows, qr), BF),
             pltpu.VMEM((8, at_rows, lanes), BF),
@@ -770,41 +753,51 @@
             pltpu.SemaphoreType.DMA((8,)),
             pltpu.SemaphoreType.DMA((16,)),
             pltpu.SemaphoreType.DMA((16,)),
-            pltpu.SemaphoreType.DMA((16,)),
         ],
         300,
     )
 
 
-def head_grads_steps(net, at_ref, at_out, at_x, at_tp, x_sems, tp_sems, rows, start):
+def head_grads_steps(net, at_ref, o_ref, o_got, at_out, at_x, at_tp, x_sems, tp_sems, start):
     p = net.place
     owner = p.d == p.t
     f = p.a * 2 + p.d
+    rows, o_rows = at_ref.shape[1], o_ref.shape[1]
     place = lambda q, side: (q // 2 * 2 + (1 - p.b if side else p.b)) * 2 + q % 2
     for side in (1, 0):
         for q in range(8):
             net.send(
                 lambda q=q, side=side: at_ref.at[place(q, side)],
-                lambda q=q, side=side: at_tp.at[side, q],
+                lambda q=q, side=side: at_tp.at[side, q, pl.ds(0, rows)],
                 tp_sems.at[side, q],
                 p.other,
                 ~owner,
             )
+
+    def join(side, q):
+        here = at_tp.at[side, q, pl.ds(0, rows)]
+        net.recv(lambda: here, tp_sems.at[side, q], owner)
+
+        def add():
+            n = place(q, side)
+            add_into(here, [here, at_ref.at[n]], rows)
+            add_into(at_tp.at[side, q, pl.ds(rows, o_rows)], [o_ref.at[n], o_got.at[n]], o_rows)
+
+        pl.when(owner)(add)
+
     for q in range(8):
-        yield start + 4 + 2 * (q + 1)
-        here = at_tp.at[1, q]
-        net.recv(lambda: here, tp_sems.at[1, q], owner)
-        pl.when(owner)(lambda: add_into(here, [here, at_ref.at[place(q, 1)]], rows))
+        yield start + 2 + q
+        join(1, q)
         net.send(
-            lambda here=here: here, lambda q=q: at_x.at[q], x_sems.at[0, q], p.across, owner
+            lambda q=q: at_tp.at[1, q], lambda q=q: at_x.at[q], x_sems.at[0, q], p.across, owner
         )
     keep = pltpu.make_async_copy(at_tp.at[0, f], at_out.at[p.a], net.sem())
     for q in range(8):
-        yield start + 20 + 2 * (q + 1)
+        yield start + 11 + 2 * q
+        join(0, q)
         here, near = at_tp.at[0, q], at_x.at[q]
-        net.recv(lambda: here, tp_sems.at[0, q], owner)
         net.recv(lambda: near, x_sems.at[0, q], owner)
-        pl.when(owner)(lambda: add_into(here, [here, near, at_ref.at[place(q, 0)]], rows))
+        pl.when(owner)(lambda: add_into(here, [here, near], rows + o_rows))
         net.send(
             lambda here=here: here,
             lambda: at_out.at[p.a],
@@ -813,7 +806,7 @@
             owner & (f != q),
         )
         pl.when(owner & (f == q))(lambda: keep.start())
-    yield start + 60
+    yield start + 55
     for s in range(4):
         net.recv(lambda s=s: at_out.at[s], x_sems.at[1, s], ~(owner & (p.a == s)))
     pl.when(owner)(lambda: keep.wait())
@@ -1133,8 +1126,8 @@
 
 
 def wind_up(
-    number, pairs, queries, at, both, x, grad_middle, down, gains, second, cosine, sine_table,
-    ff_own, ff_got, columns, widths, n_ctx,
+    number, pairs, queries, at, at_o, at_o_got, both, x, grad_middle, down, gains, second, cosine,
+    sine_table, ff_own, ff_got, columns, widths, n_ctx,
 ):
     rows, dim = x.shape
     wide = down.shape[1]
@@ -1145,7 +1138,7 @@
     traded = TRADED_FIRST + TRADED_NEXT
 
     def body(
-        pairs_ref, queries_ref, at_ref, both_ref, x_ref, middle_ref, down_hbm,
+        pairs_ref, queries_ref, at_ref, o_ref, o_got, both_ref, x_ref, middle_ref, down_hbm,
         g1_ref, gq_ref, gl_ref, second_ref, cos_ref, sin_ref, columns_ref, own_ref, got_ref,
         at_out, ff_out, down_sum, input_half, input_other, gains_out,
         own_hold, ff_sum, at_x, at_tp, core_in, tp_in, pair_sum, query_sum, grad_both, gain_blocks, gain_tp,
@@ -1208,10 +1201,8 @@
                 return block(i)
 
             out = lambda i: ff_out.at[TRADED_BACK.index(i)]
-            timed = ((8, 1), (2, 2), (3, 6), (9, 10), (12, 19), (6, 22), (1, 23), (7, 26))
-            for i, when_to in timed + ((10, 28), (11, 37)):
-                if i not in traded:
-                    continue
+            timed = ((8, 1), (5, 2), (9, 10), (6, 12), (12, 19), (7, 22), (1, 23), (13, 28), (11, 37))
+            for i, when_to in timed:
                 yield when_to
                 joined(i)
                 yield from trade_sends(net, block, out, ff_sems, ((i, when_to),))
@@ -1283,7 +1274,7 @@
             after(
                 3.5,
                 head_grads_steps(
-                    net, at_ref, at_out, at_x, at_tp, x_sems, tp_sems, at.shape[1], 12
+                    net, at_ref, o_ref, o_got, at_out, at_x, at_tp, x_sems, tp_sems, 12
                 ),
             ),
             trades(),
@@ -1292,11 +1283,12 @@
 
     lanes = pairs.shape[3]
     gain_lanes = members * sum(widths)
+    at_rows = at.shape[1] + at_o.shape[1]
     scratch = [
         pltpu.VMEM((len(TRADED_BACK),) + ff_own.shape[1:], BF),
         pltpu.VMEM((len(TRADED_BACK),) + ff_own.shape[1:], BF),
-        pltpu.VMEM((8,) + at.shape[1:], BF),
-        pltpu.VMEM((2, 8) + at.shape[1:], BF),
+        pltpu.VMEM((8, at_rows) + at.shape[2:], BF),
+        pltpu.VMEM((2, 8, at_rows) + at.shape[2:], BF),
         pltpu.VMEM((8, 2, rows, lanes), BF),
         pltpu.VMEM((8, rows, lanes), BF),
         pltpu.VMEM((rows, lanes), F32),
@@ -1322,11 +1314,11 @@
         "wind_up",
         number,
         body,
-        [pairs, queries, at, both, x, grad_middle, down, *gains, second, cosine, sine_table]
-        + [columns, ff_own, ff_got],
-        [VMEM] * 6 + [ANY] + [VMEM] * 7 + [ANY] * 2,
+        [pairs, queries, at, at_o, at_o_got, both, x, grad_middle, down, *gains, second, cosine]
+        + [sine_table, columns, ff_own, ff_got],
+        [VMEM] * 8 + [ANY] + [VMEM] * 7 + [ANY] * 2,
         [
-            shape((4,) + at.shape[1:]),
+            shape((4, at_rows) + at.shape[2:]),
             shape((len(TRADED_BACK),) + ff_own.shape[1:]),
             shape((dim // 16, wide), F32),
             shape((rows, dim)),
@@ -1455,25 +1447,29 @@
                 into[cut, at : at + lanes] = part
 
 
-def forward(number, parts, x, gain, gf, own, oth, own_last, order, units, n_ctx):
+def forward(number, parts, x, gain, gf, own, oth, late, order, units, n_ctx):
     rows, dim = x.shape
-    tokens, shard, wide = 16 * rows, own_last.shape[1], own_last.shape[2]
+    tokens, shard = 16 * rows, late[0].shape[1]
     lanes = 256
     both = 2 * lanes
     parts = parts.reshape(8, rows, dim)
-    n_own, n_oth, n_last = len(own), len(oth), own_last.shape[0]
+    n_own, n_oth, n_late = len(own), len(oth), len(late)
+    late_places = [(a, k) for a, w in enumerate(late) for k in range(w.shape[0])]
+    n_last = len(late_places)
     own_places, oth_places = [
         [(a, k) for a, w in enumerate(side) for k in range(w.shape[0])] for side in (own, oth)
     ]
     n_early = len(own_places)
 
     def body(parts_ref, x_ref, gain_ref, gf_ref, *refs):
-        own_refs, oth_refs, last_ref = refs[:n_own], refs[n_own : n_own + n_oth], refs[n_own + n_oth]
-        middle, ns_out, gf_out, acts_out, gs_out, ffn_out = refs[n_own + n_oth + 1 :][:6]
+        own_refs, oth_refs = refs[:n_own], refs[n_own : n_own + n_oth]
+        late_refs, refs = refs[n_own + n_oth :][:n_late], refs[n_own + n_oth + n_late :]
+        middle, ns_out, gf_out, acts_out, gs_out, ffn_out = refs[:6]
+        last_block = lambda k: late_refs[late_places[k][0]].at[late_places[k][1]]
         (
             branch, normed, ns_ref, gf_all, acts_ref, gs_ref, ffn_ref, wgu_ref, wd_ref, other_last,
             near, line_in, line_out, last_sems, out_sems, sems,
-        ) = refs[n_own + n_oth + 7 :]
+        ) = refs[6:]
         p = Place(n_ctx)
         greet(p, line=True, across=True, core=True, other=True)
         net = Net(p, sems)
@@ -1481,7 +1477,7 @@
         def weights():
             for k in range(n_last):
                 net.send(
-                    lambda k=k: last_ref.at[k],
+                    lambda k=k: last_block(k),
                     lambda k=k: other_last.at[k],
                     last_sems.at[k],
                     p.other,
@@ -1492,12 +1488,12 @@
             unit_weights(
                 p.g, (own_block, oth_block), order[:n_early], units, shard, lanes, wgu_ref, wd_ref
             )
-            yield 30.5
+            yield 38.0
             for k in range(n_last):
                 net.recv(lambda k=k: other_last.at[k], last_sems.at[k])
             unit_weights(
                 p.g,
-                (lambda k: last_ref[k], lambda k: other_last[k]),
+                (lambda k: last_block(k)[...], lambda k: other_last[k]),
                 order[n_early:],
                 units,
                 shard,
@@ -1559,7 +1555,7 @@
             store.wait()
         net.finish()
 
-    ins = [parts, x, gain, gf, *own, *oth, own_last]
+    ins = [parts, x, gain, gf, *own, *oth, *late]
     return comm_call(
         "forward",
         number,
@@ -1585,7 +1581,7 @@
             pltpu.VMEM((tokens, dim), BF),
             pltpu.VMEM((dim, 2 * both), BF),
             pltpu.VMEM((dim, both), BF),
-            pltpu.VMEM(own_last.shape, BF),
+            pltpu.VMEM((n_last,) + late[0].shape[1:], BF),
         ]
         + reduce_scratch(rows, dim, 8)
         + [pltpu.SemaphoreType.DMA((n_last,)), pltpu.SemaphoreType.DMA((4, 5))],
@@ -1593,20 +1589,20 @@
     )
 
 
-def backward(number, gs, ffn, ns, gf, acts, middle, out_grad, gain, units, wide, n_ctx):
+def backward(number, gs, ffn, ns, gf, acts, middle, out_grad, gain, columns, units, wide, n_ctx):
     rows, dim = middle.shape
     tokens, shard = 16 * rows, dim // 16
     lanes = 256
     both = 2 * lanes
 
     def body(
-        gs_hbm, ffn_hbm, ns_hbm, gf_hbm, acts_hbm, middle_ref, out_grad_ref, gain_ref,
-        grad_middle, gain_part, branches, output, own_out, got_out,
+        gs_hbm, ffn_hbm, ns_hbm, gf_hbm, acts_hbm, middle_ref, out_grad_ref, gain_ref, col_ref,
+        grad_middle, gain_part, branches, output, own_out, got_out, col_out,
         upstream, branch, ffn_sum, gs_ref, ffn_ref, ns_ref, gf_ref, acts_ref, own, oth,
         *rest,
     ):
         rest = list(rest)
-        sems, other_sems, own_sems, load_sems = [rest.pop() for _ in range(4)]
+        sems, col_sems, other_sems, own_sems, load_sems = [rest.pop() for _ in range(5)]
         pairs = (
             (gs_hbm, gs_ref), (ffn_hbm, ffn_ref), (ns_hbm, ns_ref), (acts_hbm, acts_ref),
             (gf_hbm, gf_ref),
@@ -1617,7 +1613,7 @@
         for load in loads:
             load.start()
         p = Place(n_ctx)
-        greet(p, line=True, across=True, core=True, other=True)
+        greet(p, everyone=16, other=True)
         net = Net(p, sems)
         stores = []
 
@@ -1679,7 +1675,25 @@
             for n in range(16):
                 net.recv(lambda n=n: got_out.at[p.g ^ n], other_sems.at[n])
 
-        run_together(chain(), after(0.5, output_sum()), after(3.5, weight_grads()))
+        def send_columns():
+            keep = pltpu.make_async_copy(col_ref.at[p.g], col_out.at[p.g], net.sem())
+            keep.start()
+            for k in range(1, 16):
+                yield 44.0 + 1.5 * k
+                net.send(
+                    lambda k=k: col_ref.at[p.g ^ k],
+                    lambda: col_out.at[p.g],
+                    col_sems.at[k],
+                    lambda k=k: ((p.g ^ k) * p.members + p.m, p.t),
+                )
+            yield 82.0
+            for k in range(1, 16):
+                net.recv(lambda k=k: col_out.at[p.g ^ k], col_sems.at[k])
+            keep.wait()
+
+        run_together(
+            chain(), after(0.5, output_sum()), after(3.5, weight_grads()), after(4.0, send_columns())
+        )
         output[...] = (middle_ref[...] + residual_scale * ffn_sum[...]).astype(BF)
         for store in stores:
             store.wait()
@@ -1690,8 +1704,8 @@
         "backward",
         number,
         body,
-        [gs, ffn, ns, gf, acts, middle, out_grad, gain],
-        [ANY] * 5 + [VMEM] * 3,
+        [gs, ffn, ns, gf, acts, middle, out_grad, gain, columns],
+        [ANY] * 5 + [VMEM] * 4,
         [
             shape((rows, dim), F32),
             shape((8, dim), F32),
@@ -1699,8 +1713,9 @@
             shape((rows, dim)),
             shape(block_shape),
             shape(block_shape),
+            shape(columns.shape),
         ],
-        [VMEM, VMEM, ANY, VMEM, ANY, ANY],
+        [VMEM, VMEM, ANY, VMEM] + [ANY] * 3,
         [
             pltpu.VMEM((rows, dim), F32),
             pltpu.VMEM((rows, dim), BF),
@@ -1718,6 +1733,7 @@
             pltpu.SemaphoreType.DMA((5,)),
             pltpu.SemaphoreType.DMA((16,)),
             pltpu.SemaphoreType.DMA((16,)),
+            pltpu.SemaphoreType.DMA((16,)),
         ],
         240,
     )
@@ -1756,18 +1772,20 @@
     return jnp.where(lane < NOPE, expanded, ropes)
 
 
-def attend(number, qn, at, pairs, cosine, sine_table, q_pos, ff, width, n_ctx):
+def attend(number, qn, at, pairs, cosine, sine_table, q_pos, ff, near, width, n_ctx):
     rows, keys, heads = qn.shape[0], pairs.shape[0], at.shape[2] // 128
     span, block = keys // 4, rows // 4
     q_rows, l_rows = qn.shape[1] // 16, KVR // 16
     dim = (at.shape[1] - q_rows - l_rows) * 32
 
     def body(
-        qn_ref, at_ref, pairs_ref, cos_ref, sin_ref, pos_ref, ff_ref,
+        qn_ref, at_ref, pairs_ref, cos_ref, sin_ref, pos_ref, ff_ref, near_ref,
         branch_ref, q_ref, o_ref, lse_ref, att_ref, q_up_ref, l_up_ref, w_ref, far_ref,
+        next_out,
         e_ref, top_ref, sum_ref, acc_ref, sems,
     ):
-        copies = trade_away(Place(n_ctx), ff_ref, far_ref, sems)
+        swaps = [(near_ref.at[pl.ds(4, near.shape[0] - 4)], next_out)]
+        copies = trade_away(Place(n_ctx), ff_ref, far_ref, sems, swaps)
         unpack_heads(at_ref, q_up_ref, l_up_ref, w_ref, q_rows, l_rows)
         by_rows(
             keys,
@@ -1827,12 +1845,13 @@
             shape((KVR, wide)),
             shape((dim, width)),
             shape(ff.shape),
+            shape((near.shape[0] - 4,) + near.shape[1:]),
         ],
-        in_specs=[VMEM] * 6 + [ANY],
-        out_specs=[VMEM] * 8 + [ANY],
+        in_specs=[VMEM] * 6 + [ANY] * 2,
+        out_specs=[VMEM] * 8 + [ANY] * 2,
         scratch_shapes=[pltpu.VMEM((keys, wide), BF)]
         + [pltpu.VMEM((rows, 128), F32)] * 3
-        + [pltpu.SemaphoreType.DMA((2, len(TRADED_LAST)))],
+        + [pltpu.SemaphoreType.DMA((2, len(TRADED_LAST) + 1))],
         compiler_params=pltpu.CompilerParams(
             collective_id=number, has_side_effects=True, vmem_limit_bytes=60 << 20
         ),
@@ -1840,7 +1859,7 @@
             flops=20_000_000_000, bytes_accessed=20 << 20, transcendentals=0
         ),
         name="attend",
-    )(qn, at, pairs, cosine, sine_table, q_pos, ff)
+    )(qn, at, pairs, cosine, sine_table, q_pos, ff, near)
 
 
 def attend_back(
@@ -1857,8 +1876,8 @@
     def body(
         gb_ref, qn_ref, q_up_ref, pairs_ref, l_up_ref, w_ref, cos_ref, sin_ref, pos_ref,
         q_ref, o_ref, lse_ref, att_ref, own_ref, got_ref, half_ref,
-        gp_ref, gqn_ref, at_ref, far_ref, other_ref,
-        e_ref, rope_ref, go_ref, gq_ref, dq_ref, inner_ref, mine_ref, theirs_ref, sems, load_sems,
+        gp_ref, gqn_ref, at_ref, at_o_ref, at_o_got, far_ref, other_ref,
+        e_ref, rope_ref, go_ref, gq_ref, dq_ref, inner_ref, mine_ref, theirs_ref, sems, load_sems, at_sems,
     ):
         loads = [
             pltpu.make_async_copy(part.at[i], hold.at[k], load_sems.at[n, k])
@@ -1871,7 +1890,9 @@
             load.wait()
         for k in range(len(TRADED_LAST)):
             add_into(mine_ref.at[k], [mine_ref.at[k], theirs_ref.at[k]], unit_rows)
-        copies = trade_away(Place(n_ctx), mine_ref, far_ref, sems, (half_ref, other_ref))
+        place = Place(n_ctx)
+        owner = place.d == place.t
+        copies = trade_away(place, mine_ref, far_ref, sems, [(half_ref, other_ref)])
 
         def expand(r):
             e_ref[r] = matmul(pairs_ref[r, :KVR], l_up_ref[...]).astype(BF)
@@ -1886,9 +1907,19 @@
             part = matmul_tn(gb_ref[:, i * dim // 4 : (i + 1) * dim // 4], att_ref[...]).astype(BF)
             for k in range(8):
                 half = k % 2
-                at_ref[4 * i + k // 2, first:, half * width : (half + 1) * width] = part[
+                at_o_ref[4 * i + k // 2, :, half * width : (half + 1) * width] = part[
                     k * o_rows : (k + 1) * o_rows
                 ]
+
+        outward = pltpu.make_async_remote_copy(
+            at_o_ref,
+            at_o_got,
+            at_sems.at[0],
+            at_sems.at[1],
+            device_id=place.other(),
+            device_id_type=MESH,
+        )
+        pl.when(~owner)(lambda: outward.start())
 
         def head(h):
             lanes = lanes_of(h)
@@ -1932,22 +1963,26 @@
         gq_up = matmul_tn(qn_ref[...], gq_ref[...]).astype(BF)
         for n in range(16):
             at_ref[n, :q_rows] = gq_up[n * q_rows : (n + 1) * q_rows]
-            at_ref[n, q_rows:first] = gl_up[n * l_rows : (n + 1) * l_rows]
+            at_ref[n, q_rows:] = gl_up[n * l_rows : (n + 1) * l_rows]
         gqn_ref[...] = matmul_nt(gq_ref[...], q_up_ref[...]).astype(BF)
         for copy in copies:
             copy.wait()
+        pl.when(~owner)(lambda: outward.wait_send())
+        pl.when(owner)(lambda: outward.wait_recv())
 
     return pl.pallas_call(
         body,
         out_shape=[
             shape(pairs.shape),
             shape(qn.shape),
-            shape((16, first + o_rows, wide)),
+            shape((16, first, wide)),
+            shape((16, o_rows, wide)),
+            shape((16, o_rows, wide)),
             shape((len(TRADED_LAST),) + ff_own.shape[1:]),
             shape(half.shape),
         ],
         in_specs=[VMEM] * 13 + [ANY] * 3,
-        out_specs=[VMEM] * 3 + [ANY] * 2,
+        out_specs=[VMEM] * 4 + [ANY] * 3,
         scratch_shapes=[
             pltpu.VMEM((keys, wide), BF),
             pltpu.VMEM((keys, 128), F32),
@@ -1959,6 +1994,7 @@
             pltpu.VMEM((len(TRADED_LAST),) + ff_own.shape[1:], BF),
             pltpu.SemaphoreType.DMA((2, len(TRADED_LAST) + 1)),
             pltpu.SemaphoreType.DMA((2, len(TRADED_LAST))),
+            pltpu.SemaphoreType.DMA((2,)),
         ],
         compiler_params=pltpu.CompilerParams(
             collective_id=number, has_side_effects=True, vmem_limit_bytes=60 << 20
@@ -2026,7 +2062,6 @@
     wide = 640
     q_rows_w, l_rows_w, o_rows_w = query_up.shape[0], latent_up.shape[0], shard_rows // 2
     q_width, o_width = heads * (NOPE + ROPE), heads * VH
-    x = lax.dynamic_slice_in_dim(layer_input, t * rows, rows, 0).astype(F32)
     out_grad_rows = lax.dynamic_slice_in_dim(out_grad, t * rows, rows, 0).astype(F32)
     grad_ffn = (residual_scale * out_grad_rows).astype(BF)
 
@@ -2046,15 +2081,16 @@
 
     if members == 1:
         (
-            both, down_full, *all_gains, pairs, qn_all, token_columns,
+            both, x, down_full, *all_gains, pairs, qn_all, token_columns,
             own_near, own_mid, own_last, oth_near, at_all,
         ) = front(
-            1, x, query_down, latent_down, gains, gate_weight, up_weight, down_weight.T,
+            1, layer_input, query_down, latent_down, gains, gate_weight, up_weight, down_weight.T,
             query_up, latent_up, out_weight.T, cosine, sine_table, widths, n_ctx,
         )
         gain_first, gain_query, gain_latent, gain_second = all_gains
         first_gains = (gain_first, gain_query, gain_latent)
     else:
+        x = lax.dynamic_slice_in_dim(layer_input, t * rows, rows, 0).astype(F32)
         down_shard = jnp.concatenate(
             [
                 query_down,
@@ -2097,7 +2133,6 @@
         own_last = jnp.stack([ff[i] for i in TRADED_LAST])
         own_near, own_mid = lax.optimization_barrier((own_near, own_mid))
         oth_near = swap_tp(own_near[:4])
-    oth_next, oth_mid = swap_tp(own_near[4:]), swap_tp(own_mid)
     lat_rope = widen(pairs).reshape(-1, KVR + 128)
     if members > 1:
         at_all = widen(at_all).reshape(n_ctx, -1, wide)
@@ -2111,27 +2146,31 @@
             ],
             axis=1,
         )
-    branch_part, queries, attended_wide, log_total, attended, q_up, l_up, w_out_t, own_far = attend(
-        5, qn_all.reshape(-1, qr), at_all, lat_rope, q_cos, q_sin, q_pos, own_last, o_width, n_ctx
+    (
+        branch_part, queries, attended_wide, log_total, attended, q_up, l_up, w_out_t,
+        own_far, oth_next,
+    ) = attend(
+        5, qn_all.reshape(-1, qr), at_all, lat_rope, q_cos, q_sin, q_pos, own_last, own_near,
+        o_width, n_ctx,
     )
     qn_all = qn_all.reshape(-1, qr)
 
     order = (0,) + TRADED_FIRST + TRADED_NEXT + TRADED_LAST
     if members == 1:
         middle, ns_all, gf_all, acts, second_part, ffn_part = forward(
-            4, branch_part, x, gain_second, grad_ffn, [own_near, own_mid], [oth_near, oth_next, oth_mid],
-            own_far, order, units, n_ctx,
-        )
-        grad_middle, second_gain_part, gb_all, out_half, grads_own, grads_got = backward(
+            4, branch_part, x, gain_second, grad_ffn, [own_near], [oth_near, oth_next],
+            [own_mid, own_far], order, units, n_ctx,
+        )
+        grad_middle, second_gain_part, gb_all, out_half, grads_own, grads_got, token_columns = backward(
             6, second_part, ffn_part, ns_all, gf_all, acts, middle, out_grad_rows, gain_second,
-            units, wide, n_ctx,
+            token_columns, units, wide, n_ctx,
         )
     else:
         middle, ns_all, gf_all = branch_and_norm(
             4, branch_part, x, gain_second, grad_ffn, n_ctx
         )
         ns_all, gf_all = ns_all.reshape(-1, dim), gf_all.reshape(-1, dim)
-        oth_far = swap_tp(own_far)
+        oth_mid, oth_far = swap_tp(own_mid), swap_tp(own_far)
         own = [own_near, own_mid, own_far]
         oth = [oth_near, oth_next, oth_mid, oth_far]
         ns_all, oth = lax.optimization_barrier((ns_all, oth))
@@ -2146,24 +2185,31 @@
             6, second_part, ffn_part, middle, out_grad_rows, gain_second, n_ctx
         )
     gb_all, grads_got = lax.optimization_barrier((gb_all, grads_got))
-    grad_pairs, gqn_part, at_part, sums_far, out_other = attend_back(
+    grad_pairs, gqn_part, at_part, at_o, at_o_got, sums_far, out_other = attend_back(
         7, gb_all.reshape(-1, dim), qn_all, q_up, lat_rope, l_up, w_out_t, q_cos, q_sin, q_pos,
         queries, attended_wide, log_total, attended, grads_own, grads_got, out_half, n_ctx,
     )
     if members > 1:
         q_part = at_part[:, : qr // 16].reshape(n_ctx, q_rows_w, wide)
         l_part = at_part[:, qr // 16 : (qr + KVR) // 16].reshape(n_ctx, l_rows_w, wide)
-        o_part = at_part[:, (qr + KVR) // 16 :].reshape(16, dim // 32, 2, o_width)
-        o_part = jnp.transpose(o_part, (0, 2, 1, 3)).reshape(n_ctx, 2, o_rows_w, o_width)
-        o_part = jnp.transpose(o_part, (0, 2, 1, 3)).reshape(n_ctx, o_rows_w, wide)
         at_part = narrow(
-            jnp.concatenate([q_part, l_part, o_part], axis=1).reshape(16, members, -1, wide)
-        )
+            jnp.concatenate([q_part, l_part], axis=1).reshape(16, members, -1, wide)
+        )
+
+        def by_ctx(o_part):
+            o_part = o_part.reshape(16, dim // 32, 2, o_width)
+            o_part = jnp.transpose(o_part, (0, 2, 1, 3)).reshape(n_ctx, 2, o_rows_w, o_width)
+            o_part = jnp.transpose(o_part, (0, 2, 1, 3)).reshape(16, members, o_rows_w, wide)
+            return narrow(o_part)
+
+        at_o, at_o_got = by_ctx(at_o), by_ctx(at_o_got)
     at_sums, sums, down_sum, input_half, input_other, gain_sums = wind_up(
         8,
         narrow(grad_pairs.reshape(16, members, 2, rows, KVR + 128)),
         gqn_part.reshape(8, rows, qr),
         at_part,
+        at_o,
+        at_o_got,
         both,
         x,
         grad_middle,

time: 535 us -> 520 us (0.972)
  the two profiles are of different devices: /device:TPU:11 before, /device:TPU:3 now
where the time goes in v7:
time: 520 us; the launch traced here: 510 us
  Pallas kernels  496 us (95%)
  other arithmetic  7.1 us (1%)
  local copies, waits for them, and re-layouts  5.43 us (1%)
    pallas_call x4, Pallas kernels, comm_call(): pl.pallas_call(body, out_shape=outs, in_specs=in_specs, out_specs=out_spe...  410 us
    pallas_call x1, Pallas kernels, attend_back(): pl.pallas_call(body, out_shape=[shape(pairs.shape), shape(qn.shape), shap...  39.8 us
    pallas_call x1, Pallas kernels, attend(): pl.pallas_call(body, out_shape=[shape((rows, dim)), shape((rows, wide)),...  37.3 us

profile of v7, /device:TPU:3, one launch (start us, length us, event | category | flops | bytes accessed | tf_op | source)
XLA Modules:
  0.0 510.0 jit_solution(3975941923336189422)
XLA Ops:
  0.7 0.8 maximum_convert_fusion
  1.5 0.1 iota_add_fusion
  1.6 0.1 add.115
  1.7 0.6 broadcast_in_dim.4.gains_ref
  2.3 0.8 multiply_sine_fusion.1
  3.1 0.8 broadcast_in_dim.5.pos_ref
  3.9 1.8 multiply_convert_fusion.gf_ref
  5.7 1.8 multiply_sine_fusion
  7.5 1.9 dynamic-slice_convert_fusion.out_grad_ref
  9.3 119.2 %front.1 = (f32[64,1152]{1,0:T(8,128)}, f32[64,2560]{1,0:T(8,128)}, bf16[2560,1152]{1,0:T(8,128)(2,1)}, f32[1,2560]{1,0:T(1,128)}, f32[1,768]{1,0:T(1,128)}, /*i...) custom-call(bf16[128,2560]{1,0:T(8,128)(2,1)} %x_ref.1, ...), custom_call_target="tpu_custom_call" | custom-call | tf_op jit(solution)/shard_map/front/pallas_call | solution.py:420
  128.5 37.3 %attend.1 = (bf16[512,2560]{1,0:T(8,128)(2,1)}, bf16[512,640]{1,0:T(8,128)(2,1)}, f32[512,640]{1,0:T(8,128)}, f32[512,640]{1,0:T(8,128)}, bf16[512,320]{1,0:T(8,...) custom-call(bf16[512,768]{1,0:T(8,128)(2,1)} %bitcast.29, ...), custom_call_target="tpu_custom_call" | custom-call | flops 20000000000 | bytes 20971520 | tf_op jit(solution)/shard_map/attend/pallas_call | solution.py:1836
  165.9 85.8 %forward.1 = (f32[64,2560]{1,0:T(8,128)}, bf16[1024,2560]{1,0:T(8,128)(2,1)}, bf16[1024,2560]{1,0:T(8,128)(2,1)}, bf16[1024,1536]{1,0:T(8,128)(2,1)}, bf16[1024,...) custom-call(bf16[8,64,2560]{2,1,0:T(8,128)(2,1)} %bitcast.17, f32[64,2560]{1,0:T(8,128)} %get-tuple-element.83.x_ref, ...), custom_call_target="tpu_custom_call" | custom-call | tf_op jit(solution)/shard_map/forward/pallas_call | solution.py:420
  251.6 98.7 %backward.1 = (f32[64,2560]{1,0:T(8,128)}, f32[8,2560]{1,0:T(8,128)}, bf16[8,64,2560]{2,1,0:T(8,128)(2,1)}, bf16[64,2560]{1,0:T(8,128)(2,1)}, bf16[16,160,640]{2...) custom-call(bf16[1024,2560]{1,0:T(8,128)(2,1)} %get-tuple-element.89.gs_hbm, ...), custom_call_target="tpu_custom_call" | custom-call | tf_op jit(solution)/shard_map/backward/pallas_call | solution.py:420
  350.4 39.8 %attend_back.1 = (bf16[2048,384]{1,0:T(8,128)(2,1)}, bf16[512,768]{1,0:T(8,128)(2,1)}, bf16[16,64,640]{2,1,0:T(8,128)(2,1)}, bf16[16,80,640]{2,1,0:T(8,128)(2,1)...) custom-call(bf16[512,2560]{1,0:T(8,128)(2,1)} %bitcast.24, ...), custom_call_target="tpu_custom_call" | custom-call | flops 40000000000 | bytes 31457280 | tf_op jit(solution)/shard_map/attend_back/pallas_call | solution.py:1973
  390.2 106.0 %wind_up.1 = (bf16[4,144,640]{2,1,0:T(8,128)(2,1)}, bf16[10,160,640]{2,1,0:T(8,128)(2,1)}, f32[160,1152]{1,0:T(8,128)}, bf16[64,2560]{1,0:T(8,128)(2,1)}, bf16[64,2560]{1,0:T(8,128)(2,1)}, /*index=5*/f32[16,384]{1,0:T(8,128)}) custom-call(bf16[16,2,64,384]{3,2,1,0:T(8,128)(2,1)} %bitcast.18, bf16[8,64,768]{2,1,0:T(8,128)(2,1)} %bitcast.20, ...), custom_call_target="tpu_custom_call" | custom-call | tf_op jit(solution)/shard_map/wind_up/pallas_call | solution.py:420
  496.2 1.3 slice_bitcast_fusion
  497.5 1.3 slice_bitcast_fusion.1
  498.7 1.4 fusion.10
  500.2 9.4 %spread.1 = (bf16[128,2560]{1,0:T(8,128)(2,1)}, f32[128,2560]{1,0:T(8,128)}, f32[160,3200]{1,0:T(8,128)}, f32[160,3200]{1,0:T(8,128)}, f32[160,3200]{1,0:T(8,128...) custom-call(s32[1]{0:T(128)} %bitcast.g_ref, ...), custom_call_target="tpu_custom_call" | custom-call | flops 1000000000 | bytes 20971520 | tf_op jit(solution)/shard_map/spread/pallas_call | solution.py:820
  (4 shorter events, 0.0 us)

commit v8 on v7

--- a/solution.py
+++ b/solution.py
@@ -1201,7 +1201,7 @@
                 return block(i)
 
             out = lambda i: ff_out.at[TRADED_BACK.index(i)]
-            timed = ((8, 1), (5, 2), (9, 10), (6, 12), (12, 19), (7, 22), (1, 23), (13, 28), (11, 37))
+            timed = ((8, 1), (5, 2), (9, 6), (6, 8), (12, 12), (7, 14), (1, 15), (13, 18), (11, 24))
             for i, when_to in timed:
                 yield when_to
                 joined(i)
@@ -1679,7 +1679,7 @@
             keep = pltpu.make_async_copy(col_ref.at[p.g], col_out.at[p.g], net.sem())
             keep.start()
             for k in range(1, 16):
-                yield 44.0 + 1.5 * k
+                yield 8.0 + 1.5 * k
                 net.send(
                     lambda k=k: col_ref.at[p.g ^ k],
                     lambda: col_out.at[p.g],

time: 520 us -> 516 us (level)
  no operation moved by 1% of the time
where the time goes in v8:
time: 516 us; the launch traced here: 507 us
  Pallas kernels  493 us (96%)
  other arithmetic  7.1 us (1%)
  local copies, waits for them, and re-layouts  5.43 us (1%)
    pallas_call x4, Pallas kernels, comm_call(): pl.pallas_call(body, out_shape=outs, in_specs=in_specs, out_specs=out_spe...  405 us
    pallas_call x1, Pallas kernels, attend_back(): pl.pallas_call(body, out_shape=[shape(pairs.shape), shape(qn.shape), shap...  40.9 us
    pallas_call x1, Pallas kernels, attend(): pl.pallas_call(body, out_shape=[shape((rows, dim)), shape((rows, wide)),...  37.3 us

profile of v8, /device:TPU:3, one launch (start us, length us, event | category | flops | bytes accessed | tf_op | source)
XLA Modules:
  0.0 506.7 jit_solution(13621780498243092335)
XLA Ops:
  0.7 0.8 maximum_convert_fusion
  1.5 0.1 iota_add_fusion
  1.6 0.1 add.115
  1.7 0.6 broadcast_in_dim.4.gains_ref
  2.3 0.8 multiply_sine_fusion.1
  3.1 0.8 broadcast_in_dim.5.pos_ref
  3.9 1.8 multiply_convert_fusion.gf_ref
  5.7 1.8 multiply_sine_fusion
  7.5 1.9 dynamic-slice_convert_fusion.out_grad_ref
  9.3 119.2 %front.1 = (f32[64,1152]{1,0:T(8,128)}, f32[64,2560]{1,0:T(8,128)}, bf16[2560,1152]{1,0:T(8,128)(2,1)}, f32[1,2560]{1,0:T(1,128)}, f32[1,768]{1,0:T(1,128)}, /*i...) custom-call(bf16[128,2560]{1,0:T(8,128)(2,1)} %x_ref.1, ...), custom_call_target="tpu_custom_call" | custom-call | tf_op jit(solution)/shard_map/front/pallas_call | solution.py:420
  128.5 37.3 %attend.1 = (bf16[512,2560]{1,0:T(8,128)(2,1)}, bf16[512,640]{1,0:T(8,128)(2,1)}, f32[512,640]{1,0:T(8,128)}, f32[512,640]{1,0:T(8,128)}, bf16[512,320]{1,0:T(8,...) custom-call(bf16[512,768]{1,0:T(8,128)(2,1)} %bitcast.29, ...), custom_call_target="tpu_custom_call" | custom-call | flops 20000000000 | bytes 20971520 | tf_op jit(solution)/shard_map/attend/pallas_call | solution.py:1836
  165.9 85.8 %forward.1 = (f32[64,2560]{1,0:T(8,128)}, bf16[1024,2560]{1,0:T(8,128)(2,1)}, bf16[1024,2560]{1,0:T(8,128)(2,1)}, bf16[1024,1536]{1,0:T(8,128)(2,1)}, bf16[1024,...) custom-call(bf16[8,64,2560]{2,1,0:T(8,128)(2,1)} %bitcast.17, f32[64,2560]{1,0:T(8,128)} %get-tuple-element.83.x_ref, ...), custom_call_target="tpu_custom_call" | custom-call | tf_op jit(solution)/shard_map/forward/pallas_call | solution.py:420
  251.6 93.3 %backward.1 = (f32[64,2560]{1,0:T(8,128)}, f32[8,2560]{1,0:T(8,128)}, bf16[8,64,2560]{2,1,0:T(8,128)(2,1)}, bf16[64,2560]{1,0:T(8,128)(2,1)}, bf16[16,160,640]{2...) custom-call(bf16[1024,2560]{1,0:T(8,128)(2,1)} %get-tuple-element.89.gs_hbm, ...), custom_call_target="tpu_custom_call" | custom-call | tf_op jit(solution)/shard_map/backward/pallas_call | solution.py:420
  345.0 40.9 %attend_back.1 = (bf16[2048,384]{1,0:T(8,128)(2,1)}, bf16[512,768]{1,0:T(8,128)(2,1)}, bf16[16,64,640]{2,1,0:T(8,128)(2,1)}, bf16[16,80,640]{2,1,0:T(8,128)(2,1)...) custom-call(bf16[512,2560]{1,0:T(8,128)(2,1)} %bitcast.24, ...), custom_call_target="tpu_custom_call" | custom-call | flops 40000000000 | bytes 31457280 | tf_op jit(solution)/shard_map/attend_back/pallas_call | solution.py:1973
  385.9 107.1 %wind_up.1 = (bf16[4,144,640]{2,1,0:T(8,128)(2,1)}, bf16[10,160,640]{2,1,0:T(8,128)(2,1)}, f32[160,1152]{1,0:T(8,128)}, bf16[64,2560]{1,0:T(8,128)(2,1)}, bf16[64,2560]{1,0:T(8,128)(2,1)}, /*index=5*/f32[16,384]{1,0:T(8,128)}) custom-call(bf16[16,2,64,384]{3,2,1,0:T(8,128)(2,1)} %bitcast.18, bf16[8,64,768]{2,1,0:T(8,128)(2,1)} %bitcast.20, ...), custom_call_target="tpu_custom_call" | custom-call | tf_op jit(solution)/shard_map/wind_up/pallas_call | solution.py:420
  493.0 1.3 slice_bitcast_fusion
  494.2 1.3 slice_bitcast_fusion.1
  495.5 1.4 fusion.10
  496.9 9.4 %spread.1 = (bf16[128,2560]{1,0:T(8,128)(2,1)}, f32[128,2560]{1,0:T(8,128)}, f32[160,3200]{1,0:T(8,128)}, f32[160,3200]{1,0:T(8,128)}, f32[160,3200]{1,0:T(8,128...) custom-call(s32[1]{0:T(128)} %bitcast.g_ref, ...), custom_call_target="tpu_custom_call" | custom-call | flops 1000000000 | bytes 20971520 | tf_op jit(solution)/shard_map/spread/pallas_call | solution.py:820
  (4 shorter events, 0.0 us)
